TPU v7x, 32 devices: a whole 2x2x4 slice. The times are simulated.
32 devices in a mesh: section: 2 (over y), group: 4 (over x, core), replica: 4 (over z).
Axes of the slice: x: 2, y: 2, z: 4, core: 2. Of those that a mesh axis runs over, the one named last changes fastest.
Arguments:
- images: bfloat16 [2, 32, 197, 1024], P(None, ('group', 'replica')), may hold values from -6 to 6
- cotangent: bfloat16 [2, 32, 197, 1024], P(None, ('group', 'replica')), may hold values from -6 to 6
- counts: int32 [2, 16], P(None, ('group', 'replica')), may hold values from 1 to 2, as said below
- qkv_weight: bfloat16 [2, 1024, 3072], P('section', 'group'), may hold values from -0.1875 to 0.1875
- out_weight: bfloat16 [2, 1024, 1024], P('section', 'group'), may hold values from -0.75 to 0.75
- expand_weight: bfloat16 [2, 1024, 4096], P('section', 'group'), may hold values from -0.1875 to 0.1875
- reduce_weight: bfloat16 [2, 4096, 1024], P('section', 'group'), may hold values from -0.09375 to 0.09375
- norm_gains: bfloat16 [2, 2, 1024], P('section', None, 'group'), may hold values from 0.5 to 1.5
- biases: bfloat16 [2, 6, 1024], P('section', None, 'group'), may hold values from -3 to 3
- expand_bias: bfloat16 [2, 4096], P('section', 'group'), may hold values from -3 to 3
Outputs:
- section_outputs: bfloat16 [2, 2, 32, 197, 1024], P('section', None, ('group', 'replica'))
- input_grads: bfloat16 [2, 2, 32, 197, 1024], P('section', None, ('group', 'replica'))
- query_key_value_gradient: float32 [2, 1024, 3072], P('section', 'group')
- projection_gradient: float32 [2, 1024, 1024], P('section', 'group')
- expand_grad: float32 [2, 1024, 4096], P('section', 'group')
- reduce_grad: float32 [2, 4096, 1024], P('section', 'group')
- gain_grad: float32 [2, 2, 1024], P('section', None, 'group')
- bias_grad: float32 [2, 6, 1024], P('section', None, 'group')
- expand_bias_grad: float32 [2, 4096], P('section', 'group')
Inputs may be any that keep to these rules, and one draw needn't show every extreme that they name: counts[m, j] is how many of device j's 2 image slots in micro-batch m hold an image (the lowest ones); in every micro-batch some device has 2 and some 1.
All inputs are finite; a program needn't handle non-finite values.
Results may differ from a plain program's by a relative error of at most 0.015.
Values may be sent and summed in bfloat16 or wider, within the bound.
No kernel may reach another device: no remote copies, remote signals or barrier semaphores. Data moves between devices by JAX's collectives and lax.ppermute only.
A program may use at most 320 MiB of HBM per device.

v0:
```python
from functools import partial

import jax
import jax.numpy as jnp
from jax import lax
from jax.sharding import PartitionSpec as P

HEADS = 16


EPSILON = 1e-06


def shifted(block, axis, distance):
    devices = range(lax.axis_size(axis))
    route = [(i - distance, i) for i in devices if i - distance in devices]
    return lax.ppermute(block, axis, route)


def normalize(values, gain, shift):
    center = values - jnp.mean(values, axis=-1, keepdims=True)
    spread = jnp.mean(center * center, axis=-1, keepdims=True)
    return center * lax.rsqrt(spread + EPSILON) * gain + shift


def split_heads(packed):
    count, length, triple = packed.shape
    width = triple // 3
    shaped = packed.reshape(count, length, 3, HEADS, width // HEADS)
    return (shaped[:, :, 0], shaped[:, :, 1], shaped[:, :, 2])


def layer_forward(inputs, alive, weights):
    (
        query_key_value_weight,
        projection_weight,
        expansion_weight,
        contraction_weight,
        gain_rows,
        bias_broadcast,
        exp_b,
    ) = weights
    gain_rows = gain_rows.astype(jnp.float32)
    bias_broadcast = bias_broadcast.astype(jnp.float32)
    count, length, width = inputs.shape
    scale = (width // HEADS) ** (-0.5)
    normalized_input = normalize(inputs, gain_rows[0], bias_broadcast[0]).astype(jnp.bfloat16)
    query_key_value_bias = jnp.concatenate(
        [bias_broadcast[2], jnp.zeros_like(bias_broadcast[2]), bias_broadcast[3]]
    )
    packed = (
        jnp.einsum(
            "qjx,xi->qji",
            normalized_input,
            query_key_value_weight,
            preferred_element_type=jnp.float32,
        )
        + query_key_value_bias
    ).astype(jnp.bfloat16)
    queries, key_rows, value_rows = split_heads(packed)
    scores = (
        jnp.einsum("sqhe,skhe->shqk", queries, key_rows, preferred_element_type=jnp.float32) * scale
    )
    peak = jnp.max(scores, axis=-1, keepdims=True)
    raised = jnp.exp(scores - peak)
    summed = jnp.sum(raised, axis=-1, keepdims=True)
    log_total = peak + jnp.log(summed)
    attend = (raised / summed).astype(jnp.bfloat16)
    attended_output = jnp.einsum(
        "shqk,skhe->sqhe", attend, value_rows, preferred_element_type=jnp.float32
    )
    attended_output = attended_output.reshape(count, length, width).astype(jnp.bfloat16)
    middle = (
        inputs
        + jnp.einsum(
            "qjx,xi->qji", attended_output, projection_weight, preferred_element_type=jnp.float32
        )
        + bias_broadcast[4]
    )
    second_residual = normalize(middle, gain_rows[1], bias_broadcast[1]).astype(jnp.bfloat16)
    hidden = jnp.einsum(
        "cje,en->cjn", second_residual, expansion_weight, preferred_element_type=jnp.float32
    ) + exp_b.astype(jnp.float32)
    activated_hidden = jax.nn.gelu(hidden, approximate=False).astype(jnp.bfloat16)
    feed = (
        jnp.einsum(
            "mzv,va->mza", activated_hidden, contraction_weight, preferred_element_type=jnp.float32
        )
        + bias_broadcast[5]
    )
    result = (middle + feed) * alive[:, None, None]
    return (
        result,
        (
            inputs,
            normalized_input,
            packed,
            log_total,
            attended_output,
            middle,
            second_residual,
            hidden,
        ),
    )


def layer_backward(upstream, alive, kept, weights):
    (
        query_key_value_weight,
        projection_weight,
        expansion_weight,
        contraction_weight,
        gain_rows,
        bias_broadcast,
        exp_b,
    ) = weights
    gain_rows = gain_rows.astype(jnp.float32)
    bias_broadcast = bias_broadcast.astype(jnp.float32)
    (
        inputs,
        normalized_input,
        packed,
        log_total,
        attended_output,
        middle,
        second_residual,
        hidden,
    ) = kept
    count, length, width = inputs.shape
    scale = (width // HEADS) ** (-0.5)
    upstream = upstream * alive[:, None, None]
    feedforward_gradient = upstream.astype(jnp.bfloat16)
    activated_hidden = jax.nn.gelu(hidden, approximate=False).astype(jnp.bfloat16)
    contraction_gradient = jnp.einsum(
        "cpn,cpu->nu", activated_hidden, feedforward_gradient, preferred_element_type=jnp.float32
    )
    red_bias = jnp.sum(feedforward_gradient.astype(jnp.float32), axis=(0, 1))
    activated_gradient = jnp.einsum(
        "vpm,tm->vpt", feedforward_gradient, contraction_weight, preferred_element_type=jnp.float32
    )
    unused, gelu_pull = jax.vjp(partial(jax.nn.gelu, approximate=False), hidden)
    hidden_state_gradient = gelu_pull(activated_gradient)[0].astype(jnp.bfloat16)
    expansion_gradient = jnp.einsum(
        "zje,zjh->eh", second_residual, hidden_state_gradient, preferred_element_type=jnp.float32
    )
    exp_bias = jnp.sum(hidden_state_gradient.astype(jnp.float32), axis=(0, 1))
    second_residual_gradient = jnp.einsum(
        "pgh,jh->pgj", hidden_state_gradient, expansion_weight, preferred_element_type=jnp.float32
    )
    unused, norm_pull = jax.vjp(normalize, middle, gain_rows[1], bias_broadcast[1])
    middle_part, gain_two, shift_two = norm_pull(second_residual_gradient)
    middle_grad = upstream + middle_part
    residual_branch_gradient = middle_grad.astype(jnp.bfloat16)
    projection_gradient = jnp.einsum(
        "pch,pcq->hq", attended_output, residual_branch_gradient, preferred_element_type=jnp.float32
    )
    out_bias = jnp.sum(residual_branch_gradient.astype(jnp.float32), axis=(0, 1))
    attended_gradient = jnp.einsum(
        "wnp,qp->wnq",
        residual_branch_gradient,
        projection_weight,
        preferred_element_type=jnp.float32,
    )
    attended_gradient = attended_gradient.astype(jnp.bfloat16).reshape(
        count, length, HEADS, width // HEADS
    )
    queries, key_rows, value_rows = split_heads(packed)
    scores = (
        jnp.einsum("sqhe,skhe->shqk", queries, key_rows, preferred_element_type=jnp.float32) * scale
    )
    chance = jnp.exp(scores - log_total)
    value_grad = jnp.einsum(
        "shqk,sqhe->skhe",
        chance.astype(jnp.bfloat16),
        attended_gradient,
        preferred_element_type=jnp.float32,
    )
    chance_grad = jnp.einsum(
        "sqhe,skhe->shqk", attended_gradient, value_rows, preferred_element_type=jnp.float32
    )
    score_grad = chance * (chance_grad - jnp.sum(chance_grad * chance, axis=-1, keepdims=True))
    score_grad = score_grad.astype(jnp.bfloat16)
    query_grad = (
        jnp.einsum("shqk,skhe->sqhe", score_grad, key_rows, preferred_element_type=jnp.float32)
        * scale
    )
    key_grad = (
        jnp.einsum("shqk,sqhe->skhe", score_grad, queries, preferred_element_type=jnp.float32)
        * scale
    )
    stacked_gradient = jnp.concatenate(
        [
            query_grad.reshape(count, length, width),
            key_grad.reshape(count, length, width),
            value_grad.reshape(count, length, width),
        ],
        axis=-1,
    ).astype(jnp.bfloat16)
    query_key_value_gradient = jnp.einsum(
        "pch,pcq->hq", normalized_input, stacked_gradient, preferred_element_type=jnp.float32
    )
    packed_sum = jnp.sum(stacked_gradient.astype(jnp.float32), axis=(0, 1))
    normalized_gradient = jnp.einsum(
        "wnp,qp->wnq", stacked_gradient, query_key_value_weight, preferred_element_type=jnp.float32
    )
    unused, first_pull = jax.vjp(normalize, inputs, gain_rows[0], bias_broadcast[0])
    input_part, gain_one, shift_one = first_pull(normalized_gradient)
    input_grad = middle_grad + input_part
    gain_grad = jnp.stack([gain_one, gain_two])
    bias_grad = jnp.stack(
        [shift_one, shift_two, packed_sum[:width], packed_sum[2 * width :], out_bias, red_bias]
    )
    return (
        input_grad,
        (
            query_key_value_gradient,
            projection_gradient,
            expansion_gradient,
            contraction_gradient,
            gain_grad,
            bias_grad,
            exp_bias,
        ),
    )


def per_device(
    images,
    cotangent,
    counts,
    qkv_weight,
    out_weight,
    expand_weight,
    reduce_weight,
    norm_gains,
    biases,
    expand_bias,
):
    micro = images.shape[0]
    slots = images.shape[1]
    first = lax.axis_index("section") == 0
    alive_all = (jnp.arange(slots)[None, :] < counts).astype(jnp.float32)
    shards = (
        qkv_weight[0],
        out_weight[0],
        expand_weight[0],
        reduce_weight[0],
        norm_gains[0],
        biases[0],
        expand_bias[0],
    )
    forward_weights = (
        lax.all_gather(shards[0], "group", axis=0, tiled=True),
        lax.all_gather(shards[1], "group", axis=0, tiled=True),
        lax.all_gather(shards[2], "group", axis=0, tiled=True),
        lax.all_gather(shards[3], "group", axis=0, tiled=True),
        lax.all_gather(shards[4], "group", axis=1, tiled=True),
        lax.all_gather(shards[5], "group", axis=1, tiled=True),
        lax.all_gather(shards[6], "group", axis=0, tiled=True),
    )
    incoming = jnp.zeros(images.shape[1:], jnp.bfloat16)
    results = []
    kept_all = []
    alive_list = []
    for tick in range(micro + 1):
        source = images[min(tick, micro - 1)].astype(jnp.float32)
        inputs = jnp.where(first, source, incoming.astype(jnp.float32))
        alive = jnp.where(first, alive_all[min(tick, micro - 1)], alive_all[max(tick - 1, 0)])
        result, kept = layer_forward(inputs, alive, forward_weights)
        result = result.astype(jnp.bfloat16)
        results.append(result)
        kept_all.append(kept)
        alive_list.append(alive)
        if tick < micro:
            incoming = shifted(result, "section", 1)
    section_outputs = jnp.stack(
        [jnp.where(first, results[index], results[index + 1]) for index in range(micro)]
    )[None]
    backward_weights = (
        lax.all_gather(shards[0], "group", axis=0, tiled=True),
        lax.all_gather(shards[1], "group", axis=0, tiled=True),
        lax.all_gather(shards[2], "group", axis=0, tiled=True),
        lax.all_gather(shards[3], "group", axis=0, tiled=True),
        lax.all_gather(shards[4], "group", axis=1, tiled=True),
        lax.all_gather(shards[5], "group", axis=1, tiled=True),
        lax.all_gather(shards[6], "group", axis=0, tiled=True),
    )
    totals = None
    returning = jnp.zeros(images.shape[1:], jnp.bfloat16)
    sent = []
    for tick in range(micro + 1):
        lower = max(tick - 1, 0)
        upper = min(tick + 1, micro)
        kept = jax.tree.map(partial(jnp.where, first), kept_all[lower], kept_all[upper])
        alive = jnp.where(first, alive_list[lower], alive_list[upper])
        target = cotangent[min(tick, micro - 1)].astype(jnp.float32) * (
            1.0 if tick < micro else 0.0
        )
        upstream = jnp.where(first, returning.astype(jnp.float32), target)
        input_grad, grads = layer_backward(upstream, alive, kept, backward_weights)
        totals = grads if totals is None else jax.tree.map(jnp.add, totals, grads)
        input_grad = input_grad.astype(jnp.bfloat16)
        sent.append(input_grad)
        if tick < micro:
            returning = shifted(input_grad, "section", -1)
    input_grads = jnp.stack(
        [jnp.where(first, sent[index + 1], sent[index]) for index in range(micro)]
    )[None]
    qkv_sum, out_sum, exp_sum, red_sum, gain_sum, bias_sum, bias_expand = totals
    owned = (
        lax.psum_scatter(
            qkv_sum.astype(jnp.bfloat16), "group", scatter_dimension=0, tiled=True
        ).astype(jnp.float32),
        lax.psum_scatter(
            out_sum.astype(jnp.bfloat16), "group", scatter_dimension=0, tiled=True
        ).astype(jnp.float32),
        lax.psum_scatter(
            exp_sum.astype(jnp.bfloat16), "group", scatter_dimension=0, tiled=True
        ).astype(jnp.float32),
        lax.psum_scatter(
            red_sum.astype(jnp.bfloat16), "group", scatter_dimension=0, tiled=True
        ).astype(jnp.float32),
        lax.psum_scatter(
            gain_sum.astype(jnp.bfloat16), "group", scatter_dimension=1, tiled=True
        ).astype(jnp.float32),
        lax.psum_scatter(
            bias_sum.astype(jnp.bfloat16), "group", scatter_dimension=1, tiled=True
        ).astype(jnp.float32),
        lax.psum_scatter(
            bias_expand.astype(jnp.bfloat16), "group", scatter_dimension=0, tiled=True
        ).astype(jnp.float32),
    )
    reduced = (
        lax.psum(owned[0].astype(jnp.bfloat16), "replica").astype(jnp.float32),
        lax.psum(owned[1].astype(jnp.bfloat16), "replica").astype(jnp.float32),
        lax.psum(owned[2].astype(jnp.bfloat16), "replica").astype(jnp.float32),
        lax.psum(owned[3].astype(jnp.bfloat16), "replica").astype(jnp.float32),
        lax.psum(owned[4].astype(jnp.bfloat16), "replica").astype(jnp.float32),
        lax.psum(owned[5].astype(jnp.bfloat16), "replica").astype(jnp.float32),
        lax.psum(owned[6].astype(jnp.bfloat16), "replica").astype(jnp.float32),
    )
    return (
        section_outputs,
        input_grads,
        reduced[0][None],
        reduced[1][None],
        reduced[2][None],
        reduced[3][None],
        reduced[4][None],
        reduced[5][None],
        reduced[6][None],
    )


def solution(mesh):
    placed = (
        P(None, ("group", "replica"), None, None),
        P(None, ("group", "replica"), None, None),
        P(None, ("group", "replica")),
        P("section", "group", None),
        P("section", "group", None),
        P("section", "group", None),
        P("section", "group", None),
        P("section", None, "group"),
        P("section", None, "group"),
        P("section", "group"),
    )
    return jax.shard_map(
        per_device,
        mesh=mesh,
        in_specs=placed,
        out_specs=(
            P("section", None, ("group", "replica"), None, None),
            P("section", None, ("group", "replica"), None, None),
            P("section", "group", None),
            P("section", "group", None),
            P("section", "group", None),
            P("section", "group", None),
            P("section", None, "group"),
            P("section", None, "group"),
            P("section", "group"),
        ),
        check_vma=False,
    )
```

profile of v0, /device:TPU:0, one launch (start us, length us, event | category | flops | bytes accessed | tf_op | source)
XLA Modules:
  0.0 1207.3 jit_solution(3661839280086478320)
XLA Ops:
  31.3 27.5 %all-gather.12.cloned.1.call-done = bf16[1,1024,3072]{2,1,0:T(8,128)(2,1)} async-done(((bf16[1,256,3072]{2,1,0:T(8,128)(2,1)}), bf16[1,1024,3072]{2,1,0:T(8,128)(2,1)}) %all-gather.12.cloned.1.call-update) | async-done | bytes 6291472 | tf_op jit(solution)/shard_map/all_gather | solution.py:253
  87.9 55.0 %all-gather.16.cloned.1.call-done = bf16[1,1024,4096]{2,1,0:T(8,128)(2,1)} async-done(((bf16[1,256,4096]{2,1,0:T(8,128)(2,1)}), bf16[1,1024,4096]{2,1,0:T(8,128)(2,1)}) %all-gather.16.cloned.1.call-update) | async-done | bytes 8388624 | tf_op jit(solution)/shard_map/all_gather | solution.py:255
  142.9 14.0 %fusion.252 = (u8[197,4096]{1,0:T(8,128)(4,1)}, u8[197,4096]{1,0:T(8,128)(4,1)}, f32[2,197,4096]{2,1,0:T(8,128)}) fusion(f32[4096]{0:T(1024)S(1)} %bitcast.630, bf16[2,197,1024]{2,1,0:T(8,128)(2,1)} %add_convert_fusion.13, bf16[1,1024,4096]{2,1,0:T(8,128)(2,1)} %all-gather.16.cloned.1.call-done), kind=kOutput, calls=%fused_computation.419 | convolution fusion | flops 3326091264 | bytes 17281024 | tf_op jit(solution)/shard_map/cje,en->cjn/dot_general | solution.py:81
  156.9 45.7 %all-gather.18.cloned.1.call-done = bf16[1,4096,1024]{2,1,0:T(8,128)(2,1)} async-done(((bf16[1,1024,1024]{2,1,0:T(8,128)(2,1)}), bf16[1,4096,1024]{2,1,0:T(8,128)(2,1)}) %all-gather.18.cloned.1.call-update) | async-done | bytes 8388624 | tf_op jit(solution)/shard_map/all_gather | solution.py:256
  202.6 20.4 %multiply_convert_fusion.17 = bf16[2,197,1024]{2,1,0:T(8,128)(2,1)S(1)} fusion(f32[2,197,1024]{2,1,0:T(8,128)S(1)} %get-tuple-element.169, bf16[1,4096,1024]{2,1,0:T(8,128)(2,1)} %all-gather.18.cloned.1.call-done, f32[2,197,4096]{2,1,0:T(8,128)} %get-tuple-element.170, u8[197,4096]{1,0:T(8,128)(4,1)} %get-tuple-element.41, ...), kind=kOutput, calls=%fused_computation.406 | convolution fusion | flops 3419693056 | bytes 18882568 | tf_op jit(solution)/shard_map/mzv,va->mza/dot_general | solution.py:86
  227.9 17.0 %collective-permute-done = bf16[2,197,1024]{2,0,1:T(2,128)(2,1)S(1)} collective-permute-done((bf16[2,197,1024]{2,0,1:T(2,128)(2,1)S(1)}, bf16[2,197,1024]{2,0,1:T(2,128)(2,1)S(1)}, u32[]{:S(2)}, u32[]{:S(2)}) %collective-permute-start) | collective-permute-done | bytes 806944 | tf_op jit(solution)/shard_map/ppermute | solution.py:17
  275.1 22.8 %multiply_convert_fusion.16 = bf16[2,197,1024]{2,1,0:T(8,128)(2,1)S(1)} fusion(f32[2,197,1024]{2,1,0:T(8,128)S(1)} %get-tuple-element.174, bf16[1,4096,1024]{2,1,0:T(8,128)(2,1)S(1)} %bitcast.652, f32[2,197,4096]{2,1,0:T(8,128)} %get-tuple-element.175, u8[197,4096]{1,0:T(8,128)(4,1)S(1)} %get-tuple-element.39, u8[197,4096]{1,0:T(8,128)(4,1)S(1)} %get-tuple-element.38, ...), kind=kOutput, calls=%fused_computation.400 | convolution fusion | flops 3419693056 | bytes 18882568 | tf_op jit(solution)/shard_map/mzv,va->mza/dot_general | solution.py:86
  312.4 9.6 collective-permute-done.1
  329.2 10.2 broadcast_select_fusion.3
  359.2 26.3 %fusion.251 = (u8[197,4096]{1,0:T(8,128)(4,1)}, f32[2,197,4096]{2,1,0:T(8,128)}, u8[197,4096]{1,0:T(8,128)(4,1)}, f32[2,197,4096]{2,1,0:T(8,128)}, u8[197,4096]{...) fusion(f32[2,197,4096]{2,1,0:T(8,128)} %get-tuple-element.175, ...), kind=kOutput, calls=%fused_computation.418 | convolution fusion | flops 3362402304 | bytes 51978240 | tf_op jit(solution)/shard_map/cje,en->cjn/dot_general | solution.py:81
  385.6 15.2 %fusion.36 = f32[2,197,4096]{2,1,0:T(8,128)S(1)} fusion(f32[2,197,4096]{2,1,0:T(8,128)} %get-tuple-element.112, u8[197,4096]{1,0:T(8,128)(4,1)S(1)} %get-tuple-element.111), kind=kLoop, calls=%fused_computation.48 | loop fusion | flops 104898560 | bytes 13717504 | tf_op jit(solution)/shard_map/jvp()/erfc | solution.py:141
  400.8 15.4 %convert_reduce_fusion.2 = (f32[4096]{0:T(1024)}, bf16[2,197,4096]{2,1,0:T(8,128)(2,1)}) fusion(f32[2,197,4096]{2,1,0:T(8,128)S(1)} %fusion.36, f32[2,197,4096]{2,1,0:T(8,128)S(1)} %copy-done, bf16[1,4096,1024]{2,1,0:T(8,128)(2,1)} %all-gather.18.cloned.1.call-done, f32[2]{0:T(128)S(1)} %get-tuple-element.161, pred[]{:T(512)S(6)} %eq.3, ...), kind=kOutput, calls=%fused_computation.72 | convolution fusion | flops 3332542464 | bytes 25350152 | tf_op jit(solution)/shard_map/vpm,tm->vpt/dot_general | solution.py:138
  494.8 14.8 %fusion.37 = f32[2,197,4096]{2,1,0:T(8,128)} fusion(f32[2,197,4096]{2,1,0:T(8,128)S(1)} %bitcast.532, u8[197,4096]{1,0:T(8,128)(4,1)S(1)} %copy-done.72), kind=kLoop, calls=%fused_computation.49 | loop fusion | flops 104898560 | bytes 13717504 | tf_op jit(solution)/shard_map/jvp()/erfc | solution.py:141
  515.8 11.1 fusion.340
  529.1 13.0 %convert_reduce_fusion.1 = (f32[4096]{0:T(1024)}, bf16[2,197,4096]{2,1,0:T(8,128)(2,1)S(1)}) fusion(f32[2,197,4096]{2,1,0:T(8,128)} %fusion.37, f32[2,197,4096]{2,1,0:T(8,128)S(1)} %bitcast.534, bf16[2,197,1024]{2,1,0:T(8,128)(2,1)S(1)} %get-tuple-element.78, bf16[1,4096,1024]{2,1,0:T(8,128)(2,1)} %all-gather.18.cloned.1.call-done), kind=kOutput, calls=%fused_computation.71 | convolution fusion | flops 3330928640 | bytes 25350144 | tf_op jit(solution)/shard_map/vpm,tm->vpt/dot_general | solution.py:138
  599.3 10.1 fusion.338
  609.3 8.3 collective-permute-done.3
  618.8 21.8 %convert_reduce_fusion = (f32[4096]{0:T(1024)}, bf16[2,197,4096]{2,1,0:T(8,128)(2,1)S(1)}) fusion(u8[197,4096]{1,0:T(8,128)(4,1)S(1)} %copy-done.130, f32[2,197,4096]{2,1,0:T(8,128)} %get-tuple-element.94, bf16[2,197,1024]{2,1,0:T(8,128)(2,1)S(1)} %get-tuple-element.84, bf16[1,4096,1024]{2,1,0:T(8,128)(2,1)S(1)} %bitcast.654), kind=kOutput, calls=%fused_computation.70 | convolution fusion | flops 3429371904 | bytes 19701760 | tf_op jit(solution)/shard_map/vpm,tm->vpt/dot_general | solution.py:138
  668.6 8.5 multiply_reduce_fusion
  695.2 16.0 %fusion.2 = bf16[1024,3072]{1,0:T(8,128)(2,1)} fusion(f32[1024,3072,1]{1,0,2:T(8,128)} %fusion.338, f32[1024,3072,1]{1,0,2:T(8,128)} %fusion.340, pred[]{:T(512)S(6)} %eq.3, bf16[2,197,1024]{2,1,0:T(8,128)(2,1)S(1)} %copy-done.41, bf16[2,197,1024]{2,1,0:T(8,128)(2,1)} %copy.199, bf16[2,197,1024]{2,1,0:T(8,128)(2,1)} %copy.198, f32[2,197]{1,0:T(2,128)S(1)} %copy-done.101, ...), kind=kOutput, calls=%fused_computation.7 | convolution fusion | flops 2501988352 | bytes 36313248 | tf_op jit(solution)/shard_map/pch,pcq->hq/dot_general | solution.py:199
  711.5 14.3 %fusion.330 = f32[1024,4096,1]{1,0,2:T(8,128)} fusion(bf16[2,197,4096]{2,1,0:T(8,128)(2,1)} %get-tuple-element.197, bf16[2,197,1024]{2,1,0:T(8,128)(2,1)} %add_convert_fusion.13, bf16[2,197,1024]{2,1,0:T(8,128)(2,1)} %copy-done.49, pred[]{:T(512)S(6)} %eq.3), kind=kOutput, calls=%fused_computation.479 | convolution fusion | flops 3305515008 | bytes 21618688 | tf_op jit(solution)/shard_map/zje,zjh->eh/dot_general | solution.py:143
  725.8 8.8 fusion.328
  734.6 17.6 %fusion.1 = bf16[1024,4096]{1,0:T(8,128)(2,1)} fusion(f32[1024,4096,1]{1,0,2:T(8,128)} %fusion.328, f32[1024,4096,1]{1,0,2:T(8,128)} %fusion.330, bf16[2,197,4096]{2,1,0:T(8,128)(2,1)} %copy-done.61, bf16[2,197,1024]{2,1,0:T(8,128)(2,1)S(1)} %copy-done.50, bf16[2,197,1024]{2,1,0:T(8,128)(2,1)S(1)} %copy-done.48, pred[]{:T(512)S(6)} %eq.3), kind=kOutput, calls=%fused_computation.4 | convolution fusion | flops 3318097920 | bytes 46784512 | tf_op jit(solution)/shard_map/zje,zjh->eh/dot_general | solution.py:143
  753.3 13.2 %fusion.121 = f32[4096,1024,1]{1,0,2:T(8,128)} fusion(f32[2,197,4096]{2,1,0:T(8,128)} %copy-done.1, f32[2,197,4096]{2,1,0:T(8,128)} %get-tuple-element.112, f32[2]{0:T(128)S(1)} %copy-done.108, pred[]{:T(512)S(6)} %eq.3, bf16[1,2,197,1024]{3,1,2,0:T(2,128)(2,1)S(1)} %copy-done.30), kind=kOutput, calls=%fused_computation.208 | convolution fusion | flops 3311566848 | bytes 30494728 | tf_op jit(solution)/shard_map/cpn,cpu->nu/dot_general | solution.py:134
  766.5 14.9 %fusion.122 = f32[4096,1024,1]{1,0,2:T(8,128)} fusion(bf16[2,197,1024]{2,1,0:T(8,128)(2,1)S(1)} %copy-done.52, f32[2,197,4096]{2,1,0:T(8,128)} %fusion.37, f32[2,197,4096]{2,1,0:T(8,128)} %get-tuple-element.110), kind=kOutput, calls=%fused_computation.209 | convolution fusion | flops 3309953024 | bytes 30494720 | tf_op jit(solution)/shard_map/cpn,cpu->nu/dot_general | solution.py:134
  781.4 29.8 %fusion = bf16[4096,1024]{1,0:T(8,128)(2,1)} fusion(f32[4096,1024,1]{1,0,2:T(8,128)} %fusion.122, f32[4096,1024,1]{1,0,2:T(8,128)} %fusion.121, bf16[2,197,1024]{2,1,0:T(8,128)(2,1)S(1)} %copy-done.71, f32[2,197,4096]{2,1,0:T(8,128)} %get-tuple-element.94, u8[197,4096]{1,0:T(8,128)(4,1)S(1)} %copy-done.131), kind=kOutput, calls=%fused_computation.1 | convolution fusion | flops 3427434496 | bytes 50012160 | tf_op jit(solution)/shard_map/cpn,cpu->nu/dot_general | solution.py:134
  829.0 14.2 %reduce-scatter.13.cloned.1.call-done = bf16[256,4096]{1,0:T(8,128)(2,1)} async-done(((bf16[1024,4096]{1,0:T(8,128)(2,1)}), bf16[256,4096]{1,0:T(8,128)(2,1)}) %reduce-scatter.13.cloned.1.call-update) | async-done | bytes 2097168 | tf_op jit(solution)/shard_map/reduce_scatter | solution.py:317
  843.3 74.5 %reduce-scatter.15.cloned.1.call-done = bf16[1024,1024]{1,0:T(8,128)(2,1)} async-done(((bf16[4096,1024]{1,0:T(8,128)(2,1)}), bf16[1024,1024]{1,0:T(8,128)(2,1)}) %reduce-scatter.15.cloned.1.call-update) | async-done | bytes 2097168 | tf_op jit(solution)/shard_map/reduce_scatter | solution.py:320
  919.1 20.6 %fusion.304 = bf16[1,2,197,1024]{3,2,1,0:T(8,128)(2,1)S(1)} fusion(bf16[2,197,1024]{2,1,0:T(8,128)(2,1)} %copy-done.59, f32[2,197,1024]{2,1,0:T(8,128)S(1)} %copy-done.47, bf16[1,4096,1024]{2,1,0:T(8,128)(2,1)} %all-gather.18.cloned.1.call-done, f32[2,197,4096]{2,1,0:T(8,128)} %get-tuple-element.180, u8[197,4096]{1,0:T(8,128)(4,1)} %get-tuple-element.113, ...), kind=kOutput, calls=%fused_computation.437 | convolution fusion | flops 3420096512 | bytes 19689480 | tf_op jit(solution)/shard_map/mzv,va->mza/dot_general | solution.py:86
  953.2 10.0 reduce-scatter.17.cloned.1.call-done
  963.9 22.3 %all-reduce.1 = (bf16[1,2,256]{2,1,0:T(2,128)(2,1)S(1)}, bf16[1,6,256]{2,0,1:T(2,128)(2,1)S(1)}, bf16[1,1024]{1,0:T(2,128)(2,1)S(1)}) all-reduce(bf16[1,2,256]{2,1,0:T(2,128)(2,1)S(1)} %bitcast.637, bf16[1,6,256]{2,0,1:T(2,128)(2,1)S(1)} %broadcast_in_dim.154, ...), channel_id=1, replica_groups=mesh['section'=2,'group'=4,'replica'=4] {'replica'}, use_global_device_ids=true, to_apply=%region_60.61 | all-reduce | flops 3072 | bytes 12288 | tf_op jit(solution)/shard_map/psum | solution.py:338
  988.0 201.9 %all-reduce.5.cloned.1.call-done = (bf16[1,256,3072]{2,1,0:T(8,128)(2,1)}, bf16[1,256,1024]{2,1,0:T(8,128)(2,1)}, bf16[1,256,4096]{2,1,0:T(8,128)(2,1)}, bf16[1,1024,1024]{2,1,0:T(8,128)(2,1)}) async-done(((bf16[1,256,3072]{2,1,0:T(8,128)(2,1)}, bf16[1,256,1024]{2,1,0:T(8,128)(2,1)}, bf16[1,256,4096]{2,1,0:T(8,128)(2,1)}, bf16[1,1024,1024]{2,1,0:T(8,128)(2,1)}), (bf16[1,256,3072]{2,1,0:T(8,128)(2,1)}, ...) | async-done | bytes 6291472 | tf_op jit(solution)/shard_map/psum | solution.py:334
  (501 shorter events, 366.1 us)
Async XLA Ops:
  7.2 23.5 %copy-start.126 = (s32[2,1]{0,1:T(1,128)S(1)}, s32[2,1]{0,1:T(1,128)}, u32[]{:S(2)}) copy-start(s32[2,1]{0,1:T(1,128)} %param.12) | copy-start | bytes 28
  7.2 51.6 %all-gather.12.cloned.1.call-start = ((), (), s32[]{:S(2)}) async-start(), calls=%async_computation.11 | async-start | bytes 7864320 | tf_op jit(solution)/shard_map/all_gather | solution.py:253
  7.9 75.0 %all-gather.14.cloned.1.call-start = ((), (), s32[]{:S(2)}) async-start(), calls=%async_computation.12 | async-start | bytes 2621440 | tf_op jit(solution)/shard_map/all_gather | solution.py:254
  8.7 134.2 %all-gather.16.cloned.1.call-start = ((), (), s32[]{:S(2)}) async-start(), calls=%async_computation.13 | async-start | bytes 10485760 | tf_op jit(solution)/shard_map/all_gather | solution.py:255
  9.4 193.2 %all-gather.18.cloned.1.call-start = ((), (), s32[]{:S(2)}) async-start(), calls=%async_computation.14 | async-start | bytes 10485760 | tf_op jit(solution)/shard_map/all_gather | solution.py:256
  10.0 819.0 %reduce-scatter.11.cloned.1.call-start = ((), (), s32[]{:S(2)}) async-start(), calls=%async_computation.7 | async-start | bytes 2621440 | tf_op jit(solution)/shard_map/reduce_scatter | solution.py:314
  27.2 247.8 %copy-start.116 = (f32[1,1,1024]{2,1,0:T(1,128)}, f32[1,1,1024]{2,1,0:T(1,128)S(1)}, u32[]{:S(2)}) copy-start(f32[1,1,1024]{2,1,0:T(1,128)S(1)} %get-tuple-element.136) | copy-start | bytes 12292
  29.8 36.1 %copy-start.31 = (bf16[1,2,197,1024]{3,1,2,0:T(2,128)(2,1)}, bf16[1,2,197,1024]{3,1,2,0:T(2,128)(2,1)S(1)}, u32[]{:S(2)}) copy-start(bf16[1,2,197,1024]{3,1,2,0:T(2,128)(2,1)S(1)} %get-tuple-element.131) | copy-start | bytes 2420740
  30.2 35.7 %copy-start.102 = (f32[2,197]{1,0:T(2,128)}, f32[2,197]{1,0:T(2,128)S(1)}, u32[]{:S(2)}) copy-start(f32[2,197]{1,0:T(2,128)S(1)} %broadcast_multiply_fusion.11) | copy-start | bytes 4732
  31.3 34.6 %copy-start.119 = (f32[2,197]{1,0:T(2,128)}, f32[2,197]{1,0:T(2,128)S(1)}, u32[]{:S(2)}) copy-start(f32[2,197]{1,0:T(2,128)S(1)} %add_rsqrt_fusion.5) | copy-start | bytes 4732
  31.3 663.9 %copy-start.76 = (f32[1,1,1024]{2,1,0:T(1,128)}, f32[1,1,1024]{2,1,0:T(1,128)S(1)}, u32[]{:S(2)}) copy-start(f32[1,1,1024]{2,1,0:T(1,128)S(1)} %get-tuple-element.149) | copy-start | bytes 12292
  223.0 21.9 %copy-start.58 = (bf16[2,197,1024]{2,1,0:T(8,128)(2,1)}, bf16[2,197,1024]{2,1,0:T(8,128)(2,1)S(1)}, u32[]{:S(2)}) copy-start(bf16[2,197,1024]{2,1,0:T(8,128)(2,1)S(1)} %multiply_convert_fusion.17) | copy-start | bytes 2420740
  223.8 21.0 %collective-permute-start = (bf16[2,197,1024]{2,0,1:T(2,128)(2,1)S(1)}, bf16[2,197,1024]{2,0,1:T(2,128)(2,1)S(1)}, u32[]{:S(2)}, u32[]{:S(2)}) collective-permute-start(bf16[2,197,1024]{2,0,1:T(2,128)(2,1)S(1)} %copy.146), channel_id=1, source_target_pairs={{0,16},{1,17},{2,18},{3,19},{4,20},{5,21},{6,22},{7,23},{8,24},{9,... | collective-permute-start | bytes 2420744 | tf_op jit(solution)/shard_map/ppermute | solution.py:17
  227.9 241.8 %copy-start.107 = (f32[2]{0:T(128)}, f32[2]{0:T(128)S(1)}, u32[]{:S(2)}) copy-start(f32[2]{0:T(128)S(1)} %get-tuple-element.161) | copy-start | bytes 28
  275.1 30.7 %copy-start.66 = (bf16[2,2,197,1024]{3,1,2,0:T(2,128)(2,1)S(1)}, bf16[2,2,197,1024]{3,1,2,0:T(2,128)(2,1)}, u32[]{:S(2)}) copy-start(bf16[2,2,197,1024]{3,1,2,0:T(2,128)(2,1)} %param.11) | copy-start | bytes 4841476
  300.5 21.5 %collective-permute-start.1 = (bf16[2,197,1024]{2,0,1:T(2,128)(2,1)}, bf16[2,197,1024]{2,0,1:T(2,128)(2,1)}, u32[]{:S(2)}, u32[]{:S(2)}) collective-permute-start(bf16[2,197,1024]{2,0,1:T(2,128)(2,1)} %copy.154), channel_id=1, source_target_pairs={{0,16},{1,17},{2,18},{3,19},{4,20},{5,21},{6,22},{7,23},{8,24},{9,... | collective-permute-start | bytes 2420744 | tf_op jit(solution)/shard_map/ppermute | solution.py:17
  473.2 53.7 %collective-permute-start.2 = (bf16[2,197,1024]{2,0,1:T(2,128)(2,1)}, bf16[2,197,1024]{2,0,1:T(2,128)(2,1)}, u32[]{:S(2)}, u32[]{:S(2)}) collective-permute-start(bf16[2,197,1024]{2,0,1:T(2,128)(2,1)} %copy.174), channel_id=1, source_target_pairs={{16,0},{17,1},{18,2},{19,3},{20,4},{21,5},{22,6},{23,7},{24,8},{25... | collective-permute-start | bytes 2420744 | tf_op jit(solution)/shard_map/ppermute | solution.py:17
  509.6 19.5 %slice-start.6 = ((s8[6553600]{0:T(1024)(128)(4,1)}), s8[2359296]{0:T(1024)(128)(4,1)S(1)}, s32[]{:S(2)}) async-start(s8[6553600]{0:T(1024)(128)(4,1)} %bitcast.533), calls=%async_computation.23 | async-start | bytes 4718592
  596.2 21.4 %collective-permute-start.3 = (bf16[2,197,1024]{2,0,1:T(2,128)(2,1)S(1)}, bf16[2,197,1024]{2,0,1:T(2,128)(2,1)S(1)}, u32[]{:S(2)}, u32[]{:S(2)}) collective-permute-start(bf16[2,197,1024]{2,0,1:T(2,128)(2,1)S(1)} %copy.188), channel_id=1, source_target_pairs={{16,0},{17,1},{18,2},{19,3},{20,4},{21,5},{22,6},{23,7},{24,8},{25... | collective-permute-start | bytes 2420744 | tf_op jit(solution)/shard_map/ppermute | solution.py:17
  597.8 20.9 %slice-start.10 = ((s8[8388608]{0:T(1024)(128)(4,1)}), s8[4194304]{0:T(1024)(128)(4,1)S(1)}, s32[]{:S(2)}) async-start(s8[8388608]{0:T(1024)(128)(4,1)} %bitcast.653), calls=%async_computation.27 | async-start | bytes 8388608
  618.7 21.8 %copy-start.70 = (bf16[2,197,1024]{2,1,0:T(8,128)(2,1)}, bf16[2,197,1024]{2,1,0:T(8,128)(2,1)S(1)}, u32[]{:S(2)}) copy-start(bf16[2,197,1024]{2,1,0:T(8,128)(2,1)S(1)} %get-tuple-element.84) | copy-start | bytes 2420740
  618.8 21.8 %copy-start.13 = (f32[2,197,1024]{2,1,0:T(8,128)S(1)}, f32[2,197,1024]{2,1,0:T(8,128)}, u32[]{:S(2)}) copy-start(f32[2,197,1024]{2,1,0:T(8,128)} %get-tuple-element.92) | copy-start | bytes 4841476
  618.8 21.8 %copy-start.83 = (f32[2,197]{1,0:T(2,128)S(1)}, f32[2,197]{1,0:T(2,128)}, u32[]{:S(2)}) copy-start(f32[2,197]{1,0:T(2,128)} %broadcast_multiply_fusion.1) | copy-start | bytes 4732
  654.2 174.8 %reduce-scatter.9.cloned.1.call-start = ((), (), s32[]{:S(2)}) async-start(), calls=%async_computation.6 | async-start | bytes 7864320 | tf_op jit(solution)/shard_map/reduce_scatter | solution.py:311
  711.2 132.0 %reduce-scatter.13.cloned.1.call-start = ((), (), s32[]{:S(2)}) async-start(), calls=%async_computation.8 | async-start | bytes 10485760 | tf_op jit(solution)/shard_map/reduce_scatter | solution.py:317
  752.2 165.5 %reduce-scatter.15.cloned.1.call-start = ((), (), s32[]{:S(2)}) async-start(), calls=%async_computation.9 | async-start | bytes 10485760 | tf_op jit(solution)/shard_map/reduce_scatter | solution.py:320
  811.3 141.0 %reduce-scatter.19.cloned.1.call-start = ((), (), s32[]{:S(2)}) async-start(), calls=%async_computation.15 | async-start | bytes 327680
  824.2 94.8 %copy-start.117 = (f32[1,1,1024]{2,1,0:T(1,128)S(1)}, f32[1,1,1024]{2,1,0:T(1,128)}, u32[]{:S(2)}) copy-start(f32[1,1,1024]{2,1,0:T(1,128)} %copy-done.116) | copy-start | bytes 12292
  824.3 94.8 %copy-start.121 = (f32[2]{0:T(128)S(1)}, f32[2]{0:T(128)}, u32[]{:S(2)}) copy-start(f32[2]{0:T(128)} %get-tuple-element.164) | copy-start | bytes 28
  826.8 92.2 %copy-start.47 = (f32[2,197,1024]{2,1,0:T(8,128)S(1)}, f32[2,197,1024]{2,1,0:T(8,128)}, u32[]{:S(2)}) copy-start(f32[2,197,1024]{2,1,0:T(8,128)} %copy-done.46) | copy-start | bytes 4841476
  826.9 136.3 %reduce-scatter.17.cloned.1.call-start = ((), (), s32[]{:S(2)}) async-start(), calls=%async_computation.10 | async-start | bytes 20480 | tf_op jit(solution)/shard_map/reduce_scatter | solution.py:326
  827.7 362.2 %all-reduce.5.cloned.1.call-start = ((), (), s32[]{:S(2)}) async-start(), calls=%async_computation.16 | async-start | bytes 12582912 | tf_op jit(solution)/shard_map/psum | solution.py:334
  (129 other events, 953.1 us)
Sparse Core Ops, SparseCore 0:
  9.6 49.1 all-gather.11
  60.3 22.5 all-gather.13
  84.5 58.2 all-gather.15
  144.3 58.2 all-gather.17
  654.3 30.5 reduce-scatter.10
  711.3 57.5 reduce-scatter.8
  771.5 71.6 reduce-scatter.12
  846.0 71.6 reduce-scatter.14
  920.8 20.0 reduce-scatter.18
  943.9 19.2 reduce-scatter.16
  965.8 224.0 all-reduce.4
where the time goes:
time: 1210 us
  waiting for transfers between devices  470 us (39%)
  matrix products  467 us (39%)
  other arithmetic  103 us (9%)
  local copies, waits for them, and re-layouts  92.2 us (8%)
  blocking collectives  45.3 us (4%)
  between operations  16.5 us (1%)
  starting transfers between devices  12.3 us (1%)
    psum x1, waiting for transfers between devices, per_device(): lax.psum(owned[0].astype(jnp.bfloat16), 'replica').astype(jnp.float32)  202 us
    reduce_scatter x1, waiting for transfers between devices, per_device(): lax.psum_scatter(red_sum.astype(jnp.bfloat16), 'group', scatter_dimension...  74.5 us
    dot_general x3, matrix products, layer_forward(): jnp.einsum('mzv,va->mza', activated_hidden, contraction_weight, preferred...  63.7 us
    dot_general x3, matrix products, layer_backward(): jnp.einsum('cpn,cpu->nu', activated_hidden, feedforward_gradient, preferr...  57.8 us
    all_gather x1, waiting for transfers between devices, per_device(): lax.all_gather(shards[2], 'group', axis=0, tiled=True)  55 us
    dot_general x3, matrix products, layer_backward(): jnp.einsum('vpm,tm->vpt', feedforward_gradient, contraction_weight, prefe...  50.2 us
    dot_general x3, matrix products, layer_forward(): jnp.einsum('cje,en->cjn', second_residual, expansion_weight, preferred_el...  48.2 us
    all_gather x1, waiting for transfers between devices, per_device(): lax.all_gather(shards[3], 'group', axis=0, tiled=True)  45.7 us
  transfers between devices with their start and end apart: 15, of which 11 were waited for; matrix products, arithmetic and copies ran while one was open for 26% of the time, Pallas kernels for 0%

commit v1 on v0

v1 whole, which is shorter than its diff:
```python
from functools import partial

import jax
import jax.numpy as jnp
from jax import lax
from jax.experimental import pallas as pl
from jax.experimental.pallas import tpu as pltpu
from jax.sharding import PartitionSpec as P

HEADS = 16
EPSILON = 1e-06
NEGATIVE = -1e30
F32 = jnp.float32
BF16 = jnp.bfloat16
VMEM_LIMIT = 58 * 2**20
ROOT_HALF = 0.7071067811865476
ROOT_TAU = 0.3989422804014327
ROWS = 32
ANY = pl.BlockSpec(memory_space=pl.ANY)
VMEM = pl.BlockSpec(memory_space=pltpu.VMEM)
SMEM = pl.BlockSpec(memory_space=pltpu.SMEM)
GAIN0, GAIN1, SHIFT0, SHIFT1, QUERY, VALUE, OUT, FEED, EXPAND = range(9)


def padded(length):
    return -(-length // 16) * 16


def contract(left, right, left_dim, right_dim):
    return lax.dot_general(
        left, right, (((left_dim,), (right_dim,)), ((), ())), preferred_element_type=F32
    )


def standardized(values):
    center = values - jnp.mean(values, axis=-1, keepdims=True)
    spread = jnp.mean(center * center, axis=-1, keepdims=True)
    scale = lax.rsqrt(spread + EPSILON)
    return center * scale, scale


def norm_pull(grad, gain, unit, scale):
    scaled = grad * gain
    mean = jnp.mean(scaled, axis=-1, keepdims=True)
    along = jnp.mean(scaled * unit, axis=-1, keepdims=True)
    return scale * (scaled - mean - unit * along)


def call(body, name, operands, specs, outs, scratch, flops):
    moved = sum(o.size * o.dtype.itemsize for o in operands)
    out_shape = [jax.ShapeDtypeStruct(shape, dtype) for shape, dtype in outs]
    moved += sum(o.size * o.dtype.itemsize for o in out_shape)
    return pl.pallas_call(
        body,
        out_shape=out_shape,
        in_specs=specs,
        out_specs=[VMEM] * len(outs),
        scratch_shapes=scratch,
        compiler_params=pltpu.CompilerParams(vmem_limit_bytes=VMEM_LIMIT),
        cost_estimate=pl.CostEstimate(flops=flops, bytes_accessed=moved, transcendentals=0),
        name=name,
    )(*operands)


def start_pieces(pieces, order_ref, target, sems, slot, columns):
    rows = pieces[0].shape[0]
    copies = []
    for index, piece in enumerate(pieces):
        where = pl.multiple_of(order_ref[index] * rows, rows)
        copy = pltpu.make_async_copy(
            piece.at[:, columns], target.at[pl.ds(where, rows), columns], sems.at[slot, index]
        )
        copy.start()
        copies.append(copy)
    return copies


def wait_all(copies):
    for copy in copies:
        copy.wait()


def start_chosen(section, lower, upper, target, sem):
    if lower is upper:
        copy = pltpu.make_async_copy(lower, target, sem)
        copy.start()
        return copy

    @pl.when(section == 0)
    def _():
        pltpu.make_async_copy(lower, target, sem).start()

    @pl.when(section != 0)
    def _():
        pltpu.make_async_copy(upper, target, sem).start()

    return pltpu.make_async_copy(lower, target, sem)


def each_chunk(count, length, whole, tail):
    full = length // ROWS
    for image in range(count):

        def step(index, carry, image=image):
            whole(image, pl.multiple_of(index * ROWS, ROWS))
            return carry

        lax.fori_loop(0, full, step, 0)
        if length > full * ROWS:
            tail(image, full * ROWS)


def row_at(image, space, row):
    return pl.multiple_of(image * space + row, 16)


def attention_forward(lower, upper, pieces, params, meta, keep):
    count, length, width = lower.shape
    space = padded(length)
    rows = count * space
    parts = len(pieces)
    head = width // HEADS
    pair = 2 * head
    scale = head**-0.5
    same = lower is upper
    extra = length % ROWS
    rest = space - length // ROWS * ROWS

    def body(*refs):
        refs = list(refs)
        low = refs.pop(0)
        up = low if same else refs.pop(0)
        weight = [refs.pop(0) for _ in range(parts)]
        vec, info = refs.pop(0), refs.pop(0)
        if keep:
            norm, packed, mixed, logs = (refs.pop(0) for _ in range(4))
        else:
            mixed = refs.pop(0)
        x, stage, full, x_sem, w_sem = (refs.pop(0) for _ in range(5))
        if not keep:
            norm, packed = (refs.pop(0) for _ in range(2))
        else:
            columns = refs.pop(0)
        section = info[parts]
        take = start_chosen(section, low, up, x, x_sem)
        loads = [
            start_pieces(weight, info, full, w_sem, block, pl.ds(block * width, width))
            for block in range(3)
        ]
        take.wait()
        gain, shift = vec[GAIN0 : GAIN0 + 1], vec[SHIFT0 : SHIFT0 + 1]
        stage[...] = jnp.zeros_like(stage)

        def whole(image, row):
            unit, _ = standardized(x[image, pl.ds(row, ROWS)].astype(F32))
            norm[pl.ds(row_at(image, space, row), ROWS)] = (unit * gain + shift).astype(BF16)

        def tail(image, row):
            unit, _ = standardized(x[image, row:length].astype(F32))
            stage[0:extra] = unit * gain + shift
            norm[pl.ds(image * space + row, rest)] = stage[0:rest].astype(BF16)

        each_chunk(count, length, whole, tail)
        for block in range(3):
            wait_all(loads[block])
            done = contract(norm[...], full[:, block * width : (block + 1) * width], 1, 0)
            if block != 1:
                bias = QUERY if block == 0 else VALUE
                done = done + vec[bias : bias + 1]
            packed[:, block * width : (block + 1) * width] = done.astype(BF16)
        lane = lax.broadcasted_iota(jnp.int32, (space, pair), 1)
        left = lane < head
        live = lax.broadcasted_iota(jnp.int32, (space, pair), 0) < length
        key_live = lax.broadcasted_iota(jnp.int32, (space, space), 1) < length
        for image in range(count):
            span = pl.ds(image * space, space)

            def heads(index, carry, span=span):
                def part(block):
                    offset = pl.multiple_of(block * width + index * pair, pair)
                    return packed[span, pl.ds(offset, pair)].astype(F32)

                query, key, value = part(0) * scale, part(1).astype(BF16), part(2)
                found = []
                tops = []
                for side in range(2):
                    mine = left if side == 0 else ~left
                    asked = jnp.where(mine, query, 0.0).astype(BF16)
                    held = jnp.where(live, jnp.where(mine, value, 1.0), 0.0).astype(BF16)
                    scores = jnp.where(key_live, contract(asked, key, 1, 1), NEGATIVE)
                    top = jnp.max(scores, axis=-1, keepdims=True)
                    raised = jnp.exp(scores - top).astype(BF16)
                    found.append(contract(raised, held, 1, 0))
                    tops.append(top)
                upper_part = jnp.where(left, found[0], found[1])
                total = jnp.where(left, found[1], found[0])
                turned = pltpu.roll(total, head, 1)
                offset = pl.multiple_of(index * pair, pair)
                mixed[span, pl.ds(offset, pair)] = (upper_part / turned).astype(BF16)
                if keep:
                    logged = jnp.log(turned)
                    first = tops[0] + logged[:, 0:1]
                    second = tops[1] + logged[:, head : head + 1]
                    held = columns[...]
                    held = jnp.where(lane == 2 * index, first, held)
                    columns[...] = jnp.where(lane == 2 * index + 1, second, held)
                return carry

            if keep:
                columns[...] = jnp.zeros_like(columns)
            lax.fori_loop(0, HEADS // 2, heads, 0)
            if keep:
                logs[image] = columns[...].T[0:HEADS]

    outs = [((rows, width), BF16)]
    scratch = [
        pltpu.VMEM((count, length, width), BF16),
        pltpu.VMEM((ROWS, width), F32),
        pltpu.VMEM((width, 3 * width), BF16),
        pltpu.SemaphoreType.DMA,
        pltpu.SemaphoreType.DMA((3, parts)),
    ]
    if keep:
        outs = (
            [((rows, width), BF16), ((rows, 3 * width), BF16)]
            + outs
            + [((count, HEADS, space), F32)]
        )
        scratch += [pltpu.VMEM((space, pair), F32)]
    else:
        scratch += [pltpu.VMEM((rows, width), BF16), pltpu.VMEM((rows, 3 * width), BF16)]
    inputs = [lower] if same else [lower, upper]
    return call(
        body,
        "attention_forward",
        inputs + list(pieces) + [params, meta],
        [ANY] * (len(inputs) + parts) + [VMEM, SMEM],
        outs,
        scratch,
        2 * rows * width * (3 * width + 2 * space),
    )


def hidden_forward(lower, upper, mixed, out_pieces, pieces, params, meta, keep):
    count, length, width = lower.shape
    space = padded(length)
    rows = count * space
    parts = len(pieces)
    inner = pieces[0].shape[1]
    same = lower is upper
    extra = length % ROWS
    rest = space - length // ROWS * ROWS
    blocks = inner // width

    def body(*refs):
        refs = list(refs)
        low = refs.pop(0)
        up = low if same else refs.pop(0)
        attended = refs.pop(0)
        project = [refs.pop(0) for _ in range(parts)]
        expand = [refs.pop(0) for _ in range(parts)]
        vec, info = refs.pop(0), refs.pop(0)
        middle, active = refs.pop(0), refs.pop(0)
        if keep:
            second, slope = refs.pop(0), refs.pop(0)
        x, full_out, full, x_sem, o_sem, w_sem = (refs.pop(0) for _ in range(6))
        if not keep:
            second = refs.pop(0)
        section = info[parts]
        take = start_chosen(section, low, up, x, x_sem)
        first_load = start_pieces(project, info, full_out, o_sem, 0, pl.ds(0, width))
        loads = [
            start_pieces(expand, info, full, w_sem, block, pl.ds(block * width, width))
            for block in range(blocks)
        ]
        wait_all(first_load)
        middle[...] = contract(attended[...], full_out[...], 1, 0) + vec[OUT : OUT + 1]
        take.wait()
        gain, shift = vec[GAIN1 : GAIN1 + 1], vec[SHIFT1 : SHIFT1 + 1]

        def whole(image, row):
            here = pl.ds(row_at(image, space, row), ROWS)
            total = middle[here] + x[image, pl.ds(row, ROWS)].astype(F32)
            middle[here] = total
            unit, _ = standardized(total)
            second[here] = (unit * gain + shift).astype(BF16)

        def tail(image, row):
            start = image * space + row
            middle[pl.ds(start, extra)] += x[image, row:length].astype(F32)
            unit, _ = standardized(middle[pl.ds(start, rest)])
            second[pl.ds(start, rest)] = (unit * gain + shift).astype(BF16)

        each_chunk(count, length, whole, tail)
        for block in range(blocks):
            wait_all(loads[block])
            part = slice(block * width, (block + 1) * width)
            value = contract(second[...], full[:, part], 1, 0) + vec[EXPAND + block - 0 : EXPAND + block + 1]
            share = 0.5 + 0.5 * lax.erf(value * ROOT_HALF)
            active[:, part] = (value * share).astype(BF16)
            if keep:
                density = ROOT_TAU * jnp.exp(-0.5 * value * value)
                slope[:, part] = (share + value * density).astype(BF16)

    outs = [((rows, width), F32), ((rows, inner), BF16)]
    scratch = [
        pltpu.VMEM((count, length, width), BF16),
        pltpu.VMEM((width, width), BF16),
        pltpu.VMEM((width, inner), BF16),
        pltpu.SemaphoreType.DMA,
        pltpu.SemaphoreType.DMA((1, parts)),
        pltpu.SemaphoreType.DMA((blocks, parts)),
    ]
    if keep:
        outs += [((rows, width), BF16), ((rows, inner), BF16)]
    else:
        scratch += [pltpu.VMEM((rows, width), BF16)]
    inputs = [lower] if same else [lower, upper]
    return call(
        body,
        "hidden_forward",
        inputs + [mixed] + list(out_pieces) + list(pieces) + [params, meta],
        [ANY] * len(inputs) + [VMEM] + [ANY] * (2 * parts) + [VMEM, SMEM],
        outs,
        scratch,
        2 * rows * width * (width + inner),
    )


def output_forward(middle, active, pieces, params, meta, count, length):
    rows, width = middle.shape
    inner = active.shape[1]
    space = padded(length)
    parts = len(pieces)
    half = width // 2

    def body(*refs):
        refs = list(refs)
        mid, act = refs.pop(0), refs.pop(0)
        reduce = [refs.pop(0) for _ in range(parts)]
        vec, info, result, full, w_sem = refs
        loads = [
            start_pieces(reduce, info, full, w_sem, block, pl.ds(block * half, half))
            for block in range(2)
        ]
        for block in range(2):
            wait_all(loads[block])
            part = slice(block * half, (block + 1) * half)
            value = contract(act[...], full[:, part], 1, 0) + mid[:, part] + vec[FEED : FEED + 1, part]
            for image in range(count):
                alive = jnp.where(info[parts + 1 + image] > 0, 1.0, 0.0)
                kept = value[image * space : image * space + length] * alive
                result[image, :, part] = kept.astype(BF16)

    return call(
        body,
        "output_forward",
        [middle, active] + list(pieces) + [params, meta],
        [VMEM, VMEM] + [ANY] * parts + [VMEM, SMEM],
        [((count, length, width), BF16)],
        [
            pltpu.VMEM((inner, width), BF16),
            pltpu.SemaphoreType.DMA((2, parts)),
        ],
        2 * rows * width * inner,
    )[0]


def hidden_backward(upstream, kept_low, kept_up, out_weights, weights, params, meta):
    count, length, width = upstream.shape
    space = padded(length)
    rows = count * space
    parts = len(weights)
    inner = weights[0].shape[1]
    same = kept_low[0] is kept_up[0]
    extra = length % ROWS
    rest = space - length // ROWS * ROWS
    half = width // 2
    deep = out_weights[0].shape[0]

    def body(*refs):
        refs = list(refs)
        grad = refs.pop(0)
        slope_low, middle_low = refs.pop(0), refs.pop(0)
        slope_up, middle_up = (slope_low, middle_low) if same else (refs.pop(0), refs.pop(0))
        reduce = [refs.pop(0) for _ in range(parts)]
        expand = [refs.pop(0) for _ in range(parts)]
        vec, info = refs.pop(0), refs.pop(0)
        hidden, mid_grad, branch, sums, inner_sums = (refs.pop(0) for _ in range(5))
        feed, second, slope, middle, full_out, full, k_sem, o_sem, w_sem = refs
        section = info[parts]
        for_slope = start_chosen(section, slope_low, slope_up, slope, k_sem.at[0])
        first_load = [
            start_pieces([piece], info_at(info, index), full_out, o_sem.at[pl.ds(index, 1)], 0, pl.ds(0, width))
            for index, piece in enumerate(reduce)
        ]
        for_middle = start_chosen(section, middle_low, middle_up, middle, k_sem.at[1])
        load = start_pieces(expand, info, full, w_sem, 0, pl.ds(0, inner))
        for image in range(count):
            alive = jnp.where(info[parts + 1 + image] > 0, 1.0, 0.0)
            feed[pl.ds(image * space + length // 16 * 16, space - length // 16 * 16)] = jnp.zeros(
                (space - length // 16 * 16, width), BF16
            )
            feed[pl.ds(image * space, length)] = (grad[image].astype(F32) * alive).astype(BF16)
        for_slope.wait()
        for index in range(parts):
            wait_all(first_load[index])
            where = pl.multiple_of(info[index] * deep, deep)
            value = contract(feed[...], full_out[pl.ds(where, deep)], 1, 1)
            value = (value * slope[:, pl.ds(where, deep)].astype(F32)).astype(BF16)
            hidden[:, pl.ds(where, deep)] = value
            inner_sums[:, pl.ds(where, deep)] = jnp.sum(value.astype(F32), axis=0, keepdims=True)
        wait_all(load)
        for block in range(2):
            second[:, block * half : (block + 1) * half] = contract(
                hidden[...], full[block * half : (block + 1) * half], 1, 1
            )
        for_middle.wait()
        gain = vec[GAIN1 : GAIN1 + 1]
        sums[...] = jnp.zeros_like(sums)

        def step(index, carry):
            here = pl.ds(pl.multiple_of(index * 16, 16), 16)
            unit, scale = standardized(middle[here])
            down = second[here]
            top = feed[here].astype(F32)
            total = top + norm_pull(down, gain, unit, scale)
            low = total.astype(BF16)
            mid_grad[here] = total
            branch[here] = low
            sums[0:1] += jnp.sum(down * unit, axis=0, keepdims=True)
            sums[1:2] += jnp.sum(down, axis=0, keepdims=True)
            sums[2:3] += jnp.sum(low.astype(F32), axis=0, keepdims=True)
            sums[3:4] += jnp.sum(top, axis=0, keepdims=True)
            return carry

        lax.fori_loop(0, rows // 16, step, 0)

    kept = list(kept_low) if same else list(kept_low) + list(kept_up)
    return call(
        body,
        "hidden_backward",
        [upstream] + kept + list(out_weights) + list(weights) + [params, meta],
        [VMEM] + [ANY] * (len(kept) + 2 * parts) + [VMEM, SMEM],
        [
            ((rows, inner), BF16),
            ((rows, width), F32),
            ((rows, width), BF16),
            ((8, width), F32),
            ((1, inner), F32),
        ],
        [
            pltpu.VMEM((rows, width), BF16),
            pltpu.VMEM((rows, width), F32),
            pltpu.VMEM((rows, inner), BF16),
            pltpu.VMEM((rows, width), F32),
            pltpu.VMEM((inner, width), BF16),
            pltpu.VMEM((width, inner), BF16),
            pltpu.SemaphoreType.DMA((2,)),
            pltpu.SemaphoreType.DMA((parts, 1)),
            pltpu.SemaphoreType.DMA((1, parts)),
        ],
        4 * rows * width * inner,
    )


class info_at:
    def __init__(self, ref, index):
        self.ref, self.index = ref, index

    def __getitem__(self, index):
        return self.ref[self.index + index]


def attention_backward(
    branch, mid_grad, lower, upper, kept_low, kept_up, out_weights, weights, params, meta
):
    count, length, width = lower.shape
    space = padded(length)
    rows = count * space
    parts = len(weights)
    head = width // HEADS
    pair = 2 * head
    scale = head**-0.5
    same = kept_low[0] is kept_up[0]
    same_in = lower is upper
    extra = length % ROWS
    rest = space - length // ROWS * ROWS
    half = width // 2

    def body(*refs):
        refs = list(refs)
        low_grad, top_grad = refs.pop(0), refs.pop(0)
        low = refs.pop(0)
        up = low if same_in else refs.pop(0)
        packed_low, mixed_low, logs_low = (refs.pop(0) for _ in range(3))
        packed_up, mixed_up, logs_up = (
            (packed_low, mixed_low, logs_low) if same else (refs.pop(0) for _ in range(3))
        )
        project = [refs.pop(0) for _ in range(parts)]
        query_key_value = [refs.pop(0) for _ in range(parts)]
        vec, info = refs.pop(0), refs.pop(0)
        result, grads, sums = (refs.pop(0) for _ in range(3))
        x, packed, mixed, logs, down, normal, stage, full_out, full, k_sem, o_sem, w_sem = refs
        section = info[parts]
        first_load = start_pieces(project, info, full_out, o_sem, 0, pl.ds(0, width))
        takes = [
            start_chosen(section, one, two, target, k_sem.at[index])
            for index, (one, two, target) in enumerate(
                (
                    (mixed_low, mixed_up, mixed),
                    (packed_low, packed_up, packed),
                    (logs_low, logs_up, logs),
                    (low, up, x),
                )
            )
        ]
        load = start_pieces(query_key_value, info, full, w_sem, 0, pl.ds(0, 3 * width))
        wait_all(first_load)
        down[...] = contract(low_grad[...], full_out[...], 1, 1).astype(BF16)
        wait_all(takes)
        owner = lax.shift_right_logical(
            lax.broadcasted_iota(jnp.int32, (HEADS, width), 1), head.bit_length() - 1
        )
        chosen = jnp.where(
            owner == lax.broadcasted_iota(jnp.int32, (HEADS, width), 0), 1.0, 0.0
        ).astype(BF16)
        left = lax.broadcasted_iota(jnp.int32, (space, pair), 1) < head
        live = lax.broadcasted_iota(jnp.int32, (space, pair), 0) < length
        key_live = lax.broadcasted_iota(jnp.int32, (space, space), 0) < length
        for image in range(count):
            span = pl.ds(image * space, space)
            product = down[span].astype(F32) * mixed[span].astype(F32)
            coarse = product.astype(BF16)
            fine = (product - coarse.astype(F32)).astype(BF16)
            stage[0:HEADS, 0:space] = contract(chosen, coarse, 1, 1) + contract(chosen, fine, 1, 1)

            def heads(index, carry, span=span, image=image):
                def part(block):
                    offset = pl.multiple_of(block * width + index * pair, pair)
                    return packed[span, pl.ds(offset, pair)]

                query, key, value = part(0), part(1), part(2)
                wide = key.astype(F32) * scale
                value = value.astype(F32)
                arrived = down[span, pl.ds(pl.multiple_of(index * pair, pair), pair)]
                found = []
                for side in range(2):
                    mine = left if side == 0 else ~left
                    log = logs[image, pl.ds(2 * index + side, 1), :]
                    dot = stage[pl.ds(2 * index + side, 1), 0:space]
                    scores = contract(jnp.where(mine, wide, 0.0).astype(BF16), query, 1, 1)
                    chance = jnp.exp(jnp.where(key_live, scores - log, NEGATIVE))
                    back = contract(jnp.where(mine, value, 0.0).astype(BF16), arrived, 1, 1)
                    change = (chance * (back - dot)).astype(BF16)
                    found.append(
                        (
                            contract(change, key, 0, 0),
                            contract(change, query, 1, 0),
                            contract(chance.astype(BF16), arrived, 1, 0),
                        )
                    )
                for block, factor in enumerate((scale, scale, 1.0)):
                    total = jnp.where(left, found[0][block], found[1][block]) * factor
                    offset = pl.multiple_of(block * width + index * pair, pair)
                    grads[span, pl.ds(offset, pair)] = jnp.where(live, total, 0.0).astype(BF16)
                return carry

            lax.fori_loop(0, HEADS // 2, heads, 0)
        wait_all(load)
        for block in range(2):
            normal[:, block * half : (block + 1) * half] = contract(
                grads[...], full[block * half : (block + 1) * half], 1, 1
            )
        gain = vec[GAIN0 : GAIN0 + 1]
        sums[...] = jnp.zeros_like(sums)
        sums[2:3] = jnp.sum(grads[:, 0:width].astype(F32), axis=0, keepdims=True)
        sums[3:4] = jnp.sum(grads[:, 2 * width : 3 * width].astype(F32), axis=0, keepdims=True)

        def step(value, grad, top):
            unit, rate = standardized(value)
            sums[0:1] += jnp.sum(grad * unit, axis=0, keepdims=True)
            sums[1:2] += jnp.sum(grad, axis=0, keepdims=True)
            return top + norm_pull(grad, gain, unit, rate)

        def whole(image, row):
            here = pl.ds(row_at(image, space, row), ROWS)
            value = x[image, pl.ds(row, ROWS)].astype(F32)
            result[image, pl.ds(row, ROWS)] = step(value, normal[here], top_grad[here]).astype(BF16)

        def tail(image, row):
            here = pl.ds(image * space + row, extra)
            value = x[image, row:length].astype(F32)
            result[image, row:length] = step(value, normal[here], top_grad[here]).astype(BF16)

        each_chunk(count, length, whole, tail)

    kept = list(kept_low) if same else list(kept_low) + list(kept_up)
    inputs = [lower] if same_in else [lower, upper]
    return call(
        body,
        "attention_backward",
        [branch, mid_grad] + inputs + kept + list(out_weights) + list(weights) + [params, meta],
        [VMEM, VMEM] + [ANY] * (len(inputs) + len(kept) + 2 * parts) + [VMEM, SMEM],
        [((count, length, width), BF16), ((rows, 3 * width), BF16), ((8, width), F32)],
        [
            pltpu.VMEM((count, length, width), BF16),
            pltpu.VMEM((rows, 3 * width), BF16),
            pltpu.VMEM((rows, width), BF16),
            pltpu.VMEM((count, HEADS, space), F32),
            pltpu.VMEM((rows, width), BF16),
            pltpu.VMEM((rows, width), F32),
            pltpu.VMEM((HEADS, 2 * pair), F32),
            pltpu.VMEM((width, width), BF16),
            pltpu.VMEM((width, 3 * width), BF16),
            pltpu.SemaphoreType.DMA((4,)),
            pltpu.SemaphoreType.DMA((1, parts)),
            pltpu.SemaphoreType.DMA((1, parts)),
        ],
        2 * rows * width * (4 * width + 5 * space),
    )


def weight_gradient(kept, lowers, uppers, meta, parts, quarter, rows_of, columns_of, name):
    micro = len(kept)
    first_row, height = rows_of
    first_column, breadth = columns_of
    rows = kept[0].shape[0]

    def body(*refs):
        refs = list(refs)
        left = [refs.pop(0) for _ in range(micro)]
        low = [refs.pop(0) for _ in range(micro)]
        up = [refs.pop(0) for _ in range(micro)]
        info = refs.pop(0)
        outs = [refs.pop(0) for _ in range(parts)]
        left_full, right_full, l_sem, r_sem = refs
        section = info[parts]
        waits = []
        for batch in range(micro):
            span = pl.ds(batch * rows, rows)
            columns = pl.ds(first_column, breadth)
            waits.append(
                start_chosen(
                    section,
                    low[batch].at[:, columns],
                    up[batch].at[:, columns],
                    right_full.at[span],
                    r_sem.at[batch],
                )
            )
        loads = []
        for part in range(parts):
            for batch in range(micro):
                start = pl.multiple_of(info[part] * quarter + first_row, 128)
                copy = pltpu.make_async_copy(
                    left[batch].at[:, pl.ds(start, height)],
                    left_full.at[part, pl.ds(batch * rows, rows)],
                    l_sem.at[part, batch],
                )
                copy.start()
                loads.append(copy)
        wait_all(waits)
        for part in range(parts):
            wait_all(loads[part * micro : (part + 1) * micro])
            outs[part][...] = contract(left_full[part], right_full[...], 0, 0).astype(BF16)

    return call(
        body,
        name,
        list(kept) + list(lowers) + list(uppers) + [meta],
        [ANY] * (3 * micro) + [SMEM],
        [((height, breadth), BF16)] * parts,
        [
            pltpu.VMEM((parts, micro * rows, height), BF16),
            pltpu.VMEM((micro * rows, breadth), BF16),
            pltpu.SemaphoreType.DMA((parts, micro)),
            pltpu.SemaphoreType.DMA((micro,)),
        ],
        2 * parts * micro * rows * height * breadth,
    )


def feed_gradient(kept, lowers, uppers, meta, parts, quarter, rows_of, count, length):
    micro = len(kept)
    first_row, height = rows_of
    rows = kept[0].shape[0]
    space = padded(length)
    width = lowers[0].shape[-1]
    base = length // 16 * 16

    def body(*refs):
        refs = list(refs)
        left = [refs.pop(0) for _ in range(micro)]
        low = [refs.pop(0) for _ in range(micro)]
        up = [refs.pop(0) for _ in range(micro)]
        info = refs.pop(0)
        outs = [refs.pop(0) for _ in range(parts)]
        left_full, taken, right_full, l_sem, r_sem = refs
        section = info[parts]
        waits = [
            start_chosen(section, low[batch], up[batch], taken.at[batch], r_sem.at[batch])
            for batch in range(micro)
        ]
        loads = []
        for part in range(parts):
            for batch in range(micro):
                start = pl.multiple_of(info[part] * quarter + first_row, 128)
                copy = pltpu.make_async_copy(
                    left[batch].at[:, pl.ds(start, height)],
                    left_full.at[part, pl.ds(batch * rows, rows)],
                    l_sem.at[part, batch],
                )
                copy.start()
                loads.append(copy)
        for batch in range(micro):
            waits[batch].wait()
            for image in range(count):
                start = batch * rows + image * space
                alive = jnp.where(info[parts + 1 + batch * count + image] > 0, 1.0, 0.0)
                right_full[pl.ds(start + base, space - base)] = jnp.zeros((space - base, width), BF16)
                right_full[pl.ds(start, length)] = (
                    taken[batch, image].astype(F32) * alive
                ).astype(BF16)
        for part in range(parts):
            wait_all(loads[part * micro : (part + 1) * micro])
            outs[part][...] = contract(left_full[part], right_full[...], 0, 0).astype(BF16)

    return call(
        body,
        "reduce_gradient",
        list(kept) + list(lowers) + list(uppers) + [meta],
        [ANY] * (3 * micro) + [SMEM],
        [((height, width), BF16)] * parts,
        [
            pltpu.VMEM((parts, micro * rows, height), BF16),
            pltpu.VMEM((micro, count, length, width), BF16),
            pltpu.VMEM((micro * rows, width), BF16),
            pltpu.SemaphoreType.DMA((parts, micro)),
            pltpu.SemaphoreType.DMA((micro,)),
        ],
        2 * parts * micro * rows * height * width,
    )


def added(*values):
    total = values[0].astype(F32)
    for value in values[1:]:
        total = total + value.astype(F32)
    return total.astype(values[0].dtype)


class FourByFour:
    parts = 4

    def __init__(self):
        self.group = lax.axis_index("group")
        self.place = lax.axis_index("replica")
        self.order = [self.group ^ part for part in range(4)]

    def core(self, block):
        return lax.ppermute(block, "group", [(i, i ^ 1) for i in range(4)])

    def across(self, block):
        return lax.ppermute(block, "group", [(i, i ^ 2) for i in range(4)])

    def gather(self, block):
        sibling = self.core(block)
        far = self.across(block)
        return [block, sibling, far, self.core(far)]

    def line(self, block, routes):
        pairs = [
            (group * 4 + source, group * 4 + target)
            for group in range(4)
            for source, target in routes[group % 2]
        ]
        return lax.ppermute(block, ("group", "replica"), pairs)

    def total(self, pieces):
        own, sibling, far, far_sibling = pieces
        sibling = self.core(sibling)
        far = self.across(added(far, self.core(far_sibling)))
        mine = added(own, sibling, far)
        inward = self.line(mine, ([(0, 1), (3, 2)], [(0, 1), (3, 2)]))
        joined = added(mine, inward)
        crossing = self.line(joined, ([(2, 1)], [(1, 2)]))
        summed = added(mine, inward, crossing)
        near = self.line(summed, ([(1, 0)], [(2, 3)]))
        inner = self.line(summed, ([(1, 2)], [(2, 1)]))
        outer = self.line(inner, ([(2, 3)], [(1, 0)]))
        odd = self.group % 2
        distance = jnp.where(odd == 0, self.place, 3 - self.place)
        return jnp.where(
            distance == 1,
            summed,
            jnp.where(distance == 0, near, jnp.where(distance == 2, inner, outer)),
        ).astype(F32)


class General:
    def __init__(self):
        self.parts = lax.axis_size("group")
        self.order = [jnp.int32(part) for part in range(self.parts)]

    def gather(self, block):
        whole = lax.all_gather(block, "group", axis=0)
        return [whole[part] for part in range(self.parts)]

    def total(self, pieces):
        mine = lax.psum_scatter(jnp.stack(pieces), "group", scatter_dimension=0)
        return lax.psum(mine, "replica").astype(F32)


def shifted(block, distance):
    devices = range(lax.axis_size("section"))
    route = [(i - distance, i) for i in devices if i - distance in devices]
    return lax.ppermute(block, "section", route)


def in_order(pieces, order):
    place = jnp.stack(order)
    stacked = []
    for block in range(len(pieces)):
        chosen = pieces[0]
        for part in range(1, len(pieces)):
            chosen = jnp.where(place[part] == block, pieces[part], chosen)
        stacked.append(chosen)
    return jnp.stack(stacked)


def out_of_order(blocks, order):
    return [lax.dynamic_index_in_dim(blocks, place, 0, keepdims=False) for place in order]


def per_device(
    images,
    cotangent,
    counts,
    qkv_weight,
    out_weight,
    expand_weight,
    reduce_weight,
    norm_gains,
    biases,
    expand_bias,
):
    micro, slots, length, width = images.shape
    section = lax.axis_index("section")
    first = section == 0
    sizes = (lax.axis_size("group"), lax.axis_size("replica"))
    net = FourByFour() if sizes == (4, 4) else General()
    parts = net.parts
    share = width // parts
    small = jnp.concatenate(
        [norm_gains[0], biases[0], expand_bias[0].reshape(-1, share)]
    )
    vectors = in_order(net.gather(small), net.order)
    qkv = net.gather(qkv_weight[0])
    out = net.gather(out_weight[0])
    expand = net.gather(expand_weight[0])
    reduce = net.gather(reduce_weight[0])
    top = vectors[:, :8].transpose(1, 0, 2).reshape(8, width)
    bottom = vectors[:, 8:].reshape(-1, width)
    params = jnp.concatenate([top, bottom]).astype(F32)
    slot = jnp.arange(slots, dtype=jnp.int32)
    alive = [(slot < counts[batch, 0]).astype(jnp.int32) for batch in range(micro)]
    head = jnp.stack(net.order + [section]).astype(jnp.int32)

    def meta(*batches):
        return jnp.concatenate([head] + [alive[batch] for batch in batches])

    batches = tuple(range(micro))
    flat = images.reshape((micro * slots, length, width))
    mixed = attention_forward(flat, flat, qkv, params, meta(*batches), False)[0]
    middle, active = hidden_forward(flat, flat, mixed, out, expand, params, meta(*batches), False)
    early = output_forward(
        middle, active, reduce, params, meta(*batches), micro * slots, length
    ).reshape(images.shape)
    incoming = [shifted(early[batch], 1) for batch in batches]
    kept = []
    late = []
    for batch in batches:
        low, up = images[batch], incoming[batch]
        norm, packed, mixed, logs = attention_forward(low, up, qkv, params, meta(batch), True)
        middle, active, second, slope = hidden_forward(
            low, up, mixed, out, expand, params, meta(batch), True
        )
        result = output_forward(middle, active, reduce, params, meta(batch), slots, length)
        late.append(result)
        kept.append((low, up, norm, packed, mixed, logs, middle, active, second, slope))
    section_outputs = jnp.stack(late)[None]

    returning = None
    upstreams, hiddens, mids, branches, grads, sent = [], [], [], [], [], []
    sums_a, sums_b, sums_c = [], [], []
    weights = [None] * 4
    for tick in range(micro + 1):
        low_batch, up_batch = max(tick - 1, 0), min(tick, micro - 1)
        upstream = cotangent[up_batch]
        if returning is not None:
            upstream = jnp.where(first, returning, upstream)
        upstreams.append(upstream)
        if tick == micro:
            left = [kept[batch][7] for batch in batches]
            quarter = left[0].shape[1] // parts
            step = quarter // 2
            weights[3] = [
                net.total(
                    feed_gradient(
                        left, upstreams[1:], upstreams[:-1], meta(*batches), parts, quarter,
                        (index * step, step), slots, length,
                    )
                )
                for index in range(2)
            ]
        low, up = kept[low_batch], kept[up_batch]
        chosen = jnp.where(first, alive[low_batch], alive[up_batch])
        info = jnp.concatenate([head, chosen])
        hidden, mid, branch, some, more = hidden_backward(
            upstream, (low[9], low[6]), (up[9], up[6]), reduce, expand, params, info
        )
        hiddens.append(hidden)
        branches.append(branch)
        sums_a.append(some)
        sums_b.append(more)
        if tick == micro:
            left = [kept[batch][8] for batch in batches]
            step = hidden.shape[1] // 2
            weights[2] = [
                net.total(
                    weight_gradient(
                        left, hiddens[1:], hiddens[:-1], meta(*batches), parts, share,
                        (0, share), (index * step, step), "expand_gradient",
                    )
                )
                for index in range(2)
            ]
            left = [kept[batch][4] for batch in batches]
            weights[1] = [
                net.total(
                    weight_gradient(
                        left, branches[1:], branches[:-1], meta(*batches), parts, share,
                        (0, share), (0, width), "project_gradient",
                    )
                )
            ]
        lower = kept[low_batch][0]
        upper = kept[up_batch][1]
        result, grad, some = attention_backward(
            branch, mid, lower, upper, low[3:6], up[3:6], out, qkv, params, info
        )
        grads.append(grad)
        sums_c.append(some)
        sent.append(result)
        if tick < micro:
            returning = shifted(result, -1)
    left = [kept[batch][2] for batch in batches]
    step = 3 * width // 2
    weights[0] = [
        net.total(
            weight_gradient(
                left, grads[1:], grads[:-1], meta(*batches), parts, share,
                (0, share), (index * step, step), "qkv_gradient",
            )
        )
        for index in range(2)
    ]
    input_grads = jnp.stack(
        [jnp.where(first, sent[batch + 1], sent[batch]) for batch in batches]
    )[None]

    def over_batches(values):
        return sum(jnp.where(first, values[batch + 1], values[batch]) for batch in batches)

    some, more, rest = over_batches(sums_a), over_batches(sums_b), over_batches(sums_c)
    rows = jnp.concatenate(
        [rest[0:1], some[0:1], rest[1:2], some[1:2], rest[2:4], some[2:4]]
    )
    rows = rows.reshape(8, parts, share).transpose(1, 0, 2)
    rows = jnp.concatenate([rows, more.reshape(parts, -1, share)], axis=1)
    vector = net.total(out_of_order(rows, net.order))
    return (
        section_outputs,
        input_grads,
        jnp.concatenate(weights[0], axis=1)[None],
        jnp.concatenate(weights[1], axis=1)[None],
        jnp.concatenate(weights[2], axis=1)[None],
        jnp.concatenate(weights[3], axis=0)[None],
        vector[None, 0:2],
        vector[None, 2:8],
        vector[8:].reshape(1, -1),
    )


def solution(mesh):
    placed = (
        P(None, ("group", "replica"), None, None),
        P(None, ("group", "replica"), None, None),
        P(None, ("group", "replica")),
        P("section", "group", None),
        P("section", "group", None),
        P("section", "group", None),
        P("section", "group", None),
        P("section", None, "group"),
        P("section", None, "group"),
        P("section", "group"),
    )
    return jax.shard_map(
        per_device,
        mesh=mesh,
        in_specs=placed,
        out_specs=(
            P("section", None, ("group", "replica"), None, None),
            P("section", None, ("group", "replica"), None, None),
            P("section", "group", None),
            P("section", "group", None),
            P("section", "group", None),
            P("section", "group", None),
            P("section", None, "group"),
            P("section", None, "group"),
            P("section", "group"),
        ),
        check_vma=False,
    )
```

time: 1210 us -> 1040 us (0.86); the launches traced: 1210 us -> 1020 us
  matrix products: 467 us -> 0 us
  Pallas kernels: 0 us -> 407 us
  starting transfers between devices: 12.3 us -> 82.6 us
  other arithmetic: 103 us -> 33.1 us
  local copies, waits for them, and re-layouts: 92.2 us -> 32 us
  blocking collectives: 45.3 us -> 0 us
  between operations: 16.5 us -> 2.88 us
    dot_general x57 -> x0, matrix products: 467 us -> none  [the longest x3 63.7 us: layer_forward(): jnp.einsum('mzv,va->mza', activated_hidden, contraction_weight, preferred...]
    ppermute x4 -> x83, waiting for transfers between devices: 35 us -> 464 us  [the longest x13 230 us: across(): return lax.ppermute(block, 'group', [(i, i ^ 2) for i in range(4)])]
    pallas_call x0 -> x22, Pallas kernels: none -> 407 us  [call(): pl.pallas_call(body, out_shape=out_shape, in_specs=specs, out_specs=[VMEM...]
    psum x1 -> x0, waiting for transfers between devices: 202 us -> none  [per_device(): lax.psum(owned[0].astype(jnp.bfloat16), 'replica').astype(jnp.float32)]
    all_gather x4 -> x0, waiting for transfers between devices: 132 us -> none  [the longest x1 55 us: per_device(): lax.all_gather(shards[2], 'group', axis=0, tiled=True)]
    reduce_scatter x5 -> x0, waiting for transfers between devices: 98.8 us -> none  [the longest x1 74.5 us: per_device(): lax.psum_scatter(red_sum.astype(jnp.bfloat16), 'group', scatter_dimension...]
    ppermute x4 -> x83, starting transfers between devices: 11.5 us -> 82.6 us  [the longest x40 54.1 us: line(): return lax.ppermute(block, ('group', 'replica'), pairs)]
    reduce_sum x28 -> x0, other arithmetic: 38.1 us -> none  [the longest x6 11.5 us: normalize(): center = values - jnp.mean(values, axis=-1, keepdims=True)]
  transfers between devices with their start and end apart: 15 -> 83, of which waited for: 11 -> 26; matrix products, arithmetic and copies ran while one was open for 26% -> 5% of each run, Pallas kernels for 0% -> 26%
where the time goes in v1:
time: 1040 us; the launch traced here: 1020 us
  waiting for transfers between devices  464 us (45%)
  Pallas kernels  407 us (39%)
  starting transfers between devices  82.6 us (8%)
  other arithmetic  33.1 us (3%)
  local copies, waits for them, and re-layouts  32 us (3%)
    pallas_call x22, Pallas kernels, call(): pl.pallas_call(body, out_shape=out_shape, in_specs=specs, out_specs=[VMEM...  407 us
    ppermute x13, waiting for transfers between devices, across(): return lax.ppermute(block, 'group', [(i, i ^ 2) for i in range(4)])  230 us
    ppermute x40, waiting for transfers between devices, line(): return lax.ppermute(block, ('group', 'replica'), pairs)  214 us
    ppermute x40, starting transfers between devices, line(): return lax.ppermute(block, ('group', 'replica'), pairs)  54.1 us
  transfers between devices with their start and end apart: 83, of which 26 were waited for; matrix products, arithmetic and copies ran while one was open for 5% of the time, Pallas kernels for 26%

profile of v1, /device:TPU:0, one launch (start us, length us, event | category | flops | bytes accessed | tf_op | source)
XLA Modules:
  0.0 1021.8 jit_solution(6051604939832961182)
XLA Ops:
  9.2 130.4 %collective-permute-done.3 = bf16[12,256]{1,0:T(8,128)(2,1)S(1)} collective-permute-done((bf16[12,256]{1,0:T(8,128)(2,1)S(1)}, bf16[12,256]{1,0:T(8,128)(2,1)S(1)}, u32[]{:S(2)}, u32[]{:S(2)}) %collective-permute-start.3) | collective-permute-done | bytes 6176 | tf_op jit(solution)/shard_map/ppermute | solution.py:765
  154.7 41.3 %attention_forward.3.refs_1_ = bf16[832,1024]{1,0:T(8,128)(2,1)} custom-call(bf16[4,197,1024]{2,1,0:T(8,128)(2,1)} %bitcast.100, bf16[256,3072]{1,0:T(8,128)(2,1)} %bitcast.114, bf16[256,3072]{1,0:T(8,128)(2,1)} %collective-permute-done.refs_2_.refs_3_.refs_12_.refs_15_, bf16[256,3072]{1,0:T(8,128)(2,1)} %collective-permute-done.1.refs_3_.refs_4_.refs_13_.refs_16_, ...), custom_call_target="tpu_custom_call" | custom-call | flops 5943328768 | bytes 9658404 | tf_op jit(solution)/shard_map/attention_forward/pallas_call | solution.py:53
  196.9 25.4 %hidden_forward.3 = (f32[832,1024]{1,0:T(8,128)}, bf16[832,4096]{1,0:T(8,128)(2,1)}) custom-call(bf16[4,197,1024]{2,1,0:T(8,128)(2,1)} %bitcast.101, bf16[832,1024]{1,0:T(8,128)(2,1)} %attention_forward.3.refs_1_, bf16[256,1024]{1,0:T(8,128)(2,1)} %bitcast.125, bf16[256,1024]{1,0:T(8,128)(2,1)} %copy-done.21, bf16[256,1024]{1,0:T(8,128)(2,1)} %copy-done.20, ...), custom_call_target="tpu_custom_call" | custom-call | flops 8724152320 | bytes 24076324 | tf_op jit(solution)/shard_map/hidden_forward/pallas_call | solution.py:53
  223.7 14.7 %output_forward.3 = bf16[4,197,1024]{2,1,0:T(8,128)(2,1)} custom-call(f32[832,1024]{1,0:T(8,128)} %get-tuple-element.79.refs_0_, bf16[832,4096]{1,0:T(8,128)(2,1)} %get-tuple-element.80.refs_1_, bf16[1024,1024]{1,0:T(8,128)(2,1)} %bitcast.93, bf16[1024,1024]{1,0:T(8,128)(2,1)} %copy-done.1, ...), custom_call_target="tpu_custom_call" | custom-call | flops 6979321856 | bytes 20275236 | tf_op jit(solution)/shard_map/output_forward/pallas_call | solution.py:53
  253.0 11.1 %collective-permute-done.15 = bf16[2,197,1024]{2,0,1:T(2,128)(2,1)} collective-permute-done((bf16[2,197,1024]{2,0,1:T(2,128)(2,1)}, bf16[2,197,1024]{2,0,1:T(2,128)(2,1)}, u32[]{:S(2)}, u32[]{:S(2)}) %collective-permute-start.15) | collective-permute-done | bytes 806944 | tf_op jit(solution)/shard_map/ppermute | solution.py:818
  266.3 24.6 %attention_forward.4 = (bf16[416,1024]{1,0:T(8,128)(2,1)}, bf16[416,3072]{1,0:T(8,128)(2,1)}, bf16[416,1024]{1,0:T(8,128)(2,1)}, f32[2,16,208]{2,1,0:T(8,128)}) custom-call(bf16[2,197,1024]{2,1,0:T(8,128)(2,1)} %get-tuple-element.169.refs_0_.refs_2_, bf16[2,197,1024]{2,1,0:T(8,128)(2,1)} %copy.30.refs_1_.refs_3_, bf16[256,3072]{1,0:T(8,128)(2,1)} %bitcast.115, ...), custom_call_target="tpu_custom_call" | custom-call | flops 2971664384 | bytes 12240924 | tf_op jit(solution)/shard_map/attention_forward/pallas_call | solution.py:53
  291.0 19.4 %hidden_forward.4 = (f32[416,1024]{1,0:T(8,128)}, bf16[416,4096]{1,0:T(8,128)(2,1)}, bf16[416,1024]{1,0:T(8,128)(2,1)}, bf16[416,4096]{1,0:T(8,128)(2,1)}) custom-call(bf16[2,197,1024]{2,1,0:T(8,128)(2,1)} %get-tuple-element.169.refs_0_.refs_2_, bf16[2,197,1024]{2,1,0:T(8,128)(2,1)} %copy.30.refs_1_.refs_3_, ...), custom_call_target="tpu_custom_call" | custom-call | flops 4362076160 | bytes 22372380 | tf_op jit(solution)/shard_map/hidden_forward/pallas_call | solution.py:53
  310.4 22.4 %hidden_backward.3 = (bf16[416,4096]{1,0:T(8,128)(2,1)}, f32[416,1024]{1,0:T(8,128)}, bf16[416,1024]{1,0:T(8,128)(2,1)}, f32[8,1024]{1,0:T(8,128)}, f32[1,4096]{1,0:T(1,128)}) custom-call(bf16[2,197,1024]{2,1,0:T(8,128)(2,1)} %bitcast.120, bf16[416,4096]{1,0:T(8,128)(2,1)} %get-tuple-element.87.refs_1_, f32[416,1024]{1,0:T(8,128)} %get-tuple-element.82.refs_0_.refs_2_, ...), custom_call_target="tpu_custom_call" | custom-call | flops 6979321856 | bytes 28758044 | tf_op jit(solution)/shard_map/hidden_backward/pallas_call | solution.py:53
  332.8 30.2 %attention_backward.3 = (bf16[2,197,1024]{2,1,0:T(8,128)(2,1)}, bf16[416,3072]{1,0:T(8,128)(2,1)}, f32[8,1024]{1,0:T(8,128)}) custom-call(bf16[416,1024]{1,0:T(8,128)(2,1)} %get-tuple-element.88.refs_0_.refs_4_, f32[416,1024]{1,0:T(8,128)} %get-tuple-element.89.refs_1_, bf16[2,197,1024]{2,1,0:T(8,128)(2,1)} %get-tuple-element.169.refs_0_.refs_2_, ...), custom_call_target="tpu_custom_call" | custom-call | flops 4375707648 | bytes 19437596 | tf_op jit(solution)/shard_map/attention_backward/pallas_call | solution.py:53
  370.1 24.6 %attention_forward.5 = (bf16[416,1024]{1,0:T(8,128)(2,1)}, bf16[416,3072]{1,0:T(8,128)(2,1)}, bf16[416,1024]{1,0:T(8,128)(2,1)}, f32[2,16,208]{2,1,0:T(8,128)}) custom-call(bf16[2,197,1024]{2,1,0:T(8,128)(2,1)} %get-tuple-element.170.refs_0_.refs_2_, bf16[2,197,1024]{2,1,0:T(8,128)(2,1)} %copy.34.refs_1_.refs_3_, bf16[256,3072]{1,0:T(8,128)(2,1)} %bitcast.117, ...), custom_call_target="tpu_custom_call" | custom-call | flops 2971664384 | bytes 12240924 | tf_op jit(solution)/shard_map/attention_forward/pallas_call | solution.py:53
  394.6 19.3 %hidden_forward.5 = (f32[416,1024]{1,0:T(8,128)}, bf16[416,4096]{1,0:T(8,128)(2,1)}, bf16[416,1024]{1,0:T(8,128)(2,1)}, bf16[416,4096]{1,0:T(8,128)(2,1)}) custom-call(bf16[2,197,1024]{2,1,0:T(8,128)(2,1)} %get-tuple-element.170.refs_0_.refs_2_, bf16[2,197,1024]{2,1,0:T(8,128)(2,1)} %copy.34.refs_1_.refs_3_, ...), custom_call_target="tpu_custom_call" | custom-call | flops 4362076160 | bytes 22372380 | tf_op jit(solution)/shard_map/hidden_forward/pallas_call | solution.py:53
  416.5 23.1 %hidden_backward.4 = (bf16[416,4096]{1,0:T(8,128)(2,1)}, f32[416,1024]{1,0:T(8,128)}, bf16[416,1024]{1,0:T(8,128)(2,1)}, f32[8,1024]{1,0:T(8,128)}, f32[1,4096]{1,0:T(1,128)}) custom-call(bf16[2,197,1024]{2,1,0:T(8,128)(2,1)} %copy_select_fusion.1.refs_0_.refs_2_.refs_5_, bf16[416,4096]{1,0:T(8,128)(2,1)} %get-tuple-element.87.refs_1_, ...), custom_call_target="tpu_custom_call" | custom-call | flops 6979321856 | bytes 33869852 | tf_op jit(solution)/shard_map/hidden_backward/pallas_call | solution.py:53
  439.6 30.2 %attention_backward.4 = (bf16[2,197,1024]{2,1,0:T(8,128)(2,1)}, bf16[416,3072]{1,0:T(8,128)(2,1)}, f32[8,1024]{1,0:T(8,128)}) custom-call(bf16[416,1024]{1,0:T(8,128)(2,1)} %get-tuple-element.94.refs_0_.refs_2_.refs_5_, f32[416,1024]{1,0:T(8,128)} %get-tuple-element.95.refs_1_, bf16[2,197,1024]{2,1,0:T(8,128)(2,1)} %get-tuple-element.169.refs_0_.refs_2_, ...), custom_call_target="tpu_custom_call" | custom-call | flops 4375707648 | bytes 22872092 | tf_op jit(solution)/shard_map/attention_backward/pallas_call | solution.py:53
  482.7 9.6 output_forward.5
  497.8 22.5 %hidden_backward.5 = (bf16[416,4096]{1,0:T(8,128)(2,1)}, f32[416,1024]{1,0:T(8,128)}, bf16[416,1024]{1,0:T(8,128)(2,1)}, f32[8,1024]{1,0:T(8,128)}, f32[1,4096]{1,0:T(1,128)}) custom-call(bf16[2,197,1024]{2,1,0:T(8,128)(2,1)} %copy_select_fusion.refs_0_.refs_3_, bf16[416,4096]{1,0:T(8,128)(2,1)} %get-tuple-element.93.refs_3_.refs_1_, ...), custom_call_target="tpu_custom_call" | custom-call | flops 6979321856 | bytes 28758044 | tf_op jit(solution)/shard_map/hidden_backward/pallas_call | solution.py:53
  521.1 30.3 %attention_backward.5 = (bf16[2,197,1024]{2,1,0:T(8,128)(2,1)}, bf16[416,3072]{1,0:T(8,128)(2,1)}, f32[8,1024]{1,0:T(8,128)}) custom-call(bf16[416,1024]{1,0:T(8,128)(2,1)} %get-tuple-element.99.refs_0_.refs_3_, f32[416,1024]{1,0:T(8,128)} %get-tuple-element.100.refs_1_, bf16[2,197,1024]{2,1,0:T(8,128)(2,1)} %get-tuple-element.170.refs_0_.refs_2_, ...), custom_call_target="tpu_custom_call" | custom-call | flops 4375707648 | bytes 19437596 | tf_op jit(solution)/shard_map/attention_backward/pallas_call | solution.py:53
  583.5 9.6 expand_gradient.3
  638.5 10.5 %collective-permute-done.37 = bf16[256,1024]{1,0:T(8,128)(2,1)S(1)} collective-permute-done((bf16[256,1024]{1,0:T(8,128)(2,1)S(1)}, bf16[256,1024]{1,0:T(8,128)(2,1)S(1)}, u32[]{:S(2)}, u32[]{:S(2)}) %collective-permute-start.37) | collective-permute-done | bytes 524320 | tf_op jit(solution)/shard_map/ppermute | solution.py:765
  651.6 14.3 %collective-permute-done.21 = bf16[256,1536]{1,0:T(8,128)(2,1)S(1)} collective-permute-done((bf16[256,1536]{1,0:T(8,128)(2,1)S(1)}, bf16[256,1536]{1,0:T(8,128)(2,1)S(1)}, u32[]{:S(2)}, u32[]{:S(2)}) %collective-permute-start.21) | collective-permute-done | bytes 786464 | tf_op jit(solution)/shard_map/ppermute | solution.py:765
  684.5 20.7 %collective-permute-done.61 = bf16[512,1024]{1,0:T(8,128)(2,1)S(1)} collective-permute-done((bf16[512,1024]{1,0:T(8,128)(2,1)S(1)}, bf16[512,1024]{1,0:T(8,128)(2,1)S(1)}, u32[]{:S(2)}, u32[]{:S(2)}) %collective-permute-start.61) | collective-permute-done | bytes 1048608 | tf_op jit(solution)/shard_map/ppermute | solution.py:765
  706.4 21.3 %collective-permute-done.69 = bf16[512,1024]{1,0:T(8,128)(2,1)S(1)} collective-permute-done((bf16[512,1024]{1,0:T(8,128)(2,1)S(1)}, bf16[512,1024]{1,0:T(8,128)(2,1)S(1)}, u32[]{:S(2)}, u32[]{:S(2)}) %collective-permute-start.69) | collective-permute-done | bytes 1048608 | tf_op jit(solution)/shard_map/ppermute | solution.py:765
  734.3 15.9 %collective-permute-done.45 = bf16[256,2048]{1,0:T(8,128)(2,1)S(1)} collective-permute-done((bf16[256,2048]{1,0:T(8,128)(2,1)S(1)}, bf16[256,2048]{1,0:T(8,128)(2,1)S(1)}, u32[]{:S(2)}, u32[]{:S(2)}) %collective-permute-start.45) | collective-permute-done | bytes 1048608 | tf_op jit(solution)/shard_map/ppermute | solution.py:765
  756.7 15.3 %collective-permute-done.53 = bf16[256,2048]{1,0:T(8,128)(2,1)S(1)} collective-permute-done((bf16[256,2048]{1,0:T(8,128)(2,1)S(1)}, bf16[256,2048]{1,0:T(8,128)(2,1)S(1)}, u32[]{:S(2)}, u32[]{:S(2)}) %collective-permute-start.53) | collective-permute-done | bytes 1048608 | tf_op jit(solution)/shard_map/ppermute | solution.py:765
  781.2 13.9 %collective-permute-done.62 = bf16[512,1024]{1,0:T(8,128)(2,1)S(1)} collective-permute-done((bf16[512,1024]{1,0:T(8,128)(2,1)S(1)}, bf16[512,1024]{1,0:T(8,128)(2,1)S(1)}, u32[]{:S(2)}, u32[]{:S(2)}) %collective-permute-start.62) | collective-permute-done | bytes 1048608 | tf_op jit(solution)/shard_map/ppermute | solution.py:778
  796.9 43.2 %collective-permute-done.46 = bf16[256,2048]{1,0:T(8,128)(2,1)S(1)} collective-permute-done((bf16[256,2048]{1,0:T(8,128)(2,1)S(1)}, bf16[256,2048]{1,0:T(8,128)(2,1)S(1)}, u32[]{:S(2)}, u32[]{:S(2)}) %collective-permute-start.46) | collective-permute-done | bytes 1048608 | tf_op jit(solution)/shard_map/ppermute | solution.py:778
  842.2 17.9 %collective-permute-done.54 = bf16[256,2048]{1,0:T(8,128)(2,1)S(1)} collective-permute-done((bf16[256,2048]{1,0:T(8,128)(2,1)S(1)}, bf16[256,2048]{1,0:T(8,128)(2,1)S(1)}, u32[]{:S(2)}, u32[]{:S(2)}) %collective-permute-start.54) | collective-permute-done | bytes 1048608 | tf_op jit(solution)/shard_map/ppermute | solution.py:778
  869.8 13.3 %collective-permute-done.24 = bf16[256,1536]{1,0:T(8,128)(2,1)S(1)} collective-permute-done((bf16[256,1536]{1,0:T(8,128)(2,1)S(1)}, bf16[256,1536]{1,0:T(8,128)(2,1)S(1)}, u32[]{:S(2)}, u32[]{:S(2)}) %collective-permute-start.24) | collective-permute-done | bytes 786464 | tf_op jit(solution)/shard_map/ppermute | solution.py:778
  887.8 18.9 %collective-permute-done.32 = bf16[256,1536]{1,0:T(8,128)(2,1)S(1)} collective-permute-done((bf16[256,1536]{1,0:T(8,128)(2,1)S(1)}, bf16[256,1536]{1,0:T(8,128)(2,1)S(1)}, u32[]{:S(2)}, u32[]{:S(2)}) %collective-permute-start.32) | collective-permute-done | bytes 786464 | tf_op jit(solution)/shard_map/ppermute | solution.py:778
  912.3 39.0 %collective-permute-done.64 = bf16[512,1024]{1,0:T(8,128)(2,1)S(1)} collective-permute-done((bf16[512,1024]{1,0:T(8,128)(2,1)S(1)}, bf16[512,1024]{1,0:T(8,128)(2,1)S(1)}, u32[]{:S(2)}, u32[]{:S(2)}) %collective-permute-start.64) | collective-permute-done | bytes 1048608 | tf_op jit(solution)/shard_map/ppermute | solution.py:778
  957.2 16.6 %collective-permute-done.72 = bf16[512,1024]{1,0:T(8,128)(2,1)S(1)} collective-permute-done((bf16[512,1024]{1,0:T(8,128)(2,1)S(1)}, bf16[512,1024]{1,0:T(8,128)(2,1)S(1)}, u32[]{:S(2)}, u32[]{:S(2)}) %collective-permute-start.72) | collective-permute-done | bytes 1048608 | tf_op jit(solution)/shard_map/ppermute | solution.py:778
  978.4 17.8 %collective-permute-done.48 = bf16[256,2048]{1,0:T(8,128)(2,1)S(1)} collective-permute-done((bf16[256,2048]{1,0:T(8,128)(2,1)S(1)}, bf16[256,2048]{1,0:T(8,128)(2,1)S(1)}, u32[]{:S(2)}, u32[]{:S(2)}) %collective-permute-start.48) | collective-permute-done | bytes 1048608 | tf_op jit(solution)/shard_map/ppermute | solution.py:778
  996.4 22.3 %collective-permute-done.56 = bf16[256,2048]{1,0:T(8,128)(2,1)S(1)} collective-permute-done((bf16[256,2048]{1,0:T(8,128)(2,1)S(1)}, bf16[256,2048]{1,0:T(8,128)(2,1)S(1)}, u32[]{:S(2)}, u32[]{:S(2)}) %collective-permute-start.56) | collective-permute-done | bytes 1048608 | tf_op jit(solution)/shard_map/ppermute | solution.py:778
  (341 shorter events, 229.2 us)
Async XLA Ops:
  0.7 146.5 %collective-permute-start.10 = (bf16[256,4096]{1,0:T(8,128)(2,1)}, bf16[256,4096]{1,0:T(8,128)(2,1)}, u32[]{:S(2)}, u32[]{:S(2)}) collective-permute-start(bf16[256,4096]{1,0:T(8,128)(2,1)} %bitcast.104), channel_id=1, source_target_pairs={{0,8},{4,12},{8,0},{12,4},{1,9},{5,13},{9,1},{13,5},{2,10},{6,14},... | collective-permute-start | bytes 6291464 | tf_op jit(solution)/shard_map/ppermute | solution.py:765
  3.7 138.8 %collective-permute-start.1 = (bf16[256,3072]{1,0:T(8,128)(2,1)}, bf16[256,3072]{1,0:T(8,128)(2,1)}, u32[]{:S(2)}, u32[]{:S(2)}) collective-permute-start(bf16[256,3072]{1,0:T(8,128)(2,1)} %bitcast.112), channel_id=1, source_target_pairs={{0,8},{4,12},{8,0},{12,4},{1,9},{5,13},{9,1},{13,5},{2,10},{6,14},... | collective-permute-start | bytes 4718600 | tf_op jit(solution)/shard_map/ppermute | solution.py:765
  3.8 149.7 %collective-permute-start.13 = (bf16[1024,1024]{1,0:T(8,128)(2,1)}, bf16[1024,1024]{1,0:T(8,128)(2,1)}, u32[]{:S(2)}, u32[]{:S(2)}) collective-permute-start(bf16[1024,1024]{1,0:T(8,128)(2,1)} %bitcast.92), channel_id=1, source_target_pairs={{0,8},{4,12},{8,0},{12,4},{1,9},{5,13},{9,1},{13,5},{2,10},{6,14},... | collective-permute-start | bytes 6291464 | tf_op jit(solution)/shard_map/ppermute | solution.py:765
  5.7 136.4 %collective-permute-start.7 = (bf16[256,1024]{1,0:T(8,128)(2,1)}, bf16[256,1024]{1,0:T(8,128)(2,1)S(1)}, u32[]{:S(2)}, u32[]{:S(2)}) collective-permute-start(bf16[256,1024]{1,0:T(8,128)(2,1)} %bitcast.123), channel_id=1, source_target_pairs={{0,8},{4,12},{8,0},{12,4},{1,9},{5,13},{9,1},{13,5},{2,10},{6,14},... | collective-permute-start | bytes 1572872 | tf_op jit(solution)/shard_map/ppermute | solution.py:765
  7.2 132.4 %collective-permute-start.3 = (bf16[12,256]{1,0:T(8,128)(2,1)S(1)}, bf16[12,256]{1,0:T(8,128)(2,1)S(1)}, u32[]{:S(2)}, u32[]{:S(2)}) collective-permute-start(bf16[12,256]{1,0:T(8,128)(2,1)S(1)} %pad_maximum_fusion.1), channel_id=1, source_target_pairs={{0,8},{4,12},{8,0},{12,4},{1,9},{5,13},{9,1},{13,5},{2,10},{6,14},... | collective-permute-start | bytes 18440 | tf_op jit(solution)/shard_map/ppermute | solution.py:765
  146.9 49.2 %collective-permute-start.9 = (bf16[256,4096]{1,0:T(8,128)(2,1)}, bf16[256,4096]{1,0:T(8,128)(2,1)}, u32[]{:S(2)}, u32[]{:S(2)}) collective-permute-start(bf16[256,4096]{1,0:T(8,128)(2,1)} %bitcast.105), channel_id=1, source_target_pairs={{0,4},{4,0},{8,12},{12,8},{1,5},{5,1},{9,13},{13,9},{2,6},{6,2},{1... | collective-permute-start | bytes 6291464 | tf_op jit(solution)/shard_map/ppermute | solution.py:762
  147.2 48.9 %collective-permute-start.11 = (bf16[256,4096]{1,0:T(8,128)(2,1)}, bf16[256,4096]{1,0:T(8,128)(2,1)}, u32[]{:S(2)}, u32[]{:S(2)}) collective-permute-start(bf16[256,4096]{1,0:T(8,128)(2,1)} %collective-permute-done.10.refs_8_.refs_9_.refs_11_), channel_id=1, source_target_pairs={{0,4},{4,0},{8,12},{12,8},{1,5},{5,1},{9,13},{13,9},{2,6},{6,2},{1... | collective-permute-start | bytes 6291464 | tf_op jit(solution)/shard_map/ppermute | solution.py:762
  153.1 69.3 %collective-permute-start.12 = (bf16[1024,1024]{1,0:T(8,128)(2,1)S(1)}, bf16[1024,1024]{1,0:T(8,128)(2,1)S(1)}, u32[]{:S(2)}, u32[]{:S(2)}) collective-permute-start(bf16[1024,1024]{1,0:T(8,128)(2,1)S(1)} %bitcast.99), channel_id=1, source_target_pairs={{0,4},{4,0},{8,12},{12,8},{1,5},{5,1},{9,13},{13,9},{2,6},{6,2},{1... | collective-permute-start | bytes 6291464 | tf_op jit(solution)/shard_map/ppermute | solution.py:762
  153.4 68.9 %collective-permute-start.14 = (bf16[1024,1024]{1,0:T(8,128)(2,1)}, bf16[1024,1024]{1,0:T(8,128)(2,1)}, u32[]{:S(2)}, u32[]{:S(2)}) collective-permute-start(bf16[1024,1024]{1,0:T(8,128)(2,1)} %collective-permute-done.13.refs_4_.refs_5_.refs_7_), channel_id=1, source_target_pairs={{0,4},{4,0},{8,12},{12,8},{1,5},{5,1},{9,13},{13,9},{2,6},{6,2},{1... | collective-permute-start | bytes 6291464 | tf_op jit(solution)/shard_map/ppermute | solution.py:762
  251.6 117.3 %collective-permute-start.16 = (bf16[2,197,1024]{2,0,1:T(2,128)(2,1)S(1)}, bf16[2,197,1024]{2,0,1:T(2,128)(2,1)S(1)}, u32[]{:S(2)}, u32[]{:S(2)}) collective-permute-start(bf16[2,197,1024]{2,0,1:T(2,128)(2,1)S(1)} %copy.32), channel_id=1, source_target_pairs={{0,16},{1,17},{2,18},{3,19},{4,20},{5,21},{6,22},{7,23},{8,24},{9,... | collective-permute-start | bytes 2420744 | tf_op jit(solution)/shard_map/ppermute | solution.py:818
  365.0 49.0 %collective-permute-start.17 = (bf16[2,197,1024]{2,0,1:T(2,128)(2,1)S(1)}, bf16[2,197,1024]{2,0,1:T(2,128)(2,1)}, u32[]{:S(2)}, u32[]{:S(2)}) collective-permute-start(bf16[2,197,1024]{2,0,1:T(2,128)(2,1)S(1)} %copy.37), channel_id=1, source_target_pairs={{16,0},{17,1},{18,2},{19,3},{20,4},{21,5},{22,6},{23,7},{24,8},{25... | collective-permute-start | bytes 2420744 | tf_op jit(solution)/shard_map/ppermute | solution.py:818
  571.9 63.0 %collective-permute-start.60 = (bf16[512,1024]{1,0:T(8,128)(2,1)}, bf16[512,1024]{1,0:T(8,128)(2,1)}, u32[]{:S(2)}, u32[]{:S(2)}) collective-permute-start(bf16[512,1024]{1,0:T(8,128)(2,1)} %get-tuple-element.135), channel_id=1, source_target_pairs={{0,4},{4,0},{8,12},{12,8},{1,5},{5,1},{9,13},{13,9},{2,6},{6,2},{1... | collective-permute-start | bytes 3145736 | tf_op jit(solution)/shard_map/ppermute | solution.py:762
  571.9 66.1 %collective-permute-start.68 = (bf16[512,1024]{1,0:T(8,128)(2,1)}, bf16[512,1024]{1,0:T(8,128)(2,1)S(1)}, u32[]{:S(2)}, u32[]{:S(2)}) collective-permute-start(bf16[512,1024]{1,0:T(8,128)(2,1)} %get-tuple-element.139), channel_id=1, source_target_pairs={{0,4},{4,0},{8,12},{12,8},{1,5},{5,1},{9,13},{13,9},{2,6},{6,2},{1... | collective-permute-start | bytes 3145736 | tf_op jit(solution)/shard_map/ppermute | solution.py:762
  650.0 55.2 %collective-permute-start.61 = (bf16[512,1024]{1,0:T(8,128)(2,1)S(1)}, bf16[512,1024]{1,0:T(8,128)(2,1)S(1)}, u32[]{:S(2)}, u32[]{:S(2)}) collective-permute-start(bf16[512,1024]{1,0:T(8,128)(2,1)S(1)} %add_convert_fusion.5), channel_id=1, source_target_pairs={{0,8},{4,12},{8,0},{12,4},{1,9},{5,13},{9,1},{13,5},{2,10},{6,14},... | collective-permute-start | bytes 3145736 | tf_op jit(solution)/shard_map/ppermute | solution.py:765
  670.8 58.3 %collective-permute-start.43 = (bf16[256,2048]{1,0:T(8,128)(2,1)S(1)}, bf16[256,2048]{1,0:T(8,128)(2,1)S(1)}, u32[]{:S(2)}, u32[]{:S(2)}) collective-permute-start(bf16[256,2048]{1,0:T(8,128)(2,1)S(1)} %copy-done.38), channel_id=1, source_target_pairs={{0,4},{4,0},{8,12},{12,8},{1,5},{5,1},{9,13},{13,9},{2,6},{6,2},{1... | collective-permute-start | bytes 3145736 | tf_op jit(solution)/shard_map/ppermute | solution.py:762
  680.4 47.3 %collective-permute-start.69 = (bf16[512,1024]{1,0:T(8,128)(2,1)S(1)}, bf16[512,1024]{1,0:T(8,128)(2,1)S(1)}, u32[]{:S(2)}, u32[]{:S(2)}) collective-permute-start(bf16[512,1024]{1,0:T(8,128)(2,1)S(1)} %add_convert_fusion.2), channel_id=1, source_target_pairs={{0,8},{4,12},{8,0},{12,4},{1,9},{5,13},{9,1},{13,5},{2,10},{6,14},... | collective-permute-start | bytes 3145736 | tf_op jit(solution)/shard_map/ppermute | solution.py:765
  682.8 67.4 %collective-permute-start.45 = (bf16[256,2048]{1,0:T(8,128)(2,1)S(1)}, bf16[256,2048]{1,0:T(8,128)(2,1)S(1)}, u32[]{:S(2)}, u32[]{:S(2)}) collective-permute-start(bf16[256,2048]{1,0:T(8,128)(2,1)S(1)} %add_convert_fusion.11), channel_id=1, source_target_pairs={{0,8},{4,12},{8,0},{12,4},{1,9},{5,13},{9,1},{13,5},{2,10},{6,14},... | collective-permute-start | bytes 3145736 | tf_op jit(solution)/shard_map/ppermute | solution.py:765
  684.5 70.9 %collective-permute-start.51 = (bf16[256,2048]{1,0:T(8,128)(2,1)S(1)}, bf16[256,2048]{1,0:T(8,128)(2,1)S(1)}, u32[]{:S(2)}, u32[]{:S(2)}) collective-permute-start(bf16[256,2048]{1,0:T(8,128)(2,1)S(1)} %copy-done.36), channel_id=1, source_target_pairs={{0,4},{4,0},{8,12},{12,8},{1,5},{5,1},{9,13},{13,9},{2,6},{6,2},{1... | collective-permute-start | bytes 3145736 | tf_op jit(solution)/shard_map/ppermute | solution.py:762
  705.2 66.8 %collective-permute-start.53 = (bf16[256,2048]{1,0:T(8,128)(2,1)S(1)}, bf16[256,2048]{1,0:T(8,128)(2,1)S(1)}, u32[]{:S(2)}, u32[]{:S(2)}) collective-permute-start(bf16[256,2048]{1,0:T(8,128)(2,1)S(1)} %add_convert_fusion.8), channel_id=1, source_target_pairs={{0,8},{4,12},{8,0},{12,4},{1,9},{5,13},{9,1},{13,5},{2,10},{6,14},... | collective-permute-start | bytes 3145736 | tf_op jit(solution)/shard_map/ppermute | solution.py:765
  727.7 49.4 %collective-permute-start.39 = (bf16[256,1024]{1,0:T(8,128)(2,1)S(1)}, bf16[256,1024]{1,0:T(8,128)(2,1)S(1)}, u32[]{:S(2)}, u32[]{:S(2)}) collective-permute-start(bf16[256,1024]{1,0:T(8,128)(2,1)S(1)} %fusion.9), channel_id=1, source_target_pairs={{2,1},{5,6},{10,9},{13,14},{18,17},{21,22},{26,25},{29,30}} | collective-permute-start | bytes 1572872 | tf_op jit(solution)/shard_map/ppermute | solution.py:778
  729.1 49.7 %collective-permute-start.22 = (bf16[256,1536]{1,0:T(8,128)(2,1)S(1)}, bf16[256,1536]{1,0:T(8,128)(2,1)S(1)}, u32[]{:S(2)}, u32[]{:S(2)}) collective-permute-start(bf16[256,1536]{1,0:T(8,128)(2,1)S(1)} %add_convert_fusion.16), channel_id=1, source_target_pairs={{0,1},{3,2},{4,5},{7,6},{8,9},{11,10},{12,13},{15,14},{16,17},{19,... | collective-permute-start | bytes 2359304 | tf_op jit(solution)/shard_map/ppermute | solution.py:778
  772.1 89.2 %collective-permute-start.70 = (bf16[512,1024]{1,0:T(8,128)(2,1)S(1)}, bf16[512,1024]{1,0:T(8,128)(2,1)S(1)}, u32[]{:S(2)}, u32[]{:S(2)}) collective-permute-start(bf16[512,1024]{1,0:T(8,128)(2,1)S(1)} %add_convert_fusion.1), channel_id=1, source_target_pairs={{0,1},{3,2},{4,5},{7,6},{8,9},{11,10},{12,13},{15,14},{16,17},{19,... | collective-permute-start | bytes 3145736 | tf_op jit(solution)/shard_map/ppermute | solution.py:778
  777.1 63.0 %collective-permute-start.46 = (bf16[256,2048]{1,0:T(8,128)(2,1)S(1)}, bf16[256,2048]{1,0:T(8,128)(2,1)S(1)}, u32[]{:S(2)}, u32[]{:S(2)}) collective-permute-start(bf16[256,2048]{1,0:T(8,128)(2,1)S(1)} %add_convert_fusion.10), channel_id=1, source_target_pairs={{0,1},{3,2},{4,5},{7,6},{8,9},{11,10},{12,13},{15,14},{16,17},{19,... | collective-permute-start | bytes 3145736 | tf_op jit(solution)/shard_map/ppermute | solution.py:778
  778.7 81.4 %collective-permute-start.54 = (bf16[256,2048]{1,0:T(8,128)(2,1)S(1)}, bf16[256,2048]{1,0:T(8,128)(2,1)S(1)}, u32[]{:S(2)}, u32[]{:S(2)}) collective-permute-start(bf16[256,2048]{1,0:T(8,128)(2,1)S(1)} %add_convert_fusion.7), channel_id=1, source_target_pairs={{0,1},{3,2},{4,5},{7,6},{8,9},{11,10},{12,13},{15,14},{16,17},{19,... | collective-permute-start | bytes 3145736 | tf_op jit(solution)/shard_map/ppermute | solution.py:778
  780.3 61.1 %collective-permute-start.41 = (bf16[256,1024]{1,0:T(8,128)(2,1)S(1)}, bf16[256,1024]{1,0:T(8,128)(2,1)S(1)}, u32[]{:S(2)}, u32[]{:S(2)}) collective-permute-start(bf16[256,1024]{1,0:T(8,128)(2,1)S(1)} %add_convert_fusion.18), channel_id=1, source_target_pairs={{1,2},{6,5},{9,10},{14,13},{17,18},{22,21},{25,26},{30,29}} | collective-permute-start | bytes 1572872 | tf_op jit(solution)/shard_map/ppermute | solution.py:778
  795.2 68.3 %collective-permute-start.40 = (bf16[256,1024]{1,0:T(8,128)(2,1)S(1)}, bf16[256,1024]{1,0:T(8,128)(2,1)S(1)}, u32[]{:S(2)}, u32[]{:S(2)}) collective-permute-start(bf16[256,1024]{1,0:T(8,128)(2,1)S(1)} %add_convert_fusion.18), channel_id=1, source_target_pairs={{1,0},{6,7},{9,8},{14,15},{17,16},{22,23},{25,24},{30,31}} | collective-permute-start | bytes 1572872 | tf_op jit(solution)/shard_map/ppermute | solution.py:778
  906.7 44.6 %collective-permute-start.64 = (bf16[512,1024]{1,0:T(8,128)(2,1)S(1)}, bf16[512,1024]{1,0:T(8,128)(2,1)S(1)}, u32[]{:S(2)}, u32[]{:S(2)}) collective-permute-start(bf16[512,1024]{1,0:T(8,128)(2,1)S(1)} %add_convert_fusion.3), channel_id=1, source_target_pairs={{1,0},{6,7},{9,8},{14,15},{17,16},{22,23},{25,24},{30,31}} | collective-permute-start | bytes 3145736 | tf_op jit(solution)/shard_map/ppermute | solution.py:778
  908.0 44.0 %collective-permute-start.73 = (bf16[512,1024]{1,0:T(8,128)(2,1)S(1)}, bf16[512,1024]{1,0:T(8,128)(2,1)S(1)}, u32[]{:S(2)}, u32[]{:S(2)}) collective-permute-start(bf16[512,1024]{1,0:T(8,128)(2,1)S(1)} %add_convert_fusion), channel_id=1, source_target_pairs={{1,2},{6,5},{9,10},{14,13},{17,18},{22,21},{25,26},{30,29}} | collective-permute-start | bytes 3145736 | tf_op jit(solution)/shard_map/ppermute | solution.py:778
  910.1 44.1 %collective-permute-start.66 = (bf16[512,1024]{1,0:T(8,128)(2,1)S(1)}, bf16[512,1024]{1,0:T(8,128)(2,1)S(1)}, u32[]{:S(2)}, u32[]{:S(2)}) collective-permute-start(bf16[512,1024]{1,0:T(8,128)(2,1)S(1)} %collective-permute-done.65), channel_id=1, source_target_pairs={{2,3},{5,4},{10,11},{13,12},{18,19},{21,20},{26,27},{29,28}} | collective-permute-start | bytes 3145736 | tf_op jit(solution)/shard_map/ppermute | solution.py:778
  911.0 62.8 %collective-permute-start.72 = (bf16[512,1024]{1,0:T(8,128)(2,1)S(1)}, bf16[512,1024]{1,0:T(8,128)(2,1)S(1)}, u32[]{:S(2)}, u32[]{:S(2)}) collective-permute-start(bf16[512,1024]{1,0:T(8,128)(2,1)S(1)} %add_convert_fusion), channel_id=1, source_target_pairs={{1,0},{6,7},{9,8},{14,15},{17,16},{22,23},{25,24},{30,31}} | collective-permute-start | bytes 3145736 | tf_op jit(solution)/shard_map/ppermute | solution.py:778
  973.8 44.9 %collective-permute-start.56 = (bf16[256,2048]{1,0:T(8,128)(2,1)S(1)}, bf16[256,2048]{1,0:T(8,128)(2,1)S(1)}, u32[]{:S(2)}, u32[]{:S(2)}) collective-permute-start(bf16[256,2048]{1,0:T(8,128)(2,1)S(1)} %add_convert_fusion.6), channel_id=1, source_target_pairs={{1,0},{6,7},{9,8},{14,15},{17,16},{22,23},{25,24},{30,31}} | collective-permute-start | bytes 3145736 | tf_op jit(solution)/shard_map/ppermute | solution.py:778
  975.1 43.6 %collective-permute-start.58 = (bf16[256,2048]{1,0:T(8,128)(2,1)S(1)}, bf16[256,2048]{1,0:T(8,128)(2,1)S(1)}, u32[]{:S(2)}, u32[]{:S(2)}) collective-permute-start(bf16[256,2048]{1,0:T(8,128)(2,1)S(1)} %collective-permute-done.57), channel_id=1, source_target_pairs={{2,3},{5,4},{10,11},{13,12},{18,19},{21,20},{26,27},{29,28}} | collective-permute-start | bytes 3145736 | tf_op jit(solution)/shard_map/ppermute | solution.py:778
  (97 other events, 2121.6 us)

commit v2 on v0

v2 whole, which is shorter than its diff:
```python
from functools import partial

import jax
import jax.numpy as jnp
from jax import lax
from jax.experimental import pallas as pl
from jax.experimental.pallas import tpu as pltpu
from jax.sharding import PartitionSpec as P

HEADS = 16
EPSILON = 1e-06
NEGATIVE = -1e30
F32 = jnp.float32
BF16 = jnp.bfloat16
VMEM_LIMIT = 58 * 2**20
ROOT_HALF = 0.7071067811865476
ROOT_TAU = 0.3989422804014327
ANY = pl.BlockSpec(memory_space=pl.ANY)
VMEM = pl.BlockSpec(memory_space=pltpu.VMEM)
SMEM = pl.BlockSpec(memory_space=pltpu.SMEM)
COST = 64
SEND_FIRST = {4: (3, 1, 2, 0)}
GAIN0, GAIN1, SHIFT0, SHIFT1, QUERY, VALUE, OUT, FEED, EXPAND = range(9)


def padded(length):
    return -(-length // 16) * 16


def contract(left, right, left_dim, right_dim):
    return lax.dot_general(
        left, right, (((left_dim,), (right_dim,)), ((), ())), preferred_element_type=F32
    )


def standardized(values):
    center = values - jnp.mean(values, axis=-1, keepdims=True)
    spread = jnp.mean(center * center, axis=-1, keepdims=True)
    scale = lax.rsqrt(spread + EPSILON)
    return center * scale, scale


def norm_pull(grad, gain, unit, scale):
    scaled = grad * gain
    mean = jnp.mean(scaled, axis=-1, keepdims=True)
    along = jnp.mean(scaled * unit, axis=-1, keepdims=True)
    return scale * (scaled - mean - unit * along)


def call(body, name, operands, specs, outs, scratch, flops):
    moved = sum(o.size * o.dtype.itemsize for o in operands)
    out_shape = [jax.ShapeDtypeStruct(shape, dtype) for shape, dtype in outs]
    moved += sum(o.size * o.dtype.itemsize for o in out_shape)
    return pl.pallas_call(
        body,
        out_shape=out_shape,
        in_specs=specs,
        out_specs=[VMEM] * len(outs),
        scratch_shapes=scratch,
        compiler_params=pltpu.CompilerParams(vmem_limit_bytes=VMEM_LIMIT),
        cost_estimate=pl.CostEstimate(flops=flops // COST, bytes_accessed=moved // COST, transcendentals=0),
        name=name,
    )(*operands)


def start_pieces(pieces, order_ref, target, sems, slot, columns):
    rows = pieces[0].shape[0]
    copies = []
    for index, piece in enumerate(pieces):
        where = pl.multiple_of(order_ref[index] * rows, rows)
        copy = pltpu.make_async_copy(
            piece.at[:, columns], target.at[pl.ds(where, rows), columns], sems.at[slot, index]
        )
        copy.start()
        copies.append(copy)
    return copies


def wait_all(copies):
    for copy in copies:
        copy.wait()


def start_chosen(section, lower, upper, target, sem):
    if lower is upper:
        copy = pltpu.make_async_copy(lower, target, sem)
        copy.start()
        return copy

    @pl.when(section == 0)
    def _():
        pltpu.make_async_copy(lower, target, sem).start()

    @pl.when(section != 0)
    def _():
        pltpu.make_async_copy(upper, target, sem).start()

    return pltpu.make_async_copy(lower, target, sem)


def eights(values):
    return jnp.sum(values.reshape(-1, 8, values.shape[-1]), axis=0)


def attention_stage(x, vec, norm, packed, mixed, logs, columns, full, loads, count, length):
    rows, width = x.shape
    space = rows // count
    head = width // HEADS
    pair = 2 * head
    scale = head**-0.5
    gain, shift = vec[GAIN0 : GAIN0 + 1], vec[SHIFT0 : SHIFT0 + 1]

    def step(here):
        unit, _ = standardized(x[here].astype(F32))
        norm[here] = (unit * gain + shift).astype(BF16)

    step(pl.ds(0, rows))
    for block in range(3):
        wait_all(loads[block])
        done = contract(norm[...], full[:, block * width : (block + 1) * width], 1, 0)
        if block != 1:
            bias = QUERY if block == 0 else VALUE
            done = done + vec[bias : bias + 1]
        packed[:, block * width : (block + 1) * width] = done.astype(BF16)
    lane = lax.broadcasted_iota(jnp.int32, (space, pair), 1)
    left = lane < head
    live = lax.broadcasted_iota(jnp.int32, (space, pair), 0) < length
    key_live = lax.broadcasted_iota(jnp.int32, (space, space), 1) < length
    columns[...] = jnp.zeros_like(columns)

    def heads(index, carry):
        for image in range(count):
            span = pl.ds(image * space, space)

            def part(block):
                offset = pl.multiple_of(block * width + index * pair, pair)
                return packed[span, pl.ds(offset, pair)]

            query, key, value = part(0).astype(F32) * scale, part(1), part(2).astype(F32)
            found = []
            tops = []
            for side in range(2):
                mine = left if side == 0 else ~left
                asked = jnp.where(mine, query, 0.0).astype(BF16)
                held = jnp.where(live, jnp.where(mine, value, 1.0), 0.0).astype(BF16)
                scores = jnp.where(key_live, contract(asked, key, 1, 1), NEGATIVE)
                top = jnp.max(scores, axis=-1, keepdims=True)
                raised = jnp.exp(scores - top).astype(BF16)
                found.append(contract(raised, held, 1, 0))
                tops.append(top)
            inside = jnp.where(left, found[0], found[1])
            total = jnp.where(left, found[1], found[0])
            turned = pltpu.roll(total, head, 1)
            offset = pl.multiple_of(index * pair, pair)
            mixed[span, pl.ds(offset, pair)] = (inside / turned).astype(BF16)
            logged = jnp.log(turned)
            first = tops[0] + logged[:, 0:1]
            second = tops[1] + logged[:, head : head + 1]
            known = columns[image]
            known = jnp.where(lane == 2 * index, first, known)
            columns[image] = jnp.where(lane == 2 * index + 1, second, known)
        return carry

    lax.fori_loop(0, HEADS // 2, heads, 0)
    for image in range(count):
        logs[image] = columns[image].T[0:HEADS]


def hidden_stage(x, vec, mixed, middle, active, second, slope, full_out, full, first_load, loads):
    rows, width = x.shape
    wait_all(first_load)
    gain, shift, bias = vec[GAIN1 : GAIN1 + 1], vec[SHIFT1 : SHIFT1 + 1], vec[OUT : OUT + 1]
    middle[...] = contract(mixed[...], full_out[...], 1, 0)

    def step(here):
        total = middle[here] + x[here].astype(F32) + bias
        middle[here] = total
        unit, _ = standardized(total)
        second[here] = (unit * gain + shift).astype(BF16)

    step(pl.ds(0, rows))
    for block, load in enumerate(loads):
        wait_all(load)
        part = slice(block * width, (block + 1) * width)
        value = contract(second[...], full[:, part], 1, 0) + vec[EXPAND + block - 0 : EXPAND + block + 1]
        share = 0.5 + 0.5 * lax.erf(value * ROOT_HALF)
        active[:, part] = (value * share).astype(BF16)
        density = ROOT_TAU * jnp.exp(-0.5 * value * value)
        slope[:, part] = (share + value * density).astype(BF16)


def forward(lower, upper, mixed_in, qkv, out, expand, params, meta, count, length):
    rows, width = lower.shape
    space = rows // count
    pair = 2 * width // HEADS
    attend, feed = qkv is not None, expand is not None
    parts = len(qkv if attend else expand)
    inner = expand[0].shape[1] if feed else 0
    blocks = inner // width
    same = lower is upper

    def body(*refs):
        refs = list(refs)
        low = refs.pop(0)
        up = low if same else refs.pop(0)
        if not attend:
            arrived = refs.pop(0)
        lists = [[refs.pop(0) for _ in range(parts)] for _ in range(attend + 2 * feed)]
        vec, info = refs.pop(0), refs.pop(0)
        if attend:
            norm, packed, mixed, logs = (refs.pop(0) for _ in range(4))
        if feed:
            middle, active, second, slope = (refs.pop(0) for _ in range(4))
        x, x_sem = refs.pop(0), refs.pop(0)
        section = info[parts]
        take = start_chosen(section, low, up, x, x_sem.at[0])
        if attend:
            columns, full, a_sem = (refs.pop(0) for _ in range(3))
            weight = lists.pop(0)
            loads = [
                start_pieces(weight, info, full, a_sem, block, pl.ds(block * width, width))
                for block in range(3)
            ]
        if feed:
            full_out, full_in, o_sem, w_sem = (refs.pop(0) for _ in range(4))
            if not attend:
                mixed = refs.pop(0)
                extra = pltpu.make_async_copy(arrived, mixed, x_sem.at[1])
                extra.start()
            first_load = start_pieces(lists[0], info, full_out, o_sem, 0, pl.ds(0, width))
            inner_loads = [
                start_pieces(lists[1], info, full_in, w_sem, block, pl.ds(block * width, width))
                for block in range(blocks)
            ]
        take.wait()
        if attend:
            attention_stage(
                x, vec, norm, packed, mixed, logs, columns, full, loads, count, length
            )
        if feed:
            if not attend:
                extra.wait()
            hidden_stage(
                x, vec, mixed, middle, active, second, slope, full_out, full_in, first_load,
                inner_loads,
            )

    outs, inputs = [], [lower] if same else [lower, upper]
    scratch = [pltpu.VMEM((rows, width), BF16), pltpu.SemaphoreType.DMA((2,))]
    flops = 0
    if attend:
        outs += [
            ((rows, width), BF16),
            ((rows, 3 * width), BF16),
            ((rows, width), BF16),
            ((count, HEADS, space), F32),
        ]
        scratch += [
            pltpu.VMEM((count, space, pair), F32),
            pltpu.VMEM((width, 3 * width), BF16),
            pltpu.SemaphoreType.DMA((3, parts)),
        ]
        flops += 2 * rows * width * (3 * width + 2 * space)
    else:
        inputs += [mixed_in]
    if feed:
        outs += [
            ((rows, width), F32),
            ((rows, inner), BF16),
            ((rows, width), BF16),
            ((rows, inner), BF16),
        ]
        scratch += [
            pltpu.VMEM((width, width), BF16),
            pltpu.VMEM((width, inner), BF16),
            pltpu.SemaphoreType.DMA((1, parts)),
            pltpu.SemaphoreType.DMA((blocks, parts)),
        ]
        if not attend:
            scratch += [pltpu.VMEM((rows, width), BF16)]
        flops += 2 * rows * width * (width + inner)
    weights = (list(qkv) if attend else []) + (list(out) + list(expand) if feed else [])
    return call(
        body,
        "forward" + "_attend" * attend + "_feed" * feed,
        inputs + weights + [params, meta],
        [ANY] * (len(inputs) + len(weights)) + [VMEM, SMEM],
        outs,
        scratch,
        flops,
    )


def output_forward(middle, active, pieces, params, meta, count):
    rows, width = middle.shape
    inner = active.shape[1]
    space = rows // count
    parts = len(pieces)
    blocks = 2
    part_width = width // blocks

    def body(*refs):
        refs = list(refs)
        mid_in, act_in = refs.pop(0), refs.pop(0)
        reduce = [refs.pop(0) for _ in range(parts)]
        vec, info, result, mid, act, full, x_sem, w_sem = refs
        copies = [
            pltpu.make_async_copy(act_in, act, x_sem.at[0]),
            pltpu.make_async_copy(mid_in, mid, x_sem.at[1]),
        ]
        copies[0].start()
        loads = [
            start_pieces(reduce, info, full, w_sem, block, pl.ds(block * part_width, part_width))
            for block in range(blocks)
        ]
        copies[1].start()
        copies[0].wait()
        for block in range(blocks):
            wait_all(loads[block])
            if block == 0:
                copies[1].wait()
            part = slice(block * part_width, (block + 1) * part_width)
            value = contract(act[...], full[:, part], 1, 0) + mid[:, part] + vec[FEED : FEED + 1, part]
            for image in range(count):
                alive = jnp.where(info[parts + 1 + image] > 0, 1.0, 0.0)
                here = slice(image * space, (image + 1) * space)
                result[here, part] = (value[here] * alive).astype(BF16)

    return call(
        body,
        "output_forward",
        [middle, active] + list(pieces) + [params, meta],
        [ANY] * (2 + parts) + [VMEM, SMEM],
        [((rows, width), BF16)],
        [
            pltpu.VMEM((rows, width), F32),
            pltpu.VMEM((rows, inner), BF16),
            pltpu.VMEM((inner, width), BF16),
            pltpu.SemaphoreType.DMA((2,)),
            pltpu.SemaphoreType.DMA((blocks, parts)),
        ],
        2 * rows * width * inner,
    )[0]


def hidden_back_stage(
    grad, vec, info, feed, slope, middle, hidden, second, mid_grad, branch, sums, inner_sums, full_out,
    full, deep, first_load, load, for_slope, for_middle, tallies, count, parts,
):
    rows, width = grad.shape
    space = rows // count
    half = width // 2
    for image in range(count):
        alive = jnp.where(info[parts + 1 + image] > 0, 1.0, 0.0)
        here = slice(image * space, (image + 1) * space)
        feed[here] = (grad[here].astype(F32) * alive).astype(BF16)
    for_slope.wait()
    for index in range(parts):
        wait_all(first_load[index])
        where = pl.multiple_of(info[index] * deep, deep)
        value = contract(feed[...], full_out[pl.ds(where, deep)], 1, 1)
        value = (value * slope[:, pl.ds(where, deep)].astype(F32)).astype(BF16)
        hidden[:, pl.ds(where, deep)] = value
        inner_sums[:, pl.ds(where, deep)] = jnp.sum(value.astype(F32), axis=0, keepdims=True)
    wait_all(load)
    for block in range(2):
        second[:, block * half : (block + 1) * half] = contract(
            hidden[...], full[block * half : (block + 1) * half], 1, 1
        )
    for_middle.wait()
    gain = vec[GAIN1 : GAIN1 + 1]
    tallies[...] = jnp.zeros_like(tallies)

    def step(here):
        unit, scale = standardized(middle[here])
        down = second[here]
        top = feed[here].astype(F32)
        total = top + norm_pull(down, gain, unit, scale)
        low = total.astype(BF16)
        mid_grad[here] = total
        branch[here] = low
        tallies[0] += eights(down * unit)
        tallies[1] += eights(down)
        tallies[2] += eights(low.astype(F32))
        tallies[3] += eights(top)

    step(pl.ds(0, rows))
    for index in range(4):
        sums[index : index + 1] = jnp.sum(tallies[index], axis=0, keepdims=True)


def attention_back_stage(
    x, vec, branch, mid_grad, packed, mixed, logs, grads, result, sums, down, normal, stage, full_out,
    full, first_load, load, takes, tallies, count, length,
):
    rows, width = x.shape
    space = rows // count
    head = width // HEADS
    pair = 2 * head
    scale = head**-0.5
    half = width // 2
    wait_all(first_load)
    down[...] = contract(branch[...], full_out[...], 1, 1).astype(BF16)
    wait_all(takes)
    owner = lax.shift_right_logical(
        lax.broadcasted_iota(jnp.int32, (HEADS, width), 1), head.bit_length() - 1
    )
    chosen = jnp.where(
        owner == lax.broadcasted_iota(jnp.int32, (HEADS, width), 0), 1.0, 0.0
    ).astype(BF16)
    left = lax.broadcasted_iota(jnp.int32, (space, pair), 1) < head
    live = lax.broadcasted_iota(jnp.int32, (space, pair), 0) < length
    key_live = lax.broadcasted_iota(jnp.int32, (space, space), 0) < length
    for image in range(count):
        span = pl.ds(image * space, space)
        product = down[span].astype(F32) * mixed[span].astype(F32)
        coarse = product.astype(BF16)
        fine = (product - coarse.astype(F32)).astype(BF16)
        stage[image, :, 0:space] = contract(chosen, coarse, 1, 1) + contract(chosen, fine, 1, 1)

    def heads(index, carry):
        for image in range(count):
            span = pl.ds(image * space, space)

            def part(block):
                offset = pl.multiple_of(block * width + index * pair, pair)
                return packed[span, pl.ds(offset, pair)]

            query, key, value = part(0), part(1), part(2)
            wide = key.astype(F32) * scale
            value = value.astype(F32)
            arrived = down[span, pl.ds(pl.multiple_of(index * pair, pair), pair)]
            found = []
            for side in range(2):
                mine = left if side == 0 else ~left
                log = logs[image, pl.ds(2 * index + side, 1), :]
                dot = stage[image, pl.ds(2 * index + side, 1), 0:space]
                scores = contract(jnp.where(mine, wide, 0.0).astype(BF16), query, 1, 1)
                chance = jnp.exp(jnp.where(key_live, scores - log, NEGATIVE))
                back = contract(jnp.where(mine, value, 0.0).astype(BF16), arrived, 1, 1)
                change = (chance * (back - dot)).astype(BF16)
                found.append(
                    (
                        contract(change, key, 0, 0),
                        contract(change, query, 1, 0),
                        contract(chance.astype(BF16), arrived, 1, 0),
                    )
                )
            for block, factor in enumerate((scale, scale, 1.0)):
                total = jnp.where(left, found[0][block], found[1][block]) * factor
                offset = pl.multiple_of(block * width + index * pair, pair)
                grads[span, pl.ds(offset, pair)] = jnp.where(live, total, 0.0).astype(BF16)
        return carry

    lax.fori_loop(0, HEADS // 2, heads, 0)
    wait_all(load)
    for block in range(2):
        normal[:, block * half : (block + 1) * half] = contract(
            grads[...], full[block * half : (block + 1) * half], 1, 1
        )
    gain = vec[GAIN0 : GAIN0 + 1]
    tallies[...] = jnp.zeros_like(tallies)

    def step(here):
        unit, rate = standardized(x[here].astype(F32))
        grad = normal[here]
        tallies[0] += eights(grad * unit)
        tallies[1] += eights(grad)
        result[here] = (mid_grad[here] + norm_pull(grad, gain, unit, rate)).astype(BF16)

    step(pl.ds(0, rows))
    for index in range(2):
        sums[index : index + 1] = jnp.sum(tallies[index], axis=0, keepdims=True)
    sums[2:3] = jnp.sum(grads[:, 0:width].astype(F32), axis=0, keepdims=True)
    sums[3:4] = jnp.sum(grads[:, 2 * width : 3 * width].astype(F32), axis=0, keepdims=True)


def backward(
    start, lower, upper, kept_low, kept_up, reduce, expand, out, qkv, params, meta, count, length
):
    feed, attend = reduce is not None, qkv is not None
    rows, width = start[0].shape
    space = rows // count
    pair = 2 * width // HEADS
    parts = len(reduce if feed else qkv)
    inner = expand[0].shape[1] if feed else 0
    deep = reduce[0].shape[0] if feed else 0
    both = feed and attend
    choices = []
    if feed:
        choices += [(kept_low[0], kept_up[0]), (kept_low[1], kept_up[1])]
        if start[0] is not start[1]:
            choices += [start]
    if attend:
        choices += [(kept_low[index], kept_up[index]) for index in (2, 3, 4)]
        choices += [(lower, upper)]
    plain = [start[0]] if feed and start[0] is start[1] else [] if feed else list(start)
    operands = []
    for low, up in choices:
        operands += [low] if low is up else [low, up]

    def body(*refs):
        refs = list(refs)
        firsts = [refs.pop(0) for _ in plain]
        pairs = []
        for low, up in choices:
            one = refs.pop(0)
            pairs.append((one, one if low is up else refs.pop(0)))
        lists = [[refs.pop(0) for _ in range(parts)] for _ in range(2 * feed + 2 * attend)]
        vec, info = refs.pop(0), refs.pop(0)
        section = info[parts]
        if feed:
            hidden, branch, feed_sums, inner_sums = (refs.pop(0) for _ in range(4))
            mid_grad = None if both else refs.pop(0)
        if attend:
            result, grads, sums = (refs.pop(0) for _ in range(3))
        tallies, x_sem = refs.pop(0), refs.pop(0)
        if feed:
            grad, keep, slope, middle, second, full_out, full, o_sem, w_sem = (
                refs.pop(0) for _ in range(9)
            )
            if both:
                mid_grad = refs.pop(0)
            begin = pairs.pop(2) if start[0] is not start[1] else (firsts[0], firsts[0])
            take = start_chosen(section, *begin, grad, x_sem.at[0])
            for_slope = start_chosen(section, *pairs.pop(0), slope, x_sem.at[1])
            first_load = [
                start_pieces(
                    [piece], Shifted(info, index), full_out, o_sem.at[pl.ds(index, 1)], 0,
                    pl.ds(0, width),
                )
                for index, piece in enumerate(lists.pop(0))
            ]
            for_middle = start_chosen(section, *pairs.pop(0), middle, x_sem.at[2])
            load = start_pieces(lists.pop(0), info, full, w_sem, 0, pl.ds(0, inner))
        if attend:
            x, packed, mixed, logs, down, normal, stage, full_o, full_q, p_sem, q_sem = (
                refs.pop(0) for _ in range(11)
            )
            if not feed:
                branch, mid_grad = refs.pop(0), refs.pop(0)
                givens = [
                    pltpu.make_async_copy(source, target, x_sem.at[index])
                    for index, (source, target) in enumerate(zip(firsts, (branch, mid_grad)))
                ]
                for given in givens:
                    given.start()
            project_load = start_pieces(lists.pop(0), info, full_o, p_sem, 0, pl.ds(0, width))
            takes = [
                start_chosen(section, *pairs[index], target, x_sem.at[3 + index])
                for index, target in ((1, mixed), (0, packed), (2, logs), (3, x))
            ]
            last_load = start_pieces(lists.pop(0), info, full_q, q_sem, 0, pl.ds(0, 3 * width))
            if not feed:
                wait_all(givens)
        if feed:
            take.wait()
            hidden_back_stage(
                grad, vec, info, keep, slope, middle, hidden, second, mid_grad, branch, feed_sums,
                inner_sums, full_out, full, deep, first_load, load, for_slope, for_middle, tallies,
                count, parts,
            )
        if attend:
            attention_back_stage(
                x, vec, branch, mid_grad, packed, mixed, logs, grads, result, sums, down, normal,
                stage, full_o, full_q, project_load, last_load, takes, tallies, count, length,
            )

    outs = []
    scratch = [pltpu.VMEM((4, 8, width), F32), pltpu.SemaphoreType.DMA((7,))]
    flops = 0
    if feed:
        outs += [
            ((rows, inner), BF16),
            ((rows, width), BF16),
            ((8, width), F32),
            ((1, inner), F32),
        ]
        if not both:
            outs += [((rows, width), F32)]
        scratch += [
            pltpu.VMEM((rows, width), BF16),
            pltpu.VMEM((rows, width), BF16),
            pltpu.VMEM((rows, inner), BF16),
            pltpu.VMEM((rows, width), F32),
            pltpu.VMEM((rows, width), F32),
            pltpu.VMEM((inner, width), BF16),
            pltpu.VMEM((width, inner), BF16),
            pltpu.SemaphoreType.DMA((parts, 1)),
            pltpu.SemaphoreType.DMA((1, parts)),
        ]
        if both:
            scratch += [pltpu.VMEM((rows, width), F32)]
        flops += 4 * rows * width * inner
    if attend:
        outs += [((rows, width), BF16), ((rows, 3 * width), BF16), ((8, width), F32)]
        scratch += [
            pltpu.VMEM((rows, width), BF16),
            pltpu.VMEM((rows, 3 * width), BF16),
            pltpu.VMEM((rows, width), BF16),
            pltpu.VMEM((count, HEADS, space), F32),
            pltpu.VMEM((rows, width), BF16),
            pltpu.VMEM((rows, width), F32),
            pltpu.VMEM((count, HEADS, 2 * pair), F32),
            pltpu.VMEM((width, width), BF16),
            pltpu.VMEM((width, 3 * width), BF16),
            pltpu.SemaphoreType.DMA((1, parts)),
            pltpu.SemaphoreType.DMA((1, parts)),
        ]
        if not feed:
            scratch += [pltpu.VMEM((rows, width), BF16), pltpu.VMEM((rows, width), F32)]
        flops += 2 * rows * width * (4 * width + 5 * space)
    weights = (list(reduce) + list(expand) if feed else []) + (
        list(out) + list(qkv) if attend else []
    )
    return call(
        body,
        "backward" + "_feed" * feed + "_attend" * attend,
        plain + operands + weights + [params, meta],
        [ANY] * (len(plain) + len(operands) + len(weights)) + [VMEM, SMEM],
        outs,
        scratch,
        flops,
    )


class Shifted:
    def __init__(self, ref, index):
        self.ref, self.index = ref, index

    def __getitem__(self, index):
        return self.ref[self.index + index]


def weight_gradient(left_pairs, pairs, meta, parts, quarter, rows_of, columns_of, name, count=0):
    micro = len(pairs)
    first_row, height = rows_of
    first_column, breadth = columns_of
    rows = pairs[0][0].shape[0]

    def body(*refs):
        refs = list(refs)
        left_low = [refs.pop(0) for _ in range(micro)]
        left_up = [refs.pop(0) for _ in range(micro)]
        low = [refs.pop(0) for _ in range(micro)]
        up = [refs.pop(0) for _ in range(micro)]
        info = refs.pop(0)
        outs = [refs.pop(0) for _ in range(2)]
        left_full, right_full, l_sem, r_sem = refs
        section = info[parts]
        waits = []
        for batch in range(micro):
            span = pl.ds(batch * rows, rows)
            columns = pl.ds(first_column, breadth)
            waits.append(
                start_chosen(
                    section,
                    low[batch].at[:, columns],
                    up[batch].at[:, columns],
                    right_full.at[span],
                    r_sem.at[batch],
                )
            )
        loads = []
        for part in range(parts):
            for batch in range(micro):
                start = pl.multiple_of(info[part] * quarter + first_row, 128)
                loads.append(
                    start_chosen(
                        section,
                        left_low[batch].at[:, pl.ds(start, height)],
                        left_up[batch].at[:, pl.ds(start, height)],
                        left_full.at[part, pl.ds(batch * rows, rows)],
                        l_sem.at[part, batch],
                    )
                )
        wait_all(waits)
        if count:
            space = rows // count
            for image in range(micro * count):
                alive = jnp.where(info[parts + 1 + image] > 0, 1.0, 0.0)
                here = slice(image * space, (image + 1) * space)
                right_full[here] = (right_full[here].astype(F32) * alive).astype(BF16)
        for part in SEND_FIRST[parts] if parts in SEND_FIRST else range(parts):
            wait_all(loads[part * micro : (part + 1) * micro])
            outs[part % 2][part // 2] = contract(left_full[part], right_full[...], 0, 0).astype(BF16)

    return call(
        body,
        name,
        [pair[side] for group in (left_pairs, pairs) for side in range(2) for pair in group] + [meta],
        [ANY] * (4 * micro) + [SMEM],
        [((parts // 2, height, breadth), BF16)] * 2,
        [
            pltpu.VMEM((parts, micro * rows, height), BF16),
            pltpu.VMEM((micro * rows, breadth), BF16),
            pltpu.SemaphoreType.DMA((parts, micro)),
            pltpu.SemaphoreType.DMA((micro,)),
        ],
        2 * parts * micro * rows * height * breadth,
    )


def after(value, *earlier):
    return lax.optimization_barrier((value,) + earlier)[0]


def added(*values):
    total = values[0].astype(F32)
    for value in values[1:]:
        total = total + value.astype(F32)
    return total.astype(values[0].dtype)


class FourByFour:
    parts = 4

    def __init__(self):
        self.group = lax.axis_index("group")
        self.place = lax.axis_index("replica")
        self.order = [self.group ^ part for part in range(4)]

    def core(self, block):
        return lax.ppermute(block, "group", [(i, i ^ 1) for i in range(4)])

    def across(self, block):
        return lax.ppermute(block, "group", [(i, i ^ 2) for i in range(4)])

    def gather(self, blocks):
        far, sibling = [], []
        for index, block in enumerate(blocks):
            far.append(self.across(after(block, far[index - 2]) if index > 1 else block))
            sibling.append(self.core(after(block, sibling[-1]) if index else block))

        def pieces(index, token):
            distant = far[index] if token is None else after(far[index], token)
            return [blocks[index], sibling[index], far[index], self.core(distant)]

        return [partial(pieces, index) for index in range(len(blocks))]

    def total(self, keep, send):
        got = self.core(send)
        token = yield
        far = after(keep[1], token)
        far = added(far, got[1])
        passed = self.across(far)
        token = yield far
        mine = added(after(keep[0], token), got[0], passed)
        inward = lax.ppermute(mine, "replica", [(0, 1), (3, 2)])
        token = yield mine
        joined = added(after(mine, token), inward)
        crossing = lax.ppermute(joined, "replica", [(1, 2), (2, 1)])
        token = yield joined
        summed = added(after(joined, token), crossing)
        outward = lax.ppermute(summed, "replica", [(1, 0), (2, 3)])
        token = yield summed
        inner = (self.place == 1) | (self.place == 2)
        yield jnp.where(inner, after(summed, token), outward).astype(F32)


class General:
    def __init__(self):
        self.parts = lax.axis_size("group")
        self.order = [jnp.int32(part) for part in range(self.parts)]

    def gather(self, blocks):
        found = []
        for block in blocks:
            whole = lax.all_gather(block, "group", axis=0)
            found.append([whole[part] for part in range(self.parts)])
        return [lambda token, pieces=pieces: pieces for pieces in found]

    def total(self, keep, send):
        yield
        mixed = jnp.stack([keep, send], axis=1)
        mixed = mixed.reshape((-1,) + keep.shape[1:])
        mine = lax.psum_scatter(mixed, "group", scatter_dimension=0)
        yield mine
        yield lax.psum(mine, "replica").astype(F32)


def shifted(block, distance):
    devices = range(lax.axis_size("section"))
    route = [(i - distance, i) for i in devices if i - distance in devices]
    return lax.ppermute(block, "section", route)


def in_order(pieces, order):
    place = jnp.stack(order)
    stacked = []
    for block in range(len(pieces)):
        chosen = pieces[0]
        for part in range(1, len(pieces)):
            chosen = jnp.where(place[part] == block, pieces[part], chosen)
        stacked.append(chosen)
    return jnp.stack(stacked)


class Sequence:
    def __init__(self, net):
        self.net, self.sums, self.results, self.token = net, {}, {}, jnp.zeros((8, 128), F32)

    def now(self, value):
        return after(value, self.token)

    def ran(self, value):
        self.token = value

    def add(self, name, keep, send):
        steps = self.net.total(keep, send)
        next(steps)
        self.sums[name] = steps

    def step(self, *names):
        for name in names:
            try:
                self.results[name] = self.token = self.sums[name].send(self.token)
            except StopIteration:
                continue

    def finish(self, name):
        while True:
            try:
                self.results[name] = self.sums[name].send(self.token)
            except StopIteration:
                return self.results[name]


def per_device(
    images,
    cotangent,
    counts,
    qkv_weight,
    out_weight,
    expand_weight,
    reduce_weight,
    norm_gains,
    biases,
    expand_bias,
):
    micro, slots, length, width = images.shape
    space = padded(length)
    section = lax.axis_index("section")
    first = section == 0
    sizes = (lax.axis_size("group"), lax.axis_size("replica"))
    net = FourByFour() if sizes == (4, 4) else General()
    parts = net.parts
    share = width // parts
    batches = tuple(range(micro))
    small = jnp.concatenate([norm_gains[0], biases[0], expand_bias[0].reshape(-1, share)])
    vectors, qkv, out, expand, reduce = net.gather(
        [small, qkv_weight[0], out_weight[0], expand_weight[0], reduce_weight[0]]
    )
    vectors = in_order(vectors(None), net.order)
    top = vectors[:, :8].transpose(1, 0, 2).reshape(8, width)
    bottom = vectors[:, 8:].reshape(-1, width)
    params = jnp.concatenate([top, bottom]).astype(F32)
    slot = jnp.arange(slots, dtype=jnp.int32)
    alive = [(slot < counts[batch, 0]).astype(jnp.int32) for batch in batches]
    head = jnp.stack(net.order + [section]).astype(jnp.int32)

    def meta(*values):
        return jnp.concatenate((head,) + values)

    def rows_of(array):
        full = jnp.pad(array, ((0, 0), (0, 0), (0, space - length), (0, 0)))
        return [full[batch].reshape(slots * space, width) for batch in batches]

    def images_of(array):
        return array.reshape(slots, space, width)[:, :length]

    inputs, targets = rows_of(images), rows_of(cotangent)
    infos = [meta(alive[batch]) for batch in batches]
    info = meta(*alive)

    qkv = qkv(params)
    attended = []
    for batch in batches:
        start = inputs[batch] if batch == 0 else after(inputs[batch], attended[-1][0])
        attended.append(
            forward(start, start, None, qkv, None, None, params, infos[batch], slots, length)
        )
    out = out(attended[-1][0])
    expand = expand(out[3])
    fed = []
    for batch in batches:
        start = inputs[batch] if batch == 0 else after(inputs[batch], fed[-1][0])
        fed.append(
            forward(start, start, attended[batch][2], None, out, expand, params, infos[batch], slots, length)
        )
    reduce = reduce(fed[-1][0])
    early, incoming = [], []
    for batch in batches:
        middle, active = fed[batch][:2]
        if batch:
            active = after(active, early[-1])
        early.append(output_forward(middle, active, reduce, params, infos[batch], slots))
        incoming.append(shifted(early[batch], 1))
    low = [attended[batch] + fed[batch] for batch in batches]

    def kept_of(values):
        norm, packed, mixed, logs, middle, active, second, slope = values
        return (slope, middle, packed, mixed, logs)

    up, results, grads, hiddens, branches = [], [], [], [], []
    sums_a, sums_b, sums_c, returning = [], [], [], []
    token = early[-1]
    for batch in batches:
        start = after(incoming[batch], token)
        up.append(
            forward(start, start, None, qkv, out, expand, params, infos[batch], slots, length)
        )
        if batch == 0:
            pair, sides = (targets[0], targets[0]), (up[0], up[0])
            lower, chosen = incoming[0], infos[0]
        else:
            pair, sides = (returning[batch - 1], targets[batch]), (low[batch - 1], up[batch])
            lower = inputs[batch - 1]
            chosen = meta(jnp.where(first, alive[batch - 1], alive[batch]))
        hidden, branch, some, more, result, grad, rest = backward(
            pair, lower, incoming[batch], kept_of(sides[0]), kept_of(sides[1]), reduce, expand, out,
            qkv, params, chosen, slots, length,
        )
        token = result
        hiddens.append(hidden)
        branches.append(branch)
        grads.append(grad)
        results.append(result)
        sums_a.append(some)
        sums_b.append(more)
        sums_c.append(rest)
        returning.append(shifted(result, -1))
    late = []
    for batch in batches:
        active = after(up[batch][5], token)
        late.append(output_forward(up[batch][4], active, reduce, params, infos[batch], slots))
        token = late[-1]

    last = micro - 1
    run = Sequence(net)
    run.ran(token)
    inner = expand[0].shape[1]
    names = ("norm", "packed", "mixed", "logs", "middle", "active", "second", "slope")

    def left_of(name):
        index = names.index(name)
        return [(low[batch][index], up[batch][index]) for batch in batches]

    def gradient(name, left, pairs, quarter, rows, columns, count=0):
        pairs = [(run.now(pairs[0][0]), pairs[0][1])] + pairs[1:]
        keep, send = weight_gradient(
            left, pairs, info, parts, quarter, rows, columns, name, count
        )
        run.ran(keep)
        run.add(name, keep, send)

    deep = inner // parts
    pairs = [(returning[batch], targets[batch]) for batch in batches]
    for index in range(2):
        step = deep // 2
        gradient(
            f"reduce{index}", left_of("active"), pairs, deep, (index * step, step), (0, width), slots
        )
    run.step("reduce0", "reduce1")
    start = run.now(returning[last])
    hidden, branch, some, more, mid = backward(
        (start, start), None, None, kept_of(low[last]), kept_of(low[last]), reduce, expand, None,
        None, params, infos[last], slots, length,
    )
    run.ran(branch)
    hiddens.append(hidden)
    branches.append(branch)
    sums_a.append(some)
    sums_b.append(more)
    run.step("reduce0")
    pairs = [(hiddens[batch + 1], hiddens[batch]) for batch in batches]
    for index in range(2):
        step = inner // 2
        gradient(
            f"expand{index}", left_of("second"), pairs, share, (0, share), (index * step, step)
        )
    run.step("expand0", "expand1", "reduce1", "reduce0")
    start = run.now(branch)
    result, grad, rest = backward(
        (start, mid), inputs[last], inputs[last], kept_of(low[last]), kept_of(low[last]), None, None,
        out, qkv, params, infos[last], slots, length,
    )
    run.ran(result)
    results.append(result)
    grads.append(grad)
    sums_c.append(rest)
    run.step("reduce0", "reduce1", "expand0")
    pairs = [(grads[batch + 1], grads[batch]) for batch in batches]
    for index in range(2):
        step = 3 * width // 2
        gradient(f"qkv{index}", left_of("norm"), pairs, share, (0, share), (index * step, step))
        if index == 0:
            run.step("expand0", "reduce1")
    run.step("qkv0", "qkv1", "expand1", "expand0")
    pairs = [(branches[batch + 1], branches[batch]) for batch in batches]
    gradient("project", left_of("mixed"), pairs, share, (0, share), (0, width))

    def over_batches(values):
        return sum(jnp.where(first, values[batch + 1], values[batch]) for batch in batches)

    some, more, rest = over_batches(sums_a), over_batches(sums_b), over_batches(sums_c)
    rows = jnp.concatenate([rest[0:1], some[0:1], rest[1:2], some[1:2], rest[2:4], some[2:4]])
    rows = rows.reshape(8, parts, share).transpose(1, 0, 2)
    rows = jnp.concatenate([rows, more.reshape(parts, -1, share)], axis=1)
    blocks = [lax.dynamic_index_in_dim(rows, place, 0, keepdims=False) for place in net.order]
    run.add("vector", jnp.stack(blocks[0::2]), jnp.stack(blocks[1::2]))
    run.step(
        "project", "vector", "qkv0", "vector", "expand1", "vector", "qkv1", "vector", "qkv0", "project",
        "expand1", "qkv1", "qkv0", "project", "qkv1", "project",
    )
    weights = {name: run.finish(name) for name in run.sums}
    vector = weights["vector"]

    def chosen(lowers, uppers):
        return jnp.stack(
            [images_of(jnp.where(first, low, up)) for low, up in zip(lowers, uppers)]
        )[None]

    return (
        chosen(early, late),
        chosen(results[1:], results[:-1]),
        jnp.concatenate([weights["qkv0"], weights["qkv1"]], axis=1)[None],
        weights["project"][None],
        jnp.concatenate([weights["expand0"], weights["expand1"]], axis=1)[None],
        jnp.concatenate([weights["reduce0"], weights["reduce1"]], axis=0)[None],
        vector[None, 0:2],
        vector[None, 2:8],
        vector[8:].reshape(1, -1),
    )


def solution(mesh):
    placed = (
        P(None, ("group", "replica"), None, None),
        P(None, ("group", "replica"), None, None),
        P(None, ("group", "replica")),
        P("section", "group", None),
        P("section", "group", None),
        P("section", "group", None),
        P("section", "group", None),
        P("section", None, "group"),
        P("section", None, "group"),
        P("section", "group"),
    )
    return jax.shard_map(
        per_device,
        mesh=mesh,
        in_specs=placed,
        out_specs=(
            P("section", None, ("group", "replica"), None, None),
            P("section", None, ("group", "replica"), None, None),
            P("section", "group", None),
            P("section", "group", None),
            P("section", "group", None),
            P("section", "group", None),
            P("section", None, "group"),
            P("section", None, "group"),
            P("section", "group"),
        ),
        check_vma=False,
    )
```

time: 1210 us -> 797 us (0.66)
  matrix products: 467 us -> 0 us
  Pallas kernels: 0 us -> 347 us
  waiting for transfers between devices: 470 us -> 227 us
  starting transfers between devices: 12.3 us -> 127 us
  local copies, waits for them, and re-layouts: 92.2 us -> 33.6 us
  other arithmetic: 103 us -> 51.3 us
  blocking collectives: 45.3 us -> 0 us
  between operations: 16.5 us -> 2.31 us
    dot_general x57 -> x0, matrix products: 467 us -> none  [the longest x3 63.7 us: layer_forward(): jnp.einsum('mzv,va->mza', activated_hidden, contraction_weight, preferred...]
    pallas_call x0 -> x21, Pallas kernels: none -> 347 us  [call(): pl.pallas_call(body, out_shape=out_shape, in_specs=specs, out_specs=[VMEM...]
    psum x1 -> x0, waiting for transfers between devices: 202 us -> none  [per_device(): lax.psum(owned[0].astype(jnp.bfloat16), 'replica').astype(jnp.float32)]
    ppermute x4 -> x59, waiting for transfers between devices: 35 us -> 227 us  [the longest x13 101 us: across(): return lax.ppermute(block, 'group', [(i, i ^ 2) for i in range(4)])]
    all_gather x4 -> x0, waiting for transfers between devices: 132 us -> none  [the longest x1 55 us: per_device(): lax.all_gather(shards[2], 'group', axis=0, tiled=True)]
    ppermute x4 -> x59, starting transfers between devices: 11.5 us -> 127 us  [the longest x8 81.5 us: total(): inward = lax.ppermute(mine, 'replica', [(0, 1), (3, 2)])]
    reduce_scatter x5 -> x0, waiting for transfers between devices: 98.8 us -> none  [the longest x1 74.5 us: per_device(): lax.psum_scatter(red_sum.astype(jnp.bfloat16), 'group', scatter_dimension...]
    reduce_sum x28 -> x0, other arithmetic: 38.1 us -> none  [the longest x6 11.5 us: normalize(): center = values - jnp.mean(values, axis=-1, keepdims=True)]
  transfers between devices with their start and end apart: 15 -> 59, of which waited for: 11 -> 22; matrix products, arithmetic and copies ran while one was open for 26% -> 9% of each run, Pallas kernels for 0% -> 35%
where the time goes in v2:
time: 797 us; the launch traced here: 788 us
  Pallas kernels  347 us (44%)
  waiting for transfers between devices  227 us (28%)
  starting transfers between devices  127 us (16%)
  other arithmetic  51.3 us (6%)
  local copies, waits for them, and re-layouts  33.6 us (4%)
    pallas_call x21, Pallas kernels, call(): pl.pallas_call(body, out_shape=out_shape, in_specs=specs, out_specs=[VMEM...  347 us
    ppermute x13, waiting for transfers between devices, across(): return lax.ppermute(block, 'group', [(i, i ^ 2) for i in range(4)])  101 us
    ppermute x8, starting transfers between devices, total(): inward = lax.ppermute(mine, 'replica', [(0, 1), (3, 2)])  81.5 us
    ppermute x8, waiting for transfers between devices, total(): outward = lax.ppermute(summed, 'replica', [(1, 0), (2, 3)])  69.4 us
    ppermute x8, waiting for transfers between devices, total(): inward = lax.ppermute(mine, 'replica', [(0, 1), (3, 2)])  40.6 us
    convert_element_type x28, other arithmetic, added(): return total.astype(values[0].dtype)  26.8 us
    ppermute x13, starting transfers between devices, across(): return lax.ppermute(block, 'group', [(i, i ^ 2) for i in range(4)])  16.3 us
  transfers between devices with their start and end apart: 59, of which 22 were waited for; matrix products, arithmetic and copies ran while one was open for 9% of the time, Pallas kernels for 35%

profile of v2, /device:TPU:0, one launch (start us, length us, event | category | flops | bytes accessed | tf_op | source)
XLA Modules:
  0.0 788.4 jit_solution(18248869014838355000)
XLA Ops:
  5.2 33.2 %collective-permute-done.3 = bf16[12,256]{1,0:T(8,128)(2,1)S(1)} collective-permute-done((bf16[12,256]{1,0:T(8,128)(2,1)S(1)}, bf16[12,256]{1,0:T(8,128)(2,1)S(1)}, u32[]{:S(2)}, u32[]{:S(2)}) %collective-permute-start.3) | collective-permute-done | bytes 6176 | tf_op jit(solution)/shard_map/ppermute | solution.py:727
  53.8 16.6 %forward_attend.2 = (bf16[416,1024]{1,0:T(8,128)(2,1)}, bf16[416,3072]{1,0:T(8,128)(2,1)}, bf16[416,1024]{1,0:T(8,128)(2,1)}, f32[2,16,208]{2,1,0:T(8,128)}) custom-call(bf16[416,1024]{1,0:T(8,128)(2,1)} %bitcast.225, bf16[256,3072]{1,0:T(8,128)(2,1)} %bitcast.206, bf16[256,3072]{1,0:T(8,128)(2,1)} %copy-done.5, bf16[256,3072]{1,0:T(8,128)(2,1)} %copy-done.4, ...), custom_call_target="tpu_custom_call" | custom-call | flops 46432256 | bytes 179360 | tf_op jit(solution)/shard_map/forward_attend/pallas_call | solution.py:54
  70.4 16.8 %forward_attend.3 = (bf16[416,1024]{1,0:T(8,128)(2,1)}, bf16[416,3072]{1,0:T(8,128)(2,1)}, bf16[416,1024]{1,0:T(8,128)(2,1)}, f32[2,16,208]{2,1,0:T(8,128)}) custom-call(bf16[416,1024]{1,0:T(8,128)(2,1)} %bitcast.222, bf16[256,3072]{1,0:T(8,128)(2,1)} %bitcast.207, bf16[256,3072]{1,0:T(8,128)(2,1)} %copy-done.5, bf16[256,3072]{1,0:T(8,128)(2,1)} %copy-done.4, ...), custom_call_target="tpu_custom_call" | custom-call | flops 46432256 | bytes 179360 | tf_op jit(solution)/shard_map/forward_attend/pallas_call | solution.py:54
  87.2 14.1 %collective-permute-done.7.refs_4_.refs_7_.refs_17_.refs_24_.refs_8_ = bf16[256,1024]{1,0:T(8,128)(2,1)} collective-permute-done((bf16[256,1024]{1,0:T(8,128)(2,1)}, bf16[256,1024]{1,0:T(8,128)(2,1)}, u32[]{:S(2)}, u32[]{:S(2)}) %collective-permute-start.7) | collective-permute-done | bytes 524320 | tf_op jit(solution)/shard_map/ppermute | solution.py:727
  109.6 16.4 %forward_feed.2 = (f32[416,1024]{1,0:T(8,128)}, bf16[416,4096]{1,0:T(8,128)(2,1)}, bf16[416,1024]{1,0:T(8,128)(2,1)}, bf16[416,4096]{1,0:T(8,128)(2,1)}) custom-call(bf16[416,1024]{1,0:T(8,128)(2,1)} %bitcast.226, bf16[416,1024]{1,0:T(8,128)(2,1)} %get-tuple-element.146.refs_1_.refs_8_.refs_0_, bf16[256,1024]{1,0:T(8,128)(2,1)} %bitcast.214, ...), custom_call_target="tpu_custom_call" | custom-call | flops 68157440 | bytes 337664 | tf_op jit(solution)/shard_map/forward_feed/pallas_call | solution.py:54
  126.0 16.9 %forward_feed.3 = (f32[416,1024]{1,0:T(8,128)}, bf16[416,4096]{1,0:T(8,128)(2,1)}, bf16[416,1024]{1,0:T(8,128)(2,1)}, bf16[416,4096]{1,0:T(8,128)(2,1)}) custom-call(bf16[416,1024]{1,0:T(8,128)(2,1)} %bitcast.223, bf16[416,1024]{1,0:T(8,128)(2,1)} %get-tuple-element.161.refs_1_.refs_3_, bf16[256,1024]{1,0:T(8,128)(2,1)} %bitcast.215, ...), custom_call_target="tpu_custom_call" | custom-call | flops 68157440 | bytes 337664 | tf_op jit(solution)/shard_map/forward_feed/pallas_call | solution.py:54
  142.9 8.9 %collective-permute-done.13.refs_4_.refs_9_.refs_16_.refs_5_ = bf16[1024,1024]{1,0:T(8,128)(2,1)} collective-permute-done((bf16[1024,1024]{1,0:T(8,128)(2,1)}, bf16[1024,1024]{1,0:T(8,128)(2,1)}, u32[]{:S(2)}, u32[]{:S(2)}) %collective-permute-start.13) | collective-permute-done | bytes 2097184 | tf_op jit(solution)/shard_map/ppermute | solution.py:727
  157.5 10.8 %output_forward.4 = bf16[416,1024]{1,0:T(8,128)(2,1)} custom-call(f32[416,1024]{1,0:T(8,128)} %get-tuple-element.156.refs_0_.refs_2_, bf16[416,4096]{1,0:T(8,128)(2,1)} %get-tuple-element.157.refs_1_.refs_0_, bf16[1024,1024]{1,0:T(8,128)(2,1)} %bitcast.197, bf16[1024,1024]{1,0:T(8,128)(2,1)} %copy-done.2, ...), custom_call_target="tpu_custom_call" | custom-call | flops 54525952 | bytes 225024 | tf_op jit(solution)/shard_map/output_forward/pallas_call | solution.py:54
  174.8 10.6 %output_forward.5 = bf16[416,1024]{1,0:T(8,128)(2,1)} custom-call(f32[416,1024]{1,0:T(8,128)} %get-tuple-element.162.refs_0_.refs_2_, bf16[416,4096]{1,0:T(8,128)(2,1)} %get-tuple-element.165.refs_1_, bf16[1024,1024]{1,0:T(8,128)(2,1)} %bitcast.198, bf16[1024,1024]{1,0:T(8,128)(2,1)} %copy-done.2, ...), custom_call_target="tpu_custom_call" | custom-call | flops 54525952 | bytes 225024 | tf_op jit(solution)/shard_map/output_forward/pallas_call | solution.py:54
  192.5 30.1 %forward_attend_feed.2 = (bf16[416,1024]{1,0:T(8,128)(2,1)}, bf16[416,3072]{1,0:T(8,128)(2,1)}, bf16[416,1024]{1,0:T(8,128)(2,1)}, f32[2,16,208]{2,1,0:T(8,128)}...) custom-call(bf16[416,1024]{1,0:T(8,128)(2,1)} %copy-done.17, ...), custom_call_target="tpu_custom_call" | custom-call | flops 114589696 | bytes 489632 | tf_op jit(solution)/shard_map/forward_attend_feed/pallas_call | solution.py:54
  222.6 36.3 %backward_feed_attend.2 = (bf16[416,4096]{1,0:T(8,128)(2,1)}, bf16[416,1024]{1,0:T(8,128)(2,1)}, f32[8,1024]{1,0:T(8,128)}, f32[1,4096]{1,0:T(1,128)}, bf16[416,...) custom-call(bf16[416,1024]{1,0:T(8,128)(2,1)} %bitcast.228, ...), custom_call_target="tpu_custom_call" | custom-call | flops 177422336 | bytes 675232 | tf_op jit(solution)/shard_map/backward_feed_attend/pallas_call | solution.py:54
  264.1 30.3 %forward_attend_feed.3 = (bf16[416,1024]{1,0:T(8,128)(2,1)}, bf16[416,3072]{1,0:T(8,128)(2,1)}, bf16[416,1024]{1,0:T(8,128)(2,1)}, f32[2,16,208]{2,1,0:T(8,128)}...) custom-call(bf16[416,1024]{1,0:T(8,128)(2,1)} %copy-done.16, ...), custom_call_target="tpu_custom_call" | custom-call | flops 114589696 | bytes 489632 | tf_op jit(solution)/shard_map/forward_attend_feed/pallas_call | solution.py:54
  295.3 36.3 %backward_feed_attend.3 = (bf16[416,4096]{1,0:T(8,128)(2,1)}, bf16[416,1024]{1,0:T(8,128)(2,1)}, f32[8,1024]{1,0:T(8,128)}, f32[1,4096]{1,0:T(1,128)}, bf16[416,...) custom-call(bf16[416,4096]{1,0:T(8,128)(2,1)} %get-tuple-element.169.refs_0_, ...), custom_call_target="tpu_custom_call" | custom-call | flops 177422336 | bytes 835392 | tf_op jit(solution)/shard_map/backward_feed_attend/pallas_call | solution.py:54
  334.0 10.7 %output_forward.6 = bf16[416,1024]{1,0:T(8,128)(2,1)} custom-call(f32[416,1024]{1,0:T(8,128)} %get-tuple-element.167.refs_2_.refs_0_, bf16[416,4096]{1,0:T(8,128)(2,1)} %get-tuple-element.184.refs_1_.refs_2_, bf16[1024,1024]{1,0:T(8,128)(2,1)} %bitcast.201, bf16[1024,1024]{1,0:T(8,128)(2,1)} %copy-done.2, ...), custom_call_target="tpu_custom_call" | custom-call | flops 54525952 | bytes 225024 | tf_op jit(solution)/shard_map/output_forward/pallas_call | solution.py:54
  344.7 10.6 %output_forward.7 = bf16[416,1024]{1,0:T(8,128)(2,1)} custom-call(f32[416,1024]{1,0:T(8,128)} %get-tuple-element.177.refs_3_.refs_0_, bf16[416,4096]{1,0:T(8,128)(2,1)} %get-tuple-element.186.refs_1_.refs_3_, bf16[1024,1024]{1,0:T(8,128)(2,1)} %bitcast.202, bf16[1024,1024]{1,0:T(8,128)(2,1)} %copy-done.2, ...), custom_call_target="tpu_custom_call" | custom-call | flops 54525952 | bytes 225024 | tf_op jit(solution)/shard_map/output_forward/pallas_call | solution.py:54
  356.3 9.8 %reduce0.1 = (bf16[2,512,1024]{2,1,0:T(8,128)(2,1)}, bf16[2,512,1024]{2,1,0:T(8,128)(2,1)}) custom-call(bf16[416,4096]{1,0:T(8,128)(2,1)} %get-tuple-element.157.refs_1_.refs_0_, bf16[416,4096]{1,0:T(8,128)(2,1)} %get-tuple-element.165.refs_1_, bf16[416,4096]{1,0:T(8,128)(2,1)} %get-tuple-element.184.refs_1_.refs_2_, ...), custom_call_target="tpu_custom_call" | custom-call | flops 54525952 | bytes 331776 | tf_op jit(solution)/shard_map/reduce0/pallas_call | solution.py:54
  366.2 9.8 %reduce1.1 = (bf16[2,512,1024]{2,1,0:T(8,128)(2,1)}, bf16[2,512,1024]{2,1,0:T(8,128)(2,1)}) custom-call(bf16[416,4096]{1,0:T(8,128)(2,1)} %get-tuple-element.157.refs_1_.refs_0_, bf16[416,4096]{1,0:T(8,128)(2,1)} %get-tuple-element.165.refs_1_, bf16[416,4096]{1,0:T(8,128)(2,1)} %get-tuple-element.184.refs_1_.refs_2_, ...), custom_call_target="tpu_custom_call" | custom-call | flops 54525952 | bytes 331776 | tf_op jit(solution)/shard_map/reduce1/pallas_call | solution.py:54
  382.0 16.9 %backward_feed.1 = (bf16[416,4096]{1,0:T(8,128)(2,1)}, bf16[416,1024]{1,0:T(8,128)(2,1)}, f32[8,1024]{1,0:T(8,128)}, f32[1,4096]{1,0:T(1,128)}, f32[416,1024]{1,0:T(8,128)}) custom-call(bf16[416,1024]{1,0:T(8,128)(2,1)} %copy-done.9, bf16[416,4096]{1,0:T(8,128)(2,1)} %get-tuple-element.196.refs_1_, f32[416,1024]{1,0:T(8,128)} %get-tuple-element.162.refs_0_.refs_2_, ...), custom_call_target="tpu_custom_call" | custom-call | flops 109051904 | bytes 450048 | tf_op jit(solution)/shard_map/backward_feed/pallas_call | solution.py:54
  407.5 10.1 %expand0.1 = (bf16[2,256,2048]{2,1,0:T(8,128)(2,1)}, bf16[2,256,2048]{2,1,0:T(8,128)(2,1)}) custom-call(bf16[416,1024]{1,0:T(8,128)(2,1)} %get-tuple-element.199.refs_0_, bf16[416,1024]{1,0:T(8,128)(2,1)} %get-tuple-element.200.refs_1_, bf16[416,1024]{1,0:T(8,128)(2,1)} %get-tuple-element.201.refs_2_, bf16[416,1024]{1,0:T(8,128)(2,1)} %get-tuple-element.202.refs_3_, ...), custom_call_target="tpu_custom_call" | custom-call | flops 54525952 | bytes 331776 | tf_op jit(solution)/shard_map/expand0/pallas_call | solution.py:54
  417.7 9.8 %expand1.1 = (bf16[2,256,2048]{2,1,0:T(8,128)(2,1)}, bf16[2,256,2048]{2,1,0:T(8,128)(2,1)}) custom-call(bf16[416,1024]{1,0:T(8,128)(2,1)} %get-tuple-element.199.refs_0_, bf16[416,1024]{1,0:T(8,128)(2,1)} %get-tuple-element.200.refs_1_, bf16[416,1024]{1,0:T(8,128)(2,1)} %get-tuple-element.201.refs_2_, bf16[416,1024]{1,0:T(8,128)(2,1)} %get-tuple-element.202.refs_3_, ...), custom_call_target="tpu_custom_call" | custom-call | flops 54525952 | bytes 331776 | tf_op jit(solution)/shard_map/expand1/pallas_call | solution.py:54
  442.3 11.0 %collective-permute-done.24 = bf16[512,1024]{1,0:T(8,128)(2,1)S(1)} collective-permute-done((bf16[512,1024]{1,0:T(8,128)(2,1)S(1)}, bf16[512,1024]{1,0:T(8,128)(2,1)S(1)}, u32[]{:S(2)}, u32[]{:S(2)}) %collective-permute-start.24) | collective-permute-done | bytes 1048608 | tf_op jit(solution)/shard_map/ppermute | solution.py:727
  470.5 24.3 %backward_attend.1 = (bf16[416,1024]{1,0:T(8,128)(2,1)}, bf16[416,3072]{1,0:T(8,128)(2,1)}, f32[8,1024]{1,0:T(8,128)}) custom-call(bf16[416,1024]{1,0:T(8,128)(2,1)} %get-tuple-element.216.refs_0_.refs_5_, f32[416,1024]{1,0:T(8,128)} %get-tuple-element.217.refs_1_, bf16[416,3072]{1,0:T(8,128)(2,1)} %get-tuple-element.218.refs_2_, ...), custom_call_target="tpu_custom_call" | custom-call | flops 68370432 | bytes 292512 | tf_op jit(solution)/shard_map/backward_attend/pallas_call | solution.py:54
  559.7 24.4 %collective-permute-start.39 = (bf16[256,2048]{1,0:T(8,128)(2,1)S(1)}, bf16[256,2048]{1,0:T(8,128)(2,1)S(1)}, u32[]{:S(2)}, u32[]{:S(2)}) collective-permute-start(bf16[256,2048]{1,0:T(8,128)(2,1)S(1)} %fusion.3), channel_id=1, source_target_pairs={{0,1},{3,2},{4,5},{7,6},{8,9},{11,10},{12,13},{15,14},{16,17},{19,... | collective-permute-start | bytes 3145736 | tf_op jit(solution)/shard_map/ppermute | solution.py:749
  587.9 16.2 %collective-permute-done.38 = f32[12,256]{1,0:T(8,128)S(1)} collective-permute-done((f32[12,256]{1,0:T(8,128)S(1)}, f32[12,256]{1,0:T(8,128)S(1)}, u32[]{:S(2)}, u32[]{:S(2)}) %collective-permute-start.38) | collective-permute-done | bytes 12320 | tf_op jit(solution)/shard_map/ppermute | solution.py:727
  604.1 10.0 %collective-permute-start.43 = (bf16[256,1536]{1,0:T(8,128)(2,1)S(1)}, bf16[256,1536]{1,0:T(8,128)(2,1)S(1)}, u32[]{:S(2)}, u32[]{:S(2)}) collective-permute-start(bf16[256,1536]{1,0:T(8,128)(2,1)S(1)} %fusion.18), channel_id=1, source_target_pairs={{0,1},{3,2},{4,5},{7,6},{8,9},{11,10},{12,13},{15,14},{16,17},{19,... | collective-permute-start | bytes 2359304 | tf_op jit(solution)/shard_map/ppermute | solution.py:749
  615.8 15.2 %collective-permute-done.40 = f32[12,256]{1,0:T(8,128)S(1)} collective-permute-done((f32[12,256]{1,0:T(8,128)S(1)}, f32[12,256]{1,0:T(8,128)S(1)}, u32[]{:S(2)}, u32[]{:S(2)}) %collective-permute-start.40) | collective-permute-done | bytes 12320 | tf_op jit(solution)/shard_map/ppermute | solution.py:749
  635.1 11.8 %collective-permute-done.44 = bf16[256,1024]{1,0:T(8,128)(2,1)S(1)} collective-permute-done((bf16[256,1024]{1,0:T(8,128)(2,1)S(1)}, bf16[256,1024]{1,0:T(8,128)(2,1)S(1)}, u32[]{:S(2)}, u32[]{:S(2)}) %collective-permute-start.44) | collective-permute-done | bytes 524320 | tf_op jit(solution)/shard_map/ppermute | solution.py:727
  646.8 27.9 %collective-permute-start.46 = (bf16[256,1536]{1,0:T(8,128)(2,1)S(1)}, bf16[256,1536]{1,0:T(8,128)(2,1)S(1)}, u32[]{:S(2)}, u32[]{:S(2)}) collective-permute-start(bf16[256,1536]{1,0:T(8,128)(2,1)S(1)} %fusion.16), channel_id=1, source_target_pairs={{0,1},{3,2},{4,5},{7,6},{8,9},{11,10},{12,13},{15,14},{16,17},{19,... | collective-permute-start | bytes 2359304 | tf_op jit(solution)/shard_map/ppermute | solution.py:749
  676.4 12.3 %collective-permute-done.46 = bf16[256,1536]{1,0:T(8,128)(2,1)S(1)} collective-permute-done((bf16[256,1536]{1,0:T(8,128)(2,1)S(1)}, bf16[256,1536]{1,0:T(8,128)(2,1)S(1)}, u32[]{:S(2)}, u32[]{:S(2)}) %collective-permute-start.46) | collective-permute-done | bytes 786464 | tf_op jit(solution)/shard_map/ppermute | solution.py:749
  714.6 32.2 %collective-permute-done.55 = bf16[256,2048]{1,0:T(8,128)(2,1)S(1)} collective-permute-done((bf16[256,2048]{1,0:T(8,128)(2,1)S(1)}, bf16[256,2048]{1,0:T(8,128)(2,1)S(1)}, u32[]{:S(2)}, u32[]{:S(2)}) %collective-permute-start.55) | collective-permute-done | bytes 1048608 | tf_op jit(solution)/shard_map/ppermute | solution.py:755
  749.4 14.2 %collective-permute-done.51 = bf16[256,1536]{1,0:T(8,128)(2,1)S(1)} collective-permute-done((bf16[256,1536]{1,0:T(8,128)(2,1)S(1)}, bf16[256,1536]{1,0:T(8,128)(2,1)S(1)}, u32[]{:S(2)}, u32[]{:S(2)}) %collective-permute-start.51) | collective-permute-done | bytes 786464 | tf_op jit(solution)/shard_map/ppermute | solution.py:755
  763.7 21.3 %collective-permute-done.53 = bf16[256,1024]{1,0:T(8,128)(2,1)S(1)} collective-permute-done((bf16[256,1024]{1,0:T(8,128)(2,1)S(1)}, bf16[256,1024]{1,0:T(8,128)(2,1)S(1)}, u32[]{:S(2)}, u32[]{:S(2)}) %collective-permute-start.53) | collective-permute-done | bytes 524320 | tf_op jit(solution)/shard_map/ppermute | solution.py:755
  (295 shorter events, 210.1 us)
Async XLA Ops:
  0.6 41.1 %collective-permute-start.2 = (bf16[256,3072]{1,0:T(8,128)(2,1)}, bf16[256,3072]{1,0:T(8,128)(2,1)S(1)}, u32[]{:S(2)}, u32[]{:S(2)}) collective-permute-start(bf16[256,3072]{1,0:T(8,128)(2,1)} %bitcast.204), channel_id=1, source_target_pairs={{0,8},{4,12},{8,0},{12,4},{1,9},{5,13},{9,1},{13,5},{2,10},{6,14},... | collective-permute-start | bytes 4718600 | tf_op jit(solution)/shard_map/ppermute | solution.py:727
  5.1 33.4 %collective-permute-start.3 = (bf16[12,256]{1,0:T(8,128)(2,1)S(1)}, bf16[12,256]{1,0:T(8,128)(2,1)S(1)}, u32[]{:S(2)}, u32[]{:S(2)}) collective-permute-start(bf16[12,256]{1,0:T(8,128)(2,1)S(1)} %pad_maximum_fusion.2), channel_id=1, source_target_pairs={{0,8},{4,12},{8,0},{12,4},{1,9},{5,13},{9,1},{13,5},{2,10},{6,14},... | collective-permute-start | bytes 18440 | tf_op jit(solution)/shard_map/ppermute | solution.py:727
  5.1 33.3 %collective-permute-start = (bf16[12,256]{1,0:T(8,128)(2,1)S(1)}, bf16[12,256]{1,0:T(8,128)(2,1)S(1)}, u32[]{:S(2)}, u32[]{:S(2)}) collective-permute-start(bf16[12,256]{1,0:T(8,128)(2,1)S(1)} %pad_maximum_fusion.2), channel_id=1, source_target_pairs={{0,4},{4,0},{8,12},{12,8},{1,5},{5,1},{9,13},{13,9},{2,6},{6,2},{1... | collective-permute-start | bytes 18440 | tf_op jit(solution)/shard_map/ppermute | solution.py:724
  41.9 60.0 %collective-permute-start.10 = (bf16[256,4096]{1,0:T(8,128)(2,1)}, bf16[256,4096]{1,0:T(8,128)(2,1)}, u32[]{:S(2)}, u32[]{:S(2)}) collective-permute-start(bf16[256,4096]{1,0:T(8,128)(2,1)} %bitcast.186), channel_id=1, source_target_pairs={{0,8},{4,12},{8,0},{12,4},{1,9},{5,13},{9,1},{13,5},{2,10},{6,14},... | collective-permute-start | bytes 6291464 | tf_op jit(solution)/shard_map/ppermute | solution.py:727
  43.6 57.7 %collective-permute-start.7 = (bf16[256,1024]{1,0:T(8,128)(2,1)}, bf16[256,1024]{1,0:T(8,128)(2,1)}, u32[]{:S(2)}, u32[]{:S(2)}) collective-permute-start(bf16[256,1024]{1,0:T(8,128)(2,1)} %bitcast.213), channel_id=1, source_target_pairs={{0,8},{4,12},{8,0},{12,4},{1,9},{5,13},{9,1},{13,5},{2,10},{6,14},... | collective-permute-start | bytes 1572872 | tf_op jit(solution)/shard_map/ppermute | solution.py:727
  52.6 48.7 %collective-permute-start.6 = (bf16[256,1024]{1,0:T(8,128)(2,1)S(1)}, bf16[256,1024]{1,0:T(8,128)(2,1)}, u32[]{:S(2)}, u32[]{:S(2)}) collective-permute-start(bf16[256,1024]{1,0:T(8,128)(2,1)S(1)} %bitcast.221), channel_id=1, source_target_pairs={{0,4},{4,0},{8,12},{12,8},{1,5},{5,1},{9,13},{13,9},{2,6},{6,2},{1... | collective-permute-start | bytes 1572872 | tf_op jit(solution)/shard_map/ppermute | solution.py:724
  103.6 48.2 %collective-permute-start.13 = (bf16[1024,1024]{1,0:T(8,128)(2,1)}, bf16[1024,1024]{1,0:T(8,128)(2,1)}, u32[]{:S(2)}, u32[]{:S(2)}) collective-permute-start(bf16[1024,1024]{1,0:T(8,128)(2,1)} %bitcast.195), channel_id=1, source_target_pairs={{0,8},{4,12},{8,0},{12,4},{1,9},{5,13},{9,1},{13,5},{2,10},{6,14},... | collective-permute-start | bytes 6291464 | tf_op jit(solution)/shard_map/ppermute | solution.py:727
  106.2 45.6 %collective-permute-start.12 = (bf16[1024,1024]{1,0:T(8,128)(2,1)}, bf16[1024,1024]{1,0:T(8,128)(2,1)S(1)}, u32[]{:S(2)}, u32[]{:S(2)}) collective-permute-start(bf16[1024,1024]{1,0:T(8,128)(2,1)} %bitcast.196), channel_id=1, source_target_pairs={{0,4},{4,0},{8,12},{12,8},{1,5},{5,1},{9,13},{13,9},{2,6},{6,2},{1... | collective-permute-start | bytes 6291464 | tf_op jit(solution)/shard_map/ppermute | solution.py:724
  185.4 77.8 %collective-permute-start.16 = (bf16[416,1024]{1,0:T(8,128)(2,1)}, bf16[416,1024]{1,0:T(8,128)(2,1)S(1)}, u32[]{:S(2)}, u32[]{:S(2)}) collective-permute-start(bf16[416,1024]{1,0:T(8,128)(2,1)} %output_forward.5), channel_id=1, source_target_pairs={{0,16},{1,17},{2,18},{3,19},{4,20},{5,21},{6,22},{7,23},{8,24},{9,... | collective-permute-start | bytes 2555912 | tf_op jit(solution)/shard_map/ppermute | solution.py:785
  258.9 35.5 %collective-permute-start.17 = (bf16[416,1024]{1,0:T(8,128)(2,1)}, bf16[416,1024]{1,0:T(8,128)(2,1)S(1)}, u32[]{:S(2)}, u32[]{:S(2)}) collective-permute-start(bf16[416,1024]{1,0:T(8,128)(2,1)} %get-tuple-element.174), channel_id=1, source_target_pairs={{16,0},{17,1},{18,2},{19,3},{20,4},{21,5},{22,6},{23,7},{24,8},{25... | collective-permute-start | bytes 2555912 | tf_op jit(solution)/shard_map/ppermute | solution.py:785
  331.7 23.7 %collective-permute-start.18 = (bf16[416,1024]{1,0:T(8,128)(2,1)}, bf16[416,1024]{1,0:T(8,128)(2,1)S(1)}, u32[]{:S(2)}, u32[]{:S(2)}) collective-permute-start(bf16[416,1024]{1,0:T(8,128)(2,1)} %get-tuple-element.183), channel_id=1, source_target_pairs={{16,0},{17,1},{18,2},{19,3},{20,4},{21,5},{22,6},{23,7},{24,8},{25... | collective-permute-start | bytes 2555912 | tf_op jit(solution)/shard_map/ppermute | solution.py:785
  379.9 25.4 %collective-permute-start.21 = (bf16[512,1024]{1,0:T(8,128)(2,1)}, bf16[512,1024]{1,0:T(8,128)(2,1)}, u32[]{:S(2)}, u32[]{:S(2)}) collective-permute-start(bf16[512,1024]{1,0:T(8,128)(2,1)} %fusion.13), channel_id=1, source_target_pairs={{0,8},{4,12},{8,0},{12,4},{1,9},{5,13},{9,1},{13,5},{2,10},{6,14},... | collective-permute-start | bytes 3145736 | tf_op jit(solution)/shard_map/ppermute | solution.py:727
  428.1 25.2 %collective-permute-start.24 = (bf16[512,1024]{1,0:T(8,128)(2,1)S(1)}, bf16[512,1024]{1,0:T(8,128)(2,1)S(1)}, u32[]{:S(2)}, u32[]{:S(2)}) collective-permute-start(bf16[512,1024]{1,0:T(8,128)(2,1)S(1)} %fusion.12), channel_id=1, source_target_pairs={{0,8},{4,12},{8,0},{12,4},{1,9},{5,13},{9,1},{13,5},{2,10},{6,14},... | collective-permute-start | bytes 3145736 | tf_op jit(solution)/shard_map/ppermute | solution.py:727
  429.5 25.9 %collective-permute-start.25 = (bf16[512,1024]{1,0:T(8,128)(2,1)S(1)}, bf16[512,1024]{1,0:T(8,128)(2,1)S(1)}, u32[]{:S(2)}, u32[]{:S(2)}) collective-permute-start(bf16[512,1024]{1,0:T(8,128)(2,1)S(1)} %fusion.11), channel_id=1, source_target_pairs={{0,1},{3,2},{4,5},{7,6},{8,9},{11,10},{12,13},{15,14},{16,17},{19,... | collective-permute-start | bytes 3145736 | tf_op jit(solution)/shard_map/ppermute | solution.py:749
  455.8 39.0 %collective-permute-start.26 = (bf16[512,1024]{1,0:T(8,128)(2,1)S(1)}, bf16[512,1024]{1,0:T(8,128)(2,1)S(1)}, u32[]{:S(2)}, u32[]{:S(2)}) collective-permute-start(bf16[512,1024]{1,0:T(8,128)(2,1)S(1)} %add_convert_fusion.7), channel_id=1, source_target_pairs={{1,2},{2,1},{5,6},{6,5},{9,10},{10,9},{13,14},{14,13},{17,18},{18,... | collective-permute-start | bytes 3145736 | tf_op jit(solution)/shard_map/ppermute | solution.py:752
  456.7 38.6 %collective-permute-start.27 = (bf16[512,1024]{1,0:T(8,128)(2,1)S(1)}, bf16[512,1024]{1,0:T(8,128)(2,1)S(1)}, u32[]{:S(2)}, u32[]{:S(2)}) collective-permute-start(bf16[512,1024]{1,0:T(8,128)(2,1)S(1)} %fusion.7), channel_id=1, source_target_pairs={{0,1},{3,2},{4,5},{7,6},{8,9},{11,10},{12,13},{15,14},{16,17},{19,... | collective-permute-start | bytes 3145736 | tf_op jit(solution)/shard_map/ppermute | solution.py:749
  464.6 31.2 %collective-permute-start.28 = (bf16[256,2048]{1,0:T(8,128)(2,1)}, bf16[256,2048]{1,0:T(8,128)(2,1)}, u32[]{:S(2)}, u32[]{:S(2)}) collective-permute-start(bf16[256,2048]{1,0:T(8,128)(2,1)} %fusion.9), channel_id=1, source_target_pairs={{0,8},{4,12},{8,0},{12,4},{1,9},{5,13},{9,1},{13,5},{2,10},{6,14},... | collective-permute-start | bytes 3145736 | tf_op jit(solution)/shard_map/ppermute | solution.py:727
  501.0 38.0 %collective-permute-start.33 = (bf16[256,2048]{1,0:T(8,128)(2,1)}, bf16[256,2048]{1,0:T(8,128)(2,1)}, u32[]{:S(2)}, u32[]{:S(2)}) collective-permute-start(bf16[256,2048]{1,0:T(8,128)(2,1)} %fusion.8), channel_id=1, source_target_pairs={{0,8},{4,12},{8,0},{12,4},{1,9},{5,13},{9,1},{13,5},{2,10},{6,14},... | collective-permute-start | bytes 3145736 | tf_op jit(solution)/shard_map/ppermute | solution.py:727
  549.7 34.6 %collective-permute-start.36 = (f32[2,12,256]{2,1,0:T(8,128)S(1)}, f32[2,12,256]{2,1,0:T(8,128)S(1)}, u32[]{:S(2)}, u32[]{:S(2)}) collective-permute-start(f32[2,12,256]{2,1,0:T(8,128)S(1)} %pad_maximum_fusion.1), channel_id=1, source_target_pairs={{0,4},{4,0},{8,12},{12,8},{1,5},{5,1},{9,13},{13,9},{2,6},{6,2},{1... | collective-permute-start | bytes 73736 | tf_op jit(solution)/shard_map/ppermute | solution.py:724
  551.9 33.9 %collective-permute-start.37 = (bf16[256,1536]{1,0:T(8,128)(2,1)S(1)}, bf16[256,1536]{1,0:T(8,128)(2,1)S(1)}, u32[]{:S(2)}, u32[]{:S(2)}) collective-permute-start(bf16[256,1536]{1,0:T(8,128)(2,1)S(1)} %copy-done.34), channel_id=1, source_target_pairs={{0,8},{4,12},{8,0},{12,4},{1,9},{5,13},{9,1},{13,5},{2,10},{6,14},... | collective-permute-start | bytes 2359304 | tf_op jit(solution)/shard_map/ppermute | solution.py:727
  556.8 150.5 %collective-permute-start.56 = (bf16[512,1024]{1,0:T(8,128)(2,1)S(1)}, bf16[512,1024]{1,0:T(8,128)(2,1)S(1)}, u32[]{:S(2)}, u32[]{:S(2)}) collective-permute-start(bf16[512,1024]{1,0:T(8,128)(2,1)S(1)} %add_convert_fusion.6), channel_id=1, source_target_pairs={{1,0},{2,3},{5,4},{6,7},{9,8},{10,11},{13,12},{14,15},{17,16},{18,... | collective-permute-start | bytes 3145736 | tf_op jit(solution)/shard_map/ppermute | solution.py:755
  558.3 150.5 %collective-permute-start.57 = (bf16[512,1024]{1,0:T(8,128)(2,1)S(1)}, bf16[512,1024]{1,0:T(8,128)(2,1)S(1)}, u32[]{:S(2)}, u32[]{:S(2)}) collective-permute-start(bf16[512,1024]{1,0:T(8,128)(2,1)S(1)} %add_convert_fusion.3), channel_id=1, source_target_pairs={{1,0},{2,3},{5,4},{6,7},{9,8},{10,11},{13,12},{14,15},{17,16},{18,... | collective-permute-start | bytes 3145736 | tf_op jit(solution)/shard_map/ppermute | solution.py:755
  559.7 54.4 %collective-permute-start.39 = (bf16[256,2048]{1,0:T(8,128)(2,1)S(1)}, bf16[256,2048]{1,0:T(8,128)(2,1)S(1)}, u32[]{:S(2)}, u32[]{:S(2)}) collective-permute-start(bf16[256,2048]{1,0:T(8,128)(2,1)S(1)} %fusion.3), channel_id=1, source_target_pairs={{0,1},{3,2},{4,5},{7,6},{8,9},{11,10},{12,13},{15,14},{16,17},{19,... | collective-permute-start | bytes 3145736 | tf_op jit(solution)/shard_map/ppermute | solution.py:749
  584.3 47.5 %collective-permute-start.41 = (bf16[256,1536]{1,0:T(8,128)(2,1)S(1)}, bf16[256,1536]{1,0:T(8,128)(2,1)S(1)}, u32[]{:S(2)}, u32[]{:S(2)}) collective-permute-start(bf16[256,1536]{1,0:T(8,128)(2,1)S(1)} %copy-done.33), channel_id=1, source_target_pairs={{0,8},{4,12},{8,0},{12,4},{1,9},{5,13},{9,1},{13,5},{2,10},{6,14},... | collective-permute-start | bytes 2359304 | tf_op jit(solution)/shard_map/ppermute | solution.py:727
  604.1 30.0 %collective-permute-start.43 = (bf16[256,1536]{1,0:T(8,128)(2,1)S(1)}, bf16[256,1536]{1,0:T(8,128)(2,1)S(1)}, u32[]{:S(2)}, u32[]{:S(2)}) collective-permute-start(bf16[256,1536]{1,0:T(8,128)(2,1)S(1)} %fusion.18), channel_id=1, source_target_pairs={{0,1},{3,2},{4,5},{7,6},{8,9},{11,10},{12,13},{15,14},{16,17},{19,... | collective-permute-start | bytes 2359304 | tf_op jit(solution)/shard_map/ppermute | solution.py:749
  631.0 44.0 %collective-permute-start.45 = (bf16[256,2048]{1,0:T(8,128)(2,1)S(1)}, bf16[256,2048]{1,0:T(8,128)(2,1)S(1)}, u32[]{:S(2)}, u32[]{:S(2)}) collective-permute-start(bf16[256,2048]{1,0:T(8,128)(2,1)S(1)} %add_convert_fusion.1), channel_id=1, source_target_pairs={{1,2},{2,1},{5,6},{6,5},{9,10},{10,9},{13,14},{14,13},{17,18},{18,... | collective-permute-start | bytes 3145736 | tf_op jit(solution)/shard_map/ppermute | solution.py:752
  632.8 81.7 %collective-permute-start.54 = (bf16[256,2048]{1,0:T(8,128)(2,1)S(1)}, bf16[256,2048]{1,0:T(8,128)(2,1)S(1)}, u32[]{:S(2)}, u32[]{:S(2)}) collective-permute-start(bf16[256,2048]{1,0:T(8,128)(2,1)S(1)} %add_convert_fusion.2), channel_id=1, source_target_pairs={{1,0},{2,3},{5,4},{6,7},{9,8},{10,11},{13,12},{14,15},{17,16},{18,... | collective-permute-start | bytes 3145736 | tf_op jit(solution)/shard_map/ppermute | solution.py:755
  646.8 41.8 %collective-permute-start.46 = (bf16[256,1536]{1,0:T(8,128)(2,1)S(1)}, bf16[256,1536]{1,0:T(8,128)(2,1)S(1)}, u32[]{:S(2)}, u32[]{:S(2)}) collective-permute-start(bf16[256,1536]{1,0:T(8,128)(2,1)S(1)} %fusion.16), channel_id=1, source_target_pairs={{0,1},{3,2},{4,5},{7,6},{8,9},{11,10},{12,13},{15,14},{16,17},{19,... | collective-permute-start | bytes 2359304 | tf_op jit(solution)/shard_map/ppermute | solution.py:749
  702.8 44.0 %collective-permute-start.55 = (bf16[256,2048]{1,0:T(8,128)(2,1)S(1)}, bf16[256,2048]{1,0:T(8,128)(2,1)S(1)}, u32[]{:S(2)}, u32[]{:S(2)}) collective-permute-start(bf16[256,2048]{1,0:T(8,128)(2,1)S(1)} %add_convert_fusion), channel_id=1, source_target_pairs={{1,0},{2,3},{5,4},{6,7},{9,8},{10,11},{13,12},{14,15},{17,16},{18,... | collective-permute-start | bytes 3145736 | tf_op jit(solution)/shard_map/ppermute | solution.py:755
  706.0 57.6 %collective-permute-start.51 = (bf16[256,1536]{1,0:T(8,128)(2,1)S(1)}, bf16[256,1536]{1,0:T(8,128)(2,1)S(1)}, u32[]{:S(2)}, u32[]{:S(2)}) collective-permute-start(bf16[256,1536]{1,0:T(8,128)(2,1)S(1)} %add_convert_fusion.9), channel_id=1, source_target_pairs={{1,0},{2,3},{5,4},{6,7},{9,8},{10,11},{13,12},{14,15},{17,16},{18,... | collective-permute-start | bytes 2359304 | tf_op jit(solution)/shard_map/ppermute | solution.py:755
  707.3 78.7 %collective-permute-start.52 = (bf16[256,1536]{1,0:T(8,128)(2,1)S(1)}, bf16[256,1536]{1,0:T(8,128)(2,1)S(1)}, u32[]{:S(2)}, u32[]{:S(2)}) collective-permute-start(bf16[256,1536]{1,0:T(8,128)(2,1)S(1)} %add_convert_fusion.8), channel_id=1, source_target_pairs={{1,0},{2,3},{5,4},{6,7},{9,8},{10,11},{13,12},{14,15},{17,16},{18,... | collective-permute-start | bytes 2359304 | tf_op jit(solution)/shard_map/ppermute | solution.py:755
  708.8 76.2 %collective-permute-start.53 = (bf16[256,1024]{1,0:T(8,128)(2,1)S(1)}, bf16[256,1024]{1,0:T(8,128)(2,1)S(1)}, u32[]{:S(2)}, u32[]{:S(2)}) collective-permute-start(bf16[256,1024]{1,0:T(8,128)(2,1)S(1)} %add_convert_fusion.12), channel_id=1, source_target_pairs={{1,0},{2,3},{5,4},{6,7},{9,8},{10,11},{13,12},{14,15},{17,16},{18,... | collective-permute-start | bytes 1572872 | tf_op jit(solution)/shard_map/ppermute | solution.py:755
  (71 other events, 677.0 us)

commit v3 on v2

--- a/solution.py
+++ b/solution.py
@@ -18,8 +18,6 @@
 ANY = pl.BlockSpec(memory_space=pl.ANY)
 VMEM = pl.BlockSpec(memory_space=pltpu.VMEM)
 SMEM = pl.BlockSpec(memory_space=pltpu.SMEM)
-COST = 64
-SEND_FIRST = {4: (3, 1, 2, 0)}
 GAIN0, GAIN1, SHIFT0, SHIFT1, QUERY, VALUE, OUT, FEED, EXPAND = range(9)
 
 
@@ -47,7 +45,7 @@
     return scale * (scaled - mean - unit * along)
 
 
-def call(body, name, operands, specs, outs, scratch, flops):
+def call(body, name, operands, specs, outs, scratch, flops, weight=1.0 / 64):
     moved = sum(o.size * o.dtype.itemsize for o in operands)
     out_shape = [jax.ShapeDtypeStruct(shape, dtype) for shape, dtype in outs]
     moved += sum(o.size * o.dtype.itemsize for o in out_shape)
@@ -58,7 +56,7 @@
         out_specs=[VMEM] * len(outs),
         scratch_shapes=scratch,
         compiler_params=pltpu.CompilerParams(vmem_limit_bytes=VMEM_LIMIT),
-        cost_estimate=pl.CostEstimate(flops=flops // COST, bytes_accessed=moved // COST, transcendentals=0),
+        cost_estimate=pl.CostEstimate(flops=int(flops * weight), bytes_accessed=int(moved * weight), transcendentals=0),
         name=name,
     )(*operands)
 
@@ -81,8 +79,8 @@
         copy.wait()
 
 
-def start_chosen(section, lower, upper, target, sem):
-    if lower is upper:
+def start_chosen(section, lower, upper, target, sem, same=False):
+    if lower is upper or same:
         copy = pltpu.make_async_copy(lower, target, sem)
         copy.start()
         return copy
@@ -182,18 +180,21 @@
     for block, load in enumerate(loads):
         wait_all(load)
         part = slice(block * width, (block + 1) * width)
-        value = contract(second[...], full[:, part], 1, 0) + vec[EXPAND + block - 0 : EXPAND + block + 1]
+        value = contract(second[...], full[:, part], 1, 0) + vec[EXPAND + block : EXPAND + block + 1]
         share = 0.5 + 0.5 * lax.erf(value * ROOT_HALF)
         active[:, part] = (value * share).astype(BF16)
         density = ROOT_TAU * jnp.exp(-0.5 * value * value)
         slope[:, part] = (share + value * density).astype(BF16)
 
 
-def forward(lower, upper, mixed_in, qkv, out, expand, params, meta, count, length):
+def forward(
+    lower, upper, mixed_in, qkv, out, expand, params, meta, count, length, weight=1.0 / 64
+):
     rows, width = lower.shape
     space = rows // count
     pair = 2 * width // HEADS
     attend, feed = qkv is not None, expand is not None
+    both = attend and feed
     parts = len(qkv if attend else expand)
     inner = expand[0].shape[1] if feed else 0
     blocks = inner // width
@@ -207,9 +208,15 @@
             arrived = refs.pop(0)
         lists = [[refs.pop(0) for _ in range(parts)] for _ in range(attend + 2 * feed)]
         vec, info = refs.pop(0), refs.pop(0)
-        if attend:
+        if both:
+            left, packed, logs, middle, slope = (refs.pop(0) for _ in range(5))
+            active, second, mixed, norm = (
+                left.at[:, pl.ds(start, size)]
+                for start, size in ((0, inner), *((inner + width * i, width) for i in range(3)))
+            )
+        elif attend:
             norm, packed, mixed, logs = (refs.pop(0) for _ in range(4))
-        if feed:
+        else:
             middle, active, second, slope = (refs.pop(0) for _ in range(4))
         x, x_sem = refs.pop(0), refs.pop(0)
         section = info[parts]
@@ -279,6 +286,8 @@
         if not attend:
             scratch += [pltpu.VMEM((rows, width), BF16)]
         flops += 2 * rows * width * (width + inner)
+    if both:
+        outs = [((rows, inner + 3 * width), BF16), outs[1], outs[3], outs[4], outs[7]]
     weights = (list(qkv) if attend else []) + (list(out) + list(expand) if feed else [])
     return call(
         body,
@@ -288,12 +297,13 @@
         outs,
         scratch,
         flops,
-    )
-
-
-def output_forward(middle, active, pieces, params, meta, count):
+        weight,
+    )
+
+
+def output_forward(middle, active, pieces, params, meta, count, weight=1.0 / 64):
     rows, width = middle.shape
-    inner = active.shape[1]
+    inner = len(pieces) * pieces[0].shape[0]
     space = rows // count
     parts = len(pieces)
     blocks = 2
@@ -305,7 +315,7 @@
         reduce = [refs.pop(0) for _ in range(parts)]
         vec, info, result, mid, act, full, x_sem, w_sem = refs
         copies = [
-            pltpu.make_async_copy(act_in, act, x_sem.at[0]),
+            pltpu.make_async_copy(act_in.at[:, pl.ds(0, inner)], act, x_sem.at[0]),
             pltpu.make_async_copy(mid_in, mid, x_sem.at[1]),
         ]
         copies[0].start()
@@ -340,6 +350,7 @@
             pltpu.SemaphoreType.DMA((blocks, parts)),
         ],
         2 * rows * width * inner,
+        weight,
     )[0]
 
 
@@ -476,7 +487,8 @@
 
 
 def backward(
-    start, lower, upper, kept_low, kept_up, reduce, expand, out, qkv, params, meta, count, length
+    start, lower, upper, kept_low, kept_up, reduce, expand, out, qkv, params, meta, count, length,
+    mixed_at, weight=1.0 / 64,
 ):
     feed, attend = reduce is not None, qkv is not None
     rows, width = start[0].shape
@@ -510,17 +522,24 @@
         vec, info = refs.pop(0), refs.pop(0)
         section = info[parts]
         if feed:
-            hidden, branch, feed_sums, inner_sums = (refs.pop(0) for _ in range(4))
+            right, feed_sums, inner_sums = (refs.pop(0) for _ in range(3))
+            hidden = right.at[:, pl.ds(0, inner)]
+            branch = right.at[:, pl.ds(inner, width)]
             mid_grad = None if both else refs.pop(0)
         if attend:
-            result, grads, sums = (refs.pop(0) for _ in range(3))
+            grads, result, sums = (refs.pop(0) for _ in range(3)) if not both else (None, refs.pop(0), refs.pop(0))
+        if both:
+            feed_grad = right.at[:, pl.ds(inner + width, width)]
+            grads = right.at[:, pl.ds(inner + 2 * width, 3 * width)]
         tallies, x_sem = refs.pop(0), refs.pop(0)
         if feed:
-            grad, keep, slope, middle, second, full_out, full, o_sem, w_sem = (
-                refs.pop(0) for _ in range(9)
+            grad, slope, middle, second, full_out, full, o_sem, w_sem = (
+                refs.pop(0) for _ in range(8)
             )
             if both:
-                mid_grad = refs.pop(0)
+                mid_grad, keep = refs.pop(0), feed_grad
+            else:
+                keep = refs.pop(0)
             begin = pairs.pop(2) if start[0] is not start[1] else (firsts[0], firsts[0])
             take = start_chosen(section, *begin, grad, x_sem.at[0])
             for_slope = start_chosen(section, *pairs.pop(0), slope, x_sem.at[1])
@@ -546,8 +565,10 @@
                 for given in givens:
                     given.start()
             project_load = start_pieces(lists.pop(0), info, full_o, p_sem, 0, pl.ds(0, width))
+            sames = [one is two for one, two in pairs]
+            pairs[1] = tuple(one.at[:, pl.ds(mixed_at, width)] for one in pairs[1])
             takes = [
-                start_chosen(section, *pairs[index], target, x_sem.at[3 + index])
+                start_chosen(section, *pairs[index], target, x_sem.at[3 + index], sames[index])
                 for index, target in ((1, mixed), (0, packed), (2, logs), (3, x))
             ]
             last_load = start_pieces(lists.pop(0), info, full_q, q_sem, 0, pl.ds(0, 3 * width))
@@ -571,15 +592,13 @@
     flops = 0
     if feed:
         outs += [
-            ((rows, inner), BF16),
-            ((rows, width), BF16),
+            ((rows, inner + (5 if both else 1) * width), BF16),
             ((8, width), F32),
             ((1, inner), F32),
         ]
         if not both:
             outs += [((rows, width), F32)]
         scratch += [
-            pltpu.VMEM((rows, width), BF16),
             pltpu.VMEM((rows, width), BF16),
             pltpu.VMEM((rows, inner), BF16),
             pltpu.VMEM((rows, width), F32),
@@ -589,11 +608,11 @@
             pltpu.SemaphoreType.DMA((parts, 1)),
             pltpu.SemaphoreType.DMA((1, parts)),
         ]
-        if both:
-            scratch += [pltpu.VMEM((rows, width), F32)]
+        scratch += [pltpu.VMEM((rows, width), F32 if both else BF16)]
         flops += 4 * rows * width * inner
     if attend:
-        outs += [((rows, width), BF16), ((rows, 3 * width), BF16), ((8, width), F32)]
+        outs += [] if both else [((rows, 3 * width), BF16)]
+        outs += [((rows, width), BF16), ((8, width), F32)]
         scratch += [
             pltpu.VMEM((rows, width), BF16),
             pltpu.VMEM((rows, 3 * width), BF16),
@@ -621,6 +640,7 @@
         outs,
         scratch,
         flops,
+        weight,
     )
 
 
@@ -632,72 +652,64 @@
         return self.ref[self.index + index]
 
 
-def weight_gradient(left_pairs, pairs, meta, parts, quarter, rows_of, columns_of, name, count=0):
-    micro = len(pairs)
+def weight_gradient(lefts, rights, meta, parts, blocks, quarter, rows_of, columns_of, name):
+    terms = len(lefts)
     first_row, height = rows_of
     first_column, breadth = columns_of
-    rows = pairs[0][0].shape[0]
+    rows = lefts[0].shape[0]
+    operands = list(lefts)
+    places = []
+    for pair in rights:
+        found = []
+        for array, _ in pair:
+            if not any(array is other for other in operands):
+                operands.append(array)
+            found.append(next(i for i, other in enumerate(operands) if other is array))
+        places.append(found)
 
     def body(*refs):
-        refs = list(refs)
-        left_low = [refs.pop(0) for _ in range(micro)]
-        left_up = [refs.pop(0) for _ in range(micro)]
-        low = [refs.pop(0) for _ in range(micro)]
-        up = [refs.pop(0) for _ in range(micro)]
-        info = refs.pop(0)
-        outs = [refs.pop(0) for _ in range(2)]
-        left_full, right_full, l_sem, r_sem = refs
+        sources, info = refs[: len(operands)], refs[len(operands)]
+        results = refs[len(operands) + 1 : len(operands) + 1 + len(blocks)]
+        left_full, right_full, l_sem, r_sem = refs[len(operands) + 1 + len(blocks) :]
         section = info[parts]
         waits = []
-        for batch in range(micro):
-            span = pl.ds(batch * rows, rows)
-            columns = pl.ds(first_column, breadth)
-            waits.append(
-                start_chosen(
-                    section,
-                    low[batch].at[:, columns],
-                    up[batch].at[:, columns],
-                    right_full.at[span],
-                    r_sem.at[batch],
+        for term in range(terms):
+            sides = [
+                sources[place].at[:, pl.ds(column + first_column, breadth)]
+                for place, (_, column) in zip(places[term], rights[term])
+            ]
+            same = rights[term][0] is rights[term][1]
+            target = right_full.at[pl.ds(term * rows, rows)]
+            waits.append(start_chosen(section, *sides, target, r_sem.at[term], same))
+        loads = []
+        for index, block in enumerate(blocks):
+            start = pl.multiple_of(info[block] * quarter + first_row, 128)
+            for term in range(terms):
+                copy = pltpu.make_async_copy(
+                    sources[term].at[:, pl.ds(start, height)],
+                    left_full.at[index, pl.ds(term * rows, rows)],
+                    l_sem.at[index, term],
                 )
-            )
-        loads = []
-        for part in range(parts):
-            for batch in range(micro):
-                start = pl.multiple_of(info[part] * quarter + first_row, 128)
-                loads.append(
-                    start_chosen(
-                        section,
-                        left_low[batch].at[:, pl.ds(start, height)],
-                        left_up[batch].at[:, pl.ds(start, height)],
-                        left_full.at[part, pl.ds(batch * rows, rows)],
-                        l_sem.at[part, batch],
-                    )
-                )
+                copy.start()
+                loads.append(copy)
         wait_all(waits)
-        if count:
-            space = rows // count
-            for image in range(micro * count):
-                alive = jnp.where(info[parts + 1 + image] > 0, 1.0, 0.0)
-                here = slice(image * space, (image + 1) * space)
-                right_full[here] = (right_full[here].astype(F32) * alive).astype(BF16)
-        for part in SEND_FIRST[parts] if parts in SEND_FIRST else range(parts):
-            wait_all(loads[part * micro : (part + 1) * micro])
-            outs[part % 2][part // 2] = contract(left_full[part], right_full[...], 0, 0).astype(BF16)
+        for index in reversed(range(len(blocks))):
+            wait_all(loads[index * terms : (index + 1) * terms])
+            results[index][...] = contract(left_full[index], right_full[...], 0, 0).astype(BF16)
 
     return call(
         body,
         name,
-        [pair[side] for group in (left_pairs, pairs) for side in range(2) for pair in group] + [meta],
-        [ANY] * (4 * micro) + [SMEM],
-        [((parts // 2, height, breadth), BF16)] * 2,
+        operands + [meta],
+        [ANY] * len(operands) + [SMEM],
+        [((height, breadth), BF16)] * len(blocks),
         [
-            pltpu.VMEM((parts, micro * rows, height), BF16),
-            pltpu.VMEM((micro * rows, breadth), BF16),
-            pltpu.SemaphoreType.DMA((parts, micro)),
-            pltpu.SemaphoreType.DMA((micro,)),
+            pltpu.VMEM((len(blocks), terms * rows, height), BF16),
+            pltpu.VMEM((terms * rows, breadth), BF16),
+            pltpu.SemaphoreType.DMA((len(blocks), terms)),
+            pltpu.SemaphoreType.DMA((terms,)),
         ],
-        2 * parts * micro * rows * height * breadth,
+        2 * len(blocks) * terms * rows * height * breadth,
     )
 
 
@@ -714,8 +726,10 @@
 
 class FourByFour:
     parts = 4
+    blocks = (0, 2)
 
     def __init__(self):
+        self.begun = 0
         self.group = lax.axis_index("group")
         self.place = lax.axis_index("replica")
         self.order = [self.group ^ part for part in range(4)]
@@ -738,14 +752,20 @@
 
         return [partial(pieces, index) for index in range(len(blocks))]
 
-    def total(self, keep, send):
-        got = self.core(send)
+    def shared(self, block):
+        return [block, self.core(block)]
+
+    def total(self, blocks, own):
+        passed = self.across(blocks[1])
         token = yield
-        far = after(keep[1], token)
-        far = added(far, got[1])
-        passed = self.across(far)
-        token = yield far
-        mine = added(after(keep[0], token), got[0], passed)
+        mine = added(after(blocks[0], token), passed)
+        if not own:
+            turn = [(place + self.begun) % 4 for place in range(4)]
+            self.begun += 1
+            whole = lax.psum(mine, "replica", axis_index_groups=[turn])
+            token = yield mine
+            yield after(whole, token)
+            return
         inward = lax.ppermute(mine, "replica", [(0, 1), (3, 2)])
         token = yield mine
         joined = added(after(mine, token), inward)
@@ -755,12 +775,13 @@
         outward = lax.ppermute(summed, "replica", [(1, 0), (2, 3)])
         token = yield summed
         inner = (self.place == 1) | (self.place == 2)
-        yield jnp.where(inner, after(summed, token), outward).astype(F32)
+        yield jnp.where(inner, after(summed, token), outward)
 
 
 class General:
     def __init__(self):
         self.parts = lax.axis_size("group")
+        self.blocks = tuple(range(self.parts))
         self.order = [jnp.int32(part) for part in range(self.parts)]
 
     def gather(self, blocks):
@@ -770,13 +791,14 @@
             found.append([whole[part] for part in range(self.parts)])
         return [lambda token, pieces=pieces: pieces for pieces in found]
 
-    def total(self, keep, send):
+    def shared(self, block):
+        return [block]
+
+    def total(self, blocks, own):
         yield
-        mixed = jnp.stack([keep, send], axis=1)
-        mixed = mixed.reshape((-1,) + keep.shape[1:])
-        mine = lax.psum_scatter(mixed, "group", scatter_dimension=0)
+        mine = lax.psum_scatter(jnp.stack(blocks), "group", scatter_dimension=0)
         yield mine
-        yield lax.psum(mine, "replica").astype(F32)
+        yield lax.psum(mine, "replica")
 
 
 def shifted(block, distance):
@@ -797,8 +819,8 @@
 
 
 class Sequence:
-    def __init__(self, net):
-        self.net, self.sums, self.results, self.token = net, {}, {}, jnp.zeros((8, 128), F32)
+    def __init__(self, net, token):
+        self.net, self.sums, self.results, self.token = net, {}, {}, token
 
     def now(self, value):
         return after(value, self.token)
@@ -806,10 +828,9 @@
     def ran(self, value):
         self.token = value
 
-    def add(self, name, keep, send):
-        steps = self.net.total(keep, send)
-        next(steps)
-        self.sums[name] = steps
+    def add(self, name, blocks, own):
+        self.sums[name] = self.net.total(blocks, own)
+        next(self.sums[name])
 
     def step(self, *names):
         for name in names:
@@ -847,11 +868,20 @@
     parts = net.parts
     share = width // parts
     batches = tuple(range(micro))
+
+    def rows_of(array):
+        full = jnp.pad(array, ((0, 0), (0, 0), (0, space - length), (0, 0)))
+        return [full[batch].reshape(slots * space, width) for batch in batches]
+
+    def images_of(array):
+        return array.reshape(slots, space, width)[:, :length]
+
+    inputs, targets = rows_of(images), rows_of(cotangent)
     small = jnp.concatenate([norm_gains[0], biases[0], expand_bias[0].reshape(-1, share)])
     vectors, qkv, out, expand, reduce = net.gather(
         [small, qkv_weight[0], out_weight[0], expand_weight[0], reduce_weight[0]]
     )
-    vectors = in_order(vectors(None), net.order)
+    vectors = in_order(vectors(after(inputs[0], *inputs[1:], *targets)), net.order)
     top = vectors[:, :8].transpose(1, 0, 2).reshape(8, width)
     bottom = vectors[:, 8:].reshape(-1, width)
     params = jnp.concatenate([top, bottom]).astype(F32)
@@ -862,26 +892,18 @@
     def meta(*values):
         return jnp.concatenate((head,) + values)
 
-    def rows_of(array):
-        full = jnp.pad(array, ((0, 0), (0, 0), (0, space - length), (0, 0)))
-        return [full[batch].reshape(slots * space, width) for batch in batches]
-
-    def images_of(array):
-        return array.reshape(slots, space, width)[:, :length]
-
-    inputs, targets = rows_of(images), rows_of(cotangent)
     infos = [meta(alive[batch]) for batch in batches]
     info = meta(*alive)
 
     qkv = qkv(params)
     attended = []
     for batch in batches:
-        start = inputs[batch] if batch == 0 else after(inputs[batch], attended[-1][0])
+        start = inputs[batch] if batch == 0 else after(inputs[batch], attended[-1][2])
         attended.append(
             forward(start, start, None, qkv, None, None, params, infos[batch], slots, length)
         )
-    out = out(attended[-1][0])
-    expand = expand(out[3])
+    out = out(attended[-1][2])
+    expand = expand(out[-1])
     fed = []
     for batch in batches:
         start = inputs[batch] if batch == 0 else after(inputs[batch], fed[-1][0])
@@ -896,35 +918,33 @@
             active = after(active, early[-1])
         early.append(output_forward(middle, active, reduce, params, infos[batch], slots))
         incoming.append(shifted(early[batch], 1))
-    low = [attended[batch] + fed[batch] for batch in batches]
-
-    def kept_of(values):
-        norm, packed, mixed, logs, middle, active, second, slope = values
-        return (slope, middle, packed, mixed, logs)
-
-    up, results, grads, hiddens, branches = [], [], [], [], []
+
+    inner = expand[0].shape[1]
+    mixed_at = inner + width
+    kept, lefts, rights, results = [], [], [], []
     sums_a, sums_b, sums_c, returning = [], [], [], []
     token = early[-1]
     for batch in batches:
         start = after(incoming[batch], token)
-        up.append(
-            forward(start, start, None, qkv, out, expand, params, infos[batch], slots, length)
+        left, packed, logs, middle, slope = forward(
+            inputs[batch], start, None, qkv, out, expand, params, infos[batch], slots, length, 8.0
         )
+        kept.append((slope, middle, packed, left, logs))
+        lefts.append(net.shared(left))
         if batch == 0:
-            pair, sides = (targets[0], targets[0]), (up[0], up[0])
+            pair, sides = (targets[0], targets[0]), (kept[0], kept[0])
             lower, chosen = incoming[0], infos[0]
         else:
-            pair, sides = (returning[batch - 1], targets[batch]), (low[batch - 1], up[batch])
+            pair = (returning[batch - 1], targets[batch])
+            sides = (kept[batch - 1], kept[batch])
             lower = inputs[batch - 1]
             chosen = meta(jnp.where(first, alive[batch - 1], alive[batch]))
-        hidden, branch, some, more, result, grad, rest = backward(
-            pair, lower, incoming[batch], kept_of(sides[0]), kept_of(sides[1]), reduce, expand, out,
-            qkv, params, chosen, slots, length,
+        right, some, more, result, rest = backward(
+            pair, lower, incoming[batch], sides[0], sides[1], reduce, expand, out, qkv, params, chosen,
+            slots, length, mixed_at, 8.0,
         )
         token = result
-        hiddens.append(hidden)
-        branches.append(branch)
-        grads.append(grad)
+        rights.append(net.shared(right))
         results.append(result)
         sums_a.append(some)
         sums_b.append(more)
@@ -932,73 +952,74 @@
         returning.append(shifted(result, -1))
     late = []
     for batch in batches:
-        active = after(up[batch][5], token)
-        late.append(output_forward(up[batch][4], active, reduce, params, infos[batch], slots))
+        ready = lefts[batch][1:] + (rights[batch][1:] if batch < micro - 1 else [])
+        active = after(kept[batch][3], token, *ready)
+        late.append(output_forward(kept[batch][1], active, reduce, params, infos[batch], slots, 8.0))
         token = late[-1]
 
     last = micro - 1
-    run = Sequence(net)
-    run.ran(token)
-    inner = expand[0].shape[1]
-    names = ("norm", "packed", "mixed", "logs", "middle", "active", "second", "slope")
-
-    def left_of(name):
-        index = names.index(name)
-        return [(low[batch][index], up[batch][index]) for batch in batches]
-
-    def gradient(name, left, pairs, quarter, rows, columns, count=0):
-        pairs = [(run.now(pairs[0][0]), pairs[0][1])] + pairs[1:]
-        keep, send = weight_gradient(
-            left, pairs, info, parts, quarter, rows, columns, name, count
+    run = Sequence(net, token)
+    arrived = run.now(returning[last])
+    living = jnp.repeat(alive[last] > 0, space)[:, None]
+    masked = net.shared(jnp.where(living, arrived, jnp.zeros_like(arrived)))
+    many = len(masked)
+
+    def gradient(name, left_at, final, final_at, right_at, quarter, rows, columns, own):
+        left = [lefts[batch][side] for batch in batches for side in range(many)]
+        right = []
+        for batch in batches:
+            for side in range(many):
+                upper = (rights[batch][side], right_at)
+                lower = (final[side], final_at) if batch == last else (rights[batch + 1][side], right_at)
+                right.append((lower, upper))
+        blocks = weight_gradient(
+            left, right, run.now(info), parts, net.blocks, quarter, (left_at + rows[0], rows[1]), columns,
+            name,
         )
-        run.ran(keep)
-        run.add(name, keep, send)
-
-    deep = inner // parts
-    pairs = [(returning[batch], targets[batch]) for batch in batches]
-    for index in range(2):
+        run.ran(blocks[0])
+        return blocks
+
+    def summed(name, *rest):
+        run.add(name, gradient(name, *rest), rest[-1])
+
+    def reduce_part(index, own):
+        deep = inner // parts
         step = deep // 2
-        gradient(
-            f"reduce{index}", left_of("active"), pairs, deep, (index * step, step), (0, width), slots
+        summed(
+            f"reduce{index}", 0, masked, 0, inner + width, deep, (index * step, step), (0, width), own
         )
-    run.step("reduce0", "reduce1")
-    start = run.now(returning[last])
-    hidden, branch, some, more, mid = backward(
-        (start, start), None, None, kept_of(low[last]), kept_of(low[last]), reduce, expand, None,
-        None, params, infos[last], slots, length,
-    )
-    run.ran(branch)
-    hiddens.append(hidden)
-    branches.append(branch)
+
+    reduce_part(0, False)
+    start = run.now(arrived)
+    final, some, more, mid = backward(
+        (start, start), None, None, kept[last], kept[last], reduce, expand, None, None, params,
+        infos[last], slots, length, mixed_at,
+    )
+    run.ran(final)
+    branch = final[:, inner:]
+    finals, branches = net.shared(final[:, :inner]), net.shared(branch)
     sums_a.append(some)
     sums_b.append(more)
+    reduce_part(1, False)
     run.step("reduce0")
-    pairs = [(hiddens[batch + 1], hiddens[batch]) for batch in batches]
-    for index in range(2):
+    summed("project", mixed_at, branches, 0, inner, share, (0, share), (0, width), False)
+    grads, result, rest = backward(
+        (run.now(branch), mid), inputs[last], inputs[last], kept[last], kept[last], None, None, out, qkv,
+        params, infos[last], slots, length, mixed_at, 16.0,
+    )
+    run.ran(result)
+    grads = net.shared(grads)
+    results.append(result)
+    sums_c.append(rest)
+    run.step("reduce1", "project")
+
+    def expand_part(index, own):
         step = inner // 2
-        gradient(
-            f"expand{index}", left_of("second"), pairs, share, (0, share), (index * step, step)
-        )
-    run.step("expand0", "expand1", "reduce1", "reduce0")
-    start = run.now(branch)
-    result, grad, rest = backward(
-        (start, mid), inputs[last], inputs[last], kept_of(low[last]), kept_of(low[last]), None, None,
-        out, qkv, params, infos[last], slots, length,
-    )
-    run.ran(result)
-    results.append(result)
-    grads.append(grad)
-    sums_c.append(rest)
-    run.step("reduce0", "reduce1", "expand0")
-    pairs = [(grads[batch + 1], grads[batch]) for batch in batches]
-    for index in range(2):
-        step = 3 * width // 2
-        gradient(f"qkv{index}", left_of("norm"), pairs, share, (0, share), (index * step, step))
-        if index == 0:
-            run.step("expand0", "reduce1")
-    run.step("qkv0", "qkv1", "expand1", "expand0")
-    pairs = [(branches[batch + 1], branches[batch]) for batch in batches]
-    gradient("project", left_of("mixed"), pairs, share, (0, share), (0, width))
+        summed(f"expand{index}", inner, finals, 0, 0, share, (0, share), (index * step, step), own)
+
+    expand_part(0, True)
+    run.step("reduce0")
+    expand_part(1, True)
 
     def over_batches(values):
         return sum(jnp.where(first, values[batch + 1], values[batch]) for batch in batches)
@@ -1007,27 +1028,47 @@
     rows = jnp.concatenate([rest[0:1], some[0:1], rest[1:2], some[1:2], rest[2:4], some[2:4]])
     rows = rows.reshape(8, parts, share).transpose(1, 0, 2)
     rows = jnp.concatenate([rows, more.reshape(parts, -1, share)], axis=1)
-    blocks = [lax.dynamic_index_in_dim(rows, place, 0, keepdims=False) for place in net.order]
-    run.add("vector", jnp.stack(blocks[0::2]), jnp.stack(blocks[1::2]))
+    rows = sum(net.shared(rows))
+    rows = jnp.stack(
+        [lax.dynamic_index_in_dim(rows, net.order[block], 0, keepdims=False) for block in net.blocks]
+    )
+    count, step = rows.shape[1], width // 2
+    rows = rows.reshape(len(net.blocks), -1)
+    rows = jnp.pad(rows, ((0, 0), (0, -rows.shape[1] % (16 * step)))).reshape(len(net.blocks), -1, step)
+
+    def qkv_part(index):
+        begin, breadth = ((0, 3 * step), (3 * step, 2 * step), (5 * step, step))[index]
+        return gradient(
+            f"qkv{index}", inner + 2 * width, grads, 0, inner + 2 * width, share, (0, share),
+            (begin, breadth), True,
+        )
+
+    run.add("qkv0", qkv_part(0), True)
+    run.add("qkv1", qkv_part(1), True)
+    blocks = qkv_part(2)
+    run.add("qkv2", [jnp.concatenate([one, two]) for one, two in zip(blocks, rows.astype(BF16))], True)
     run.step(
-        "project", "vector", "qkv0", "vector", "expand1", "vector", "qkv1", "vector", "qkv0", "project",
-        "expand1", "qkv1", "qkv0", "project", "qkv1", "project",
+        "expand0", "reduce1", "expand1", "expand0", "project", "qkv0", "expand1", "qkv1", "expand0", "qkv2", "qkv0", "qkv1", "expand1",
+        "qkv2", "expand0", "qkv0", "expand1", "qkv1", "qkv2", "qkv0", "qkv1", "qkv2",
     )
     weights = {name: run.finish(name) for name in run.sums}
-    vector = weights["vector"]
+    vector = weights["qkv2"][share:].reshape(-1)[: count * share].reshape(count, share).astype(F32)
 
     def chosen(lowers, uppers):
         return jnp.stack(
             [images_of(jnp.where(first, low, up)) for low, up in zip(lowers, uppers)]
         )[None]
 
+    def joined(axis, *names):
+        return jnp.concatenate([weights[name] for name in names], axis=axis).astype(F32)[None]
+
     return (
         chosen(early, late),
         chosen(results[1:], results[:-1]),
-        jnp.concatenate([weights["qkv0"], weights["qkv1"]], axis=1)[None],
-        weights["project"][None],
-        jnp.concatenate([weights["expand0"], weights["expand1"]], axis=1)[None],
-        jnp.concatenate([weights["reduce0"], weights["reduce1"]], axis=0)[None],
+        jnp.concatenate([weights["qkv0"], weights["qkv1"], weights["qkv2"][:share]], axis=1).astype(F32)[None],
+        weights["project"].astype(F32)[None],
+        joined(1, "expand0", "expand1"),
+        joined(0, "reduce0", "reduce1"),
         vector[None, 0:2],
         vector[None, 2:8],
         vector[8:].reshape(1, -1),

time: 797 us -> 714 us (0.90)
  starting transfers between devices: 127 us -> 76.1 us
  waiting for transfers between devices: 227 us -> 191 us
  between operations: 2.31 us -> 15.2 us
    ppermute x8 -> x5, starting transfers between devices: 81.5 us -> 37.7 us  [total(): inward = lax.ppermute(mine, 'replica', [(0, 1), (3, 2)])]
    ppermute x13, waiting for transfers between devices: 101 us -> 68.9 us  [across(): return lax.ppermute(block, 'group', [(i, i ^ 2) for i in range(4)])]
    psum x0 -> x3, waiting for transfers between devices: none -> 26.1 us  [total(): whole = lax.psum(mine, 'replica', axis_index_groups=[turn])]
    ppermute x8 -> x5, waiting for transfers between devices: 40.6 us -> 14.7 us  [total(): inward = lax.ppermute(mine, 'replica', [(0, 1), (3, 2)])]
    convert_element_type x28 -> x18, other arithmetic: 26.8 us -> 18.4 us  [added(): return total.astype(values[0].dtype)]
    convert_element_type x0 -> x4, other arithmetic: none -> 8.23 us  [the longest x2 6.2 us: joined(): jnp.concatenate([weights[name] for name in names], axis=axis).astype(F32)]
    pallas_call x21 -> x22, Pallas kernels: 347 us -> 348 us  [call(): pl.pallas_call(body, out_shape=out_shape, in_specs=specs, out_specs=[VMEM...]
    ppermute x8 -> x5, waiting for transfers between devices: 69.4 us -> 69 us  [total(): outward = lax.ppermute(summed, 'replica', [(1, 0), (2, 3)])]
  transfers between devices with their start and end apart: 59 -> 54, of which waited for: 22 -> 19; matrix products, arithmetic and copies ran while one was open for 9% -> 9% of each run, Pallas kernels for 35% -> 47%
where the time goes in v3:
time: 714 us; the launch traced here: 705 us
  Pallas kernels  348 us (49%)
  waiting for transfers between devices  191 us (27%)
  starting transfers between devices  76.1 us (11%)
  other arithmetic  45.6 us (6%)
  local copies, waits for them, and re-layouts  28.5 us (4%)
  between operations  15.2 us (2%)
    pallas_call x22, Pallas kernels, call(): pl.pallas_call(body, out_shape=out_shape, in_specs=specs, out_specs=[VMEM...  348 us
    ppermute x5, waiting for transfers between devices, total(): outward = lax.ppermute(summed, 'replica', [(1, 0), (2, 3)])  69 us
    ppermute x13, waiting for transfers between devices, across(): return lax.ppermute(block, 'group', [(i, i ^ 2) for i in range(4)])  68.9 us
    ppermute x5, starting transfers between devices, total(): inward = lax.ppermute(mine, 'replica', [(0, 1), (3, 2)])  37.7 us
    psum x3, waiting for transfers between devices, total(): whole = lax.psum(mine, 'replica', axis_index_groups=[turn])  26.1 us
    convert_element_type x18, other arithmetic, added(): return total.astype(values[0].dtype)  18.4 us
    ppermute x13, starting transfers between devices, across(): return lax.ppermute(block, 'group', [(i, i ^ 2) for i in range(4)])  15.7 us
    ppermute x5, waiting for transfers between devices, total(): inward = lax.ppermute(mine, 'replica', [(0, 1), (3, 2)])  14.7 us
  transfers between devices with their start and end apart: 54, of which 19 were waited for; matrix products, arithmetic and copies ran while one was open for 9% of the time, Pallas kernels for 47%

profile of v3, /device:TPU:0, one launch (start us, length us, event | category | flops | bytes accessed | tf_op | source)
XLA Modules:
  0.0 704.8 jit_solution(3642084369139058993)
XLA Ops:
  11.8 33.2 %collective-permute-done.3 = bf16[12,256]{1,0:T(8,128)(2,1)S(1)} collective-permute-done((bf16[12,256]{1,0:T(8,128)(2,1)S(1)}, bf16[12,256]{1,0:T(8,128)(2,1)S(1)}, u32[]{:S(2)}, u32[]{:S(2)}) %collective-permute-start.3) | collective-permute-done | bytes 6176 | tf_op jit(solution)/shard_map/ppermute | solution.py:741
  60.4 16.6 %forward_attend.2 = (bf16[416,1024]{1,0:T(8,128)(2,1)}, bf16[416,3072]{1,0:T(8,128)(2,1)}, bf16[416,1024]{1,0:T(8,128)(2,1)}, f32[2,16,208]{2,1,0:T(8,128)}) custom-call(bf16[416,1024]{1,0:T(8,128)(2,1)} %bitcast.90, bf16[256,3072]{1,0:T(8,128)(2,1)} %bitcast.96, bf16[256,3072]{1,0:T(8,128)(2,1)} %copy-done.7, bf16[256,3072]{1,0:T(8,128)(2,1)} %copy-done.6, ...), custom_call_target="tpu_custom_call" | custom-call | flops 46432256 | bytes 179360 | tf_op jit(solution)/shard_map/forward_attend/pallas_call | solution.py:52
  77.0 17.1 %forward_attend.3 = (bf16[416,1024]{1,0:T(8,128)(2,1)}, bf16[416,3072]{1,0:T(8,128)(2,1)}, bf16[416,1024]{1,0:T(8,128)(2,1)}, f32[2,16,208]{2,1,0:T(8,128)}) custom-call(bf16[416,1024]{1,0:T(8,128)(2,1)} %bitcast.86, bf16[256,3072]{1,0:T(8,128)(2,1)} %bitcast.97, bf16[256,3072]{1,0:T(8,128)(2,1)} %copy-done.7, bf16[256,3072]{1,0:T(8,128)(2,1)} %copy-done.6, ...), custom_call_target="tpu_custom_call" | custom-call | flops 46432256 | bytes 179360 | tf_op jit(solution)/shard_map/forward_attend/pallas_call | solution.py:52
  94.2 13.7 %collective-permute-done.7.refs_4_.refs_8_.refs_17_.refs_24_ = bf16[256,1024]{1,0:T(8,128)(2,1)} collective-permute-done((bf16[256,1024]{1,0:T(8,128)(2,1)}, bf16[256,1024]{1,0:T(8,128)(2,1)}, u32[]{:S(2)}, u32[]{:S(2)}) %collective-permute-start.7) | collective-permute-done | bytes 524320 | tf_op jit(solution)/shard_map/ppermute | solution.py:741
  116.2 16.5 %forward_feed.2 = (f32[416,1024]{1,0:T(8,128)}, bf16[416,4096]{1,0:T(8,128)(2,1)}, bf16[416,1024]{1,0:T(8,128)(2,1)}, bf16[416,4096]{1,0:T(8,128)(2,1)}) custom-call(bf16[416,1024]{1,0:T(8,128)(2,1)} %bitcast.91, bf16[416,1024]{1,0:T(8,128)(2,1)} %get-tuple-element.115.refs_1_, bf16[256,1024]{1,0:T(8,128)(2,1)} %bitcast.16.refs_2_.refs_6_.refs_15_.refs_22_, ...), custom_call_target="tpu_custom_call" | custom-call | flops 68157440 | bytes 337664 | tf_op jit(solution)/shard_map/forward_feed/pallas_call | solution.py:52
  132.7 16.7 %forward_feed.3 = (f32[416,1024]{1,0:T(8,128)}, bf16[416,4096]{1,0:T(8,128)(2,1)}, bf16[416,1024]{1,0:T(8,128)(2,1)}, bf16[416,4096]{1,0:T(8,128)(2,1)}) custom-call(bf16[416,1024]{1,0:T(8,128)(2,1)} %bitcast.87, bf16[416,1024]{1,0:T(8,128)(2,1)} %get-tuple-element.119.refs_1_, bf16[256,1024]{1,0:T(8,128)(2,1)} %bitcast.16.refs_2_.refs_6_.refs_15_.refs_22_, ...), custom_call_target="tpu_custom_call" | custom-call | flops 68157440 | bytes 337664 | tf_op jit(solution)/shard_map/forward_feed/pallas_call | solution.py:52
  149.4 8.8 %collective-permute-done.13.refs_4_.refs_9_.refs_16_.refs_5_ = bf16[1024,1024]{1,0:T(8,128)(2,1)} collective-permute-done((bf16[1024,1024]{1,0:T(8,128)(2,1)S(1)}, bf16[1024,1024]{1,0:T(8,128)(2,1)}, u32[]{:S(2)}, u32[]{:S(2)}) %collective-permute-start.13) | collective-permute-done | bytes 2097184 | tf_op jit(solution)/shard_map/ppermute | solution.py:741
  162.7 10.8 %output_forward.4 = bf16[416,1024]{1,0:T(8,128)(2,1)} custom-call(f32[416,1024]{1,0:T(8,128)} %get-tuple-element.124.refs_0_, bf16[416,4096]{1,0:T(8,128)(2,1)} %get-tuple-element.125.refs_1_, bf16[1024,1024]{1,0:T(8,128)(2,1)} %bitcast.77, bf16[1024,1024]{1,0:T(8,128)(2,1)} %copy-done.4, ...), custom_call_target="tpu_custom_call" | custom-call | flops 54525952 | bytes 225024 | tf_op jit(solution)/shard_map/output_forward/pallas_call | solution.py:52
  182.8 10.6 %output_forward.5 = bf16[416,1024]{1,0:T(8,128)(2,1)} custom-call(f32[416,1024]{1,0:T(8,128)} %get-tuple-element.129.refs_0_, bf16[416,4096]{1,0:T(8,128)(2,1)} %get-tuple-element.132.refs_1_, bf16[1024,1024]{1,0:T(8,128)(2,1)} %bitcast.78, bf16[1024,1024]{1,0:T(8,128)(2,1)} %copy-done.4, ...), custom_call_target="tpu_custom_call" | custom-call | flops 54525952 | bytes 225024 | tf_op jit(solution)/shard_map/output_forward/pallas_call | solution.py:52
  197.4 30.0 %forward_attend_feed.2 = (bf16[416,7168]{1,0:T(8,128)(2,1)}, bf16[416,3072]{1,0:T(8,128)(2,1)}, f32[2,16,208]{2,1,0:T(8,128)}, f32[416,1024]{1,0:T(8,128)}, bf16[416,4096]{1,0:T(8,128)(2,1)}) custom-call(bf16[416,1024]{1,0:T(8,128)(2,1)} %bitcast.92, bf16[416,1024]{1,0:T(8,128)(2,1)} %copy-done.41, bf16[256,3072]{1,0:T(8,128)(2,1)} %bitcast.98, ...), custom_call_target="tpu_custom_call" | custom-call | flops 58669924352 | bytes 257507552 | tf_op jit(solution)/shard_map/forward_attend_feed/pallas_call | solution.py:52
  227.5 36.5 %backward_feed_attend.2 = (bf16[416,9216]{1,0:T(8,128)(2,1)}, f32[8,1024]{1,0:T(8,128)}, f32[1,4096]{1,0:T(1,128)}, bf16[416,1024]{1,0:T(8,128)(2,1)}, f32[8,1024]{1,0:T(8,128)}) custom-call(bf16[416,1024]{1,0:T(8,128)(2,1)} %bitcast.114, bf16[416,4096]{1,0:T(8,128)(2,1)} %get-tuple-element.136.refs_1_.refs_0_, ...), custom_call_target="tpu_custom_call" | custom-call | flops 90840236032 | bytes 393429216 | tf_op jit(solution)/shard_map/backward_feed_attend/pallas_call | solution.py:52
  265.8 29.9 %forward_attend_feed.3 = (bf16[416,7168]{1,0:T(8,128)(2,1)}, bf16[416,3072]{1,0:T(8,128)(2,1)}, f32[2,16,208]{2,1,0:T(8,128)}, f32[416,1024]{1,0:T(8,128)}, bf16[416,4096]{1,0:T(8,128)(2,1)}) custom-call(bf16[416,1024]{1,0:T(8,128)(2,1)} %bitcast.88, bf16[416,1024]{1,0:T(8,128)(2,1)} %collective-permute-done.16.refs_1_.refs_13_, ...), custom_call_target="tpu_custom_call" | custom-call | flops 58669924352 | bytes 257507552 | tf_op jit(solution)/shard_map/forward_attend_feed/pallas_call | solution.py:52
  296.8 36.4 %backward_feed_attend.3 = (bf16[416,9216]{1,0:T(8,128)(2,1)}, f32[8,1024]{1,0:T(8,128)}, f32[1,4096]{1,0:T(1,128)}, bf16[416,1024]{1,0:T(8,128)(2,1)}, f32[8,1024]{1,0:T(8,128)}) custom-call(bf16[416,4096]{1,0:T(8,128)(2,1)} %get-tuple-element.136.refs_1_.refs_0_, bf16[416,4096]{1,0:T(8,128)(2,1)} %get-tuple-element.141.refs_1_, ...), custom_call_target="tpu_custom_call" | custom-call | flops 90840236032 | bytes 516325600 | tf_op jit(solution)/shard_map/backward_feed_attend/pallas_call | solution.py:52
  336.2 10.7 %output_forward.6 = bf16[416,1024]{1,0:T(8,128)(2,1)} custom-call(f32[416,1024]{1,0:T(8,128)} %get-tuple-element.134.refs_2_.refs_0_, bf16[416,7168]{1,0:T(8,128)(2,1)} %get-tuple-element.148.refs_4_.refs_8_.refs_1_.refs_0_, bf16[1024,1024]{1,0:T(8,128)(2,1)} %bitcast.81, bf16[1024,1024]{1,0:T(8,128)(2,1)} %copy-done.4, ...), custom_call_target="tpu_custom_call" | custom-call | flops 27917287424 | bytes 135659744 | tf_op jit(solution)/shard_map/output_forward/pallas_call | solution.py:52
  346.9 10.6 %output_forward.7 = bf16[416,1024]{1,0:T(8,128)(2,1)} custom-call(f32[416,1024]{1,0:T(8,128)} %get-tuple-element.142.refs_3_.refs_0_.refs_2_, bf16[416,7168]{1,0:T(8,128)(2,1)} %get-tuple-element.149.refs_9_.refs_1_.refs_2_.refs_3_, bf16[1024,1024]{1,0:T(8,128)(2,1)} %bitcast.82, bf16[1024,1024]{1,0:T(8,128)(2,1)} %copy-done.4, ...), custom_call_target="tpu_custom_call" | custom-call | flops 27917287424 | bytes 135659744 | tf_op jit(solution)/shard_map/output_forward/pallas_call | solution.py:52
  361.4 8.9 %reduce0.1 = (bf16[512,1024]{1,0:T(8,128)(2,1)}, bf16[512,1024]{1,0:T(8,128)(2,1)}) custom-call(bf16[416,7168]{1,0:T(8,128)(2,1)} %get-tuple-element.148.refs_4_.refs_8_.refs_1_.refs_0_, bf16[416,7168]{1,0:T(8,128)(2,1)} %collective-permute-done.18.refs_1_, bf16[416,7168]{1,0:T(8,128)(2,1)} %get-tuple-element.149.refs_9_.refs_1_.refs_2_.refs_3_, ...), custom_call_target="tpu_custom_call" | custom-call | flops 54525952 | bytes 911360 | tf_op jit(solution)/shard_map/reduce0/pallas_call | solution.py:52
  372.2 18.1 %backward_feed.1 = (bf16[416,5120]{1,0:T(8,128)(2,1)}, f32[8,1024]{1,0:T(8,128)}, f32[1,4096]{1,0:T(1,128)}, f32[416,1024]{1,0:T(8,128)}) custom-call(bf16[416,1024]{1,0:T(8,128)(2,1)} %copy-done.11, bf16[416,4096]{1,0:T(8,128)(2,1)} %get-tuple-element.141.refs_1_, f32[416,1024]{1,0:T(8,128)} %get-tuple-element.142.refs_3_.refs_0_.refs_2_, ...), custom_call_target="tpu_custom_call" | custom-call | flops 109051904 | bytes 450048 | tf_op jit(solution)/shard_map/backward_feed/pallas_call | solution.py:52
  398.4 9.2 %reduce1.1 = (bf16[512,1024]{1,0:T(8,128)(2,1)}, bf16[512,1024]{1,0:T(8,128)(2,1)}) custom-call(bf16[416,7168]{1,0:T(8,128)(2,1)} %get-tuple-element.148.refs_4_.refs_8_.refs_1_.refs_0_, bf16[416,7168]{1,0:T(8,128)(2,1)} %collective-permute-done.18.refs_1_, bf16[416,7168]{1,0:T(8,128)(2,1)} %get-tuple-element.149.refs_9_.refs_1_.refs_2_.refs_3_, ...), custom_call_target="tpu_custom_call" | custom-call | flops 54525952 | bytes 911360 | tf_op jit(solution)/shard_map/reduce1/pallas_call | solution.py:52
  412.0 6.5 project.1
  418.5 24.8 %backward_attend.1 = (bf16[416,3072]{1,0:T(8,128)(2,1)}, bf16[416,1024]{1,0:T(8,128)(2,1)}, f32[8,1024]{1,0:T(8,128)}) custom-call(bf16[416,1024]{1,0:T(8,128)(2,1)} %slice.94.refs_8_.refs_0_, f32[416,1024]{1,0:T(8,128)} %get-tuple-element.163.refs_1_, bf16[416,3072]{1,0:T(8,128)(2,1)} %get-tuple-element.143.refs_7_.refs_2_, ...), custom_call_target="tpu_custom_call" | custom-call | flops 70011322368 | bytes 381321664 | tf_op jit(solution)/shard_map/backward_attend/pallas_call | solution.py:52
  451.7 10.4 %collective-permute-done.29 = bf16[256,1024]{1,0:T(8,128)(2,1)} collective-permute-done((bf16[256,1024]{1,0:T(8,128)(2,1)}, bf16[256,1024]{1,0:T(8,128)(2,1)}, u32[]{:S(2)}, u32[]{:S(2)}) %collective-permute-start.29) | collective-permute-done | bytes 524320 | tf_op jit(solution)/shard_map/ppermute | solution.py:741
  464.3 9.5 %expand0.1 = (bf16[256,2048]{1,0:T(8,128)(2,1)}, bf16[256,2048]{1,0:T(8,128)(2,1)}) custom-call(bf16[416,7168]{1,0:T(8,128)(2,1)} %get-tuple-element.148.refs_4_.refs_8_.refs_1_.refs_0_, bf16[416,7168]{1,0:T(8,128)(2,1)} %collective-permute-done.18.refs_1_, bf16[416,7168]{1,0:T(8,128)(2,1)} %get-tuple-element.149.refs_9_.refs_1_.refs_2_.refs_3_, ...), custom_call_target="tpu_custom_call" | custom-call | flops 54525952 | bytes 991232 | tf_op jit(solution)/shard_map/expand0/pallas_call | solution.py:52
  480.0 9.4 %expand1.1 = (bf16[256,2048]{1,0:T(8,128)(2,1)}, bf16[256,2048]{1,0:T(8,128)(2,1)}) custom-call(bf16[416,7168]{1,0:T(8,128)(2,1)} %get-tuple-element.148.refs_4_.refs_8_.refs_1_.refs_0_, bf16[416,7168]{1,0:T(8,128)(2,1)} %collective-permute-done.18.refs_1_, bf16[416,7168]{1,0:T(8,128)(2,1)} %get-tuple-element.149.refs_9_.refs_1_.refs_2_.refs_3_, ...), custom_call_target="tpu_custom_call" | custom-call | flops 54525952 | bytes 991232 | tf_op jit(solution)/shard_map/expand1/pallas_call | solution.py:52
  490.6 8.1 %qkv0.1 = (bf16[256,1536]{1,0:T(8,128)(2,1)}, bf16[256,1536]{1,0:T(8,128)(2,1)}) custom-call(bf16[416,7168]{1,0:T(8,128)(2,1)} %get-tuple-element.148.refs_4_.refs_8_.refs_1_.refs_0_, bf16[416,7168]{1,0:T(8,128)(2,1)} %collective-permute-done.18.refs_1_, bf16[416,7168]{1,0:T(8,128)(2,1)} %get-tuple-element.149.refs_9_.refs_1_.refs_2_.refs_3_, ...), custom_call_target="tpu_custom_call" | custom-call | flops 40894464 | bytes 956416 | tf_op jit(solution)/shard_map/qkv0/pallas_call | solution.py:52
  498.7 6.5 qkv1.1
  532.6 14.7 %collective-permute-done.32 = bf16[256,2048]{1,0:T(8,128)(2,1)} collective-permute-done((bf16[256,2048]{1,0:T(8,128)(2,1)S(1)}, bf16[256,2048]{1,0:T(8,128)(2,1)}, u32[]{:S(2)}, u32[]{:S(2)}) %collective-permute-start.32) | collective-permute-done | bytes 1048608 | tf_op jit(solution)/shard_map/ppermute | solution.py:769
  548.8 26.1 %all-reduce.9.cloned.1.call-done = bf16[256,1024]{1,0:T(8,128)(2,1)} async-done(((bf16[256,1024]{1,0:T(8,128)(2,1)}), bf16[256,1024]{1,0:T(8,128)(2,1)}) %all-reduce.9.cloned.1.call-update) | async-done | bytes 524304 | tf_op jit(solution)/shard_map/psum | solution.py:765
  592.1 20.0 %collective-permute-start.42 = (bf16[272,512]{1,0:T(8,128)(2,1)S(1)}, bf16[272,512]{1,0:T(8,128)(2,1)S(1)}, u32[]{:S(2)}, u32[]{:S(2)}) collective-permute-start(bf16[272,512]{1,0:T(8,128)(2,1)S(1)} %add_convert_fusion.17), channel_id=1, source_target_pairs={{0,1},{3,2},{4,5},{7,6},{8,9},{11,10},{12,13},{15,14},{16,17},{19,... | collective-permute-start | bytes 835592 | tf_op jit(solution)/shard_map/ppermute | solution.py:769
  617.8 22.4 %collective-permute-done.43 = bf16[256,2048]{1,0:T(8,128)(2,1)S(1)} collective-permute-done((bf16[256,2048]{1,0:T(8,128)(2,1)S(1)}, bf16[256,2048]{1,0:T(8,128)(2,1)S(1)}, u32[]{:S(2)}, u32[]{:S(2)}) %collective-permute-start.43) | collective-permute-done | bytes 1048608 | tf_op jit(solution)/shard_map/ppermute | solution.py:775
  641.8 17.8 %collective-permute-done.45 = bf16[256,2048]{1,0:T(8,128)(2,1)S(1)} collective-permute-done((bf16[256,2048]{1,0:T(8,128)(2,1)S(1)}, bf16[256,2048]{1,0:T(8,128)(2,1)S(1)}, u32[]{:S(2)}, u32[]{:S(2)}) %collective-permute-start.45) | collective-permute-done | bytes 1048608 | tf_op jit(solution)/shard_map/ppermute | solution.py:775
  665.1 14.2 %collective-permute-done.48 = bf16[256,1536]{1,0:T(8,128)(2,1)S(1)} collective-permute-done((bf16[256,1536]{1,0:T(8,128)(2,1)S(1)}, bf16[256,1536]{1,0:T(8,128)(2,1)S(1)}, u32[]{:S(2)}, u32[]{:S(2)}) %collective-permute-start.48) | collective-permute-done | bytes 786464 | tf_op jit(solution)/shard_map/ppermute | solution.py:775
  679.4 14.7 %collective-permute-done.49 = bf16[256,1024]{1,0:T(8,128)(2,1)S(1)} collective-permute-done((bf16[256,1024]{1,0:T(8,128)(2,1)S(1)}, bf16[256,1024]{1,0:T(8,128)(2,1)S(1)}, u32[]{:S(2)}, u32[]{:S(2)}) %collective-permute-start.49) | collective-permute-done | bytes 524320 | tf_op jit(solution)/shard_map/ppermute | solution.py:775
  (281 shorter events, 150.4 us)
Async XLA Ops:
  7.2 472.8 %all-reduce.7.cloned.1.call-start = ((), (), s32[]{:S(2)}) async-start(), calls=%async_computation | async-start | bytes 2097152 | tf_op jit(solution)/shard_map/psum | solution.py:765
  7.2 41.1 %collective-permute-start.2 = (bf16[256,3072]{1,0:T(8,128)(2,1)}, bf16[256,3072]{1,0:T(8,128)(2,1)S(1)}, u32[]{:S(2)}, u32[]{:S(2)}) collective-permute-start(bf16[256,3072]{1,0:T(8,128)(2,1)} %bitcast.94), channel_id=1, source_target_pairs={{0,8},{4,12},{8,0},{12,4},{1,9},{5,13},{9,1},{13,5},{2,10},{6,14},... | collective-permute-start | bytes 4718600 | tf_op jit(solution)/shard_map/ppermute | solution.py:741
  11.7 33.4 %collective-permute-start.3 = (bf16[12,256]{1,0:T(8,128)(2,1)S(1)}, bf16[12,256]{1,0:T(8,128)(2,1)S(1)}, u32[]{:S(2)}, u32[]{:S(2)}) collective-permute-start(bf16[12,256]{1,0:T(8,128)(2,1)S(1)} %pad_maximum_fusion.4), channel_id=1, source_target_pairs={{0,8},{4,12},{8,0},{12,4},{1,9},{5,13},{9,1},{13,5},{2,10},{6,14},... | collective-permute-start | bytes 18440 | tf_op jit(solution)/shard_map/ppermute | solution.py:741
  11.7 33.3 %collective-permute-start = (bf16[12,256]{1,0:T(8,128)(2,1)S(1)}, bf16[12,256]{1,0:T(8,128)(2,1)S(1)}, u32[]{:S(2)}, u32[]{:S(2)}) collective-permute-start(bf16[12,256]{1,0:T(8,128)(2,1)S(1)} %pad_maximum_fusion.4), channel_id=1, source_target_pairs={{0,4},{4,0},{8,12},{12,8},{1,5},{5,1},{9,13},{13,9},{2,6},{6,2},{1... | collective-permute-start | bytes 18440 | tf_op jit(solution)/shard_map/ppermute | solution.py:738
  48.5 60.0 %collective-permute-start.10 = (bf16[256,4096]{1,0:T(8,128)(2,1)}, bf16[256,4096]{1,0:T(8,128)(2,1)}, u32[]{:S(2)}, u32[]{:S(2)}) collective-permute-start(bf16[256,4096]{1,0:T(8,128)(2,1)} %bitcast.68), channel_id=1, source_target_pairs={{0,8},{4,12},{8,0},{12,4},{1,9},{5,13},{9,1},{13,5},{2,10},{6,14},... | collective-permute-start | bytes 6291464 | tf_op jit(solution)/shard_map/ppermute | solution.py:741
  50.2 57.7 %collective-permute-start.7 = (bf16[256,1024]{1,0:T(8,128)(2,1)}, bf16[256,1024]{1,0:T(8,128)(2,1)}, u32[]{:S(2)}, u32[]{:S(2)}) collective-permute-start(bf16[256,1024]{1,0:T(8,128)(2,1)} %bitcast.16.refs_2_.refs_6_.refs_15_.refs_22_), channel_id=1, source_target_pairs={{0,8},{4,12},{8,0},{12,4},{1,9},{5,13},{9,1},{13,5},{2,10},{6,14},... | collective-permute-start | bytes 1572872 | tf_op jit(solution)/shard_map/ppermute | solution.py:741
  59.2 48.7 %collective-permute-start.6 = (bf16[256,1024]{1,0:T(8,128)(2,1)}, bf16[256,1024]{1,0:T(8,128)(2,1)}, u32[]{:S(2)}, u32[]{:S(2)}) collective-permute-start(bf16[256,1024]{1,0:T(8,128)(2,1)} %bitcast.16.refs_2_.refs_6_.refs_15_.refs_22_), channel_id=1, source_target_pairs={{0,4},{4,0},{8,12},{12,8},{1,5},{5,1},{9,13},{13,9},{2,6},{6,2},{1... | collective-permute-start | bytes 1572872 | tf_op jit(solution)/shard_map/ppermute | solution.py:738
  110.2 48.0 %collective-permute-start.13 = (bf16[1024,1024]{1,0:T(8,128)(2,1)S(1)}, bf16[1024,1024]{1,0:T(8,128)(2,1)}, u32[]{:S(2)}, u32[]{:S(2)}) collective-permute-start(bf16[1024,1024]{1,0:T(8,128)(2,1)S(1)} %bitcast.84), channel_id=1, source_target_pairs={{0,8},{4,12},{8,0},{12,4},{1,9},{5,13},{9,1},{13,5},{2,10},{6,14},... | collective-permute-start | bytes 6291464 | tf_op jit(solution)/shard_map/ppermute | solution.py:741
  112.8 45.4 %collective-permute-start.12 = (bf16[1024,1024]{1,0:T(8,128)(2,1)S(1)}, bf16[1024,1024]{1,0:T(8,128)(2,1)S(1)}, u32[]{:S(2)}, u32[]{:S(2)}) collective-permute-start(bf16[1024,1024]{1,0:T(8,128)(2,1)S(1)} %bitcast.85), channel_id=1, source_target_pairs={{0,4},{4,0},{8,12},{12,8},{1,5},{5,1},{9,13},{13,9},{2,6},{6,2},{1... | collective-permute-start | bytes 6291464 | tf_op jit(solution)/shard_map/ppermute | solution.py:738
  193.5 71.8 %collective-permute-start.16 = (bf16[416,1024]{1,0:T(8,128)(2,1)}, bf16[416,1024]{1,0:T(8,128)(2,1)}, u32[]{:S(2)}, u32[]{:S(2)}) collective-permute-start(bf16[416,1024]{1,0:T(8,128)(2,1)} %output_forward.5), channel_id=1, source_target_pairs={{0,16},{1,17},{2,18},{3,19},{4,20},{5,21},{6,22},{7,23},{8,24},{9,... | collective-permute-start | bytes 2555912 | tf_op jit(solution)/shard_map/ppermute | solution.py:807
  227.4 108.7 %collective-permute-start.18 = (bf16[416,7168]{1,0:T(8,128)(2,1)}, bf16[416,7168]{1,0:T(8,128)(2,1)}, u32[]{:S(2)}, u32[]{:S(2)}) collective-permute-start(bf16[416,7168]{1,0:T(8,128)(2,1)} %get-tuple-element.148.refs_4_.refs_8_.refs_1_.refs_0_), channel_id=1, source_target_pairs={{0,4},{4,0},{8,12},{12,8},{1,5},{5,1},{9,13},{13,9},{2,6},{6,2},{1... | collective-permute-start | bytes 17891336 | tf_op jit(solution)/shard_map/ppermute | solution.py:738
  265.3 70.9 %collective-permute-start.19 = (bf16[416,9216]{1,0:T(8,128)(2,1)}, bf16[416,9216]{1,0:T(8,128)(2,1)}, u32[]{:S(2)}, u32[]{:S(2)}) collective-permute-start(bf16[416,9216]{1,0:T(8,128)(2,1)} %get-tuple-element.147.refs_5_), channel_id=1, source_target_pairs={{0,4},{4,0},{8,12},{12,8},{1,5},{5,1},{9,13},{13,9},{2,6},{6,2},{1... | collective-permute-start | bytes 23003144 | tf_op jit(solution)/shard_map/ppermute | solution.py:738
  295.7 51.2 %collective-permute-start.20 = (bf16[416,7168]{1,0:T(8,128)(2,1)}, bf16[416,7168]{1,0:T(8,128)(2,1)}, u32[]{:S(2)}, u32[]{:S(2)}) collective-permute-start(bf16[416,7168]{1,0:T(8,128)(2,1)} %get-tuple-element.149.refs_9_.refs_1_.refs_2_.refs_3_), channel_id=1, source_target_pairs={{0,4},{4,0},{8,12},{12,8},{1,5},{5,1},{9,13},{13,9},{2,6},{6,2},{1... | collective-permute-start | bytes 17891336 | tf_op jit(solution)/shard_map/ppermute | solution.py:738
  370.3 38.8 %collective-permute-start.25 = (bf16[512,1024]{1,0:T(8,128)(2,1)}, bf16[512,1024]{1,0:T(8,128)(2,1)}, u32[]{:S(2)}, u32[]{:S(2)}) collective-permute-start(bf16[512,1024]{1,0:T(8,128)(2,1)} %get-tuple-element.159), channel_id=1, source_target_pairs={{0,8},{4,12},{8,0},{12,4},{1,9},{5,13},{9,1},{13,5},{2,10},{6,14},... | collective-permute-start | bytes 3145736 | tf_op jit(solution)/shard_map/ppermute | solution.py:741
  407.6 40.9 %collective-permute-start.28 = (bf16[512,1024]{1,0:T(8,128)(2,1)}, bf16[512,1024]{1,0:T(8,128)(2,1)}, u32[]{:S(2)}, u32[]{:S(2)}) collective-permute-start(bf16[512,1024]{1,0:T(8,128)(2,1)} %get-tuple-element.167), channel_id=1, source_target_pairs={{0,8},{4,12},{8,0},{12,4},{1,9},{5,13},{9,1},{13,5},{2,10},{6,14},... | collective-permute-start | bytes 3145736 | tf_op jit(solution)/shard_map/ppermute | solution.py:741
  409.0 55.3 %collective-permute-start.27 = (bf16[416,4096]{1,0:T(8,128)(2,1)S(1)}, bf16[416,4096]{1,0:T(8,128)(2,1)}, u32[]{:S(2)}, u32[]{:S(2)}) collective-permute-start(bf16[416,4096]{1,0:T(8,128)(2,1)S(1)} %slice.96.refs_8_), channel_id=1, source_target_pairs={{0,4},{4,0},{8,12},{12,8},{1,5},{5,1},{9,13},{13,9},{2,6},{6,2},{1... | collective-permute-start | bytes 10223624 | tf_op jit(solution)/shard_map/ppermute | solution.py:738
  411.9 108.0 %all-reduce.11.cloned.1.call-start = ((), (), s32[]{:S(2)}) async-start(), calls=%async_computation.2 | async-start | bytes 2097152 | tf_op jit(solution)/shard_map/psum | solution.py:765
  443.3 47.3 %collective-permute-start.26 = (bf16[416,3072]{1,0:T(8,128)(2,1)}, bf16[416,3072]{1,0:T(8,128)(2,1)}, u32[]{:S(2)}, u32[]{:S(2)}) collective-permute-start(bf16[416,3072]{1,0:T(8,128)(2,1)} %get-tuple-element.165.refs_8_), channel_id=1, source_target_pairs={{0,4},{4,0},{8,12},{12,8},{1,5},{5,1},{9,13},{13,9},{2,6},{6,2},{1... | collective-permute-start | bytes 7667720 | tf_op jit(solution)/shard_map/ppermute | solution.py:738
  451.2 123.8 %all-reduce.9.cloned.1.call-start = ((), (), s32[]{:S(2)}) async-start(), calls=%async_computation.1 | async-start | bytes 1048576 | tf_op jit(solution)/shard_map/psum | solution.py:765
  473.8 36.3 %collective-permute-start.30 = (bf16[256,2048]{1,0:T(8,128)(2,1)}, bf16[256,2048]{1,0:T(8,128)(2,1)S(1)}, u32[]{:S(2)}, u32[]{:S(2)}) collective-permute-start(bf16[256,2048]{1,0:T(8,128)(2,1)} %get-tuple-element.182), channel_id=1, source_target_pairs={{0,8},{4,12},{8,0},{12,4},{1,9},{5,13},{9,1},{13,5},{2,10},{6,14},... | collective-permute-start | bytes 3145736 | tf_op jit(solution)/shard_map/ppermute | solution.py:741
  489.4 33.3 %collective-permute-start.31 = (bf16[256,2048]{1,0:T(8,128)(2,1)}, bf16[256,2048]{1,0:T(8,128)(2,1)}, u32[]{:S(2)}, u32[]{:S(2)}) collective-permute-start(bf16[256,2048]{1,0:T(8,128)(2,1)} %get-tuple-element.185), channel_id=1, source_target_pairs={{0,8},{4,12},{8,0},{12,4},{1,9},{5,13},{9,1},{13,5},{2,10},{6,14},... | collective-permute-start | bytes 3145736 | tf_op jit(solution)/shard_map/ppermute | solution.py:741
  510.5 36.7 %collective-permute-start.32 = (bf16[256,2048]{1,0:T(8,128)(2,1)S(1)}, bf16[256,2048]{1,0:T(8,128)(2,1)}, u32[]{:S(2)}, u32[]{:S(2)}) collective-permute-start(bf16[256,2048]{1,0:T(8,128)(2,1)S(1)} %add_convert_fusion.5), channel_id=1, source_target_pairs={{0,1},{3,2},{4,5},{7,6},{8,9},{11,10},{12,13},{15,14},{16,17},{19,... | collective-permute-start | bytes 3145736 | tf_op jit(solution)/shard_map/ppermute | solution.py:769
  515.2 59.7 %collective-permute-start.33 = (bf16[256,1536]{1,0:T(8,128)(2,1)}, bf16[256,1536]{1,0:T(8,128)(2,1)}, u32[]{:S(2)}, u32[]{:S(2)}) collective-permute-start(bf16[256,1536]{1,0:T(8,128)(2,1)} %get-tuple-element.189), channel_id=1, source_target_pairs={{0,8},{4,12},{8,0},{12,4},{1,9},{5,13},{9,1},{13,5},{2,10},{6,14},... | collective-permute-start | bytes 2359304 | tf_op jit(solution)/shard_map/ppermute | solution.py:741
  516.9 74.2 %collective-permute-start.38 = (bf16[272,512]{1,0:T(8,128)(2,1)}, bf16[272,512]{1,0:T(8,128)(2,1)}, u32[]{:S(2)}, u32[]{:S(2)}) collective-permute-start(bf16[272,512]{1,0:T(8,128)(2,1)} %pad_maximum_fusion.1), channel_id=1, source_target_pairs={{0,8},{4,12},{8,0},{12,4},{1,9},{5,13},{9,1},{13,5},{2,10},{6,14},... | collective-permute-start | bytes 835592 | tf_op jit(solution)/shard_map/ppermute | solution.py:741
  518.1 66.9 %collective-permute-start.36 = (bf16[256,1024]{1,0:T(8,128)(2,1)}, bf16[256,1024]{1,0:T(8,128)(2,1)}, u32[]{:S(2)}, u32[]{:S(2)}) collective-permute-start(bf16[256,1024]{1,0:T(8,128)(2,1)} %get-tuple-element.201), channel_id=1, source_target_pairs={{0,8},{4,12},{8,0},{12,4},{1,9},{5,13},{9,1},{13,5},{2,10},{6,14},... | collective-permute-start | bytes 1572872 | tf_op jit(solution)/shard_map/ppermute | solution.py:741
  524.4 57.9 %collective-permute-start.35 = (bf16[256,2048]{1,0:T(8,128)(2,1)S(1)}, bf16[256,2048]{1,0:T(8,128)(2,1)}, u32[]{:S(2)}, u32[]{:S(2)}) collective-permute-start(bf16[256,2048]{1,0:T(8,128)(2,1)S(1)} %add_convert_fusion.4), channel_id=1, source_target_pairs={{0,1},{3,2},{4,5},{7,6},{8,9},{11,10},{12,13},{15,14},{16,17},{19,... | collective-permute-start | bytes 3145736 | tf_op jit(solution)/shard_map/ppermute | solution.py:769
  576.5 36.9 %collective-permute-start.39 = (bf16[256,1536]{1,0:T(8,128)(2,1)S(1)}, bf16[256,1536]{1,0:T(8,128)(2,1)S(1)}, u32[]{:S(2)}, u32[]{:S(2)}) collective-permute-start(bf16[256,1536]{1,0:T(8,128)(2,1)S(1)} %add_convert_fusion.10), channel_id=1, source_target_pairs={{0,1},{3,2},{4,5},{7,6},{8,9},{11,10},{12,13},{15,14},{16,17},{19,... | collective-permute-start | bytes 2359304 | tf_op jit(solution)/shard_map/ppermute | solution.py:769
  613.9 45.9 %collective-permute-start.46 = (bf16[256,1024]{1,0:T(8,128)(2,1)S(1)}, bf16[256,1024]{1,0:T(8,128)(2,1)S(1)}, u32[]{:S(2)}, u32[]{:S(2)}) collective-permute-start(bf16[256,1024]{1,0:T(8,128)(2,1)S(1)} %add_convert_fusion.12), channel_id=1, source_target_pairs={{1,2},{2,1},{5,6},{6,5},{9,10},{10,9},{13,14},{14,13},{17,18},{18,... | collective-permute-start | bytes 1572872 | tf_op jit(solution)/shard_map/ppermute | solution.py:772
  615.7 43.9 %collective-permute-start.45 = (bf16[256,2048]{1,0:T(8,128)(2,1)S(1)}, bf16[256,2048]{1,0:T(8,128)(2,1)S(1)}, u32[]{:S(2)}, u32[]{:S(2)}) collective-permute-start(bf16[256,2048]{1,0:T(8,128)(2,1)S(1)} %add_convert_fusion), channel_id=1, source_target_pairs={{1,0},{2,3},{5,4},{6,7},{9,8},{10,11},{13,12},{14,15},{17,16},{18,... | collective-permute-start | bytes 3145736 | tf_op jit(solution)/shard_map/ppermute | solution.py:775
  617.1 42.9 %collective-permute-start.47 = (bf16[272,512]{1,0:T(8,128)(2,1)S(1)}, bf16[272,512]{1,0:T(8,128)(2,1)S(1)}, u32[]{:S(2)}, u32[]{:S(2)}) collective-permute-start(bf16[272,512]{1,0:T(8,128)(2,1)S(1)} %add_convert_fusion.16), channel_id=1, source_target_pairs={{1,2},{2,1},{5,6},{6,5},{9,10},{10,9},{13,14},{14,13},{17,18},{18,... | collective-permute-start | bytes 835592 | tf_op jit(solution)/shard_map/ppermute | solution.py:772
  640.5 38.8 %collective-permute-start.48 = (bf16[256,1536]{1,0:T(8,128)(2,1)S(1)}, bf16[256,1536]{1,0:T(8,128)(2,1)S(1)}, u32[]{:S(2)}, u32[]{:S(2)}) collective-permute-start(bf16[256,1536]{1,0:T(8,128)(2,1)S(1)} %add_convert_fusion.8), channel_id=1, source_target_pairs={{1,0},{2,3},{5,4},{6,7},{9,8},{10,11},{13,12},{14,15},{17,16},{18,... | collective-permute-start | bytes 2359304 | tf_op jit(solution)/shard_map/ppermute | solution.py:775
  660.0 34.1 %collective-permute-start.50 = (bf16[272,512]{1,0:T(8,128)(2,1)S(1)}, bf16[272,512]{1,0:T(8,128)(2,1)S(1)}, u32[]{:S(2)}, u32[]{:S(2)}) collective-permute-start(bf16[272,512]{1,0:T(8,128)(2,1)S(1)} %add_convert_fusion.15), channel_id=1, source_target_pairs={{1,0},{2,3},{5,4},{6,7},{9,8},{10,11},{13,12},{14,15},{17,16},{18,... | collective-permute-start | bytes 835592 | tf_op jit(solution)/shard_map/ppermute | solution.py:775
  (65 other events, 837.0 us)
Sparse Core Ops, SparseCore 0:
  412.0 53.4 all-reduce.6
  468.0 50.9 all-reduce.10
  521.3 53.5 all-reduce.8

commit v4 on v3

--- a/solution.py
+++ b/solution.py
@@ -61,11 +61,15 @@
     )(*operands)
 
 
-def start_pieces(pieces, order_ref, target, sems, slot, columns):
-    rows = pieces[0].shape[0]
+def flat(groups):
+    return [piece for group in groups for piece in group]
+
+
+def start_pieces(pieces, info, first, target, sems, slot, columns):
     copies = []
     for index, piece in enumerate(pieces):
-        where = pl.multiple_of(order_ref[index] * rows, rows)
+        rows = piece.shape[0]
+        where = pl.multiple_of(info[first + index] * rows, rows)
         copy = pltpu.make_async_copy(
             piece.at[:, columns], target.at[pl.ds(where, rows), columns], sems.at[slot, index]
         )
@@ -151,6 +155,8 @@
             turned = pltpu.roll(total, head, 1)
             offset = pl.multiple_of(index * pair, pair)
             mixed[span, pl.ds(offset, pair)] = (inside / turned).astype(BF16)
+            if logs is None:
+                continue
             logged = jnp.log(turned)
             first = tops[0] + logged[:, 0:1]
             second = tops[1] + logged[:, head : head + 1]
@@ -160,8 +166,9 @@
         return carry
 
     lax.fori_loop(0, HEADS // 2, heads, 0)
-    for image in range(count):
-        logs[image] = columns[image].T[0:HEADS]
+    if logs is not None:
+        for image in range(count):
+            logs[image] = columns[image].T[0:HEADS]
 
 
 def hidden_stage(x, vec, mixed, middle, active, second, slope, full_out, full, first_load, loads):
@@ -183,8 +190,9 @@
         value = contract(second[...], full[:, part], 1, 0) + vec[EXPAND + block : EXPAND + block + 1]
         share = 0.5 + 0.5 * lax.erf(value * ROOT_HALF)
         active[:, part] = (value * share).astype(BF16)
-        density = ROOT_TAU * jnp.exp(-0.5 * value * value)
-        slope[:, part] = (share + value * density).astype(BF16)
+        if slope is not None:
+            density = ROOT_TAU * jnp.exp(-0.5 * value * value)
+            slope[:, part] = (share + value * density).astype(BF16)
 
 
 def forward(
@@ -196,7 +204,9 @@
     attend, feed = qkv is not None, expand is not None
     both = attend and feed
     parts = len(qkv if attend else expand)
-    inner = expand[0].shape[1] if feed else 0
+    many = len(flat(qkv if attend else expand))
+    spots = parts + 1 + count
+    inner = expand[0][0].shape[1] if feed else 0
     blocks = inner // width
     same = lower is upper
 
@@ -206,7 +216,7 @@
         up = low if same else refs.pop(0)
         if not attend:
             arrived = refs.pop(0)
-        lists = [[refs.pop(0) for _ in range(parts)] for _ in range(attend + 2 * feed)]
+        lists = [[refs.pop(0) for _ in range(many)] for _ in range(attend + 2 * feed)]
         vec, info = refs.pop(0), refs.pop(0)
         if both:
             left, packed, logs, middle, slope = (refs.pop(0) for _ in range(5))
@@ -215,28 +225,30 @@
                 for start, size in ((0, inner), *((inner + width * i, width) for i in range(3)))
             )
         elif attend:
-            norm, packed, mixed, logs = (refs.pop(0) for _ in range(4))
+            mixed = refs.pop(0)
         else:
-            middle, active, second, slope = (refs.pop(0) for _ in range(4))
+            middle, active = refs.pop(0), refs.pop(0)
         x, x_sem = refs.pop(0), refs.pop(0)
         section = info[parts]
         take = start_chosen(section, low, up, x, x_sem.at[0])
         if attend:
             columns, full, a_sem = (refs.pop(0) for _ in range(3))
+            if not both:
+                norm, packed, logs = refs.pop(0), refs.pop(0), None
             weight = lists.pop(0)
             loads = [
-                start_pieces(weight, info, full, a_sem, block, pl.ds(block * width, width))
+                start_pieces(weight, info, spots, full, a_sem, block, pl.ds(block * width, width))
                 for block in range(3)
             ]
         if feed:
             full_out, full_in, o_sem, w_sem = (refs.pop(0) for _ in range(4))
             if not attend:
-                mixed = refs.pop(0)
+                mixed, second, slope = refs.pop(0), refs.pop(0), None
                 extra = pltpu.make_async_copy(arrived, mixed, x_sem.at[1])
                 extra.start()
-            first_load = start_pieces(lists[0], info, full_out, o_sem, 0, pl.ds(0, width))
+            first_load = start_pieces(lists[0], info, spots, full_out, o_sem, 0, pl.ds(0, width))
             inner_loads = [
-                start_pieces(lists[1], info, full_in, w_sem, block, pl.ds(block * width, width))
+                start_pieces(lists[1], info, spots, full_in, w_sem, block, pl.ds(block * width, width))
                 for block in range(blocks)
             ]
         take.wait()
@@ -265,8 +277,10 @@
         scratch += [
             pltpu.VMEM((count, space, pair), F32),
             pltpu.VMEM((width, 3 * width), BF16),
-            pltpu.SemaphoreType.DMA((3, parts)),
+            pltpu.SemaphoreType.DMA((3, many)),
         ]
+        if not feed:
+            scratch += [pltpu.VMEM((rows, width), BF16), pltpu.VMEM((rows, 3 * width), BF16)]
         flops += 2 * rows * width * (3 * width + 2 * space)
     else:
         inputs += [mixed_in]
@@ -280,15 +294,17 @@
         scratch += [
             pltpu.VMEM((width, width), BF16),
             pltpu.VMEM((width, inner), BF16),
-            pltpu.SemaphoreType.DMA((1, parts)),
-            pltpu.SemaphoreType.DMA((blocks, parts)),
+            pltpu.SemaphoreType.DMA((1, many)),
+            pltpu.SemaphoreType.DMA((blocks, many)),
         ]
         if not attend:
-            scratch += [pltpu.VMEM((rows, width), BF16)]
+            scratch += [pltpu.VMEM((rows, width), BF16), pltpu.VMEM((rows, width), BF16)]
         flops += 2 * rows * width * (width + inner)
     if both:
         outs = [((rows, inner + 3 * width), BF16), outs[1], outs[3], outs[4], outs[7]]
-    weights = (list(qkv) if attend else []) + (list(out) + list(expand) if feed else [])
+    else:
+        outs = [outs[2]] if attend else outs[:2]
+    weights = (flat(qkv) if attend else []) + (flat(out) + flat(expand) if feed else [])
     return call(
         body,
         "forward" + "_attend" * attend + "_feed" * feed,
@@ -303,16 +319,17 @@
 
 def output_forward(middle, active, pieces, params, meta, count, weight=1.0 / 64):
     rows, width = middle.shape
-    inner = len(pieces) * pieces[0].shape[0]
+    inner = sum(piece.shape[0] for piece in flat(pieces))
     space = rows // count
-    parts = len(pieces)
+    parts, many = len(pieces), len(flat(pieces))
+    spots = parts + 1 + count
     blocks = 2
     part_width = width // blocks
 
     def body(*refs):
         refs = list(refs)
         mid_in, act_in = refs.pop(0), refs.pop(0)
-        reduce = [refs.pop(0) for _ in range(parts)]
+        reduce = [refs.pop(0) for _ in range(many)]
         vec, info, result, mid, act, full, x_sem, w_sem = refs
         copies = [
             pltpu.make_async_copy(act_in.at[:, pl.ds(0, inner)], act, x_sem.at[0]),
@@ -320,7 +337,7 @@
         ]
         copies[0].start()
         loads = [
-            start_pieces(reduce, info, full, w_sem, block, pl.ds(block * part_width, part_width))
+            start_pieces(reduce, info, spots, full, w_sem, block, pl.ds(block * part_width, part_width))
             for block in range(blocks)
         ]
         copies[1].start()
@@ -339,15 +356,15 @@
     return call(
         body,
         "output_forward",
-        [middle, active] + list(pieces) + [params, meta],
-        [ANY] * (2 + parts) + [VMEM, SMEM],
+        [middle, active] + flat(pieces) + [params, meta],
+        [ANY] * (2 + many) + [VMEM, SMEM],
         [((rows, width), BF16)],
         [
             pltpu.VMEM((rows, width), F32),
             pltpu.VMEM((rows, inner), BF16),
             pltpu.VMEM((inner, width), BF16),
             pltpu.SemaphoreType.DMA((2,)),
-            pltpu.SemaphoreType.DMA((blocks, parts)),
+            pltpu.SemaphoreType.DMA((blocks, many)),
         ],
         2 * rows * width * inner,
         weight,
@@ -495,8 +512,10 @@
     space = rows // count
     pair = 2 * width // HEADS
     parts = len(reduce if feed else qkv)
-    inner = expand[0].shape[1] if feed else 0
-    deep = reduce[0].shape[0] if feed else 0
+    many = len(flat(reduce if feed else qkv))
+    spots = parts + 1 + count
+    inner = expand[0][0].shape[1] if feed else 0
+    deep = inner // parts
     both = feed and attend
     choices = []
     if feed:
@@ -518,7 +537,7 @@
         for low, up in choices:
             one = refs.pop(0)
             pairs.append((one, one if low is up else refs.pop(0)))
-        lists = [[refs.pop(0) for _ in range(parts)] for _ in range(2 * feed + 2 * attend)]
+        lists = [[refs.pop(0) for _ in range(many)] for _ in range(2 * feed + 2 * attend)]
         vec, info = refs.pop(0), refs.pop(0)
         section = info[parts]
         if feed:
@@ -543,15 +562,10 @@
             begin = pairs.pop(2) if start[0] is not start[1] else (firsts[0], firsts[0])
             take = start_chosen(section, *begin, grad, x_sem.at[0])
             for_slope = start_chosen(section, *pairs.pop(0), slope, x_sem.at[1])
-            first_load = [
-                start_pieces(
-                    [piece], Shifted(info, index), full_out, o_sem.at[pl.ds(index, 1)], 0,
-                    pl.ds(0, width),
-                )
-                for index, piece in enumerate(lists.pop(0))
-            ]
+            every = start_pieces(lists.pop(0), info, spots, full_out, o_sem, 0, pl.ds(0, width))
+            first_load = [[every.pop(0) for _ in group] for group in reduce]
             for_middle = start_chosen(section, *pairs.pop(0), middle, x_sem.at[2])
-            load = start_pieces(lists.pop(0), info, full, w_sem, 0, pl.ds(0, inner))
+            load = start_pieces(lists.pop(0), info, spots, full, w_sem, 0, pl.ds(0, inner))
         if attend:
             x, packed, mixed, logs, down, normal, stage, full_o, full_q, p_sem, q_sem = (
                 refs.pop(0) for _ in range(11)
@@ -564,14 +578,14 @@
                 ]
                 for given in givens:
                     given.start()
-            project_load = start_pieces(lists.pop(0), info, full_o, p_sem, 0, pl.ds(0, width))
+            project_load = start_pieces(lists.pop(0), info, spots, full_o, p_sem, 0, pl.ds(0, width))
             sames = [one is two for one, two in pairs]
             pairs[1] = tuple(one.at[:, pl.ds(mixed_at, width)] for one in pairs[1])
             takes = [
                 start_chosen(section, *pairs[index], target, x_sem.at[3 + index], sames[index])
                 for index, target in ((1, mixed), (0, packed), (2, logs), (3, x))
             ]
-            last_load = start_pieces(lists.pop(0), info, full_q, q_sem, 0, pl.ds(0, 3 * width))
+            last_load = start_pieces(lists.pop(0), info, spots, full_q, q_sem, 0, pl.ds(0, 3 * width))
             if not feed:
                 wait_all(givens)
         if feed:
@@ -605,8 +619,8 @@
             pltpu.VMEM((rows, width), F32),
             pltpu.VMEM((inner, width), BF16),
             pltpu.VMEM((width, inner), BF16),
-            pltpu.SemaphoreType.DMA((parts, 1)),
-            pltpu.SemaphoreType.DMA((1, parts)),
+            pltpu.SemaphoreType.DMA((1, many)),
+            pltpu.SemaphoreType.DMA((1, many)),
         ]
         scratch += [pltpu.VMEM((rows, width), F32 if both else BF16)]
         flops += 4 * rows * width * inner
@@ -623,14 +637,14 @@
             pltpu.VMEM((count, HEADS, 2 * pair), F32),
             pltpu.VMEM((width, width), BF16),
             pltpu.VMEM((width, 3 * width), BF16),
-            pltpu.SemaphoreType.DMA((1, parts)),
-            pltpu.SemaphoreType.DMA((1, parts)),
+            pltpu.SemaphoreType.DMA((1, many)),
+            pltpu.SemaphoreType.DMA((1, many)),
         ]
         if not feed:
             scratch += [pltpu.VMEM((rows, width), BF16), pltpu.VMEM((rows, width), F32)]
         flops += 2 * rows * width * (4 * width + 5 * space)
-    weights = (list(reduce) + list(expand) if feed else []) + (
-        list(out) + list(qkv) if attend else []
+    weights = (flat(reduce) + flat(expand) if feed else []) + (
+        flat(out) + flat(qkv) if attend else []
     )
     return call(
         body,
@@ -644,15 +658,9 @@
     )
 
 
-class Shifted:
-    def __init__(self, ref, index):
-        self.ref, self.index = ref, index
-
-    def __getitem__(self, index):
-        return self.ref[self.index + index]
-
-
-def weight_gradient(lefts, rights, meta, parts, blocks, quarter, rows_of, columns_of, name):
+def weight_gradient(
+    lefts, rights, meta, parts, blocks, quarter, rows_of, columns_of, name, weight=1.0 / 64
+):
     terms = len(lefts)
     first_row, height = rows_of
     first_column, breadth = columns_of
@@ -710,6 +718,7 @@
             pltpu.SemaphoreType.DMA((terms,)),
         ],
         2 * len(blocks) * terms * rows * height * breadth,
+        weight,
     )
 
 
@@ -733,6 +742,9 @@
         self.group = lax.axis_index("group")
         self.place = lax.axis_index("replica")
         self.order = [self.group ^ part for part in range(4)]
+        odd = self.place % 2
+        halves = [2 * self.order[part] + half for part in (2, 3) for half in (odd, 1 - odd)]
+        self.spots = self.order[:2] + halves
 
     def core(self, block):
         return lax.ppermute(block, "group", [(i, i ^ 1) for i in range(4)])
@@ -740,17 +752,35 @@
     def across(self, block):
         return lax.ppermute(block, "group", [(i, i ^ 2) for i in range(4)])
 
-    def gather(self, blocks):
-        far, sibling = [], []
+    def beside(self, block):
+        return lax.ppermute(block, "replica", [(i, i ^ 1) for i in range(4)])
+
+    def gather(self, small, blocks):
+        far, halves, sibling = self.across(small), [], []
+        odd = self.place % 2
         for index, block in enumerate(blocks):
-            far.append(self.across(after(block, far[index - 2]) if index > 1 else block))
+            rows = block.shape[0] // 2
+            half = lax.dynamic_slice_in_dim(block, odd * rows, rows)
+            half = after(half, far if index < 2 else halves[index - 2])
+            halves.append(self.across(half))
             sibling.append(self.core(after(block, sibling[-1]) if index else block))
-
-        def pieces(index, token):
-            distant = far[index] if token is None else after(far[index], token)
-            return [blocks[index], sibling[index], far[index], self.core(distant)]
-
-        return [partial(pieces, index) for index in range(len(blocks))]
+        others = []
+        for half in halves:
+            others.append(self.beside(after(half, others[-1]) if others else half))
+
+        def pieces(index, *tokens):
+            one, two = (after(half, *tokens) for half in (halves[index], others[index]))
+            return [
+                [blocks[index]],
+                [sibling[index]],
+                [halves[index], others[index]],
+                [self.core(one), self.core(two)],
+            ]
+
+        near = self.core(small)
+        return [small, near, far, self.core(far)], [
+            partial(pieces, index) for index in range(len(blocks))
+        ]
 
     def shared(self, block):
         return [block, self.core(block)]
@@ -782,14 +812,15 @@
     def __init__(self):
         self.parts = lax.axis_size("group")
         self.blocks = tuple(range(self.parts))
-        self.order = [jnp.int32(part) for part in range(self.parts)]
-
-    def gather(self, blocks):
-        found = []
-        for block in blocks:
+        self.order = self.spots = [jnp.int32(part) for part in range(self.parts)]
+
+    def gather(self, small, blocks):
+        def pieces(block):
             whole = lax.all_gather(block, "group", axis=0)
-            found.append([whole[part] for part in range(self.parts)])
-        return [lambda token, pieces=pieces: pieces for pieces in found]
+            return [whole[part] for part in range(self.parts)]
+
+        found = [[[piece] for piece in pieces(block)] for block in blocks]
+        return pieces(small), [lambda *tokens, groups=groups: groups for groups in found]
 
     def shared(self, block):
         return [block]
@@ -870,18 +901,18 @@
     batches = tuple(range(micro))
 
     def rows_of(array):
-        full = jnp.pad(array, ((0, 0), (0, 0), (0, space - length), (0, 0)))
-        return [full[batch].reshape(slots * space, width) for batch in batches]
+        fulls = [jnp.pad(array[batch], ((0, 0), (0, space - length), (0, 0))) for batch in batches]
+        return [full.reshape(slots * space, width) for full in fulls]
 
     def images_of(array):
         return array.reshape(slots, space, width)[:, :length]
 
     inputs, targets = rows_of(images), rows_of(cotangent)
     small = jnp.concatenate([norm_gains[0], biases[0], expand_bias[0].reshape(-1, share)])
-    vectors, qkv, out, expand, reduce = net.gather(
-        [small, qkv_weight[0], out_weight[0], expand_weight[0], reduce_weight[0]]
-    )
-    vectors = in_order(vectors(after(inputs[0], *inputs[1:], *targets)), net.order)
+    vectors, (qkv, out, expand, reduce) = net.gather(
+        small, [qkv_weight[0], out_weight[0], expand_weight[0], reduce_weight[0]]
+    )
+    vectors = in_order(vectors, net.order)
     top = vectors[:, :8].transpose(1, 0, 2).reshape(8, width)
     bottom = vectors[:, 8:].reshape(-1, width)
     params = jnp.concatenate([top, bottom]).astype(F32)
@@ -889,26 +920,27 @@
     alive = [(slot < counts[batch, 0]).astype(jnp.int32) for batch in batches]
     head = jnp.stack(net.order + [section]).astype(jnp.int32)
 
-    def meta(*values):
-        return jnp.concatenate((head,) + values)
+    spots = jnp.stack(net.spots).astype(jnp.int32)
+
+    def meta(living):
+        return jnp.concatenate([head, living, spots])
 
     infos = [meta(alive[batch]) for batch in batches]
-    info = meta(*alive)
-
-    qkv = qkv(params)
+
+    qkv = qkv(params, *inputs, *targets)
     attended = []
     for batch in batches:
-        start = inputs[batch] if batch == 0 else after(inputs[batch], attended[-1][2])
+        start = inputs[batch] if batch == 0 else after(inputs[batch], attended[-1][0])
         attended.append(
             forward(start, start, None, qkv, None, None, params, infos[batch], slots, length)
         )
-    out = out(attended[-1][2])
-    expand = expand(out[-1])
+    out = out(attended[-1][0])
+    expand = expand(out[-1][0])
     fed = []
     for batch in batches:
         start = inputs[batch] if batch == 0 else after(inputs[batch], fed[-1][0])
         fed.append(
-            forward(start, start, attended[batch][2], None, out, expand, params, infos[batch], slots, length)
+            forward(start, start, attended[batch][0], None, out, expand, params, infos[batch], slots, length)
         )
     reduce = reduce(fed[-1][0])
     early, incoming = [], []
@@ -919,7 +951,7 @@
         early.append(output_forward(middle, active, reduce, params, infos[batch], slots))
         incoming.append(shifted(early[batch], 1))
 
-    inner = expand[0].shape[1]
+    inner = expand[0][0].shape[1]
     mixed_at = inner + width
     kept, lefts, rights, results = [], [], [], []
     sums_a, sums_b, sums_c, returning = [], [], [], []
@@ -964,7 +996,7 @@
     masked = net.shared(jnp.where(living, arrived, jnp.zeros_like(arrived)))
     many = len(masked)
 
-    def gradient(name, left_at, final, final_at, right_at, quarter, rows, columns, own):
+    def gradient(name, left_at, final, final_at, right_at, quarter, rows, columns, own, weight=1.0 / 64):
         left = [lefts[batch][side] for batch in batches for side in range(many)]
         right = []
         for batch in batches:
@@ -973,20 +1005,21 @@
                 lower = (final[side], final_at) if batch == last else (rights[batch + 1][side], right_at)
                 right.append((lower, upper))
         blocks = weight_gradient(
-            left, right, run.now(info), parts, net.blocks, quarter, (left_at + rows[0], rows[1]), columns,
-            name,
+            left, right, run.now(head), parts, net.blocks, quarter, (left_at + rows[0], rows[1]), columns,
+            name, weight,
         )
         run.ran(blocks[0])
         return blocks
 
     def summed(name, *rest):
-        run.add(name, gradient(name, *rest), rest[-1])
-
-    def reduce_part(index, own):
+        run.add(name, gradient(name, *rest), rest[7])
+
+    def reduce_part(index, own, weight=1.0 / 64):
         deep = inner // parts
         step = deep // 2
         summed(
-            f"reduce{index}", 0, masked, 0, inner + width, deep, (index * step, step), (0, width), own
+            f"reduce{index}", 0, masked, 0, inner + width, deep, (index * step, step), (0, width), own,
+            weight,
         )
 
     reduce_part(0, False)
@@ -1000,9 +1033,19 @@
     finals, branches = net.shared(final[:, :inner]), net.shared(branch)
     sums_a.append(some)
     sums_b.append(more)
-    reduce_part(1, False)
     run.step("reduce0")
-    summed("project", mixed_at, branches, 0, inner, share, (0, share), (0, width), False)
+    reduce_part(1, False, 16.0)
+
+    def expand_part(index, cut, own):
+        begin, step = cut
+        summed(f"expand{index}", inner, finals, 0, 0, share, (0, share), (begin, step), own)
+
+    quarter = inner // 4
+    expand_part(0, (0, 2 * quarter), True)
+    expand_part(1, (2 * quarter, quarter), True)
+    expand_part(2, (3 * quarter, quarter), True)
+    run.step("reduce1")
+    summed("project", mixed_at, branches, 0, inner, share, (0, share), (0, width), True)
     grads, result, rest = backward(
         (run.now(branch), mid), inputs[last], inputs[last], kept[last], kept[last], None, None, out, qkv,
         params, infos[last], slots, length, mixed_at, 16.0,
@@ -1011,15 +1054,7 @@
     grads = net.shared(grads)
     results.append(result)
     sums_c.append(rest)
-    run.step("reduce1", "project")
-
-    def expand_part(index, own):
-        step = inner // 2
-        summed(f"expand{index}", inner, finals, 0, 0, share, (0, share), (index * step, step), own)
-
-    expand_part(0, True)
-    run.step("reduce0")
-    expand_part(1, True)
+    run.step("expand0")
 
     def over_batches(values):
         return sum(jnp.where(first, values[batch + 1], values[batch]) for batch in batches)
@@ -1034,22 +1069,25 @@
     )
     count, step = rows.shape[1], width // 2
     rows = rows.reshape(len(net.blocks), -1)
-    rows = jnp.pad(rows, ((0, 0), (0, -rows.shape[1] % (16 * step)))).reshape(len(net.blocks), -1, step)
+    rows = jnp.pad(rows, ((0, 0), (0, -rows.shape[1] % (32 * step)))).reshape(len(net.blocks), -1, 2 * step)
 
     def qkv_part(index):
-        begin, breadth = ((0, 3 * step), (3 * step, 2 * step), (5 * step, step))[index]
+        begin, breadth = ((0, 2 * step), (2 * step, 2 * step), (4 * step, 2 * step))[index]
         return gradient(
             f"qkv{index}", inner + 2 * width, grads, 0, inner + 2 * width, share, (0, share),
             (begin, breadth), True,
         )
 
     run.add("qkv0", qkv_part(0), True)
+    run.step("expand1")
     run.add("qkv1", qkv_part(1), True)
+    run.step("expand0", "reduce0")
     blocks = qkv_part(2)
     run.add("qkv2", [jnp.concatenate([one, two]) for one, two in zip(blocks, rows.astype(BF16))], True)
     run.step(
-        "expand0", "reduce1", "expand1", "expand0", "project", "qkv0", "expand1", "qkv1", "expand0", "qkv2", "qkv0", "qkv1", "expand1",
-        "qkv2", "expand0", "qkv0", "expand1", "qkv1", "qkv2", "qkv0", "qkv1", "qkv2",
+        "expand2", "reduce1", "project", "expand1", "expand2", "expand0", "qkv0", "expand1", "qkv1", "project",
+        "expand2", "qkv2", "qkv0", "expand0", "expand1", "qkv1", "project", "expand2", "qkv0", "qkv2", "project",
+        "qkv1", "qkv0", "qkv2", "qkv1", "qkv2",
     )
     weights = {name: run.finish(name) for name in run.sums}
     vector = weights["qkv2"][share:].reshape(-1)[: count * share].reshape(count, share).astype(F32)
@@ -1067,7 +1105,7 @@
         chosen(results[1:], results[:-1]),
         jnp.concatenate([weights["qkv0"], weights["qkv1"], weights["qkv2"][:share]], axis=1).astype(F32)[None],
         weights["project"].astype(F32)[None],
-        joined(1, "expand0", "expand1"),
+        joined(1, "expand0", "expand1", "expand2"),
         joined(0, "reduce0", "reduce1"),
         vector[None, 0:2],
         vector[None, 2:8],

time: 714 us -> 698 us (0.978)
  waiting for transfers between devices: 191 us -> 144 us
  starting transfers between devices: 76.1 us -> 89.5 us
  local copies, waits for them, and re-layouts: 28.5 us -> 41.8 us
    ppermute x13 -> x14, waiting for transfers between devices: 68.9 us -> 38.9 us  [across(): return lax.ppermute(block, 'group', [(i, i ^ 2) for i in range(4)])]
    psum x3 -> x2, waiting for transfers between devices: 26.1 us -> 12.2 us  [total(): whole = lax.psum(mine, 'replica', axis_index_groups=[turn])]
    ppermute x5 -> x7, waiting for transfers between devices: 69 us -> 60.7 us  [total(): outward = lax.ppermute(summed, 'replica', [(1, 0), (2, 3)])]
    slice x7 -> x1, local copies, waits for them, and re-layouts: 8.78 us -> 0.6 us  [per_device(): vector[8:].reshape(1, -1)]
    dynamic_slice x0 -> x4, local copies, waits for them, and re-layouts: none -> 7.41 us  [gather(): half = lax.dynamic_slice_in_dim(block, odd * rows, rows)]
    ppermute x5 -> x7, waiting for transfers between devices: 14.7 us -> 9.68 us  [total(): inward = lax.ppermute(mine, 'replica', [(0, 1), (3, 2)])]
    ppermute x5 -> x7, starting transfers between devices: 37.7 us -> 40.5 us  [total(): inward = lax.ppermute(mine, 'replica', [(0, 1), (3, 2)])]
    convert_element_type x18 -> x23, other arithmetic: 18.4 us -> 20.7 us  [added(): return total.astype(values[0].dtype)]
  transfers between devices with their start and end apart: 54 -> 68, of which waited for: 19 -> 23; matrix products, arithmetic and copies ran while one was open for 9% -> 11% of each run, Pallas kernels for 47% -> 48%
where the time goes in v4:
time: 698 us; the launch traced here: 685 us
  Pallas kernels  348 us (50%)
  waiting for transfers between devices  144 us (21%)
  starting transfers between devices  89.5 us (13%)
  other arithmetic  46 us (7%)
  local copies, waits for them, and re-layouts  41.8 us (6%)
  between operations  15.7 us (2%)
    pallas_call x23, Pallas kernels, call(): pl.pallas_call(body, out_shape=out_shape, in_specs=specs, out_specs=[VMEM...  348 us
    ppermute x7, waiting for transfers between devices, total(): outward = lax.ppermute(summed, 'replica', [(1, 0), (2, 3)])  60.7 us
    ppermute x7, starting transfers between devices, total(): inward = lax.ppermute(mine, 'replica', [(0, 1), (3, 2)])  40.5 us
    ppermute x14, waiting for transfers between devices, across(): return lax.ppermute(block, 'group', [(i, i ^ 2) for i in range(4)])  38.9 us
    convert_element_type x23, other arithmetic, added(): return total.astype(values[0].dtype)  20.7 us
    ppermute x14, starting transfers between devices, across(): return lax.ppermute(block, 'group', [(i, i ^ 2) for i in range(4)])  16.3 us
  transfers between devices with their start and end apart: 68, of which 23 were waited for; matrix products, arithmetic and copies ran while one was open for 11% of the time, Pallas kernels for 48%

profile of v4, /device:TPU:0, one launch (start us, length us, event | category | flops | bytes accessed | tf_op | source)
XLA Modules:
  0.0 684.5 jit_solution(3913524072002723146)
XLA Ops:
  21.2 11.6 %collective-permute-done.2.refs_3_.refs_4_.refs_27_.refs_34_.refs_14_ = bf16[128,3072]{1,0:T(8,128)(2,1)} collective-permute-done((bf16[128,3072]{1,0:T(8,128)(2,1)S(1)}, bf16[128,3072]{1,0:T(8,128)(2,1)}, u32[]{:S(2)}, u32[]{:S(2)}) %collective-permute-start.2) | collective-permute-done | bytes 786464 | tf_op jit(solution)/shard_map/ppermute | solution.py:753
  47.3 15.3 %collective-permute-done.9.refs_4_.refs_10_.refs_21_.refs_28_.refs_8_ = bf16[128,1024]{1,0:T(8,128)(2,1)S(1)} collective-permute-done((bf16[128,1024]{1,0:T(8,128)(2,1)}, bf16[128,1024]{1,0:T(8,128)(2,1)S(1)}, u32[]{:S(2)}, u32[]{:S(2)}) %collective-permute-start.9) | collective-permute-done | bytes 262176 | tf_op jit(solution)/shard_map/ppermute | solution.py:753
  78.1 15.9 %forward_attend.2.refs_1_ = bf16[416,1024]{1,0:T(8,128)(2,1)} custom-call(bf16[416,1024]{1,0:T(8,128)(2,1)} %bitcast.115, bf16[256,3072]{1,0:T(8,128)(2,1)} %bitcast.104, bf16[256,3072]{1,0:T(8,128)(2,1)} %copy-done.9, bf16[128,3072]{1,0:T(8,128)(2,1)} %collective-permute-done.2.refs_3_.refs_4_.refs_27_.refs_34_.refs_14_, ...), custom_call_target="tpu_custom_call" | custom-call | flops 46432256 | bytes 125696 | tf_op jit(solution)/shard_map/forward_attend/pallas_call | solution.py:52
  94.0 15.9 %forward_attend.3.refs_1_ = bf16[416,1024]{1,0:T(8,128)(2,1)} custom-call(bf16[416,1024]{1,0:T(8,128)(2,1)} %bitcast.111, bf16[256,3072]{1,0:T(8,128)(2,1)} %bitcast.105, bf16[256,3072]{1,0:T(8,128)(2,1)} %copy-done.9, bf16[128,3072]{1,0:T(8,128)(2,1)} %collective-permute-done.2.refs_3_.refs_4_.refs_27_.refs_34_.refs_14_, ...), custom_call_target="tpu_custom_call" | custom-call | flops 46432256 | bytes 125696 | tf_op jit(solution)/shard_map/forward_attend/pallas_call | solution.py:52
  120.2 13.8 %forward_feed.2 = (f32[416,1024]{1,0:T(8,128)}, bf16[416,4096]{1,0:T(8,128)(2,1)}) custom-call(bf16[416,1024]{1,0:T(8,128)(2,1)} %bitcast.116, bf16[416,1024]{1,0:T(8,128)(2,1)} %forward_attend.2.refs_1_, bf16[256,1024]{1,0:T(8,128)(2,1)} %bitcast.28.refs_2_.refs_8_.refs_19_.refs_26_.refs_6_, bf16[256,1024]{1,0:T(8,128)(2,1)} %copy-done.19, ...), custom_call_target="tpu_custom_call" | custom-call | flops 68157440 | bytes 271104 | tf_op jit(solution)/shard_map/forward_feed/pallas_call | solution.py:52
  133.9 13.8 %forward_feed.3 = (f32[416,1024]{1,0:T(8,128)}, bf16[416,4096]{1,0:T(8,128)(2,1)}) custom-call(bf16[416,1024]{1,0:T(8,128)(2,1)} %bitcast.112, bf16[416,1024]{1,0:T(8,128)(2,1)} %forward_attend.3.refs_1_, bf16[256,1024]{1,0:T(8,128)(2,1)} %bitcast.28.refs_2_.refs_8_.refs_19_.refs_26_.refs_6_, bf16[256,1024]{1,0:T(8,128)(2,1)} %copy-done.19, ...), custom_call_target="tpu_custom_call" | custom-call | flops 68157440 | bytes 271104 | tf_op jit(solution)/shard_map/forward_feed/pallas_call | solution.py:52
  154.5 10.9 %output_forward.4 = bf16[416,1024]{1,0:T(8,128)(2,1)} custom-call(f32[416,1024]{1,0:T(8,128)} %get-tuple-element.141.refs_0_, bf16[416,4096]{1,0:T(8,128)(2,1)} %get-tuple-element.142.refs_1_, bf16[1024,1024]{1,0:T(8,128)(2,1)} %bitcast.95, bf16[1024,1024]{1,0:T(8,128)(2,1)} %copy-done.4, ...), custom_call_target="tpu_custom_call" | custom-call | flops 54525952 | bytes 225024 | tf_op jit(solution)/shard_map/output_forward/pallas_call | solution.py:52
  171.0 10.7 %output_forward.5 = bf16[416,1024]{1,0:T(8,128)(2,1)} custom-call(f32[416,1024]{1,0:T(8,128)} %get-tuple-element.147.refs_0_, bf16[416,4096]{1,0:T(8,128)(2,1)} %get-tuple-element.151.refs_1_, bf16[1024,1024]{1,0:T(8,128)(2,1)} %bitcast.96, bf16[1024,1024]{1,0:T(8,128)(2,1)} %copy-done.4, ...), custom_call_target="tpu_custom_call" | custom-call | flops 54525952 | bytes 225024 | tf_op jit(solution)/shard_map/output_forward/pallas_call | solution.py:52
  189.4 30.7 %forward_attend_feed.2 = (bf16[416,7168]{1,0:T(8,128)(2,1)}, bf16[416,3072]{1,0:T(8,128)(2,1)}, f32[2,16,208]{2,1,0:T(8,128)}, f32[416,1024]{1,0:T(8,128)}, bf16[416,4096]{1,0:T(8,128)(2,1)}) custom-call(bf16[416,1024]{1,0:T(8,128)(2,1)} %bitcast.117, bf16[416,1024]{1,0:T(8,128)(2,1)} %copy-done.49, bf16[256,3072]{1,0:T(8,128)(2,1)} %bitcast.106, ...), custom_call_target="tpu_custom_call" | custom-call | flops 58669924352 | bytes 257507744 | tf_op jit(solution)/shard_map/forward_attend_feed/pallas_call | solution.py:52
  220.2 37.0 %backward_feed_attend.2 = (bf16[416,9216]{1,0:T(8,128)(2,1)}, f32[8,1024]{1,0:T(8,128)}, f32[1,4096]{1,0:T(1,128)}, bf16[416,1024]{1,0:T(8,128)(2,1)}, f32[8,1024]{1,0:T(8,128)}) custom-call(bf16[416,1024]{1,0:T(8,128)(2,1)} %bitcast.131, bf16[416,4096]{1,0:T(8,128)(2,1)} %get-tuple-element.155.refs_1_.refs_0_, ...), custom_call_target="tpu_custom_call" | custom-call | flops 90840236032 | bytes 393429408 | tf_op jit(solution)/shard_map/backward_feed_attend/pallas_call | solution.py:52
  259.0 30.5 %forward_attend_feed.3 = (bf16[416,7168]{1,0:T(8,128)(2,1)}, bf16[416,3072]{1,0:T(8,128)(2,1)}, f32[2,16,208]{2,1,0:T(8,128)}, f32[416,1024]{1,0:T(8,128)}, bf16[416,4096]{1,0:T(8,128)(2,1)}) custom-call(bf16[416,1024]{1,0:T(8,128)(2,1)} %bitcast.113, bf16[416,1024]{1,0:T(8,128)(2,1)} %collective-permute-done.24.refs_1_.refs_13_, ...), custom_call_target="tpu_custom_call" | custom-call | flops 58669924352 | bytes 257507744 | tf_op jit(solution)/shard_map/forward_attend_feed/pallas_call | solution.py:52
  290.6 37.3 %backward_feed_attend.3 = (bf16[416,9216]{1,0:T(8,128)(2,1)}, f32[8,1024]{1,0:T(8,128)}, f32[1,4096]{1,0:T(1,128)}, bf16[416,1024]{1,0:T(8,128)(2,1)}, f32[8,1024]{1,0:T(8,128)}) custom-call(bf16[416,4096]{1,0:T(8,128)(2,1)} %get-tuple-element.155.refs_1_.refs_0_, bf16[416,4096]{1,0:T(8,128)(2,1)} %get-tuple-element.160.refs_1_, ...), custom_call_target="tpu_custom_call" | custom-call | flops 90840236032 | bytes 516325792 | tf_op jit(solution)/shard_map/backward_feed_attend/pallas_call | solution.py:52
  330.8 10.7 %output_forward.6 = bf16[416,1024]{1,0:T(8,128)(2,1)} custom-call(f32[416,1024]{1,0:T(8,128)} %get-tuple-element.153.refs_2_.refs_0_, bf16[416,7168]{1,0:T(8,128)(2,1)} %get-tuple-element.167.refs_4_.refs_8_.refs_1_.refs_0_, bf16[1024,1024]{1,0:T(8,128)(2,1)} %bitcast.99, bf16[1024,1024]{1,0:T(8,128)(2,1)} %copy-done.4, ...), custom_call_target="tpu_custom_call" | custom-call | flops 27917287424 | bytes 135659936 | tf_op jit(solution)/shard_map/output_forward/pallas_call | solution.py:52
  341.5 10.7 %output_forward.7 = bf16[416,1024]{1,0:T(8,128)(2,1)} custom-call(f32[416,1024]{1,0:T(8,128)} %get-tuple-element.161.refs_3_.refs_0_.refs_2_, bf16[416,7168]{1,0:T(8,128)(2,1)} %get-tuple-element.168.refs_9_.refs_1_.refs_2_.refs_3_, bf16[1024,1024]{1,0:T(8,128)(2,1)} %bitcast.100, bf16[1024,1024]{1,0:T(8,128)(2,1)} %copy-done.4, ...), custom_call_target="tpu_custom_call" | custom-call | flops 27917287424 | bytes 135659936 | tf_op jit(solution)/shard_map/output_forward/pallas_call | solution.py:52
  355.1 8.9 %reduce0.1 = (bf16[512,1024]{1,0:T(8,128)(2,1)}, bf16[512,1024]{1,0:T(8,128)(2,1)}) custom-call(bf16[416,7168]{1,0:T(8,128)(2,1)} %get-tuple-element.167.refs_4_.refs_8_.refs_1_.refs_0_, bf16[416,7168]{1,0:T(8,128)(2,1)} %collective-permute-done.26.refs_1_, bf16[416,7168]{1,0:T(8,128)(2,1)} %get-tuple-element.168.refs_9_.refs_1_.refs_2_.refs_3_, ...), custom_call_target="tpu_custom_call" | custom-call | flops 54525952 | bytes 911360 | tf_op jit(solution)/shard_map/reduce0/pallas_call | solution.py:52
  365.8 19.4 %backward_feed.1 = (bf16[416,5120]{1,0:T(8,128)(2,1)}, f32[8,1024]{1,0:T(8,128)}, f32[1,4096]{1,0:T(1,128)}, f32[416,1024]{1,0:T(8,128)}) custom-call(bf16[416,1024]{1,0:T(8,128)(2,1)} %copy-done.13, bf16[416,4096]{1,0:T(8,128)(2,1)} %get-tuple-element.160.refs_1_, f32[416,1024]{1,0:T(8,128)} %get-tuple-element.161.refs_3_.refs_0_.refs_2_, ...), custom_call_target="tpu_custom_call" | custom-call | flops 109051904 | bytes 450048 | tf_op jit(solution)/shard_map/backward_feed/pallas_call | solution.py:52
  392.2 9.1 %reduce1.1 = (bf16[512,1024]{1,0:T(8,128)(2,1)}, bf16[512,1024]{1,0:T(8,128)(2,1)}) custom-call(bf16[416,7168]{1,0:T(8,128)(2,1)} %get-tuple-element.167.refs_4_.refs_8_.refs_1_.refs_0_, bf16[416,7168]{1,0:T(8,128)(2,1)} %collective-permute-done.26.refs_1_, bf16[416,7168]{1,0:T(8,128)(2,1)} %get-tuple-element.168.refs_9_.refs_1_.refs_2_.refs_3_, ...), custom_call_target="tpu_custom_call" | custom-call | flops 55834574848 | bytes 933232960 | tf_op jit(solution)/shard_map/reduce1/pallas_call | solution.py:52
  410.0 9.3 %expand0.1 = (bf16[256,2048]{1,0:T(8,128)(2,1)}, bf16[256,2048]{1,0:T(8,128)(2,1)}) custom-call(bf16[416,7168]{1,0:T(8,128)(2,1)} %get-tuple-element.167.refs_4_.refs_8_.refs_1_.refs_0_, bf16[416,7168]{1,0:T(8,128)(2,1)} %collective-permute-done.26.refs_1_, bf16[416,7168]{1,0:T(8,128)(2,1)} %get-tuple-element.168.refs_9_.refs_1_.refs_2_.refs_3_, ...), custom_call_target="tpu_custom_call" | custom-call | flops 54525952 | bytes 991232 | tf_op jit(solution)/shard_map/expand0/pallas_call | solution.py:52
  419.3 6.3 expand1.1
  425.7 6.5 expand2.1
  434.9 6.4 project.1
  442.8 24.9 %backward_attend.1 = (bf16[416,3072]{1,0:T(8,128)(2,1)}, bf16[416,1024]{1,0:T(8,128)(2,1)}, f32[8,1024]{1,0:T(8,128)}) custom-call(bf16[416,1024]{1,0:T(8,128)(2,1)} %slice.92.refs_8_.refs_0_, f32[416,1024]{1,0:T(8,128)} %get-tuple-element.190.refs_1_, bf16[416,3072]{1,0:T(8,128)(2,1)} %get-tuple-element.162.refs_7_.refs_2_, ...), custom_call_target="tpu_custom_call" | custom-call | flops 70011322368 | bytes 381322048 | tf_op jit(solution)/shard_map/backward_attend/pallas_call | solution.py:52
  487.9 6.4 qkv0.1
  517.8 6.4 qkv2.1
  525.6 9.0 %collective-permute-start.43 = (bf16[256,1024]{1,0:T(8,128)(2,1)S(1)}, bf16[256,1024]{1,0:T(8,128)(2,1)}, u32[]{:S(2)}, u32[]{:S(2)}) collective-permute-start(bf16[256,1024]{1,0:T(8,128)(2,1)S(1)} %add_convert_fusion.21), channel_id=1, source_target_pairs={{0,1},{3,2},{4,5},{7,6},{8,9},{11,10},{12,13},{15,14},{16,17},{19,... | collective-permute-start | bytes 1572872 | tf_op jit(solution)/shard_map/ppermute | solution.py:799
  534.6 12.2 %all-reduce.10.cloned.1.call-done = bf16[512,1024]{1,0:T(8,128)(2,1)} async-done(((bf16[512,1024]{1,0:T(8,128)(2,1)}), bf16[512,1024]{1,0:T(8,128)(2,1)}) %all-reduce.10.cloned.1.call-update) | async-done | bytes 1048592 | tf_op jit(solution)/shard_map/psum | solution.py:795
  573.3 12.6 %collective-permute-start.52 = (bf16[256,1024]{1,0:T(8,128)(2,1)S(1)}, bf16[256,1024]{1,0:T(8,128)(2,1)S(1)}, u32[]{:S(2)}, u32[]{:S(2)}) collective-permute-start(bf16[256,1024]{1,0:T(8,128)(2,1)S(1)} %add_convert_fusion.17), channel_id=1, source_target_pairs={{0,1},{3,2},{4,5},{7,6},{8,9},{11,10},{12,13},{15,14},{16,17},{19,... | collective-permute-start | bytes 1572872 | tf_op jit(solution)/shard_map/ppermute | solution.py:799
  605.0 17.6 %collective-permute-done.54 = bf16[256,1024]{1,0:T(8,128)(2,1)S(1)} collective-permute-done((bf16[256,1024]{1,0:T(8,128)(2,1)S(1)}, bf16[256,1024]{1,0:T(8,128)(2,1)S(1)}, u32[]{:S(2)}, u32[]{:S(2)}) %collective-permute-start.54) | collective-permute-done | bytes 524320 | tf_op jit(solution)/shard_map/ppermute | solution.py:805
  628.3 11.4 %collective-permute-done.60 = bf16[256,1024]{1,0:T(8,128)(2,1)S(1)} collective-permute-done((bf16[256,1024]{1,0:T(8,128)(2,1)S(1)}, bf16[256,1024]{1,0:T(8,128)(2,1)S(1)}, u32[]{:S(2)}, u32[]{:S(2)}) %collective-permute-start.60) | collective-permute-done | bytes 524320 | tf_op jit(solution)/shard_map/ppermute | solution.py:805
  642.2 7.7 %collective-permute-done.62 = bf16[256,1024]{1,0:T(8,128)(2,1)S(1)} collective-permute-done((bf16[256,1024]{1,0:T(8,128)(2,1)S(1)}, bf16[256,1024]{1,0:T(8,128)(2,1)S(1)}, u32[]{:S(2)}, u32[]{:S(2)}) %collective-permute-start.62) | collective-permute-done | bytes 524320 | tf_op jit(solution)/shard_map/ppermute | solution.py:805
  654.0 12.1 %collective-permute-done.64 = bf16[256,1024]{1,0:T(8,128)(2,1)S(1)} collective-permute-done((bf16[256,1024]{1,0:T(8,128)(2,1)S(1)}, bf16[256,1024]{1,0:T(8,128)(2,1)S(1)}, u32[]{:S(2)}, u32[]{:S(2)}) %collective-permute-start.64) | collective-permute-done | bytes 524320 | tf_op jit(solution)/shard_map/ppermute | solution.py:805
  666.2 7.4 %collective-permute-done.65 = bf16[272,1024]{1,0:T(8,128)(2,1)S(1)} collective-permute-done((bf16[272,1024]{1,0:T(8,128)(2,1)S(1)}, bf16[272,1024]{1,0:T(8,128)(2,1)S(1)}, u32[]{:S(2)}, u32[]{:S(2)}) %collective-permute-start.65) | collective-permute-done | bytes 557088 | tf_op jit(solution)/shard_map/ppermute | solution.py:805
  (340 shorter events, 210.5 us)
Async XLA Ops:
  7.2 510.6 %all-reduce.8.cloned.1.call-start = ((), (), s32[]{:S(2)}) async-start(), calls=%async_computation | async-start | bytes 2097152 | tf_op jit(solution)/shard_map/psum | solution.py:795
  15.5 31.3 %collective-permute-start.5 = (bf16[12,256]{1,0:T(8,128)(2,1)S(1)}, bf16[12,256]{1,0:T(8,128)(2,1)S(1)}, u32[]{:S(2)}, u32[]{:S(2)}) collective-permute-start(bf16[12,256]{1,0:T(8,128)(2,1)S(1)} %pad_maximum_fusion.4), channel_id=1, source_target_pairs={{0,4},{4,0},{8,12},{12,8},{1,5},{5,1},{9,13},{13,9},{2,6},{6,2},{1... | collective-permute-start | bytes 18440 | tf_op jit(solution)/shard_map/ppermute | solution.py:750
  32.8 36.2 %collective-permute-start.14 = (bf16[128,4096]{1,0:T(8,128)(2,1)}, bf16[128,4096]{1,0:T(8,128)(2,1)S(1)}, u32[]{:S(2)}, u32[]{:S(2)}) collective-permute-start(bf16[128,4096]{1,0:T(8,128)(2,1)} %dynamic-slice_bitcast_fusion.1), channel_id=1, source_target_pairs={{0,8},{4,12},{8,0},{12,4},{1,9},{5,13},{9,1},{13,5},{2,10},{6,14},... | collective-permute-start | bytes 3145736 | tf_op jit(solution)/shard_map/ppermute | solution.py:753
  34.3 28.3 %collective-permute-start.3 = (bf16[128,3072]{1,0:T(8,128)(2,1)}, bf16[128,3072]{1,0:T(8,128)(2,1)}, u32[]{:S(2)}, u32[]{:S(2)}) collective-permute-start(bf16[128,3072]{1,0:T(8,128)(2,1)} %collective-permute-done.2.refs_3_.refs_4_.refs_27_.refs_34_.refs_14_), channel_id=1, source_target_pairs={{0,1},{1,0},{2,3},{3,2},{4,5},{5,4},{6,7},{7,6},{8,9},{9,8},{10,11... | collective-permute-start | bytes 2359304 | tf_op jit(solution)/shard_map/ppermute | solution.py:756
  38.2 74.3 %collective-permute-start.13 = (bf16[256,4096]{1,0:T(8,128)(2,1)S(1)}, bf16[256,4096]{1,0:T(8,128)(2,1)}, u32[]{:S(2)}, u32[]{:S(2)}) collective-permute-start(bf16[256,4096]{1,0:T(8,128)(2,1)S(1)} %bitcast.94), channel_id=1, source_target_pairs={{0,4},{4,0},{8,12},{12,8},{1,5},{5,1},{9,13},{13,9},{2,6},{6,2},{1... | collective-permute-start | bytes 6291464 | tf_op jit(solution)/shard_map/ppermute | solution.py:750
  69.7 42.0 %collective-permute-start.15 = (bf16[128,4096]{1,0:T(8,128)(2,1)S(1)}, bf16[128,4096]{1,0:T(8,128)(2,1)}, u32[]{:S(2)}, u32[]{:S(2)}) collective-permute-start(bf16[128,4096]{1,0:T(8,128)(2,1)S(1)} %collective-permute-done.14.refs_10_.refs_16_.refs_15_.refs_22_.refs_11_), channel_id=1, source_target_pairs={{0,1},{1,0},{2,3},{3,2},{4,5},{5,4},{6,7},{7,6},{8,9},{9,8},{10,11... | collective-permute-start | bytes 3145736 | tf_op jit(solution)/shard_map/ppermute | solution.py:756
  73.3 38.7 %collective-permute-start.19 = (bf16[512,1024]{1,0:T(8,128)(2,1)}, bf16[512,1024]{1,0:T(8,128)(2,1)}, u32[]{:S(2)}, u32[]{:S(2)}) collective-permute-start(bf16[512,1024]{1,0:T(8,128)(2,1)} %dynamic-slice_bitcast_fusion), channel_id=1, source_target_pairs={{0,8},{4,12},{8,0},{12,4},{1,9},{5,13},{9,1},{13,5},{2,10},{6,14},... | collective-permute-start | bytes 3145736 | tf_op jit(solution)/shard_map/ppermute | solution.py:753
  112.1 35.6 %collective-permute-start.20 = (bf16[512,1024]{1,0:T(8,128)(2,1)}, bf16[512,1024]{1,0:T(8,128)(2,1)}, u32[]{:S(2)}, u32[]{:S(2)}) collective-permute-start(bf16[512,1024]{1,0:T(8,128)(2,1)} %collective-permute-done.19.refs_4_.refs_9_.refs_16_.refs_5_), channel_id=1, source_target_pairs={{0,1},{1,0},{2,3},{3,2},{4,5},{5,4},{6,7},{7,6},{8,9},{9,8},{10,11... | collective-permute-start | bytes 3145736 | tf_op jit(solution)/shard_map/ppermute | solution.py:756
  112.5 39.7 %collective-permute-start.18 = (bf16[1024,1024]{1,0:T(8,128)(2,1)S(1)}, bf16[1024,1024]{1,0:T(8,128)(2,1)S(1)}, u32[]{:S(2)}, u32[]{:S(2)}) collective-permute-start(bf16[1024,1024]{1,0:T(8,128)(2,1)S(1)} %bitcast.102), channel_id=1, source_target_pairs={{0,4},{4,0},{8,12},{12,8},{1,5},{5,1},{9,13},{13,9},{2,6},{6,2},{1... | collective-permute-start | bytes 6291464 | tf_op jit(solution)/shard_map/ppermute | solution.py:750
  181.7 76.8 %collective-permute-start.24 = (bf16[416,1024]{1,0:T(8,128)(2,1)}, bf16[416,1024]{1,0:T(8,128)(2,1)}, u32[]{:S(2)}, u32[]{:S(2)}) collective-permute-start(bf16[416,1024]{1,0:T(8,128)(2,1)} %output_forward.5), channel_id=1, source_target_pairs={{0,16},{1,17},{2,18},{3,19},{4,20},{5,21},{6,22},{7,23},{8,24},{9,... | collective-permute-start | bytes 2555912 | tf_op jit(solution)/shard_map/ppermute | solution.py:838
  220.1 110.7 %collective-permute-start.26 = (bf16[416,7168]{1,0:T(8,128)(2,1)}, bf16[416,7168]{1,0:T(8,128)(2,1)}, u32[]{:S(2)}, u32[]{:S(2)}) collective-permute-start(bf16[416,7168]{1,0:T(8,128)(2,1)} %get-tuple-element.167.refs_4_.refs_8_.refs_1_.refs_0_), channel_id=1, source_target_pairs={{0,4},{4,0},{8,12},{12,8},{1,5},{5,1},{9,13},{13,9},{2,6},{6,2},{1... | collective-permute-start | bytes 17891336 | tf_op jit(solution)/shard_map/ppermute | solution.py:750
  257.2 32.5 %collective-permute-start.25 = (bf16[416,1024]{1,0:T(8,128)(2,1)}, bf16[416,1024]{1,0:T(8,128)(2,1)S(1)}, u32[]{:S(2)}, u32[]{:S(2)}) collective-permute-start(bf16[416,1024]{1,0:T(8,128)(2,1)} %get-tuple-element.158), channel_id=1, source_target_pairs={{16,0},{17,1},{18,2},{19,3},{20,4},{21,5},{22,6},{23,7},{24,8},{25... | collective-permute-start | bytes 2555912 | tf_op jit(solution)/shard_map/ppermute | solution.py:838
  258.5 72.3 %collective-permute-start.27 = (bf16[416,9216]{1,0:T(8,128)(2,1)}, bf16[416,9216]{1,0:T(8,128)(2,1)}, u32[]{:S(2)}, u32[]{:S(2)}) collective-permute-start(bf16[416,9216]{1,0:T(8,128)(2,1)} %get-tuple-element.166.refs_5_), channel_id=1, source_target_pairs={{0,4},{4,0},{8,12},{12,8},{1,5},{5,1},{9,13},{13,9},{2,6},{6,2},{1... | collective-permute-start | bytes 23003144 | tf_op jit(solution)/shard_map/ppermute | solution.py:750
  289.6 51.9 %collective-permute-start.28 = (bf16[416,7168]{1,0:T(8,128)(2,1)}, bf16[416,7168]{1,0:T(8,128)(2,1)}, u32[]{:S(2)}, u32[]{:S(2)}) collective-permute-start(bf16[416,7168]{1,0:T(8,128)(2,1)} %get-tuple-element.168.refs_9_.refs_1_.refs_2_.refs_3_), channel_id=1, source_target_pairs={{0,4},{4,0},{8,12},{12,8},{1,5},{5,1},{9,13},{13,9},{2,6},{6,2},{1... | collective-permute-start | bytes 17891336 | tf_op jit(solution)/shard_map/ppermute | solution.py:750
  328.0 27.1 %collective-permute-start.30 = (bf16[416,9216]{1,0:T(8,128)(2,1)}, bf16[416,9216]{1,0:T(8,128)(2,1)}, u32[]{:S(2)}, u32[]{:S(2)}) collective-permute-start(bf16[416,9216]{1,0:T(8,128)(2,1)} %get-tuple-element.170.refs_4_), channel_id=1, source_target_pairs={{0,4},{4,0},{8,12},{12,8},{1,5},{5,1},{9,13},{13,9},{2,6},{6,2},{1... | collective-permute-start | bytes 23003144 | tf_op jit(solution)/shard_map/ppermute | solution.py:750
  401.3 30.9 %collective-permute-start.35 = (bf16[512,1024]{1,0:T(8,128)(2,1)}, bf16[512,1024]{1,0:T(8,128)(2,1)}, u32[]{:S(2)}, u32[]{:S(2)}) collective-permute-start(bf16[512,1024]{1,0:T(8,128)(2,1)} %get-tuple-element.186), channel_id=1, source_target_pairs={{0,8},{4,12},{8,0},{12,4},{1,9},{5,13},{9,1},{13,5},{2,10},{6,14},... | collective-permute-start | bytes 3145736 | tf_op jit(solution)/shard_map/ppermute | solution.py:753
  404.3 30.6 %collective-permute-start.32 = (bf16[416,1024]{1,0:T(8,128)(2,1)}, bf16[416,1024]{1,0:T(8,128)(2,1)}, u32[]{:S(2)}, u32[]{:S(2)}) collective-permute-start(bf16[416,1024]{1,0:T(8,128)(2,1)} %slice.92.refs_8_.refs_0_), channel_id=1, source_target_pairs={{0,4},{4,0},{8,12},{12,8},{1,5},{5,1},{9,13},{13,9},{2,6},{6,2},{1... | collective-permute-start | bytes 2555912 | tf_op jit(solution)/shard_map/ppermute | solution.py:750
  409.9 136.9 %all-reduce.10.cloned.1.call-start = ((), (), s32[]{:S(2)}) async-start(), calls=%async_computation.1 | async-start | bytes 2097152 | tf_op jit(solution)/shard_map/psum | solution.py:795
  441.2 32.8 %collective-permute-start.37 = (bf16[256,2048]{1,0:T(8,128)(2,1)}, bf16[256,2048]{1,0:T(8,128)(2,1)}, u32[]{:S(2)}, u32[]{:S(2)}) collective-permute-start(bf16[256,2048]{1,0:T(8,128)(2,1)} %get-tuple-element.194), channel_id=1, source_target_pairs={{0,8},{4,12},{8,0},{12,4},{1,9},{5,13},{9,1},{13,5},{2,10},{6,14},... | collective-permute-start | bytes 3145736 | tf_op jit(solution)/shard_map/ppermute | solution.py:753
  472.0 74.8 %collective-permute-start.41 = (bf16[256,1024]{1,0:T(8,128)(2,1)}, bf16[256,1024]{1,0:T(8,128)(2,1)}, u32[]{:S(2)}, u32[]{:S(2)}) collective-permute-start(bf16[256,1024]{1,0:T(8,128)(2,1)} %get-tuple-element.209), channel_id=1, source_target_pairs={{0,8},{4,12},{8,0},{12,4},{1,9},{5,13},{9,1},{13,5},{2,10},{6,14},... | collective-permute-start | bytes 1572872 | tf_op jit(solution)/shard_map/ppermute | solution.py:753
  472.7 25.7 %collective-permute-start.38 = (bf16[256,1024]{1,0:T(8,128)(2,1)}, bf16[256,1024]{1,0:T(8,128)(2,1)}, u32[]{:S(2)}, u32[]{:S(2)}) collective-permute-start(bf16[256,1024]{1,0:T(8,128)(2,1)} %get-tuple-element.198), channel_id=1, source_target_pairs={{0,8},{4,12},{8,0},{12,4},{1,9},{5,13},{9,1},{13,5},{2,10},{6,14},... | collective-permute-start | bytes 1572872 | tf_op jit(solution)/shard_map/ppermute | solution.py:753
  477.0 38.1 %collective-permute-start.39 = (bf16[256,2048]{1,0:T(8,128)(2,1)}, bf16[256,2048]{1,0:T(8,128)(2,1)}, u32[]{:S(2)}, u32[]{:S(2)}) collective-permute-start(bf16[256,2048]{1,0:T(8,128)(2,1)} %add_convert_fusion.2), channel_id=1, source_target_pairs={{0,1},{3,2},{4,5},{7,6},{8,9},{11,10},{12,13},{15,14},{16,17},{19,... | collective-permute-start | bytes 3145736 | tf_op jit(solution)/shard_map/ppermute | solution.py:799
  485.5 38.7 %collective-permute-start.40 = (bf16[256,1024]{1,0:T(8,128)(2,1)}, bf16[256,1024]{1,0:T(8,128)(2,1)}, u32[]{:S(2)}, u32[]{:S(2)}) collective-permute-start(bf16[256,1024]{1,0:T(8,128)(2,1)} %get-tuple-element.206), channel_id=1, source_target_pairs={{0,8},{4,12},{8,0},{12,4},{1,9},{5,13},{9,1},{13,5},{2,10},{6,14},... | collective-permute-start | bytes 1572872 | tf_op jit(solution)/shard_map/ppermute | solution.py:753
  499.6 57.8 %collective-permute-start.42 = (bf16[256,1024]{1,0:T(8,128)(2,1)S(1)}, bf16[256,1024]{1,0:T(8,128)(2,1)}, u32[]{:S(2)}, u32[]{:S(2)}) collective-permute-start(bf16[256,1024]{1,0:T(8,128)(2,1)S(1)} %add_convert_fusion.22), channel_id=1, source_target_pairs={{0,1},{3,2},{4,5},{7,6},{8,9},{11,10},{12,13},{15,14},{16,17},{19,... | collective-permute-start | bytes 1572872 | tf_op jit(solution)/shard_map/ppermute | solution.py:799
  502.9 60.2 %collective-permute-start.45 = (bf16[256,1024]{1,0:T(8,128)(2,1)}, bf16[256,1024]{1,0:T(8,128)(2,1)}, u32[]{:S(2)}, u32[]{:S(2)}) collective-permute-start(bf16[256,1024]{1,0:T(8,128)(2,1)} %get-tuple-element.214), channel_id=1, source_target_pairs={{0,8},{4,12},{8,0},{12,4},{1,9},{5,13},{9,1},{13,5},{2,10},{6,14},... | collective-permute-start | bytes 1572872 | tf_op jit(solution)/shard_map/ppermute | solution.py:753
  517.1 44.9 %collective-permute-start.44 = (bf16[256,2048]{1,0:T(8,128)(2,1)S(1)}, bf16[256,2048]{1,0:T(8,128)(2,1)S(1)}, u32[]{:S(2)}, u32[]{:S(2)}) collective-permute-start(bf16[256,2048]{1,0:T(8,128)(2,1)S(1)} %add_convert_fusion.1), channel_id=1, source_target_pairs={{1,2},{2,1},{5,6},{6,5},{9,10},{10,9},{13,14},{14,13},{17,18},{18,... | collective-permute-start | bytes 3145736 | tf_op jit(solution)/shard_map/ppermute | solution.py:802
  525.6 34.5 %collective-permute-start.43 = (bf16[256,1024]{1,0:T(8,128)(2,1)S(1)}, bf16[256,1024]{1,0:T(8,128)(2,1)}, u32[]{:S(2)}, u32[]{:S(2)}) collective-permute-start(bf16[256,1024]{1,0:T(8,128)(2,1)S(1)} %add_convert_fusion.21), channel_id=1, source_target_pairs={{0,1},{3,2},{4,5},{7,6},{8,9},{11,10},{12,13},{15,14},{16,17},{19,... | collective-permute-start | bytes 1572872 | tf_op jit(solution)/shard_map/ppermute | solution.py:799
  560.1 27.3 %collective-permute-start.51 = (bf16[272,1024]{1,0:T(8,128)(2,1)S(1)}, bf16[272,1024]{1,0:T(8,128)(2,1)S(1)}, u32[]{:S(2)}, u32[]{:S(2)}) collective-permute-start(bf16[272,1024]{1,0:T(8,128)(2,1)S(1)} %pad_maximum_fusion.1), channel_id=1, source_target_pairs={{0,8},{4,12},{8,0},{12,4},{1,9},{5,13},{9,1},{13,5},{2,10},{6,14},... | collective-permute-start | bytes 1671176 | tf_op jit(solution)/shard_map/ppermute | solution.py:753
  565.2 38.2 %collective-permute-start.53 = (bf16[256,2048]{1,0:T(8,128)(2,1)S(1)}, bf16[256,2048]{1,0:T(8,128)(2,1)S(1)}, u32[]{:S(2)}, u32[]{:S(2)}) collective-permute-start(bf16[256,2048]{1,0:T(8,128)(2,1)S(1)} %add_convert_fusion), channel_id=1, source_target_pairs={{1,0},{2,3},{5,4},{6,7},{9,8},{10,11},{13,12},{14,15},{17,16},{18,... | collective-permute-start | bytes 3145736 | tf_op jit(solution)/shard_map/ppermute | solution.py:805
  572.6 50.9 %collective-permute-start.56 = (bf16[256,1024]{1,0:T(8,128)(2,1)S(1)}, bf16[256,1024]{1,0:T(8,128)(2,1)S(1)}, u32[]{:S(2)}, u32[]{:S(2)}) collective-permute-start(bf16[256,1024]{1,0:T(8,128)(2,1)S(1)} %add_convert_fusion.14), channel_id=1, source_target_pairs={{1,2},{2,1},{5,6},{6,5},{9,10},{10,9},{13,14},{14,13},{17,18},{18,... | collective-permute-start | bytes 1572872 | tf_op jit(solution)/shard_map/ppermute | solution.py:802
  586.1 39.0 %collective-permute-start.57 = (bf16[256,1024]{1,0:T(8,128)(2,1)S(1)}, bf16[256,1024]{1,0:T(8,128)(2,1)S(1)}, u32[]{:S(2)}, u32[]{:S(2)}) collective-permute-start(bf16[256,1024]{1,0:T(8,128)(2,1)S(1)} %add_convert_fusion.13), channel_id=1, source_target_pairs={{1,0},{2,3},{5,4},{6,7},{9,8},{10,11},{13,12},{14,15},{17,16},{18,... | collective-permute-start | bytes 1572872 | tf_op jit(solution)/shard_map/ppermute | solution.py:805
  587.4 35.9 %collective-permute-start.55 = (bf16[256,1024]{1,0:T(8,128)(2,1)S(1)}, bf16[256,1024]{1,0:T(8,128)(2,1)S(1)}, u32[]{:S(2)}, u32[]{:S(2)}) collective-permute-start(bf16[256,1024]{1,0:T(8,128)(2,1)S(1)} %add_convert_fusion.15), channel_id=1, source_target_pairs={{0,1},{3,2},{4,5},{7,6},{8,9},{11,10},{12,13},{15,14},{16,17},{19,... | collective-permute-start | bytes 1572872 | tf_op jit(solution)/shard_map/ppermute | solution.py:799
  (88 other events, 1083.3 us)
Sparse Core Ops, SparseCore 0:
  410.0 53.2 all-reduce.7
  468.4 78.3 all-reduce.9

commit v5 on v4

--- a/solution.py
+++ b/solution.py
@@ -12,6 +12,7 @@
 NEGATIVE = -1e30
 F32 = jnp.float32
 BF16 = jnp.bfloat16
+LIGHT, HEAVY = 1.0 / 64, 16.0
 VMEM_LIMIT = 58 * 2**20
 ROOT_HALF = 0.7071067811865476
 ROOT_TAU = 0.3989422804014327
@@ -45,7 +46,7 @@
     return scale * (scaled - mean - unit * along)
 
 
-def call(body, name, operands, specs, outs, scratch, flops, weight=1.0 / 64):
+def call(body, name, operands, specs, outs, scratch, flops, weight=LIGHT):
     moved = sum(o.size * o.dtype.itemsize for o in operands)
     out_shape = [jax.ShapeDtypeStruct(shape, dtype) for shape, dtype in outs]
     moved += sum(o.size * o.dtype.itemsize for o in out_shape)
@@ -65,13 +66,17 @@
     return [piece for group in groups for piece in group]
 
 
-def start_pieces(pieces, info, first, target, sems, slot, columns):
+def start_pieces(pieces, info, first, target, sems, slot, columns, shift=0):
+    begin, size = columns
+    columns = pl.ds(begin, size)
     copies = []
     for index, piece in enumerate(pieces):
         rows = piece.shape[0]
         where = pl.multiple_of(info[first + index] * rows, rows)
         copy = pltpu.make_async_copy(
-            piece.at[:, columns], target.at[pl.ds(where, rows), columns], sems.at[slot, index]
+            piece.at[:, pl.ds(begin + shift, size)],
+            target.at[pl.ds(where, rows), columns],
+            sems.at[slot, index],
         )
         copy.start()
         copies.append(copy)
@@ -196,17 +201,17 @@
 
 
 def forward(
-    lower, upper, mixed_in, qkv, out, expand, params, meta, count, length, weight=1.0 / 64
+    lower, upper, mixed_in, qkv, wide, params, meta, count, length, weight=LIGHT
 ):
     rows, width = lower.shape
     space = rows // count
     pair = 2 * width // HEADS
-    attend, feed = qkv is not None, expand is not None
+    attend, feed = qkv is not None, wide is not None
     both = attend and feed
-    parts = len(qkv if attend else expand)
-    many = len(flat(qkv if attend else expand))
+    parts = len(qkv if attend else wide)
+    many = len(flat(qkv if attend else wide))
     spots = parts + 1 + count
-    inner = expand[0][0].shape[1] if feed else 0
+    inner = wide[0][0].shape[1] - width if feed else 0
     blocks = inner // width
     same = lower is upper
 
@@ -237,7 +242,7 @@
                 norm, packed, logs = refs.pop(0), refs.pop(0), None
             weight = lists.pop(0)
             loads = [
-                start_pieces(weight, info, spots, full, a_sem, block, pl.ds(block * width, width))
+                start_pieces(weight, info, spots, full, a_sem, block, (block * width, width))
                 for block in range(3)
             ]
         if feed:
@@ -246,9 +251,9 @@
                 mixed, second, slope = refs.pop(0), refs.pop(0), None
                 extra = pltpu.make_async_copy(arrived, mixed, x_sem.at[1])
                 extra.start()
-            first_load = start_pieces(lists[0], info, spots, full_out, o_sem, 0, pl.ds(0, width))
+            first_load = start_pieces(lists[0], info, spots, full_out, o_sem, 0, (0, width))
             inner_loads = [
-                start_pieces(lists[1], info, spots, full_in, w_sem, block, pl.ds(block * width, width))
+                start_pieces(lists[1], info, spots, full_in, w_sem, block, (block * width, width), width)
                 for block in range(blocks)
             ]
         take.wait()
@@ -304,7 +309,7 @@
         outs = [((rows, inner + 3 * width), BF16), outs[1], outs[3], outs[4], outs[7]]
     else:
         outs = [outs[2]] if attend else outs[:2]
-    weights = (flat(qkv) if attend else []) + (flat(out) + flat(expand) if feed else [])
+    weights = (flat(qkv) if attend else []) + (2 * flat(wide) if feed else [])
     return call(
         body,
         "forward" + "_attend" * attend + "_feed" * feed,
@@ -317,7 +322,7 @@
     )
 
 
-def output_forward(middle, active, pieces, params, meta, count, weight=1.0 / 64):
+def output_forward(middle, active, pieces, params, meta, count, weight=LIGHT):
     rows, width = middle.shape
     inner = sum(piece.shape[0] for piece in flat(pieces))
     space = rows // count
@@ -337,7 +342,7 @@
         ]
         copies[0].start()
         loads = [
-            start_pieces(reduce, info, spots, full, w_sem, block, pl.ds(block * part_width, part_width))
+            start_pieces(reduce, info, spots, full, w_sem, block, (block * part_width, part_width))
             for block in range(blocks)
         ]
         copies[1].start()
@@ -504,8 +509,8 @@
 
 
 def backward(
-    start, lower, upper, kept_low, kept_up, reduce, expand, out, qkv, params, meta, count, length,
-    mixed_at, weight=1.0 / 64,
+    start, lower, upper, kept_low, kept_up, reduce, wide, qkv, params, meta, count, length,
+    mixed_at, weight=LIGHT,
 ):
     feed, attend = reduce is not None, qkv is not None
     rows, width = start[0].shape
@@ -514,7 +519,7 @@
     parts = len(reduce if feed else qkv)
     many = len(flat(reduce if feed else qkv))
     spots = parts + 1 + count
-    inner = expand[0][0].shape[1] if feed else 0
+    inner = wide[0][0].shape[1] - width if feed else 0
     deep = inner // parts
     both = feed and attend
     choices = []
@@ -541,9 +546,12 @@
         vec, info = refs.pop(0), refs.pop(0)
         section = info[parts]
         if feed:
-            right, feed_sums, inner_sums = (refs.pop(0) for _ in range(3))
-            hidden = right.at[:, pl.ds(0, inner)]
-            branch = right.at[:, pl.ds(inner, width)]
+            if both:
+                right = refs.pop(0)
+                hidden, branch = right.at[:, pl.ds(0, inner)], right.at[:, pl.ds(inner, width)]
+            else:
+                hidden, branch = refs.pop(0), refs.pop(0)
+            feed_sums, inner_sums = refs.pop(0), refs.pop(0)
             mid_grad = None if both else refs.pop(0)
         if attend:
             grads, result, sums = (refs.pop(0) for _ in range(3)) if not both else (None, refs.pop(0), refs.pop(0))
@@ -562,10 +570,10 @@
             begin = pairs.pop(2) if start[0] is not start[1] else (firsts[0], firsts[0])
             take = start_chosen(section, *begin, grad, x_sem.at[0])
             for_slope = start_chosen(section, *pairs.pop(0), slope, x_sem.at[1])
-            every = start_pieces(lists.pop(0), info, spots, full_out, o_sem, 0, pl.ds(0, width))
+            every = start_pieces(lists.pop(0), info, spots, full_out, o_sem, 0, (0, width))
             first_load = [[every.pop(0) for _ in group] for group in reduce]
             for_middle = start_chosen(section, *pairs.pop(0), middle, x_sem.at[2])
-            load = start_pieces(lists.pop(0), info, spots, full, w_sem, 0, pl.ds(0, inner))
+            load = start_pieces(lists.pop(0), info, spots, full, w_sem, 0, (0, inner), width)
         if attend:
             x, packed, mixed, logs, down, normal, stage, full_o, full_q, p_sem, q_sem = (
                 refs.pop(0) for _ in range(11)
@@ -578,14 +586,14 @@
                 ]
                 for given in givens:
                     given.start()
-            project_load = start_pieces(lists.pop(0), info, spots, full_o, p_sem, 0, pl.ds(0, width))
+            project_load = start_pieces(lists.pop(0), info, spots, full_o, p_sem, 0, (0, width))
             sames = [one is two for one, two in pairs]
             pairs[1] = tuple(one.at[:, pl.ds(mixed_at, width)] for one in pairs[1])
             takes = [
                 start_chosen(section, *pairs[index], target, x_sem.at[3 + index], sames[index])
                 for index, target in ((1, mixed), (0, packed), (2, logs), (3, x))
             ]
-            last_load = start_pieces(lists.pop(0), info, spots, full_q, q_sem, 0, pl.ds(0, 3 * width))
+            last_load = start_pieces(lists.pop(0), info, spots, full_q, q_sem, 0, (0, 3 * width))
             if not feed:
                 wait_all(givens)
         if feed:
@@ -605,8 +613,8 @@
     scratch = [pltpu.VMEM((4, 8, width), F32), pltpu.SemaphoreType.DMA((7,))]
     flops = 0
     if feed:
+        outs += [((rows, inner + 5 * width), BF16)] if both else [((rows, inner), BF16), ((rows, width), BF16)]
         outs += [
-            ((rows, inner + (5 if both else 1) * width), BF16),
             ((8, width), F32),
             ((1, inner), F32),
         ]
@@ -643,8 +651,8 @@
         if not feed:
             scratch += [pltpu.VMEM((rows, width), BF16), pltpu.VMEM((rows, width), F32)]
         flops += 2 * rows * width * (4 * width + 5 * space)
-    weights = (flat(reduce) + flat(expand) if feed else []) + (
-        flat(out) + flat(qkv) if attend else []
+    weights = (flat(reduce) + flat(wide) if feed else []) + (
+        flat(wide) + flat(qkv) if attend else []
     )
     return call(
         body,
@@ -659,7 +667,7 @@
 
 
 def weight_gradient(
-    lefts, rights, meta, parts, blocks, quarter, rows_of, columns_of, name, weight=1.0 / 64
+    lefts, rights, meta, parts, blocks, quarter, rows_of, columns_of, name, weight=LIGHT
 ):
     terms = len(lefts)
     first_row, height = rows_of
@@ -738,7 +746,6 @@
     blocks = (0, 2)
 
     def __init__(self):
-        self.begun = 0
         self.group = lax.axis_index("group")
         self.place = lax.axis_index("replica")
         self.order = [self.group ^ part for part in range(4)]
@@ -755,18 +762,24 @@
     def beside(self, block):
         return lax.ppermute(block, "replica", [(i, i ^ 1) for i in range(4)])
 
-    def gather(self, small, blocks):
-        far, halves, sibling = self.across(small), [], []
+    def gather_small(self, block):
+        near, far = self.core(block), self.across(block)
+        return [block, near, far, self.core(far)]
+
+    def gather(self, blocks, prepare):
         odd = self.place % 2
+        asked = [
+            lax.dynamic_slice_in_dim(block, odd * (block.shape[0] // 2), block.shape[0] // 2)
+            for block in blocks
+        ]
+        halves, sibling = [], []
         for index, block in enumerate(blocks):
-            rows = block.shape[0] // 2
-            half = lax.dynamic_slice_in_dim(block, odd * rows, rows)
-            half = after(half, far if index < 2 else halves[index - 2])
-            halves.append(self.across(half))
+            halves.append(self.across(after(asked[index], *halves[: max(index - 1, 0)])))
             sibling.append(self.core(after(block, sibling[-1]) if index else block))
         others = []
-        for half in halves:
-            others.append(self.beside(after(half, others[-1]) if others else half))
+        tokens = prepare(halves[0]) + asked[2:]
+        for index, half in enumerate(halves):
+            others.append(self.beside(after(half, *others[-1:], *(tokens if index == 1 else []))))
 
         def pieces(index, *tokens):
             one, two = (after(half, *tokens) for half in (halves[index], others[index]))
@@ -777,25 +790,15 @@
                 [self.core(one), self.core(two)],
             ]
 
-        near = self.core(small)
-        return [small, near, far, self.core(far)], [
-            partial(pieces, index) for index in range(len(blocks))
-        ]
+        return [partial(pieces, index) for index in range(len(blocks))]
 
     def shared(self, block):
         return [block, self.core(block)]
 
-    def total(self, blocks, own):
+    def total(self, blocks):
         passed = self.across(blocks[1])
         token = yield
         mine = added(after(blocks[0], token), passed)
-        if not own:
-            turn = [(place + self.begun) % 4 for place in range(4)]
-            self.begun += 1
-            whole = lax.psum(mine, "replica", axis_index_groups=[turn])
-            token = yield mine
-            yield after(whole, token)
-            return
         inward = lax.ppermute(mine, "replica", [(0, 1), (3, 2)])
         token = yield mine
         joined = added(after(mine, token), inward)
@@ -814,18 +817,19 @@
         self.blocks = tuple(range(self.parts))
         self.order = self.spots = [jnp.int32(part) for part in range(self.parts)]
 
-    def gather(self, small, blocks):
-        def pieces(block):
-            whole = lax.all_gather(block, "group", axis=0)
-            return [whole[part] for part in range(self.parts)]
-
-        found = [[[piece] for piece in pieces(block)] for block in blocks]
-        return pieces(small), [lambda *tokens, groups=groups: groups for groups in found]
+    def gather_small(self, block):
+        whole = lax.all_gather(block, "group", axis=0)
+        return [whole[part] for part in range(self.parts)]
+
+    def gather(self, blocks, prepare):
+        prepare(blocks[0])
+        found = [[[piece] for piece in self.gather_small(block)] for block in blocks]
+        return [lambda *tokens, groups=groups: groups for groups in found]
 
     def shared(self, block):
         return [block]
 
-    def total(self, blocks, own):
+    def total(self, blocks):
         yield
         mine = lax.psum_scatter(jnp.stack(blocks), "group", scatter_dimension=0)
         yield mine
@@ -859,8 +863,8 @@
     def ran(self, value):
         self.token = value
 
-    def add(self, name, blocks, own):
-        self.sums[name] = self.net.total(blocks, own)
+    def add(self, name, blocks):
+        self.sums[name] = self.net.total(blocks)
         next(self.sums[name])
 
     def step(self, *names):
@@ -907,40 +911,56 @@
     def images_of(array):
         return array.reshape(slots, space, width)[:, :length]
 
-    inputs, targets = rows_of(images), rows_of(cotangent)
     small = jnp.concatenate([norm_gains[0], biases[0], expand_bias[0].reshape(-1, share)])
-    vectors, (qkv, out, expand, reduce) = net.gather(
-        small, [qkv_weight[0], out_weight[0], expand_weight[0], reduce_weight[0]]
-    )
-    vectors = in_order(vectors, net.order)
+    slot = jnp.arange(slots, dtype=jnp.int32)
+    alive = [(slot < counts[batch, 0]).astype(jnp.int32) for batch in batches]
+    head = jnp.stack(net.order + [section]).astype(jnp.int32)
+
+    spots = jnp.stack(net.spots).astype(jnp.int32)
+
+    def meta(living):
+        return jnp.concatenate([head, living, spots])
+
+    infos = [meta(alive[batch]) for batch in batches]
+    pieces = net.gather_small(small)
+    vectors = in_order(pieces, net.order)
     top = vectors[:, :8].transpose(1, 0, 2).reshape(8, width)
     bottom = vectors[:, 8:].reshape(-1, width)
     params = jnp.concatenate([top, bottom]).astype(F32)
     slot = jnp.arange(slots, dtype=jnp.int32)
     alive = [(slot < counts[batch, 0]).astype(jnp.int32) for batch in batches]
     head = jnp.stack(net.order + [section]).astype(jnp.int32)
-
     spots = jnp.stack(net.spots).astype(jnp.int32)
 
     def meta(living):
         return jnp.concatenate([head, living, spots])
 
     infos = [meta(alive[batch]) for batch in batches]
-
-    qkv = qkv(params, *inputs, *targets)
+    inputs, targets = [], []
+
+    def prepare(token):
+        inputs.extend(rows_of(after(images, token)))
+        targets.extend(rows_of(after(cotangent, token)))
+        return [params, *inputs, *targets, *infos]
+
+    qkv, wide, reduce = net.gather(
+        [qkv_weight[0], jnp.concatenate([out_weight[0], expand_weight[0]], axis=1), reduce_weight[0]],
+        prepare,
+    )
+
+    qkv = qkv()
     attended = []
     for batch in batches:
         start = inputs[batch] if batch == 0 else after(inputs[batch], attended[-1][0])
         attended.append(
-            forward(start, start, None, qkv, None, None, params, infos[batch], slots, length)
+            forward(start, start, None, qkv, None, params, infos[batch], slots, length)
         )
-    out = out(attended[-1][0])
-    expand = expand(out[-1][0])
+    wide = wide(attended[-1][0])
     fed = []
     for batch in batches:
         start = inputs[batch] if batch == 0 else after(inputs[batch], fed[-1][0])
         fed.append(
-            forward(start, start, attended[batch][0], None, out, expand, params, infos[batch], slots, length)
+            forward(start, start, attended[batch][0], None, wide, params, infos[batch], slots, length)
         )
     reduce = reduce(fed[-1][0])
     early, incoming = [], []
@@ -951,7 +971,7 @@
         early.append(output_forward(middle, active, reduce, params, infos[batch], slots))
         incoming.append(shifted(early[batch], 1))
 
-    inner = expand[0][0].shape[1]
+    inner = wide[0][0].shape[1] - width
     mixed_at = inner + width
     kept, lefts, rights, results = [], [], [], []
     sums_a, sums_b, sums_c, returning = [], [], [], []
@@ -959,7 +979,7 @@
     for batch in batches:
         start = after(incoming[batch], token)
         left, packed, logs, middle, slope = forward(
-            inputs[batch], start, None, qkv, out, expand, params, infos[batch], slots, length, 8.0
+            inputs[batch], start, None, qkv, wide, params, infos[batch], slots, length, 8.0
         )
         kept.append((slope, middle, packed, left, logs))
         lefts.append(net.shared(left))
@@ -972,7 +992,7 @@
             lower = inputs[batch - 1]
             chosen = meta(jnp.where(first, alive[batch - 1], alive[batch]))
         right, some, more, result, rest = backward(
-            pair, lower, incoming[batch], sides[0], sides[1], reduce, expand, out, qkv, params, chosen,
+            pair, lower, incoming[batch], sides[0], sides[1], reduce, wide, qkv, params, chosen,
             slots, length, mixed_at, 8.0,
         )
         token = result
@@ -996,7 +1016,7 @@
     masked = net.shared(jnp.where(living, arrived, jnp.zeros_like(arrived)))
     many = len(masked)
 
-    def gradient(name, left_at, final, final_at, right_at, quarter, rows, columns, own, weight=1.0 / 64):
+    def gradient(name, left_at, final, final_at, right_at, quarter, rows, columns, weight=LIGHT):
         left = [lefts[batch][side] for batch in batches for side in range(many)]
         right = []
         for batch in batches:
@@ -1011,50 +1031,52 @@
         run.ran(blocks[0])
         return blocks
 
-    def summed(name, *rest):
-        run.add(name, gradient(name, *rest), rest[7])
-
-    def reduce_part(index, own, weight=1.0 / 64):
-        deep = inner // parts
-        step = deep // 2
-        summed(
-            f"reduce{index}", 0, masked, 0, inner + width, deep, (index * step, step), (0, width), own,
-            weight,
+    def reduce_part(index, weight=LIGHT):
+        step = inner // parts // 2
+        blocks = gradient(
+            "reduce", 0, masked, 0, inner + width, inner // parts, (index * step, step), (0, width), weight
         )
-
-    reduce_part(0, False)
+        run.add(f"reduce{index}", blocks)
+
+    def expand_part(index):
+        step = inner // 2
+        blocks = gradient("expand", inner, finals, 0, 0, share, (0, share), (index * step, step))
+        run.add(f"expand{index}", blocks)
+
+    def qkv_part(index):
+        step = 3 * width // 2
+        at = inner + 2 * width
+        run.add(f"qkv{index}", gradient("qkv", at, grads, 0, at, share, (0, share), (index * step, step)))
+
+    reduce_part(0)
     start = run.now(arrived)
-    final, some, more, mid = backward(
-        (start, start), None, None, kept[last], kept[last], reduce, expand, None, None, params,
-        infos[last], slots, length, mixed_at,
+    final, branch, some, more, mid = backward(
+        (start, start), None, None, kept[last], kept[last], reduce, wide, None, params, infos[last],
+        slots, length, mixed_at,
     )
     run.ran(final)
-    branch = final[:, inner:]
-    finals, branches = net.shared(final[:, :inner]), net.shared(branch)
+    finals, branches = net.shared(final), net.shared(branch)
     sums_a.append(some)
     sums_b.append(more)
     run.step("reduce0")
-    reduce_part(1, False, 16.0)
-
-    def expand_part(index, cut, own):
-        begin, step = cut
-        summed(f"expand{index}", inner, finals, 0, 0, share, (0, share), (begin, step), own)
-
-    quarter = inner // 4
-    expand_part(0, (0, 2 * quarter), True)
-    expand_part(1, (2 * quarter, quarter), True)
-    expand_part(2, (3 * quarter, quarter), True)
-    run.step("reduce1")
-    summed("project", mixed_at, branches, 0, inner, share, (0, share), (0, width), True)
+    reduce_part(1, HEAVY)
+    expand_part(0)
+    expand_part(1)
+    run.step("reduce1", "reduce0")
     grads, result, rest = backward(
-        (run.now(branch), mid), inputs[last], inputs[last], kept[last], kept[last], None, None, out, qkv,
-        params, infos[last], slots, length, mixed_at, 16.0,
+        (run.now(after(branch, *branches[1:])), mid), inputs[last], inputs[last], kept[last], kept[last], None, wide, qkv,
+        params, infos[last], slots, length, mixed_at, HEAVY,
     )
     run.ran(result)
     grads = net.shared(grads)
     results.append(result)
     sums_c.append(rest)
-    run.step("expand0")
+    run.step("expand0", "reduce1", "reduce0")
+    qkv_part(0)
+    run.step("expand1", "expand0", "reduce1", "reduce0")
+    qkv_part(1)
+
+    run.step("qkv0", "expand1", "expand0", "reduce1", "qkv1", "qkv0")
 
     def over_batches(values):
         return sum(jnp.where(first, values[batch + 1], values[batch]) for batch in batches)
@@ -1063,49 +1085,33 @@
     rows = jnp.concatenate([rest[0:1], some[0:1], rest[1:2], some[1:2], rest[2:4], some[2:4]])
     rows = rows.reshape(8, parts, share).transpose(1, 0, 2)
     rows = jnp.concatenate([rows, more.reshape(parts, -1, share)], axis=1)
-    rows = sum(net.shared(rows))
+    rows = sum(net.shared(run.now(rows)))
     rows = jnp.stack(
         [lax.dynamic_index_in_dim(rows, net.order[block], 0, keepdims=False) for block in net.blocks]
     )
-    count, step = rows.shape[1], width // 2
+    count = rows.shape[1]
     rows = rows.reshape(len(net.blocks), -1)
-    rows = jnp.pad(rows, ((0, 0), (0, -rows.shape[1] % (32 * step)))).reshape(len(net.blocks), -1, 2 * step)
-
-    def qkv_part(index):
-        begin, breadth = ((0, 2 * step), (2 * step, 2 * step), (4 * step, 2 * step))[index]
-        return gradient(
-            f"qkv{index}", inner + 2 * width, grads, 0, inner + 2 * width, share, (0, share),
-            (begin, breadth), True,
-        )
-
-    run.add("qkv0", qkv_part(0), True)
-    run.step("expand1")
-    run.add("qkv1", qkv_part(1), True)
-    run.step("expand0", "reduce0")
-    blocks = qkv_part(2)
-    run.add("qkv2", [jnp.concatenate([one, two]) for one, two in zip(blocks, rows.astype(BF16))], True)
-    run.step(
-        "expand2", "reduce1", "project", "expand1", "expand2", "expand0", "qkv0", "expand1", "qkv1", "project",
-        "expand2", "qkv2", "qkv0", "expand0", "expand1", "qkv1", "project", "expand2", "qkv0", "qkv2", "project",
-        "qkv1", "qkv0", "qkv2", "qkv1", "qkv2",
-    )
+    rows = jnp.pad(rows, ((0, 0), (0, -rows.shape[1] % (16 * width)))).reshape(len(net.blocks), -1, width)
+    blocks = gradient("project", mixed_at, branches, 0, inner, share, (0, share), (0, width))
+    run.add("project", [jnp.concatenate([one, two]) for one, two in zip(blocks, rows.astype(BF16))])
+    run.step("expand1", "expand0", "qkv1", "project", "qkv0")
+    outputs = [
+        images_of(jnp.where(first, run.now(low), up))
+        for low, up in zip(early + results[1:], late + results[:-1])
+    ]
+    run.step("expand1", "qkv1", "project", "qkv0", "project", "qkv1", "project")
     weights = {name: run.finish(name) for name in run.sums}
-    vector = weights["qkv2"][share:].reshape(-1)[: count * share].reshape(count, share).astype(F32)
-
-    def chosen(lowers, uppers):
-        return jnp.stack(
-            [images_of(jnp.where(first, low, up)) for low, up in zip(lowers, uppers)]
-        )[None]
+    vector = weights["project"][share:].reshape(-1)[: count * share].reshape(count, share).astype(F32)
 
     def joined(axis, *names):
         return jnp.concatenate([weights[name] for name in names], axis=axis).astype(F32)[None]
 
     return (
-        chosen(early, late),
-        chosen(results[1:], results[:-1]),
-        jnp.concatenate([weights["qkv0"], weights["qkv1"], weights["qkv2"][:share]], axis=1).astype(F32)[None],
-        weights["project"].astype(F32)[None],
-        joined(1, "expand0", "expand1", "expand2"),
+        jnp.stack(outputs[:micro])[None],
+        jnp.stack(outputs[micro:])[None],
+        joined(1, "qkv0", "qkv1"),
+        weights["project"][:share].astype(F32)[None],
+        joined(1, "expand0", "expand1"),
         joined(0, "reduce0", "reduce1"),
         vector[None, 0:2],
         vector[None, 2:8],

time: 698 us -> 651 us (0.933)
  waiting for transfers between devices: 144 us -> 105 us
  starting transfers between devices: 89.5 us -> 106 us
  other arithmetic: 46 us -> 60 us
  between operations: 15.7 us -> 2.17 us
  local copies, waits for them, and re-layouts: 41.8 us -> 30.5 us
  Pallas kernels: 348 us -> 340 us
    ppermute x7, waiting for transfers between devices: 60.7 us -> 33.3 us  [total(): outward = lax.ppermute(summed, 'replica', [(1, 0), (2, 3)])]
    ppermute x7, starting transfers between devices: 40.5 us -> 57.5 us  [total(): inward = lax.ppermute(mine, 'replica', [(0, 1), (3, 2)])]
    ppermute x14 -> x11, waiting for transfers between devices: 38.9 us -> 51.2 us  [across(): return lax.ppermute(block, 'group', [(i, i ^ 2) for i in range(4)])]
    psum x2 -> x0, waiting for transfers between devices: 12.2 us -> none  [total(): whole = lax.psum(mine, 'replica', axis_index_groups=[turn])]
    pallas_call x23 -> x21, Pallas kernels: 348 us -> 340 us  [call(): pl.pallas_call(body, out_shape=out_shape, in_specs=specs, out_specs=[VMEM...]
    ppermute x7, waiting for transfers between devices: 9.68 us -> 1.56 us  [total(): inward = lax.ppermute(mine, 'replica', [(0, 1), (3, 2)])]
    convert_element_type x23 -> x21, other arithmetic: 20.7 us -> 27 us  [added(): return total.astype(values[0].dtype)]
    ppermute x14 -> x11, starting transfers between devices: 16.3 us -> 11.8 us  [across(): return lax.ppermute(block, 'group', [(i, i ^ 2) for i in range(4)])]
  transfers between devices with their start and end apart: 68 -> 59, of which waited for: 23 -> 21; matrix products, arithmetic and copies ran while one was open for 11% -> 11% of each run, Pallas kernels for 48% -> 46%
where the time goes in v5:
time: 651 us; the launch traced here: 643 us
  Pallas kernels  340 us (52%)
  starting transfers between devices  106 us (16%)
  waiting for transfers between devices  105 us (16%)
  other arithmetic  60 us (9%)
  local copies, waits for them, and re-layouts  30.5 us (5%)
    pallas_call x21, Pallas kernels, call(): pl.pallas_call(body, out_shape=out_shape, in_specs=specs, out_specs=[VMEM...  340 us
    ppermute x7, starting transfers between devices, total(): inward = lax.ppermute(mine, 'replica', [(0, 1), (3, 2)])  57.5 us
    ppermute x11, waiting for transfers between devices, across(): return lax.ppermute(block, 'group', [(i, i ^ 2) for i in range(4)])  51.2 us
    ppermute x7, waiting for transfers between devices, total(): outward = lax.ppermute(summed, 'replica', [(1, 0), (2, 3)])  33.3 us
    convert_element_type x21, other arithmetic, added(): return total.astype(values[0].dtype)  27 us
    ppermute x20, waiting for transfers between devices, core(): return lax.ppermute(block, 'group', [(i, i ^ 1) for i in range(4)])  14 us
    unnamed x102, local copies, waits for them, and re-layouts  14 us
  transfers between devices with their start and end apart: 59, of which 21 were waited for; matrix products, arithmetic and copies ran while one was open for 11% of the time, Pallas kernels for 46%

profile of v5, /device:TPU:0, one launch (start us, length us, event | category | flops | bytes accessed | tf_op | source)
XLA Modules:
  0.0 643.0 jit_solution(13995502584934590981)
XLA Ops:
  18.0 9.8 %collective-permute-done.refs_3_.refs_4_.refs_27_.refs_34_.refs_14_ = bf16[128,3072]{1,0:T(8,128)(2,1)S(1)} collective-permute-done((bf16[128,3072]{1,0:T(8,128)(2,1)}, bf16[128,3072]{1,0:T(8,128)(2,1)S(1)}, u32[]{:S(2)}, u32[]{:S(2)}) %collective-permute-start) | collective-permute-done | bytes 786464 | tf_op jit(solution)/shard_map/ppermute | solution.py:760
  38.5 16.7 %collective-permute-done.9.refs_4_.refs_10_.refs_16_.refs_15_.refs_21_.refs_22_.refs_28_.refs_11_.refs_8_ = bf16[128,5120]{1,0:T(8,128)(2,1)} collective-permute-done((bf16[128,5120]{1,0:T(8,128)(2,1)}, bf16[128,5120]{1,0:T(8,128)(2,1)}, u32[]{:S(2)}, u32[]{:S(2)}) %collective-permute-start.9) | collective-permute-done | bytes 1310752 | tf_op jit(solution)/shard_map/ppermute | solution.py:760
  61.1 16.2 %forward_attend.2.refs_1_ = bf16[416,1024]{1,0:T(8,128)(2,1)} custom-call(bf16[416,1024]{1,0:T(8,128)(2,1)} %bitcast.108, bf16[256,3072]{1,0:T(8,128)(2,1)} %bitcast.95, bf16[256,3072]{1,0:T(8,128)(2,1)} %collective-permute-done.1.refs_2_.refs_3_.refs_26_.refs_33_.refs_13_, bf16[128,3072]{1,0:T(8,128)(2,1)} %copy-done.18, bf16[128,3072]{1,0:T(8,128)(2,1)} %copy-done.19, ...), custom_call_target="tpu_custom_call" | custom-call | flops 46432256 | bytes 125696 | tf_op jit(solution)/shard_map/forward_attend/pallas_call | solution.py:53
  77.3 15.7 %forward_attend.3.refs_1_ = bf16[416,1024]{1,0:T(8,128)(2,1)} custom-call(bf16[416,1024]{1,0:T(8,128)(2,1)} %bitcast.104, bf16[256,3072]{1,0:T(8,128)(2,1)} %bitcast.96, bf16[256,3072]{1,0:T(8,128)(2,1)} %collective-permute-done.1.refs_2_.refs_3_.refs_26_.refs_33_.refs_13_, bf16[128,3072]{1,0:T(8,128)(2,1)} %copy-done.18, bf16[128,3072]{1,0:T(8,128)(2,1)} %copy-done.19, ...), custom_call_target="tpu_custom_call" | custom-call | flops 46432256 | bytes 125696 | tf_op jit(solution)/shard_map/forward_attend/pallas_call | solution.py:53
  100.2 13.7 %forward_feed.2 = (f32[416,1024]{1,0:T(8,128)}, bf16[416,4096]{1,0:T(8,128)(2,1)}) custom-call(bf16[416,1024]{1,0:T(8,128)(2,1)} %bitcast.109, bf16[416,1024]{1,0:T(8,128)(2,1)} %forward_attend.2.refs_1_, bf16[256,5120]{1,0:T(8,128)(2,1)} %copy-done, bf16[256,5120]{1,0:T(8,128)(2,1)} %copy-done.1, ...), custom_call_target="tpu_custom_call" | custom-call | flops 68157440 | bytes 434944 | tf_op jit(solution)/shard_map/forward_feed/pallas_call | solution.py:53
  113.9 13.7 %forward_feed.3 = (f32[416,1024]{1,0:T(8,128)}, bf16[416,4096]{1,0:T(8,128)(2,1)}) custom-call(bf16[416,1024]{1,0:T(8,128)(2,1)} %bitcast.105, bf16[416,1024]{1,0:T(8,128)(2,1)} %forward_attend.3.refs_1_, bf16[256,5120]{1,0:T(8,128)(2,1)} %copy-done, bf16[256,5120]{1,0:T(8,128)(2,1)} %copy-done.1, ...), custom_call_target="tpu_custom_call" | custom-call | flops 68157440 | bytes 434944 | tf_op jit(solution)/shard_map/forward_feed/pallas_call | solution.py:53
  133.8 10.8 %output_forward.4 = bf16[416,1024]{1,0:T(8,128)(2,1)} custom-call(f32[416,1024]{1,0:T(8,128)} %get-tuple-element.124.refs_0_, bf16[416,4096]{1,0:T(8,128)(2,1)} %get-tuple-element.125.refs_1_, bf16[1024,1024]{1,0:T(8,128)(2,1)} %bitcast.87, bf16[1024,1024]{1,0:T(8,128)(2,1)} %copy-done.3, ...), custom_call_target="tpu_custom_call" | custom-call | flops 54525952 | bytes 225024 | tf_op jit(solution)/shard_map/output_forward/pallas_call | solution.py:53
  150.0 10.7 %output_forward.5 = bf16[416,1024]{1,0:T(8,128)(2,1)} custom-call(f32[416,1024]{1,0:T(8,128)} %get-tuple-element.130.refs_0_, bf16[416,4096]{1,0:T(8,128)(2,1)} %get-tuple-element.134.refs_1_, bf16[1024,1024]{1,0:T(8,128)(2,1)} %bitcast.88, bf16[1024,1024]{1,0:T(8,128)(2,1)} %copy-done.3, ...), custom_call_target="tpu_custom_call" | custom-call | flops 54525952 | bytes 225024 | tf_op jit(solution)/shard_map/output_forward/pallas_call | solution.py:53
  168.6 30.6 %forward_attend_feed.2 = (bf16[416,7168]{1,0:T(8,128)(2,1)}, bf16[416,3072]{1,0:T(8,128)(2,1)}, f32[2,16,208]{2,1,0:T(8,128)}, f32[416,1024]{1,0:T(8,128)}, bf16[416,4096]{1,0:T(8,128)(2,1)}) custom-call(bf16[416,1024]{1,0:T(8,128)(2,1)} %bitcast.110, bf16[416,1024]{1,0:T(8,128)(2,1)} %copy-done.44, bf16[256,3072]{1,0:T(8,128)(2,1)} %bitcast.97, ...), custom_call_target="tpu_custom_call" | custom-call | flops 58669924352 | bytes 341393824 | tf_op jit(solution)/shard_map/forward_attend_feed/pallas_call | solution.py:53
  199.2 37.2 %backward_feed_attend.2 = (bf16[416,9216]{1,0:T(8,128)(2,1)}, f32[8,1024]{1,0:T(8,128)}, f32[1,4096]{1,0:T(1,128)}, bf16[416,1024]{1,0:T(8,128)(2,1)}, f32[8,1024]{1,0:T(8,128)}) custom-call(bf16[416,1024]{1,0:T(8,128)(2,1)} %bitcast.129, bf16[416,4096]{1,0:T(8,128)(2,1)} %get-tuple-element.137.refs_1_.refs_0_, ...), custom_call_target="tpu_custom_call" | custom-call | flops 90840236032 | bytes 477315488 | tf_op jit(solution)/shard_map/backward_feed_attend/pallas_call | solution.py:53
  238.2 30.5 %forward_attend_feed.3 = (bf16[416,7168]{1,0:T(8,128)(2,1)}, bf16[416,3072]{1,0:T(8,128)(2,1)}, f32[2,16,208]{2,1,0:T(8,128)}, f32[416,1024]{1,0:T(8,128)}, bf16[416,4096]{1,0:T(8,128)(2,1)}) custom-call(bf16[416,1024]{1,0:T(8,128)(2,1)} %bitcast.106, bf16[416,1024]{1,0:T(8,128)(2,1)} %collective-permute-done.20.refs_1_.refs_13_, ...), custom_call_target="tpu_custom_call" | custom-call | flops 58669924352 | bytes 341393824 | tf_op jit(solution)/shard_map/forward_attend_feed/pallas_call | solution.py:53
  269.8 37.1 %backward_feed_attend.3 = (bf16[416,9216]{1,0:T(8,128)(2,1)}, f32[8,1024]{1,0:T(8,128)}, f32[1,4096]{1,0:T(1,128)}, bf16[416,1024]{1,0:T(8,128)(2,1)}, f32[8,1024]{1,0:T(8,128)}) custom-call(bf16[416,4096]{1,0:T(8,128)(2,1)} %get-tuple-element.137.refs_1_.refs_0_, bf16[416,4096]{1,0:T(8,128)(2,1)} %get-tuple-element.144.refs_1_, ...), custom_call_target="tpu_custom_call" | custom-call | flops 90840236032 | bytes 600211840 | tf_op jit(solution)/shard_map/backward_feed_attend/pallas_call | solution.py:53
  309.9 10.7 %output_forward.6 = bf16[416,1024]{1,0:T(8,128)(2,1)} custom-call(f32[416,1024]{1,0:T(8,128)} %get-tuple-element.138.refs_2_.refs_0_, bf16[416,7168]{1,0:T(8,128)(2,1)} %get-tuple-element.151.refs_4_.refs_8_.refs_1_.refs_0_, bf16[1024,1024]{1,0:T(8,128)(2,1)} %bitcast.91, bf16[1024,1024]{1,0:T(8,128)(2,1)} %copy-done.3, ...), custom_call_target="tpu_custom_call" | custom-call | flops 27917287424 | bytes 135659936 | tf_op jit(solution)/shard_map/output_forward/pallas_call | solution.py:53
  320.7 10.7 %output_forward.7 = bf16[416,1024]{1,0:T(8,128)(2,1)} custom-call(f32[416,1024]{1,0:T(8,128)} %get-tuple-element.145.refs_3_.refs_0_.refs_2_, bf16[416,7168]{1,0:T(8,128)(2,1)} %get-tuple-element.152.refs_9_.refs_1_.refs_2_.refs_3_, bf16[1024,1024]{1,0:T(8,128)(2,1)} %bitcast.92, bf16[1024,1024]{1,0:T(8,128)(2,1)} %copy-done.3, ...), custom_call_target="tpu_custom_call" | custom-call | flops 27917287424 | bytes 135659936 | tf_op jit(solution)/shard_map/output_forward/pallas_call | solution.py:53
  334.9 8.9 %reduce.11 = (bf16[512,1024]{1,0:T(8,128)(2,1)}, bf16[512,1024]{1,0:T(8,128)(2,1)}) custom-call(bf16[416,7168]{1,0:T(8,128)(2,1)} %get-tuple-element.151.refs_4_.refs_8_.refs_1_.refs_0_, bf16[416,7168]{1,0:T(8,128)(2,1)} %collective-permute-done.19.refs_1_, bf16[416,7168]{1,0:T(8,128)(2,1)} %get-tuple-element.152.refs_9_.refs_1_.refs_2_.refs_3_, ...), custom_call_target="tpu_custom_call" | custom-call | flops 54525952 | bytes 911360 | tf_op jit(solution)/shard_map/reduce/pallas_call | solution.py:53
  344.4 18.3 %backward_feed.1 = (bf16[416,4096]{1,0:T(8,128)(2,1)}, bf16[416,1024]{1,0:T(8,128)(2,1)}, f32[8,1024]{1,0:T(8,128)}, f32[1,4096]{1,0:T(1,128)}, f32[416,1024]{1,0:T(8,128)}) custom-call(bf16[416,1024]{1,0:T(8,128)(2,1)} %copy-done.16, bf16[416,4096]{1,0:T(8,128)(2,1)} %get-tuple-element.144.refs_1_, f32[416,1024]{1,0:T(8,128)} %get-tuple-element.145.refs_3_.refs_0_.refs_2_, ...), custom_call_target="tpu_custom_call" | custom-call | flops 109051904 | bytes 482816 | tf_op jit(solution)/shard_map/backward_feed/pallas_call | solution.py:53
  362.8 6.5 %collective-permute-done.28 = bf16[512,1024]{1,0:T(8,128)(2,1)} collective-permute-done((bf16[512,1024]{1,0:T(8,128)(2,1)}, bf16[512,1024]{1,0:T(8,128)(2,1)}, u32[]{:S(2)}, u32[]{:S(2)}) %collective-permute-start.28) | collective-permute-done | bytes 1048608 | tf_op jit(solution)/shard_map/ppermute | solution.py:760
  370.9 9.0 %reduce.12 = (bf16[512,1024]{1,0:T(8,128)(2,1)}, bf16[512,1024]{1,0:T(8,128)(2,1)}) custom-call(bf16[416,7168]{1,0:T(8,128)(2,1)} %get-tuple-element.151.refs_4_.refs_8_.refs_1_.refs_0_, bf16[416,7168]{1,0:T(8,128)(2,1)} %collective-permute-done.19.refs_1_, bf16[416,7168]{1,0:T(8,128)(2,1)} %get-tuple-element.152.refs_9_.refs_1_.refs_2_.refs_3_, ...), custom_call_target="tpu_custom_call" | custom-call | flops 55834574848 | bytes 933232960 | tf_op jit(solution)/shard_map/reduce/pallas_call | solution.py:53
  385.9 9.3 %expand.2 = (bf16[256,2048]{1,0:T(8,128)(2,1)}, bf16[256,2048]{1,0:T(8,128)(2,1)}) custom-call(bf16[416,7168]{1,0:T(8,128)(2,1)} %get-tuple-element.151.refs_4_.refs_8_.refs_1_.refs_0_, bf16[416,7168]{1,0:T(8,128)(2,1)} %collective-permute-done.19.refs_1_, bf16[416,7168]{1,0:T(8,128)(2,1)} %get-tuple-element.152.refs_9_.refs_1_.refs_2_.refs_3_, ...), custom_call_target="tpu_custom_call" | custom-call | flops 54525952 | bytes 991232 | tf_op jit(solution)/shard_map/expand/pallas_call | solution.py:53
  395.3 9.5 %expand.3 = (bf16[256,2048]{1,0:T(8,128)(2,1)}, bf16[256,2048]{1,0:T(8,128)(2,1)}) custom-call(bf16[416,7168]{1,0:T(8,128)(2,1)} %get-tuple-element.151.refs_4_.refs_8_.refs_1_.refs_0_, bf16[416,7168]{1,0:T(8,128)(2,1)} %collective-permute-done.19.refs_1_, bf16[416,7168]{1,0:T(8,128)(2,1)} %get-tuple-element.152.refs_9_.refs_1_.refs_2_.refs_3_, ...), custom_call_target="tpu_custom_call" | custom-call | flops 54525952 | bytes 991232 | tf_op jit(solution)/shard_map/expand/pallas_call | solution.py:53
  408.8 24.9 %backward_attend.1 = (bf16[416,3072]{1,0:T(8,128)(2,1)}, bf16[416,1024]{1,0:T(8,128)(2,1)}, f32[8,1024]{1,0:T(8,128)}) custom-call(bf16[416,1024]{1,0:T(8,128)(2,1)} %get-tuple-element.171.refs_0_.refs_8_, f32[416,1024]{1,0:T(8,128)} %get-tuple-element.172.refs_1_, bf16[416,3072]{1,0:T(8,128)(2,1)} %get-tuple-element.146.refs_7_.refs_2_, ...), custom_call_target="tpu_custom_call" | custom-call | flops 70011322368 | bytes 515539776 | tf_op jit(solution)/shard_map/backward_attend/pallas_call | solution.py:53
  437.5 8.0 %collective-permute-start.34 = (bf16[512,1024]{1,0:T(8,128)(2,1)}, bf16[512,1024]{1,0:T(8,128)(2,1)}, u32[]{:S(2)}, u32[]{:S(2)}) collective-permute-start(bf16[512,1024]{1,0:T(8,128)(2,1)} %add_convert_fusion.10), channel_id=1, source_target_pairs={{0,1},{3,2},{4,5},{7,6},{8,9},{11,10},{12,13},{15,14},{16,17},{19,... | collective-permute-start | bytes 3145736 | tf_op jit(solution)/shard_map/ppermute | solution.py:802
  446.9 13.6 %collective-permute-done.33 = bf16[256,2048]{1,0:T(8,128)(2,1)} collective-permute-done((bf16[256,2048]{1,0:T(8,128)(2,1)}, bf16[256,2048]{1,0:T(8,128)(2,1)}, u32[]{:S(2)}, u32[]{:S(2)}) %collective-permute-start.33) | collective-permute-done | bytes 1048608 | tf_op jit(solution)/shard_map/ppermute | solution.py:760
  478.0 7.8 %qkv.2 = (bf16[256,1536]{1,0:T(8,128)(2,1)}, bf16[256,1536]{1,0:T(8,128)(2,1)}) custom-call(bf16[416,7168]{1,0:T(8,128)(2,1)} %get-tuple-element.151.refs_4_.refs_8_.refs_1_.refs_0_, bf16[416,7168]{1,0:T(8,128)(2,1)} %collective-permute-done.19.refs_1_, bf16[416,7168]{1,0:T(8,128)(2,1)} %get-tuple-element.152.refs_9_.refs_1_.refs_2_.refs_3_, ...), custom_call_target="tpu_custom_call" | custom-call | flops 40894464 | bytes 956416 | tf_op jit(solution)/shard_map/qkv/pallas_call | solution.py:53
  487.9 7.8 %collective-permute-start.41 = (bf16[256,2048]{1,0:T(8,128)(2,1)S(1)}, bf16[256,2048]{1,0:T(8,128)(2,1)S(1)}, u32[]{:S(2)}, u32[]{:S(2)}) collective-permute-start(bf16[256,2048]{1,0:T(8,128)(2,1)S(1)} %add_convert_fusion.5), channel_id=1, source_target_pairs={{0,1},{3,2},{4,5},{7,6},{8,9},{11,10},{12,13},{15,14},{16,17},{19,... | collective-permute-start | bytes 3145736 | tf_op jit(solution)/shard_map/ppermute | solution.py:802
  506.6 7.9 %qkv.3 = (bf16[256,1536]{1,0:T(8,128)(2,1)}, bf16[256,1536]{1,0:T(8,128)(2,1)}) custom-call(bf16[416,7168]{1,0:T(8,128)(2,1)} %get-tuple-element.151.refs_4_.refs_8_.refs_1_.refs_0_, bf16[416,7168]{1,0:T(8,128)(2,1)} %collective-permute-done.19.refs_1_, bf16[416,7168]{1,0:T(8,128)(2,1)} %get-tuple-element.152.refs_9_.refs_1_.refs_2_.refs_3_, ...), custom_call_target="tpu_custom_call" | custom-call | flops 40894464 | bytes 956416 | tf_op jit(solution)/shard_map/qkv/pallas_call | solution.py:53
  515.3 11.6 %collective-permute-start.45 = (bf16[256,1536]{1,0:T(8,128)(2,1)S(1)}, bf16[256,1536]{1,0:T(8,128)(2,1)S(1)}, u32[]{:S(2)}, u32[]{:S(2)}) collective-permute-start(bf16[256,1536]{1,0:T(8,128)(2,1)S(1)} %add_convert_fusion.17), channel_id=1, source_target_pairs={{0,1},{3,2},{4,5},{7,6},{8,9},{11,10},{12,13},{15,14},{16,17},{19,... | collective-permute-start | bytes 2359304 | tf_op jit(solution)/shard_map/ppermute | solution.py:802
  533.1 11.1 %collective-permute-start.49 = (bf16[256,1536]{1,0:T(8,128)(2,1)}, bf16[256,1536]{1,0:T(8,128)(2,1)}, u32[]{:S(2)}, u32[]{:S(2)}) collective-permute-start(bf16[256,1536]{1,0:T(8,128)(2,1)} %add_convert_fusion.16), channel_id=1, source_target_pairs={{0,1},{3,2},{4,5},{7,6},{8,9},{11,10},{12,13},{15,14},{16,17},{19,... | collective-permute-start | bytes 2359304 | tf_op jit(solution)/shard_map/ppermute | solution.py:802
  551.5 6.3 project.1
  574.4 12.2 %collective-permute-start.54 = (bf16[272,1024]{1,0:T(8,128)(2,1)S(1)}, bf16[272,1024]{1,0:T(8,128)(2,1)S(1)}, u32[]{:S(2)}, u32[]{:S(2)}) collective-permute-start(bf16[272,1024]{1,0:T(8,128)(2,1)S(1)} %add_convert_fusion.20), channel_id=1, source_target_pairs={{0,1},{3,2},{4,5},{7,6},{8,9},{11,10},{12,13},{15,14},{16,17},{19,... | collective-permute-start | bytes 1671176 | tf_op jit(solution)/shard_map/ppermute | solution.py:802
  603.5 12.8 %collective-permute-done.55 = bf16[256,1536]{1,0:T(8,128)(2,1)S(1)} collective-permute-done((bf16[256,1536]{1,0:T(8,128)(2,1)S(1)}, bf16[256,1536]{1,0:T(8,128)(2,1)S(1)}, u32[]{:S(2)}, u32[]{:S(2)}) %collective-permute-start.55) | collective-permute-done | bytes 786464 | tf_op jit(solution)/shard_map/ppermute | solution.py:808
  620.4 12.7 %collective-permute-done.57 = bf16[256,1536]{1,0:T(8,128)(2,1)S(1)} collective-permute-done((bf16[256,1536]{1,0:T(8,128)(2,1)S(1)}, bf16[256,1536]{1,0:T(8,128)(2,1)S(1)}, u32[]{:S(2)}, u32[]{:S(2)}) %collective-permute-start.57) | collective-permute-done | bytes 786464 | tf_op jit(solution)/shard_map/ppermute | solution.py:808
  (304 shorter events, 178.4 us)
Async XLA Ops:
  10.0 45.2 %collective-permute-start.9 = (bf16[128,5120]{1,0:T(8,128)(2,1)}, bf16[128,5120]{1,0:T(8,128)(2,1)}, u32[]{:S(2)}, u32[]{:S(2)}) collective-permute-start(bf16[128,5120]{1,0:T(8,128)(2,1)} %fusion), channel_id=1, source_target_pairs={{0,8},{4,12},{8,0},{12,4},{1,9},{5,13},{9,1},{13,5},{2,10},{6,14},... | collective-permute-start | bytes 3932168 | tf_op jit(solution)/shard_map/ppermute | solution.py:760
  17.6 76.4 %collective-permute-start.8 = (bf16[256,5120]{1,0:T(8,128)(2,1)S(1)}, bf16[256,5120]{1,0:T(8,128)(2,1)S(1)}, u32[]{:S(2)}, u32[]{:S(2)}) collective-permute-start(bf16[256,5120]{1,0:T(8,128)(2,1)S(1)} %pad_maximum_fusion.refs_2_.refs_8_.refs_14_.refs_13_.refs_19_.refs_20_.refs_26_.refs_9_.refs_6_), channel_id=1, source_target_pairs={{0,4},{4,0},{8,12},{12,8},{1,5},{5,1},{9,13},{13,9},{2,6},{6,2},{1... | collective-permute-start | bytes 7864328 | tf_op jit(solution)/shard_map/ppermute | solution.py:757
  27.8 27.4 %collective-permute-start.2 = (bf16[128,3072]{1,0:T(8,128)(2,1)S(1)}, bf16[128,3072]{1,0:T(8,128)(2,1)S(1)}, u32[]{:S(2)}, u32[]{:S(2)}) collective-permute-start(bf16[128,3072]{1,0:T(8,128)(2,1)S(1)} %collective-permute-done.refs_3_.refs_4_.refs_27_.refs_34_.refs_14_), channel_id=1, source_target_pairs={{0,1},{1,0},{2,3},{3,2},{4,5},{5,4},{6,7},{7,6},{8,9},{9,8},{10,11... | collective-permute-start | bytes 2359304 | tf_op jit(solution)/shard_map/ppermute | solution.py:763
  55.2 38.0 %collective-permute-start.10 = (bf16[128,5120]{1,0:T(8,128)(2,1)}, bf16[128,5120]{1,0:T(8,128)(2,1)}, u32[]{:S(2)}, u32[]{:S(2)}) collective-permute-start(bf16[128,5120]{1,0:T(8,128)(2,1)} %collective-permute-done.9.refs_4_.refs_10_.refs_16_.refs_15_.refs_21_.refs_22_.refs_28_.refs_11_.refs_8_), channel_id=1, source_target_pairs={{0,1},{1,0},{2,3},{3,2},{4,5},{5,4},{6,7},{7,6},{8,9},{9,8},{10,11... | collective-permute-start | bytes 3932168 | tf_op jit(solution)/shard_map/ppermute | solution.py:763
  57.3 36.2 %collective-permute-start.14 = (bf16[512,1024]{1,0:T(8,128)(2,1)}, bf16[512,1024]{1,0:T(8,128)(2,1)}, u32[]{:S(2)}, u32[]{:S(2)}) collective-permute-start(bf16[512,1024]{1,0:T(8,128)(2,1)} %dynamic-slice_bitcast_fusion), channel_id=1, source_target_pairs={{0,8},{4,12},{8,0},{12,4},{1,9},{5,13},{9,1},{13,5},{2,10},{6,14},... | collective-permute-start | bytes 3145736 | tf_op jit(solution)/shard_map/ppermute | solution.py:760
  93.6 34.0 %collective-permute-start.15 = (bf16[512,1024]{1,0:T(8,128)(2,1)}, bf16[512,1024]{1,0:T(8,128)(2,1)}, u32[]{:S(2)}, u32[]{:S(2)}) collective-permute-start(bf16[512,1024]{1,0:T(8,128)(2,1)} %collective-permute-done.14.refs_4_.refs_9_.refs_16_.refs_5_), channel_id=1, source_target_pairs={{0,1},{1,0},{2,3},{3,2},{4,5},{5,4},{6,7},{7,6},{8,9},{9,8},{10,11... | collective-permute-start | bytes 3145736 | tf_op jit(solution)/shard_map/ppermute | solution.py:763
  94.0 38.0 %collective-permute-start.13 = (bf16[1024,1024]{1,0:T(8,128)(2,1)}, bf16[1024,1024]{1,0:T(8,128)(2,1)S(1)}, u32[]{:S(2)}, u32[]{:S(2)}) collective-permute-start(bf16[1024,1024]{1,0:T(8,128)(2,1)} %bitcast.86), channel_id=1, source_target_pairs={{0,4},{4,0},{8,12},{12,8},{1,5},{5,1},{9,13},{13,9},{2,6},{6,2},{1... | collective-permute-start | bytes 6291464 | tf_op jit(solution)/shard_map/ppermute | solution.py:757
  160.8 77.0 %collective-permute-start.20 = (bf16[416,1024]{1,0:T(8,128)(2,1)}, bf16[416,1024]{1,0:T(8,128)(2,1)}, u32[]{:S(2)}, u32[]{:S(2)}) collective-permute-start(bf16[416,1024]{1,0:T(8,128)(2,1)} %output_forward.5), channel_id=1, source_target_pairs={{0,16},{1,17},{2,18},{3,19},{4,20},{5,21},{6,22},{7,23},{8,24},{9,... | collective-permute-start | bytes 2555912 | tf_op jit(solution)/shard_map/ppermute | solution.py:842
  199.1 110.8 %collective-permute-start.19 = (bf16[416,7168]{1,0:T(8,128)(2,1)}, bf16[416,7168]{1,0:T(8,128)(2,1)}, u32[]{:S(2)}, u32[]{:S(2)}) collective-permute-start(bf16[416,7168]{1,0:T(8,128)(2,1)} %get-tuple-element.151.refs_4_.refs_8_.refs_1_.refs_0_), channel_id=1, source_target_pairs={{0,4},{4,0},{8,12},{12,8},{1,5},{5,1},{9,13},{13,9},{2,6},{6,2},{1... | collective-permute-start | bytes 17891336 | tf_op jit(solution)/shard_map/ppermute | solution.py:757
  236.4 32.4 %collective-permute-start.22 = (bf16[416,1024]{1,0:T(8,128)(2,1)}, bf16[416,1024]{1,0:T(8,128)(2,1)S(1)}, u32[]{:S(2)}, u32[]{:S(2)}) collective-permute-start(bf16[416,1024]{1,0:T(8,128)(2,1)} %get-tuple-element.141), channel_id=1, source_target_pairs={{16,0},{17,1},{18,2},{19,3},{20,4},{21,5},{22,6},{23,7},{24,8},{25... | collective-permute-start | bytes 2555912 | tf_op jit(solution)/shard_map/ppermute | solution.py:842
  237.7 72.2 %collective-permute-start.24 = (bf16[416,9216]{1,0:T(8,128)(2,1)}, bf16[416,9216]{1,0:T(8,128)(2,1)}, u32[]{:S(2)}, u32[]{:S(2)}) collective-permute-start(bf16[416,9216]{1,0:T(8,128)(2,1)} %get-tuple-element.149.refs_5_), channel_id=1, source_target_pairs={{0,4},{4,0},{8,12},{12,8},{1,5},{5,1},{9,13},{13,9},{2,6},{6,2},{1... | collective-permute-start | bytes 23003144 | tf_op jit(solution)/shard_map/ppermute | solution.py:757
  268.7 51.9 %collective-permute-start.21 = (bf16[416,7168]{1,0:T(8,128)(2,1)}, bf16[416,7168]{1,0:T(8,128)(2,1)}, u32[]{:S(2)}, u32[]{:S(2)}) collective-permute-start(bf16[416,7168]{1,0:T(8,128)(2,1)} %get-tuple-element.152.refs_9_.refs_1_.refs_2_.refs_3_), channel_id=1, source_target_pairs={{0,4},{4,0},{8,12},{12,8},{1,5},{5,1},{9,13},{13,9},{2,6},{6,2},{1... | collective-permute-start | bytes 17891336 | tf_op jit(solution)/shard_map/ppermute | solution.py:757
  306.9 27.0 %collective-permute-start.23 = (bf16[416,9216]{1,0:T(8,128)(2,1)}, bf16[416,9216]{1,0:T(8,128)(2,1)}, u32[]{:S(2)}, u32[]{:S(2)}) collective-permute-start(bf16[416,9216]{1,0:T(8,128)(2,1)} %get-tuple-element.148.refs_4_), channel_id=1, source_target_pairs={{0,4},{4,0},{8,12},{12,8},{1,5},{5,1},{9,13},{13,9},{2,6},{6,2},{1... | collective-permute-start | bytes 23003144 | tf_op jit(solution)/shard_map/ppermute | solution.py:757
  343.8 25.6 %collective-permute-start.28 = (bf16[512,1024]{1,0:T(8,128)(2,1)}, bf16[512,1024]{1,0:T(8,128)(2,1)}, u32[]{:S(2)}, u32[]{:S(2)}) collective-permute-start(bf16[512,1024]{1,0:T(8,128)(2,1)} %get-tuple-element.161), channel_id=1, source_target_pairs={{0,8},{4,12},{8,0},{12,4},{1,9},{5,13},{9,1},{13,5},{2,10},{6,14},... | collective-permute-start | bytes 3145736 | tf_op jit(solution)/shard_map/ppermute | solution.py:760
  380.6 25.6 %collective-permute-start.31 = (bf16[512,1024]{1,0:T(8,128)(2,1)S(1)}, bf16[512,1024]{1,0:T(8,128)(2,1)}, u32[]{:S(2)}, u32[]{:S(2)}) collective-permute-start(bf16[512,1024]{1,0:T(8,128)(2,1)S(1)} %add_convert_fusion.11), channel_id=1, source_target_pairs={{0,1},{3,2},{4,5},{7,6},{8,9},{11,10},{12,13},{15,14},{16,17},{19,... | collective-permute-start | bytes 3145736 | tf_op jit(solution)/shard_map/ppermute | solution.py:802
  433.7 42.8 %collective-permute-start.32 = (bf16[416,3072]{1,0:T(8,128)(2,1)}, bf16[416,3072]{1,0:T(8,128)(2,1)S(1)}, u32[]{:S(2)}, u32[]{:S(2)}) collective-permute-start(bf16[416,3072]{1,0:T(8,128)(2,1)} %get-tuple-element.173.refs_8_), channel_id=1, source_target_pairs={{0,4},{4,0},{8,12},{12,8},{1,5},{5,1},{9,13},{13,9},{2,6},{6,2},{1... | collective-permute-start | bytes 7667720 | tf_op jit(solution)/shard_map/ppermute | solution.py:757
  434.1 26.3 %collective-permute-start.33 = (bf16[256,2048]{1,0:T(8,128)(2,1)}, bf16[256,2048]{1,0:T(8,128)(2,1)}, u32[]{:S(2)}, u32[]{:S(2)}) collective-permute-start(bf16[256,2048]{1,0:T(8,128)(2,1)} %get-tuple-element.176), channel_id=1, source_target_pairs={{0,8},{4,12},{8,0},{12,4},{1,9},{5,13},{9,1},{13,5},{2,10},{6,14},... | collective-permute-start | bytes 3145736 | tf_op jit(solution)/shard_map/ppermute | solution.py:760
  435.8 35.1 %collective-permute-start.35 = (bf16[512,1024]{1,0:T(8,128)(2,1)}, bf16[512,1024]{1,0:T(8,128)(2,1)}, u32[]{:S(2)}, u32[]{:S(2)}) collective-permute-start(bf16[512,1024]{1,0:T(8,128)(2,1)} %add_convert_fusion.9), channel_id=1, source_target_pairs={{1,2},{2,1},{5,6},{6,5},{9,10},{10,9},{13,14},{14,13},{17,18},{18,... | collective-permute-start | bytes 3145736 | tf_op jit(solution)/shard_map/ppermute | solution.py:805
  437.5 30.8 %collective-permute-start.34 = (bf16[512,1024]{1,0:T(8,128)(2,1)}, bf16[512,1024]{1,0:T(8,128)(2,1)}, u32[]{:S(2)}, u32[]{:S(2)}) collective-permute-start(bf16[512,1024]{1,0:T(8,128)(2,1)} %add_convert_fusion.10), channel_id=1, source_target_pairs={{0,1},{3,2},{4,5},{7,6},{8,9},{11,10},{12,13},{15,14},{16,17},{19,... | collective-permute-start | bytes 3145736 | tf_op jit(solution)/shard_map/ppermute | solution.py:802
  446.2 39.6 %collective-permute-start.36 = (bf16[256,2048]{1,0:T(8,128)(2,1)}, bf16[256,2048]{1,0:T(8,128)(2,1)}, u32[]{:S(2)}, u32[]{:S(2)}) collective-permute-start(bf16[256,2048]{1,0:T(8,128)(2,1)} %get-tuple-element.182), channel_id=1, source_target_pairs={{0,8},{4,12},{8,0},{12,4},{1,9},{5,13},{9,1},{13,5},{2,10},{6,14},... | collective-permute-start | bytes 3145736 | tf_op jit(solution)/shard_map/ppermute | solution.py:760
  462.4 34.8 %collective-permute-start.37 = (bf16[256,2048]{1,0:T(8,128)(2,1)S(1)}, bf16[256,2048]{1,0:T(8,128)(2,1)}, u32[]{:S(2)}, u32[]{:S(2)}) collective-permute-start(bf16[256,2048]{1,0:T(8,128)(2,1)S(1)} %add_convert_fusion.8), channel_id=1, source_target_pairs={{0,1},{3,2},{4,5},{7,6},{8,9},{11,10},{12,13},{15,14},{16,17},{19,... | collective-permute-start | bytes 3145736 | tf_op jit(solution)/shard_map/ppermute | solution.py:802
  473.5 30.7 %collective-permute-start.39 = (bf16[512,1024]{1,0:T(8,128)(2,1)}, bf16[512,1024]{1,0:T(8,128)(2,1)}, u32[]{:S(2)}, u32[]{:S(2)}) collective-permute-start(bf16[512,1024]{1,0:T(8,128)(2,1)} %add_convert_fusion.6), channel_id=1, source_target_pairs={{1,0},{2,3},{5,4},{6,7},{9,8},{10,11},{13,12},{14,15},{17,16},{18,... | collective-permute-start | bytes 3145736 | tf_op jit(solution)/shard_map/ppermute | solution.py:808
  487.9 39.0 %collective-permute-start.41 = (bf16[256,2048]{1,0:T(8,128)(2,1)S(1)}, bf16[256,2048]{1,0:T(8,128)(2,1)S(1)}, u32[]{:S(2)}, u32[]{:S(2)}) collective-permute-start(bf16[256,2048]{1,0:T(8,128)(2,1)S(1)} %add_convert_fusion.5), channel_id=1, source_target_pairs={{0,1},{3,2},{4,5},{7,6},{8,9},{11,10},{12,13},{15,14},{16,17},{19,... | collective-permute-start | bytes 3145736 | tf_op jit(solution)/shard_map/ppermute | solution.py:802
  500.8 28.3 %collective-permute-start.43 = (bf16[512,1024]{1,0:T(8,128)(2,1)S(1)}, bf16[512,1024]{1,0:T(8,128)(2,1)}, u32[]{:S(2)}, u32[]{:S(2)}) collective-permute-start(bf16[512,1024]{1,0:T(8,128)(2,1)S(1)} %add_convert_fusion.3), channel_id=1, source_target_pairs={{1,0},{2,3},{5,4},{6,7},{9,8},{10,11},{13,12},{14,15},{17,16},{18,... | collective-permute-start | bytes 3145736 | tf_op jit(solution)/shard_map/ppermute | solution.py:808
  515.3 31.8 %collective-permute-start.45 = (bf16[256,1536]{1,0:T(8,128)(2,1)S(1)}, bf16[256,1536]{1,0:T(8,128)(2,1)S(1)}, u32[]{:S(2)}, u32[]{:S(2)}) collective-permute-start(bf16[256,1536]{1,0:T(8,128)(2,1)S(1)} %add_convert_fusion.17), channel_id=1, source_target_pairs={{0,1},{3,2},{4,5},{7,6},{8,9},{11,10},{12,13},{15,14},{16,17},{19,... | collective-permute-start | bytes 2359304 | tf_op jit(solution)/shard_map/ppermute | solution.py:802
  533.1 35.7 %collective-permute-start.49 = (bf16[256,1536]{1,0:T(8,128)(2,1)}, bf16[256,1536]{1,0:T(8,128)(2,1)}, u32[]{:S(2)}, u32[]{:S(2)}) collective-permute-start(bf16[256,1536]{1,0:T(8,128)(2,1)} %add_convert_fusion.16), channel_id=1, source_target_pairs={{0,1},{3,2},{4,5},{7,6},{8,9},{11,10},{12,13},{15,14},{16,17},{19,... | collective-permute-start | bytes 2359304 | tf_op jit(solution)/shard_map/ppermute | solution.py:802
  549.9 36.8 %collective-permute-start.51 = (bf16[256,1536]{1,0:T(8,128)(2,1)S(1)}, bf16[256,1536]{1,0:T(8,128)(2,1)}, u32[]{:S(2)}, u32[]{:S(2)}) collective-permute-start(bf16[256,1536]{1,0:T(8,128)(2,1)S(1)} %add_convert_fusion.15), channel_id=1, source_target_pairs={{1,2},{2,1},{5,6},{6,5},{9,10},{10,9},{13,14},{14,13},{17,18},{18,... | collective-permute-start | bytes 2359304 | tf_op jit(solution)/shard_map/ppermute | solution.py:805
  563.4 37.5 %collective-permute-start.52 = (bf16[256,2048]{1,0:T(8,128)(2,1)S(1)}, bf16[256,2048]{1,0:T(8,128)(2,1)S(1)}, u32[]{:S(2)}, u32[]{:S(2)}) collective-permute-start(bf16[256,2048]{1,0:T(8,128)(2,1)S(1)} %add_convert_fusion), channel_id=1, source_target_pairs={{1,0},{2,3},{5,4},{6,7},{9,8},{10,11},{13,12},{14,15},{17,16},{18,... | collective-permute-start | bytes 3145736 | tf_op jit(solution)/shard_map/ppermute | solution.py:808
  570.4 30.7 %collective-permute-start.53 = (bf16[256,1536]{1,0:T(8,128)(2,1)S(1)}, bf16[256,1536]{1,0:T(8,128)(2,1)S(1)}, u32[]{:S(2)}, u32[]{:S(2)}) collective-permute-start(bf16[256,1536]{1,0:T(8,128)(2,1)S(1)} %add_convert_fusion.14), channel_id=1, source_target_pairs={{1,2},{2,1},{5,6},{6,5},{9,10},{10,9},{13,14},{14,13},{17,18},{18,... | collective-permute-start | bytes 2359304 | tf_op jit(solution)/shard_map/ppermute | solution.py:805
  574.4 26.8 %collective-permute-start.54 = (bf16[272,1024]{1,0:T(8,128)(2,1)S(1)}, bf16[272,1024]{1,0:T(8,128)(2,1)S(1)}, u32[]{:S(2)}, u32[]{:S(2)}) collective-permute-start(bf16[272,1024]{1,0:T(8,128)(2,1)S(1)} %add_convert_fusion.20), channel_id=1, source_target_pairs={{0,1},{3,2},{4,5},{7,6},{8,9},{11,10},{12,13},{15,14},{16,17},{19,... | collective-permute-start | bytes 1671176 | tf_op jit(solution)/shard_map/ppermute | solution.py:802
  588.0 28.3 %collective-permute-start.55 = (bf16[256,1536]{1,0:T(8,128)(2,1)S(1)}, bf16[256,1536]{1,0:T(8,128)(2,1)S(1)}, u32[]{:S(2)}, u32[]{:S(2)}) collective-permute-start(bf16[256,1536]{1,0:T(8,128)(2,1)S(1)} %add_convert_fusion.13), channel_id=1, source_target_pairs={{1,0},{2,3},{5,4},{6,7},{9,8},{10,11},{13,12},{14,15},{17,16},{18,... | collective-permute-start | bytes 2359304 | tf_op jit(solution)/shard_map/ppermute | solution.py:808
  602.2 30.9 %collective-permute-start.57 = (bf16[256,1536]{1,0:T(8,128)(2,1)S(1)}, bf16[256,1536]{1,0:T(8,128)(2,1)S(1)}, u32[]{:S(2)}, u32[]{:S(2)}) collective-permute-start(bf16[256,1536]{1,0:T(8,128)(2,1)S(1)} %add_convert_fusion.12), channel_id=1, source_target_pairs={{1,0},{2,3},{5,4},{6,7},{9,8},{10,11},{13,12},{14,15},{17,16},{18,... | collective-permute-start | bytes 2359304 | tf_op jit(solution)/shard_map/ppermute | solution.py:808
  (73 other events, 895.4 us)

commit v6 on v5

--- a/solution.py
+++ b/solution.py
@@ -322,8 +322,9 @@
     )
 
 
-def output_forward(middle, active, pieces, params, meta, count, weight=LIGHT):
+def output_forward(middle, active, pieces, params, meta, count, weight=LIGHT, columns=None):
     rows, width = middle.shape
+    first, width = columns or (0, width)
     inner = sum(piece.shape[0] for piece in flat(pieces))
     space = rows // count
     parts, many = len(pieces), len(flat(pieces))
@@ -338,11 +339,11 @@
         vec, info, result, mid, act, full, x_sem, w_sem = refs
         copies = [
             pltpu.make_async_copy(act_in.at[:, pl.ds(0, inner)], act, x_sem.at[0]),
-            pltpu.make_async_copy(mid_in, mid, x_sem.at[1]),
+            pltpu.make_async_copy(mid_in.at[:, pl.ds(first, width)], mid, x_sem.at[1]),
         ]
         copies[0].start()
         loads = [
-            start_pieces(reduce, info, spots, full, w_sem, block, (block * part_width, part_width))
+            start_pieces(reduce, info, spots, full, w_sem, block, (block * part_width, part_width), first)
             for block in range(blocks)
         ]
         copies[1].start()
@@ -352,7 +353,8 @@
             if block == 0:
                 copies[1].wait()
             part = slice(block * part_width, (block + 1) * part_width)
-            value = contract(act[...], full[:, part], 1, 0) + mid[:, part] + vec[FEED : FEED + 1, part]
+            value = contract(act[...], full[:, part], 1, 0) + mid[:, part]
+            value = value + vec[FEED : FEED + 1, first + block * part_width : first + (block + 1) * part_width]
             for image in range(count):
                 alive = jnp.where(info[parts + 1 + image] > 0, 1.0, 0.0)
                 here = slice(image * space, (image + 1) * space)
@@ -779,7 +781,9 @@
         others = []
         tokens = prepare(halves[0]) + asked[2:]
         for index, half in enumerate(halves):
-            others.append(self.beside(after(half, *others[-1:], *(tokens if index == 1 else []))))
+            earlier = others[-1:] if index == 1 else []
+            others.append(self.beside(after(half, *earlier, *(tokens if index == 1 else []))))
+        self.arrived = halves[-1]
 
         def pieces(index, *tokens):
             one, two = (after(half, *tokens) for half in (halves[index], others[index]))
@@ -823,6 +827,7 @@
 
     def gather(self, blocks, prepare):
         prepare(blocks[0])
+        self.arrived = blocks[0]
         found = [[[piece] for piece in self.gather_small(block)] for block in blocks]
         return [lambda *tokens, groups=groups: groups for groups in found]
 
@@ -951,7 +956,7 @@
     qkv = qkv()
     attended = []
     for batch in batches:
-        start = inputs[batch] if batch == 0 else after(inputs[batch], attended[-1][0])
+        start = inputs[batch] if batch == 0 else after(inputs[batch], attended[-1][0], net.arrived)
         attended.append(
             forward(start, start, None, qkv, None, params, infos[batch], slots, length)
         )
@@ -965,17 +970,27 @@
     reduce = reduce(fed[-1][0])
     early, incoming = [], []
     for batch in batches:
-        middle, active = fed[batch][:2]
+        middle, active = fed[batch]
         if batch:
-            active = after(active, early[-1])
-        early.append(output_forward(middle, active, reduce, params, infos[batch], slots))
-        incoming.append(shifted(early[batch], 1))
+            active = after(active, made[-1])
+        cuts = 2 if batch == 0 else 1
+        made, sent = [], []
+        for cut in range(cuts):
+            part = width // cuts
+            made.append(
+                output_forward(
+                    middle, after(active, *made), reduce, params, infos[batch], slots, LIGHT, (cut * part, part)
+                )
+            )
+            sent.append(shifted(made[-1], 1))
+        early.append(jnp.concatenate(made, axis=1))
+        incoming.append(jnp.concatenate(sent, axis=1))
 
     inner = wide[0][0].shape[1] - width
     mixed_at = inner + width
     kept, lefts, rights, results = [], [], [], []
     sums_a, sums_b, sums_c, returning = [], [], [], []
-    token = early[-1]
+    token = made[-1]
     for batch in batches:
         start = after(incoming[batch], token)
         left, packed, logs, middle, slope = forward(
@@ -1043,10 +1058,9 @@
         blocks = gradient("expand", inner, finals, 0, 0, share, (0, share), (index * step, step))
         run.add(f"expand{index}", blocks)
 
-    def qkv_part(index):
-        step = 3 * width // 2
+    def qkv_part(begin, size):
         at = inner + 2 * width
-        run.add(f"qkv{index}", gradient("qkv", at, grads, 0, at, share, (0, share), (index * step, step)))
+        return gradient("qkv", at, grads, 0, at, share, (0, share), (begin, size))
 
     reduce_part(0)
     start = run.now(arrived)
@@ -1072,11 +1086,10 @@
     results.append(result)
     sums_c.append(rest)
     run.step("expand0", "reduce1", "reduce0")
-    qkv_part(0)
+    project = gradient("project", mixed_at, branches, 0, inner, share, (0, share), (0, width), HEAVY)
+    mixed_part = qkv_part(0, width)
+    run.add("mixed", [jnp.concatenate(pair, axis=1) for pair in zip(project, mixed_part)])
     run.step("expand1", "expand0", "reduce1", "reduce0")
-    qkv_part(1)
-
-    run.step("qkv0", "expand1", "expand0", "reduce1", "qkv1", "qkv0")
 
     def over_batches(values):
         return sum(jnp.where(first, values[batch + 1], values[batch]) for batch in batches)
@@ -1089,19 +1102,19 @@
     rows = jnp.stack(
         [lax.dynamic_index_in_dim(rows, net.order[block], 0, keepdims=False) for block in net.blocks]
     )
-    count = rows.shape[1]
+    count, step = rows.shape[1], 2 * width
     rows = rows.reshape(len(net.blocks), -1)
-    rows = jnp.pad(rows, ((0, 0), (0, -rows.shape[1] % (16 * width)))).reshape(len(net.blocks), -1, width)
-    blocks = gradient("project", mixed_at, branches, 0, inner, share, (0, share), (0, width))
-    run.add("project", [jnp.concatenate([one, two]) for one, two in zip(blocks, rows.astype(BF16))])
-    run.step("expand1", "expand0", "qkv1", "project", "qkv0")
+    rows = jnp.pad(rows, ((0, 0), (0, -rows.shape[1] % (16 * step)))).reshape(len(net.blocks), -1, step)
+    blocks = qkv_part(width, step)
+    run.add("qkv", [jnp.concatenate([one, two]) for one, two in zip(blocks, rows.astype(BF16))])
+    run.step("mixed", "expand1", "expand0", "reduce1", "qkv", "mixed", "expand1", "expand0", "qkv")
     outputs = [
         images_of(jnp.where(first, run.now(low), up))
         for low, up in zip(early + results[1:], late + results[:-1])
     ]
-    run.step("expand1", "qkv1", "project", "qkv0", "project", "qkv1", "project")
+    run.step("mixed", "expand1", "qkv", "mixed", "qkv")
     weights = {name: run.finish(name) for name in run.sums}
-    vector = weights["project"][share:].reshape(-1)[: count * share].reshape(count, share).astype(F32)
+    vector = weights["qkv"][share:].reshape(-1)[: count * share].reshape(count, share).astype(F32)
 
     def joined(axis, *names):
         return jnp.concatenate([weights[name] for name in names], axis=axis).astype(F32)[None]
@@ -1109,8 +1122,8 @@
     return (
         jnp.stack(outputs[:micro])[None],
         jnp.stack(outputs[micro:])[None],
-        joined(1, "qkv0", "qkv1"),
-        weights["project"][:share].astype(F32)[None],
+        jnp.concatenate([weights["mixed"][:, width:], weights["qkv"][:share]], axis=1).astype(F32)[None],
+        weights["mixed"][:, :width].astype(F32)[None],
         joined(1, "expand0", "expand1"),
         joined(0, "reduce0", "reduce1"),
         vector[None, 0:2],

time: 651 us -> 677 us (1.040)
  waiting for transfers between devices: 105 us -> 139 us
  starting transfers between devices: 106 us -> 77.1 us
  Pallas kernels: 340 us -> 358 us
    ppermute x7 -> x6, waiting for transfers between devices: 1.56 us -> 48.6 us  [total(): inward = lax.ppermute(mine, 'replica', [(0, 1), (3, 2)])]
    ppermute x7 -> x6, starting transfers between devices: 57.5 us -> 31.8 us  [total(): inward = lax.ppermute(mine, 'replica', [(0, 1), (3, 2)])]
    ppermute x11 -> x10, waiting for transfers between devices: 51.2 us -> 32.1 us  [across(): return lax.ppermute(block, 'group', [(i, i ^ 2) for i in range(4)])]
    pallas_call x21 -> x22, Pallas kernels: 340 us -> 358 us  [call(): pl.pallas_call(body, out_shape=out_shape, in_specs=specs, out_specs=[VMEM...]
    ppermute x7 -> x6, waiting for transfers between devices: 33.3 us -> 43.3 us  [total(): outward = lax.ppermute(summed, 'replica', [(1, 0), (2, 3)])]
    convert_element_type x21 -> x18, other arithmetic: 27 us -> 26.3 us  [added(): return total.astype(values[0].dtype)]
    unnamed x102 -> x101, local copies, waits for them, and re-layouts: 14 us -> 14.2 us
  transfers between devices with their start and end apart: 59 -> 56, of which waited for: 21 -> 15; matrix products, arithmetic and copies ran while one was open for 11% -> 12% of each run, Pallas kernels for 46% -> 51%
where the time goes in v6:
time: 677 us; the launch traced here: 669 us
  Pallas kernels  358 us (53%)
  waiting for transfers between devices  139 us (21%)
  starting transfers between devices  77.1 us (11%)
  other arithmetic  62.6 us (9%)
  local copies, waits for them, and re-layouts  30.4 us (4%)
    pallas_call x22, Pallas kernels, call(): pl.pallas_call(body, out_shape=out_shape, in_specs=specs, out_specs=[VMEM...  358 us
    ppermute x6, waiting for transfers between devices, total(): inward = lax.ppermute(mine, 'replica', [(0, 1), (3, 2)])  48.6 us
    ppermute x6, waiting for transfers between devices, total(): outward = lax.ppermute(summed, 'replica', [(1, 0), (2, 3)])  43.3 us
    ppermute x10, waiting for transfers between devices, across(): return lax.ppermute(block, 'group', [(i, i ^ 2) for i in range(4)])  32.1 us
    ppermute x6, starting transfers between devices, total(): inward = lax.ppermute(mine, 'replica', [(0, 1), (3, 2)])  31.8 us
    convert_element_type x18, other arithmetic, added(): return total.astype(values[0].dtype)  26.3 us
    ppermute x20, waiting for transfers between devices, core(): return lax.ppermute(block, 'group', [(i, i ^ 1) for i in range(4)])  14.7 us
    unnamed x101, local copies, waits for them, and re-layouts  14.2 us
  transfers between devices with their start and end apart: 56, of which 15 were waited for; matrix products, arithmetic and copies ran while one was open for 12% of the time, Pallas kernels for 51%

profile of v6, /device:TPU:0, one launch (start us, length us, event | category | flops | bytes accessed | tf_op | source)
XLA Modules:
  0.0 668.9 jit_solution(16762978521702886029)
XLA Ops:
  18.0 9.8 %collective-permute-done.refs_3_.refs_4_.refs_27_.refs_34_.refs_14_ = bf16[128,3072]{1,0:T(8,128)(2,1)S(1)} collective-permute-done((bf16[128,3072]{1,0:T(8,128)(2,1)}, bf16[128,3072]{1,0:T(8,128)(2,1)S(1)}, u32[]{:S(2)}, u32[]{:S(2)}) %collective-permute-start) | collective-permute-done | bytes 786464 | tf_op jit(solution)/shard_map/ppermute | solution.py:762
  38.5 16.7 %collective-permute-done.9.refs_4_.refs_10_.refs_16_.refs_15_.refs_21_.refs_22_.refs_28_.refs_11_.refs_8_ = bf16[128,5120]{1,0:T(8,128)(2,1)} collective-permute-done((bf16[128,5120]{1,0:T(8,128)(2,1)}, bf16[128,5120]{1,0:T(8,128)(2,1)}, u32[]{:S(2)}, u32[]{:S(2)}) %collective-permute-start.9) | collective-permute-done | bytes 1310752 | tf_op jit(solution)/shard_map/ppermute | solution.py:762
  61.6 27.2 %forward_attend.2.refs_1_ = bf16[416,1024]{1,0:T(8,128)(2,1)} custom-call(bf16[416,1024]{1,0:T(8,128)(2,1)} %bitcast.115, bf16[256,3072]{1,0:T(8,128)(2,1)} %bitcast.102, bf16[256,3072]{1,0:T(8,128)(2,1)} %collective-permute-done.1.refs_2_.refs_3_.refs_26_.refs_33_.refs_13_, bf16[128,3072]{1,0:T(8,128)(2,1)} %copy-done.15, bf16[128,3072]{1,0:T(8,128)(2,1)} %copy-done.16, ...), custom_call_target="tpu_custom_call" | custom-call | flops 46432256 | bytes 125696 | tf_op jit(solution)/shard_map/forward_attend/pallas_call | solution.py:53
  88.8 15.7 %forward_attend.3.refs_1_ = bf16[416,1024]{1,0:T(8,128)(2,1)} custom-call(bf16[416,1024]{1,0:T(8,128)(2,1)} %bitcast.111, bf16[256,3072]{1,0:T(8,128)(2,1)} %bitcast.103, bf16[256,3072]{1,0:T(8,128)(2,1)} %collective-permute-done.1.refs_2_.refs_3_.refs_26_.refs_33_.refs_13_, bf16[128,3072]{1,0:T(8,128)(2,1)} %copy-done.15, bf16[128,3072]{1,0:T(8,128)(2,1)} %copy-done.16, ...), custom_call_target="tpu_custom_call" | custom-call | flops 46432256 | bytes 125696 | tf_op jit(solution)/shard_map/forward_attend/pallas_call | solution.py:53
  111.7 13.7 %forward_feed.2 = (f32[416,1024]{1,0:T(8,128)}, bf16[416,4096]{1,0:T(8,128)(2,1)}) custom-call(bf16[416,1024]{1,0:T(8,128)(2,1)} %bitcast.116, bf16[416,1024]{1,0:T(8,128)(2,1)} %forward_attend.2.refs_1_, bf16[256,5120]{1,0:T(8,128)(2,1)} %copy-done, bf16[256,5120]{1,0:T(8,128)(2,1)} %copy-done.1, ...), custom_call_target="tpu_custom_call" | custom-call | flops 68157440 | bytes 434944 | tf_op jit(solution)/shard_map/forward_feed/pallas_call | solution.py:53
  125.4 13.7 %forward_feed.3 = (f32[416,1024]{1,0:T(8,128)}, bf16[416,4096]{1,0:T(8,128)(2,1)}) custom-call(bf16[416,1024]{1,0:T(8,128)(2,1)} %bitcast.112, bf16[416,1024]{1,0:T(8,128)(2,1)} %forward_attend.3.refs_1_, bf16[256,5120]{1,0:T(8,128)(2,1)} %copy-done, bf16[256,5120]{1,0:T(8,128)(2,1)} %copy-done.1, ...), custom_call_target="tpu_custom_call" | custom-call | flops 68157440 | bytes 434944 | tf_op jit(solution)/shard_map/forward_feed/pallas_call | solution.py:53
  145.9 9.4 %output_forward.5 = bf16[416,512]{1,0:T(8,128)(2,1)} custom-call(f32[416,1024]{1,0:T(8,128)} %get-tuple-element.121.refs_0_, bf16[416,4096]{1,0:T(8,128)(2,1)} %get-tuple-element.128.refs_1_, bf16[1024,1024]{1,0:T(8,128)(2,1)} %bitcast.93, bf16[1024,1024]{1,0:T(8,128)(2,1)} %copy-done.3, ...), custom_call_target="tpu_custom_call" | custom-call | flops 27262976 | bytes 218368 | tf_op jit(solution)/shard_map/output_forward/pallas_call | solution.py:53
  158.8 9.0 %output_forward.6 = bf16[416,512]{1,0:T(8,128)(2,1)} custom-call(f32[416,1024]{1,0:T(8,128)} %get-tuple-element.121.refs_0_, bf16[416,4096]{1,0:T(8,128)(2,1)} %get-tuple-element.128.refs_1_, bf16[1024,1024]{1,0:T(8,128)(2,1)} %bitcast.94, bf16[1024,1024]{1,0:T(8,128)(2,1)} %copy-done.3, ...), custom_call_target="tpu_custom_call" | custom-call | flops 27262976 | bytes 218368 | tf_op jit(solution)/shard_map/output_forward/pallas_call | solution.py:53
  171.1 10.7 %output_forward.7 = bf16[416,1024]{1,0:T(8,128)(2,1)} custom-call(f32[416,1024]{1,0:T(8,128)} %get-tuple-element.125.refs_0_, bf16[416,4096]{1,0:T(8,128)(2,1)} %get-tuple-element.130.refs_1_, bf16[1024,1024]{1,0:T(8,128)(2,1)} %bitcast.95, bf16[1024,1024]{1,0:T(8,128)(2,1)} %copy-done.3, ...), custom_call_target="tpu_custom_call" | custom-call | flops 54525952 | bytes 225024 | tf_op jit(solution)/shard_map/output_forward/pallas_call | solution.py:53
  185.0 30.5 %forward_attend_feed.2 = (bf16[416,7168]{1,0:T(8,128)(2,1)}, bf16[416,3072]{1,0:T(8,128)(2,1)}, f32[2,16,208]{2,1,0:T(8,128)}, f32[416,1024]{1,0:T(8,128)}, bf16[416,4096]{1,0:T(8,128)(2,1)}) custom-call(bf16[416,1024]{1,0:T(8,128)(2,1)} %bitcast.117, bf16[416,1024]{1,0:T(8,128)(2,1)} %copy-done.32, bf16[256,3072]{1,0:T(8,128)(2,1)} %bitcast.104, ...), custom_call_target="tpu_custom_call" | custom-call | flops 58669924352 | bytes 341393824 | tf_op jit(solution)/shard_map/forward_attend_feed/pallas_call | solution.py:53
  215.6 37.0 %backward_feed_attend.2 = (bf16[416,9216]{1,0:T(8,128)(2,1)}, f32[8,1024]{1,0:T(8,128)}, f32[1,4096]{1,0:T(1,128)}, bf16[416,1024]{1,0:T(8,128)(2,1)}, f32[8,1024]{1,0:T(8,128)}) custom-call(bf16[416,1024]{1,0:T(8,128)(2,1)} %bitcast.134, bf16[416,4096]{1,0:T(8,128)(2,1)} %get-tuple-element.133.refs_1_.refs_0_, ...), custom_call_target="tpu_custom_call" | custom-call | flops 90840236032 | bytes 477315488 | tf_op jit(solution)/shard_map/backward_feed_attend/pallas_call | solution.py:53
  254.4 30.5 %forward_attend_feed.3 = (bf16[416,7168]{1,0:T(8,128)(2,1)}, bf16[416,3072]{1,0:T(8,128)(2,1)}, f32[2,16,208]{2,1,0:T(8,128)}, f32[416,1024]{1,0:T(8,128)}, bf16[416,4096]{1,0:T(8,128)(2,1)}) custom-call(bf16[416,1024]{1,0:T(8,128)(2,1)} %bitcast.113, bf16[416,1024]{1,0:T(8,128)(2,1)} %collective-permute-done.21.refs_1_.refs_13_, ...), custom_call_target="tpu_custom_call" | custom-call | flops 58669924352 | bytes 341393824 | tf_op jit(solution)/shard_map/forward_attend_feed/pallas_call | solution.py:53
  286.0 37.1 %backward_feed_attend.3 = (bf16[416,9216]{1,0:T(8,128)(2,1)}, f32[8,1024]{1,0:T(8,128)}, f32[1,4096]{1,0:T(1,128)}, bf16[416,1024]{1,0:T(8,128)(2,1)}, f32[8,1024]{1,0:T(8,128)}) custom-call(bf16[416,4096]{1,0:T(8,128)(2,1)} %get-tuple-element.133.refs_1_.refs_0_, bf16[416,4096]{1,0:T(8,128)(2,1)} %get-tuple-element.140.refs_1_, ...), custom_call_target="tpu_custom_call" | custom-call | flops 90840236032 | bytes 600211840 | tf_op jit(solution)/shard_map/backward_feed_attend/pallas_call | solution.py:53
  326.1 10.9 %output_forward.8 = bf16[416,1024]{1,0:T(8,128)(2,1)} custom-call(f32[416,1024]{1,0:T(8,128)} %get-tuple-element.134.refs_2_.refs_0_, bf16[416,7168]{1,0:T(8,128)(2,1)} %get-tuple-element.147.refs_4_.refs_8_.refs_1_.refs_0_, bf16[1024,1024]{1,0:T(8,128)(2,1)} %bitcast.98, bf16[1024,1024]{1,0:T(8,128)(2,1)} %copy-done.3, ...), custom_call_target="tpu_custom_call" | custom-call | flops 27917287424 | bytes 135659936 | tf_op jit(solution)/shard_map/output_forward/pallas_call | solution.py:53
  336.9 10.7 %output_forward.9 = bf16[416,1024]{1,0:T(8,128)(2,1)} custom-call(f32[416,1024]{1,0:T(8,128)} %get-tuple-element.141.refs_3_.refs_0_.refs_2_, bf16[416,7168]{1,0:T(8,128)(2,1)} %get-tuple-element.148.refs_9_.refs_1_.refs_2_.refs_3_, bf16[1024,1024]{1,0:T(8,128)(2,1)} %bitcast.99, bf16[1024,1024]{1,0:T(8,128)(2,1)} %copy-done.3, ...), custom_call_target="tpu_custom_call" | custom-call | flops 27917287424 | bytes 135659936 | tf_op jit(solution)/shard_map/output_forward/pallas_call | solution.py:53
  351.1 8.9 %reduce.11 = (bf16[512,1024]{1,0:T(8,128)(2,1)}, bf16[512,1024]{1,0:T(8,128)(2,1)}) custom-call(bf16[416,7168]{1,0:T(8,128)(2,1)} %get-tuple-element.147.refs_4_.refs_8_.refs_1_.refs_0_, bf16[416,7168]{1,0:T(8,128)(2,1)} %collective-permute-done.20.refs_1_, bf16[416,7168]{1,0:T(8,128)(2,1)} %get-tuple-element.148.refs_9_.refs_1_.refs_2_.refs_3_, ...), custom_call_target="tpu_custom_call" | custom-call | flops 54525952 | bytes 911360 | tf_op jit(solution)/shard_map/reduce/pallas_call | solution.py:53
  361.6 18.3 %backward_feed.1 = (bf16[416,4096]{1,0:T(8,128)(2,1)}, bf16[416,1024]{1,0:T(8,128)(2,1)}, f32[8,1024]{1,0:T(8,128)}, f32[1,4096]{1,0:T(1,128)}, f32[416,1024]{1,0:T(8,128)}) custom-call(bf16[416,1024]{1,0:T(8,128)(2,1)} %copy-done.13, bf16[416,4096]{1,0:T(8,128)(2,1)} %get-tuple-element.140.refs_1_, f32[416,1024]{1,0:T(8,128)} %get-tuple-element.141.refs_3_.refs_0_.refs_2_, ...), custom_call_target="tpu_custom_call" | custom-call | flops 109051904 | bytes 482816 | tf_op jit(solution)/shard_map/backward_feed/pallas_call | solution.py:53
  387.0 9.0 %reduce.12 = (bf16[512,1024]{1,0:T(8,128)(2,1)}, bf16[512,1024]{1,0:T(8,128)(2,1)}) custom-call(bf16[416,7168]{1,0:T(8,128)(2,1)} %get-tuple-element.147.refs_4_.refs_8_.refs_1_.refs_0_, bf16[416,7168]{1,0:T(8,128)(2,1)} %collective-permute-done.20.refs_1_, bf16[416,7168]{1,0:T(8,128)(2,1)} %get-tuple-element.148.refs_9_.refs_1_.refs_2_.refs_3_, ...), custom_call_target="tpu_custom_call" | custom-call | flops 55834574848 | bytes 933232960 | tf_op jit(solution)/shard_map/reduce/pallas_call | solution.py:53
  404.9 9.3 %expand.2 = (bf16[256,2048]{1,0:T(8,128)(2,1)}, bf16[256,2048]{1,0:T(8,128)(2,1)}) custom-call(bf16[416,7168]{1,0:T(8,128)(2,1)} %get-tuple-element.147.refs_4_.refs_8_.refs_1_.refs_0_, bf16[416,7168]{1,0:T(8,128)(2,1)} %collective-permute-done.20.refs_1_, bf16[416,7168]{1,0:T(8,128)(2,1)} %get-tuple-element.148.refs_9_.refs_1_.refs_2_.refs_3_, ...), custom_call_target="tpu_custom_call" | custom-call | flops 54525952 | bytes 991232 | tf_op jit(solution)/shard_map/expand/pallas_call | solution.py:53
  414.2 9.5 %expand.3 = (bf16[256,2048]{1,0:T(8,128)(2,1)}, bf16[256,2048]{1,0:T(8,128)(2,1)}) custom-call(bf16[416,7168]{1,0:T(8,128)(2,1)} %get-tuple-element.147.refs_4_.refs_8_.refs_1_.refs_0_, bf16[416,7168]{1,0:T(8,128)(2,1)} %collective-permute-done.20.refs_1_, bf16[416,7168]{1,0:T(8,128)(2,1)} %get-tuple-element.148.refs_9_.refs_1_.refs_2_.refs_3_, ...), custom_call_target="tpu_custom_call" | custom-call | flops 54525952 | bytes 991232 | tf_op jit(solution)/shard_map/expand/pallas_call | solution.py:53
  434.1 24.6 %backward_attend.1 = (bf16[416,3072]{1,0:T(8,128)(2,1)}, bf16[416,1024]{1,0:T(8,128)(2,1)}, f32[8,1024]{1,0:T(8,128)}) custom-call(bf16[416,1024]{1,0:T(8,128)(2,1)} %get-tuple-element.167.refs_0_.refs_8_, f32[416,1024]{1,0:T(8,128)} %get-tuple-element.168.refs_1_, bf16[416,3072]{1,0:T(8,128)(2,1)} %get-tuple-element.142.refs_7_.refs_2_, ...), custom_call_target="tpu_custom_call" | custom-call | flops 70011322368 | bytes 515539776 | tf_op jit(solution)/shard_map/backward_attend/pallas_call | solution.py:53
  471.0 10.9 %collective-permute-start.38 = (bf16[256,2048]{1,0:T(8,128)(2,1)S(1)}, bf16[256,2048]{1,0:T(8,128)(2,1)}, u32[]{:S(2)}, u32[]{:S(2)}) collective-permute-start(bf16[256,2048]{1,0:T(8,128)(2,1)S(1)} %add_convert_fusion.14), channel_id=1, source_target_pairs={{0,1},{3,2},{4,5},{7,6},{8,9},{11,10},{12,13},{15,14},{16,17},{19,... | collective-permute-start | bytes 3145736 | tf_op jit(solution)/shard_map/ppermute | solution.py:806
  481.9 6.3 project.1
  489.7 6.3 qkv.2
  514.3 7.1 %collective-permute-start.43 = (bf16[256,2048]{1,0:T(8,128)(2,1)S(1)}, bf16[256,2048]{1,0:T(8,128)(2,1)}, u32[]{:S(2)}, u32[]{:S(2)}) collective-permute-start(bf16[256,2048]{1,0:T(8,128)(2,1)S(1)} %add_convert_fusion.11), channel_id=1, source_target_pairs={{0,1},{3,2},{4,5},{7,6},{8,9},{11,10},{12,13},{15,14},{16,17},{19,... | collective-permute-start | bytes 3145736 | tf_op jit(solution)/shard_map/ppermute | solution.py:806
  521.4 9.5 %qkv.3 = (bf16[256,2048]{1,0:T(8,128)(2,1)}, bf16[256,2048]{1,0:T(8,128)(2,1)}) custom-call(bf16[416,7168]{1,0:T(8,128)(2,1)} %get-tuple-element.147.refs_4_.refs_8_.refs_1_.refs_0_, bf16[416,7168]{1,0:T(8,128)(2,1)} %collective-permute-done.20.refs_1_, bf16[416,7168]{1,0:T(8,128)(2,1)} %get-tuple-element.148.refs_9_.refs_1_.refs_2_.refs_3_, ...), custom_call_target="tpu_custom_call" | custom-call | flops 54525952 | bytes 964608 | tf_op jit(solution)/shard_map/qkv/pallas_call | solution.py:53
  536.1 7.0 %collective-permute-done.43 = bf16[256,2048]{1,0:T(8,128)(2,1)} collective-permute-done((bf16[256,2048]{1,0:T(8,128)(2,1)S(1)}, bf16[256,2048]{1,0:T(8,128)(2,1)}, u32[]{:S(2)}, u32[]{:S(2)}) %collective-permute-start.43) | collective-permute-done | bytes 1048608 | tf_op jit(solution)/shard_map/ppermute | solution.py:806
  548.6 7.6 %collective-permute-start.47 = (bf16[256,2048]{1,0:T(8,128)(2,1)S(1)}, bf16[256,2048]{1,0:T(8,128)(2,1)S(1)}, u32[]{:S(2)}, u32[]{:S(2)}) collective-permute-start(bf16[256,2048]{1,0:T(8,128)(2,1)S(1)} %add_convert_fusion.8), channel_id=1, source_target_pairs={{0,1},{3,2},{4,5},{7,6},{8,9},{11,10},{12,13},{15,14},{16,17},{19,... | collective-permute-start | bytes 3145736 | tf_op jit(solution)/shard_map/ppermute | solution.py:806
  562.0 17.7 %collective-permute-done.47 = bf16[256,2048]{1,0:T(8,128)(2,1)S(1)} collective-permute-done((bf16[256,2048]{1,0:T(8,128)(2,1)S(1)}, bf16[256,2048]{1,0:T(8,128)(2,1)S(1)}, u32[]{:S(2)}, u32[]{:S(2)}) %collective-permute-start.47) | collective-permute-done | bytes 1048608 | tf_op jit(solution)/shard_map/ppermute | solution.py:806
  582.7 18.9 %collective-permute-done.50 = bf16[272,2048]{1,0:T(8,128)(2,1)S(1)} collective-permute-done((bf16[272,2048]{1,0:T(8,128)(2,1)S(1)}, bf16[272,2048]{1,0:T(8,128)(2,1)S(1)}, u32[]{:S(2)}, u32[]{:S(2)}) %collective-permute-start.50) | collective-permute-done | bytes 1114144 | tf_op jit(solution)/shard_map/ppermute | solution.py:806
  620.0 23.6 %collective-permute-done.54 = bf16[256,2048]{1,0:T(8,128)(2,1)S(1)} collective-permute-done((bf16[256,2048]{1,0:T(8,128)(2,1)S(1)}, bf16[256,2048]{1,0:T(8,128)(2,1)S(1)}, u32[]{:S(2)}, u32[]{:S(2)}) %collective-permute-start.54) | collective-permute-done | bytes 1048608 | tf_op jit(solution)/shard_map/ppermute | solution.py:812
  644.9 19.7 %collective-permute-done.55 = bf16[272,2048]{1,0:T(8,128)(2,1)S(1)} collective-permute-done((bf16[272,2048]{1,0:T(8,128)(2,1)S(1)}, bf16[272,2048]{1,0:T(8,128)(2,1)S(1)}, u32[]{:S(2)}, u32[]{:S(2)}) %collective-permute-start.55) | collective-permute-done | bytes 1114144 | tf_op jit(solution)/shard_map/ppermute | solution.py:812
  (299 shorter events, 169.8 us)
Async XLA Ops:
  10.0 45.2 %collective-permute-start.9 = (bf16[128,5120]{1,0:T(8,128)(2,1)}, bf16[128,5120]{1,0:T(8,128)(2,1)}, u32[]{:S(2)}, u32[]{:S(2)}) collective-permute-start(bf16[128,5120]{1,0:T(8,128)(2,1)} %fusion), channel_id=1, source_target_pairs={{0,8},{4,12},{8,0},{12,4},{1,9},{5,13},{9,1},{13,5},{2,10},{6,14},... | collective-permute-start | bytes 3932168 | tf_op jit(solution)/shard_map/ppermute | solution.py:762
  17.6 87.7 %collective-permute-start.8 = (bf16[256,5120]{1,0:T(8,128)(2,1)S(1)}, bf16[256,5120]{1,0:T(8,128)(2,1)S(1)}, u32[]{:S(2)}, u32[]{:S(2)}) collective-permute-start(bf16[256,5120]{1,0:T(8,128)(2,1)S(1)} %pad_maximum_fusion.refs_2_.refs_8_.refs_14_.refs_13_.refs_19_.refs_20_.refs_26_.refs_9_.refs_6_), channel_id=1, source_target_pairs={{0,4},{4,0},{8,12},{12,8},{1,5},{5,1},{9,13},{13,9},{2,6},{6,2},{1... | collective-permute-start | bytes 7864328 | tf_op jit(solution)/shard_map/ppermute | solution.py:759
  55.2 49.5 %collective-permute-start.10 = (bf16[128,5120]{1,0:T(8,128)(2,1)}, bf16[128,5120]{1,0:T(8,128)(2,1)}, u32[]{:S(2)}, u32[]{:S(2)}) collective-permute-start(bf16[128,5120]{1,0:T(8,128)(2,1)} %collective-permute-done.9.refs_4_.refs_10_.refs_16_.refs_15_.refs_21_.refs_22_.refs_28_.refs_11_.refs_8_), channel_id=1, source_target_pairs={{0,1},{1,0},{2,3},{3,2},{4,5},{5,4},{6,7},{7,6},{8,9},{9,8},{10,11... | collective-permute-start | bytes 3932168 | tf_op jit(solution)/shard_map/ppermute | solution.py:765
  56.8 32.0 %collective-permute-start.11 = (bf16[512,1024]{1,0:T(8,128)(2,1)}, bf16[512,1024]{1,0:T(8,128)(2,1)}, u32[]{:S(2)}, u32[]{:S(2)}) collective-permute-start(bf16[512,1024]{1,0:T(8,128)(2,1)} %dynamic-slice_bitcast_fusion), channel_id=1, source_target_pairs={{0,8},{4,12},{8,0},{12,4},{1,9},{5,13},{9,1},{13,5},{2,10},{6,14},... | collective-permute-start | bytes 3145736 | tf_op jit(solution)/shard_map/ppermute | solution.py:762
  105.1 34.0 %collective-permute-start.15 = (bf16[512,1024]{1,0:T(8,128)(2,1)}, bf16[512,1024]{1,0:T(8,128)(2,1)}, u32[]{:S(2)}, u32[]{:S(2)}) collective-permute-start(bf16[512,1024]{1,0:T(8,128)(2,1)} %collective-permute-done.11.refs_4_.refs_9_.refs_16_.refs_5_), channel_id=1, source_target_pairs={{0,1},{1,0},{2,3},{3,2},{4,5},{5,4},{6,7},{7,6},{8,9},{9,8},{10,11... | collective-permute-start | bytes 3145736 | tf_op jit(solution)/shard_map/ppermute | solution.py:765
  105.3 38.3 %collective-permute-start.14 = (bf16[1024,1024]{1,0:T(8,128)(2,1)}, bf16[1024,1024]{1,0:T(8,128)(2,1)S(1)}, u32[]{:S(2)}, u32[]{:S(2)}) collective-permute-start(bf16[1024,1024]{1,0:T(8,128)(2,1)} %bitcast.92), channel_id=1, source_target_pairs={{0,4},{4,0},{8,12},{12,8},{1,5},{5,1},{9,13},{13,9},{2,6},{6,2},{1... | collective-permute-start | bytes 6291464 | tf_op jit(solution)/shard_map/ppermute | solution.py:759
  155.3 28.6 %collective-permute-start.18 = (bf16[416,512]{1,0:T(8,128)(2,1)}, bf16[416,512]{1,0:T(8,128)(2,1)S(1)}, u32[]{:S(2)}, u32[]{:S(2)}) collective-permute-start(bf16[416,512]{1,0:T(8,128)(2,1)} %output_forward.5), channel_id=1, source_target_pairs={{0,16},{1,17},{2,18},{3,19},{4,20},{5,21},{6,22},{7,23},{8,24},{9,... | collective-permute-start | bytes 1277960 | tf_op jit(solution)/shard_map/ppermute | solution.py:847
  181.7 72.7 %collective-permute-start.21 = (bf16[416,1024]{1,0:T(8,128)(2,1)}, bf16[416,1024]{1,0:T(8,128)(2,1)}, u32[]{:S(2)}, u32[]{:S(2)}) collective-permute-start(bf16[416,1024]{1,0:T(8,128)(2,1)} %output_forward.7), channel_id=1, source_target_pairs={{0,16},{1,17},{2,18},{3,19},{4,20},{5,21},{6,22},{7,23},{8,24},{9,... | collective-permute-start | bytes 2555912 | tf_op jit(solution)/shard_map/ppermute | solution.py:847
  215.5 110.5 %collective-permute-start.20 = (bf16[416,7168]{1,0:T(8,128)(2,1)}, bf16[416,7168]{1,0:T(8,128)(2,1)}, u32[]{:S(2)}, u32[]{:S(2)}) collective-permute-start(bf16[416,7168]{1,0:T(8,128)(2,1)} %get-tuple-element.147.refs_4_.refs_8_.refs_1_.refs_0_), channel_id=1, source_target_pairs={{0,4},{4,0},{8,12},{12,8},{1,5},{5,1},{9,13},{13,9},{2,6},{6,2},{1... | collective-permute-start | bytes 17891336 | tf_op jit(solution)/shard_map/ppermute | solution.py:759
  252.6 32.4 %collective-permute-start.23 = (bf16[416,1024]{1,0:T(8,128)(2,1)}, bf16[416,1024]{1,0:T(8,128)(2,1)S(1)}, u32[]{:S(2)}, u32[]{:S(2)}) collective-permute-start(bf16[416,1024]{1,0:T(8,128)(2,1)} %get-tuple-element.137), channel_id=1, source_target_pairs={{16,0},{17,1},{18,2},{19,3},{20,4},{21,5},{22,6},{23,7},{24,8},{25... | collective-permute-start | bytes 2555912 | tf_op jit(solution)/shard_map/ppermute | solution.py:847
  253.9 72.1 %collective-permute-start.25 = (bf16[416,9216]{1,0:T(8,128)(2,1)}, bf16[416,9216]{1,0:T(8,128)(2,1)}, u32[]{:S(2)}, u32[]{:S(2)}) collective-permute-start(bf16[416,9216]{1,0:T(8,128)(2,1)} %get-tuple-element.145.refs_5_), channel_id=1, source_target_pairs={{0,4},{4,0},{8,12},{12,8},{1,5},{5,1},{9,13},{13,9},{2,6},{6,2},{1... | collective-permute-start | bytes 23003144 | tf_op jit(solution)/shard_map/ppermute | solution.py:759
  284.9 52.0 %collective-permute-start.22 = (bf16[416,7168]{1,0:T(8,128)(2,1)}, bf16[416,7168]{1,0:T(8,128)(2,1)}, u32[]{:S(2)}, u32[]{:S(2)}) collective-permute-start(bf16[416,7168]{1,0:T(8,128)(2,1)} %get-tuple-element.148.refs_9_.refs_1_.refs_2_.refs_3_), channel_id=1, source_target_pairs={{0,4},{4,0},{8,12},{12,8},{1,5},{5,1},{9,13},{13,9},{2,6},{6,2},{1... | collective-permute-start | bytes 17891336 | tf_op jit(solution)/shard_map/ppermute | solution.py:759
  396.0 27.7 %collective-permute-start.31 = (bf16[512,1024]{1,0:T(8,128)(2,1)}, bf16[512,1024]{1,0:T(8,128)(2,1)}, u32[]{:S(2)}, u32[]{:S(2)}) collective-permute-start(bf16[512,1024]{1,0:T(8,128)(2,1)} %get-tuple-element.165), channel_id=1, source_target_pairs={{0,8},{4,12},{8,0},{12,4},{1,9},{5,13},{9,1},{13,5},{2,10},{6,14},... | collective-permute-start | bytes 3145736 | tf_op jit(solution)/shard_map/ppermute | solution.py:762
  397.6 31.0 %collective-permute-start.32 = (bf16[512,1024]{1,0:T(8,128)(2,1)}, bf16[512,1024]{1,0:T(8,128)(2,1)}, u32[]{:S(2)}, u32[]{:S(2)}) collective-permute-start(bf16[512,1024]{1,0:T(8,128)(2,1)} %add_convert_fusion.17), channel_id=1, source_target_pairs={{0,1},{3,2},{4,5},{7,6},{8,9},{11,10},{12,13},{15,14},{16,17},{19,... | collective-permute-start | bytes 3145736 | tf_op jit(solution)/shard_map/ppermute | solution.py:806
  426.3 36.8 %collective-permute-start.35 = (bf16[512,1024]{1,0:T(8,128)(2,1)}, bf16[512,1024]{1,0:T(8,128)(2,1)}, u32[]{:S(2)}, u32[]{:S(2)}) collective-permute-start(bf16[512,1024]{1,0:T(8,128)(2,1)} %add_convert_fusion.16), channel_id=1, source_target_pairs={{0,1},{3,2},{4,5},{7,6},{8,9},{11,10},{12,13},{15,14},{16,17},{19,... | collective-permute-start | bytes 3145736 | tf_op jit(solution)/shard_map/ppermute | solution.py:806
  431.6 33.5 %collective-permute-start.36 = (bf16[512,1024]{1,0:T(8,128)(2,1)}, bf16[512,1024]{1,0:T(8,128)(2,1)}, u32[]{:S(2)}, u32[]{:S(2)}) collective-permute-start(bf16[512,1024]{1,0:T(8,128)(2,1)} %add_convert_fusion.15), channel_id=1, source_target_pairs={{1,2},{2,1},{5,6},{6,5},{9,10},{10,9},{13,14},{14,13},{17,18},{18,... | collective-permute-start | bytes 3145736 | tf_op jit(solution)/shard_map/ppermute | solution.py:809
  433.5 27.7 %collective-permute-start.34 = (bf16[256,2048]{1,0:T(8,128)(2,1)}, bf16[256,2048]{1,0:T(8,128)(2,1)}, u32[]{:S(2)}, u32[]{:S(2)}) collective-permute-start(bf16[256,2048]{1,0:T(8,128)(2,1)} %get-tuple-element.172), channel_id=1, source_target_pairs={{0,8},{4,12},{8,0},{12,4},{1,9},{5,13},{9,1},{13,5},{2,10},{6,14},... | collective-permute-start | bytes 3145736 | tf_op jit(solution)/shard_map/ppermute | solution.py:762
  459.5 36.5 %collective-permute-start.37 = (bf16[256,2048]{1,0:T(8,128)(2,1)}, bf16[256,2048]{1,0:T(8,128)(2,1)}, u32[]{:S(2)}, u32[]{:S(2)}) collective-permute-start(bf16[256,2048]{1,0:T(8,128)(2,1)} %get-tuple-element.180), channel_id=1, source_target_pairs={{0,8},{4,12},{8,0},{12,4},{1,9},{5,13},{9,1},{13,5},{2,10},{6,14},... | collective-permute-start | bytes 3145736 | tf_op jit(solution)/shard_map/ppermute | solution.py:762
  468.0 40.0 %collective-permute-start.40 = (bf16[512,1024]{1,0:T(8,128)(2,1)}, bf16[512,1024]{1,0:T(8,128)(2,1)}, u32[]{:S(2)}, u32[]{:S(2)}) collective-permute-start(bf16[512,1024]{1,0:T(8,128)(2,1)} %add_convert_fusion.12), channel_id=1, source_target_pairs={{1,0},{2,3},{5,4},{6,7},{9,8},{10,11},{13,12},{14,15},{17,16},{18,... | collective-permute-start | bytes 3145736 | tf_op jit(solution)/shard_map/ppermute | solution.py:812
  469.3 35.4 %collective-permute-start.39 = (bf16[512,1024]{1,0:T(8,128)(2,1)S(1)}, bf16[512,1024]{1,0:T(8,128)(2,1)}, u32[]{:S(2)}, u32[]{:S(2)}) collective-permute-start(bf16[512,1024]{1,0:T(8,128)(2,1)S(1)} %add_convert_fusion.13), channel_id=1, source_target_pairs={{1,2},{2,1},{5,6},{6,5},{9,10},{10,9},{13,14},{14,13},{17,18},{18,... | collective-permute-start | bytes 3145736 | tf_op jit(solution)/shard_map/ppermute | solution.py:809
  471.0 32.0 %collective-permute-start.38 = (bf16[256,2048]{1,0:T(8,128)(2,1)S(1)}, bf16[256,2048]{1,0:T(8,128)(2,1)}, u32[]{:S(2)}, u32[]{:S(2)}) collective-permute-start(bf16[256,2048]{1,0:T(8,128)(2,1)S(1)} %add_convert_fusion.14), channel_id=1, source_target_pairs={{0,1},{3,2},{4,5},{7,6},{8,9},{11,10},{12,13},{15,14},{16,17},{19,... | collective-permute-start | bytes 3145736 | tf_op jit(solution)/shard_map/ppermute | solution.py:806
  511.4 44.8 %collective-permute-start.45 = (bf16[512,1024]{1,0:T(8,128)(2,1)S(1)}, bf16[512,1024]{1,0:T(8,128)(2,1)}, u32[]{:S(2)}, u32[]{:S(2)}) collective-permute-start(bf16[512,1024]{1,0:T(8,128)(2,1)S(1)} %add_convert_fusion.9), channel_id=1, source_target_pairs={{1,0},{2,3},{5,4},{6,7},{9,8},{10,11},{13,12},{14,15},{17,16},{18,... | collective-permute-start | bytes 3145736 | tf_op jit(solution)/shard_map/ppermute | solution.py:812
  512.7 32.1 %collective-permute-start.44 = (bf16[256,2048]{1,0:T(8,128)(2,1)S(1)}, bf16[256,2048]{1,0:T(8,128)(2,1)}, u32[]{:S(2)}, u32[]{:S(2)}) collective-permute-start(bf16[256,2048]{1,0:T(8,128)(2,1)S(1)} %add_convert_fusion.10), channel_id=1, source_target_pairs={{1,2},{2,1},{5,6},{6,5},{9,10},{10,9},{13,14},{14,13},{17,18},{18,... | collective-permute-start | bytes 3145736 | tf_op jit(solution)/shard_map/ppermute | solution.py:809
  514.3 28.8 %collective-permute-start.43 = (bf16[256,2048]{1,0:T(8,128)(2,1)S(1)}, bf16[256,2048]{1,0:T(8,128)(2,1)}, u32[]{:S(2)}, u32[]{:S(2)}) collective-permute-start(bf16[256,2048]{1,0:T(8,128)(2,1)S(1)} %add_convert_fusion.11), channel_id=1, source_target_pairs={{0,1},{3,2},{4,5},{7,6},{8,9},{11,10},{12,13},{15,14},{16,17},{19,... | collective-permute-start | bytes 3145736 | tf_op jit(solution)/shard_map/ppermute | solution.py:806
  546.4 36.1 %collective-permute-start.49 = (bf16[256,2048]{1,0:T(8,128)(2,1)S(1)}, bf16[256,2048]{1,0:T(8,128)(2,1)S(1)}, u32[]{:S(2)}, u32[]{:S(2)}) collective-permute-start(bf16[256,2048]{1,0:T(8,128)(2,1)S(1)} %add_convert_fusion.6), channel_id=1, source_target_pairs={{1,0},{2,3},{5,4},{6,7},{9,8},{10,11},{13,12},{14,15},{17,16},{18,... | collective-permute-start | bytes 3145736 | tf_op jit(solution)/shard_map/ppermute | solution.py:812
  547.9 32.3 %collective-permute-start.48 = (bf16[256,2048]{1,0:T(8,128)(2,1)S(1)}, bf16[256,2048]{1,0:T(8,128)(2,1)S(1)}, u32[]{:S(2)}, u32[]{:S(2)}) collective-permute-start(bf16[256,2048]{1,0:T(8,128)(2,1)S(1)} %add_convert_fusion.7), channel_id=1, source_target_pairs={{1,2},{2,1},{5,6},{6,5},{9,10},{10,9},{13,14},{14,13},{17,18},{18,... | collective-permute-start | bytes 3145736 | tf_op jit(solution)/shard_map/ppermute | solution.py:809
  548.6 31.1 %collective-permute-start.47 = (bf16[256,2048]{1,0:T(8,128)(2,1)S(1)}, bf16[256,2048]{1,0:T(8,128)(2,1)S(1)}, u32[]{:S(2)}, u32[]{:S(2)}) collective-permute-start(bf16[256,2048]{1,0:T(8,128)(2,1)S(1)} %add_convert_fusion.8), channel_id=1, source_target_pairs={{0,1},{3,2},{4,5},{7,6},{8,9},{11,10},{12,13},{15,14},{16,17},{19,... | collective-permute-start | bytes 3145736 | tf_op jit(solution)/shard_map/ppermute | solution.py:806
  560.5 41.1 %collective-permute-start.50 = (bf16[272,2048]{1,0:T(8,128)(2,1)S(1)}, bf16[272,2048]{1,0:T(8,128)(2,1)S(1)}, u32[]{:S(2)}, u32[]{:S(2)}) collective-permute-start(bf16[272,2048]{1,0:T(8,128)(2,1)S(1)} %add_convert_fusion.2), channel_id=1, source_target_pairs={{0,1},{3,2},{4,5},{7,6},{8,9},{11,10},{12,13},{15,14},{16,17},{19,... | collective-permute-start | bytes 3342344 | tf_op jit(solution)/shard_map/ppermute | solution.py:806
  580.6 35.1 %collective-permute-start.52 = (bf16[256,2048]{1,0:T(8,128)(2,1)S(1)}, bf16[256,2048]{1,0:T(8,128)(2,1)S(1)}, u32[]{:S(2)}, u32[]{:S(2)}) collective-permute-start(bf16[256,2048]{1,0:T(8,128)(2,1)S(1)} %add_convert_fusion.4), channel_id=1, source_target_pairs={{1,0},{2,3},{5,4},{6,7},{9,8},{10,11},{13,12},{14,15},{17,16},{18,... | collective-permute-start | bytes 3145736 | tf_op jit(solution)/shard_map/ppermute | solution.py:812
  581.9 32.1 %collective-permute-start.51 = (bf16[256,2048]{1,0:T(8,128)(2,1)S(1)}, bf16[256,2048]{1,0:T(8,128)(2,1)S(1)}, u32[]{:S(2)}, u32[]{:S(2)}) collective-permute-start(bf16[256,2048]{1,0:T(8,128)(2,1)S(1)} %add_convert_fusion.5), channel_id=1, source_target_pairs={{1,2},{2,1},{5,6},{6,5},{9,10},{10,9},{13,14},{14,13},{17,18},{18,... | collective-permute-start | bytes 3145736 | tf_op jit(solution)/shard_map/ppermute | solution.py:809
  614.3 29.3 %collective-permute-start.54 = (bf16[256,2048]{1,0:T(8,128)(2,1)S(1)}, bf16[256,2048]{1,0:T(8,128)(2,1)S(1)}, u32[]{:S(2)}, u32[]{:S(2)}) collective-permute-start(bf16[256,2048]{1,0:T(8,128)(2,1)S(1)} %add_convert_fusion.3), channel_id=1, source_target_pairs={{1,0},{2,3},{5,4},{6,7},{9,8},{10,11},{13,12},{14,15},{17,16},{18,... | collective-permute-start | bytes 3145736 | tf_op jit(solution)/shard_map/ppermute | solution.py:812
  616.2 48.4 %collective-permute-start.55 = (bf16[272,2048]{1,0:T(8,128)(2,1)S(1)}, bf16[272,2048]{1,0:T(8,128)(2,1)S(1)}, u32[]{:S(2)}, u32[]{:S(2)}) collective-permute-start(bf16[272,2048]{1,0:T(8,128)(2,1)S(1)} %add_convert_fusion), channel_id=1, source_target_pairs={{1,0},{2,3},{5,4},{6,7},{9,8},{10,11},{13,12},{14,15},{17,16},{18,... | collective-permute-start | bytes 3342344 | tf_op jit(solution)/shard_map/ppermute | solution.py:812
  (68 other events, 715.5 us)

commit v7 on v6

--- a/solution.py
+++ b/solution.py
@@ -13,6 +13,20 @@
 F32 = jnp.float32
 BF16 = jnp.bfloat16
 LIGHT, HEAVY = 1.0 / 64, 16.0
+PLAN = (
+    "R0 BF r0 R1*",
+    "BA r0 r1 E0*",
+    "Q0 r0 r1 e0",
+    "E1 q0 r0 r1",
+    "e0 Q1 e1 q0",
+    "r1 e0 V P0",
+    "q1 e1 q0 e0",
+    "p0 O q1 e1",
+    "q0 p0 O O",
+    "q1 e1 p0 O",
+    "q1 p0",
+)
+LAST = "P0"
 VMEM_LIMIT = 58 * 2**20
 ROOT_HALF = 0.7071067811865476
 ROOT_TAU = 0.3989422804014327
@@ -1046,86 +1060,128 @@
         run.ran(blocks[0])
         return blocks
 
-    def reduce_part(index, weight=LIGHT):
-        step = inner // parts // 2
-        blocks = gradient(
-            "reduce", 0, masked, 0, inner + width, inner // parts, (index * step, step), (0, width), weight
+    half, at = inner // 2, inner + 2 * width
+    deep = inner // parts
+    state = {"mid": None, "rows": None}
+
+    def feed_back(weight):
+        start = run.now(arrived)
+        hidden, branch, some, more, mid = backward(
+            (start, start), None, None, kept[last], kept[last], reduce, wide, None, params, infos[last],
+            slots, length, mixed_at, weight,
         )
-        run.add(f"reduce{index}", blocks)
-
-    def expand_part(index):
-        step = inner // 2
-        blocks = gradient("expand", inner, finals, 0, 0, share, (0, share), (index * step, step))
-        run.add(f"expand{index}", blocks)
-
-    def qkv_part(begin, size):
-        at = inner + 2 * width
-        return gradient("qkv", at, grads, 0, at, share, (0, share), (begin, size))
-
-    reduce_part(0)
-    start = run.now(arrived)
-    final, branch, some, more, mid = backward(
-        (start, start), None, None, kept[last], kept[last], reduce, wide, None, params, infos[last],
-        slots, length, mixed_at,
-    )
-    run.ran(final)
-    finals, branches = net.shared(final), net.shared(branch)
-    sums_a.append(some)
-    sums_b.append(more)
-    run.step("reduce0")
-    reduce_part(1, HEAVY)
-    expand_part(0)
-    expand_part(1)
-    run.step("reduce1", "reduce0")
-    grads, result, rest = backward(
-        (run.now(after(branch, *branches[1:])), mid), inputs[last], inputs[last], kept[last], kept[last], None, wide, qkv,
-        params, infos[last], slots, length, mixed_at, HEAVY,
-    )
-    run.ran(result)
-    grads = net.shared(grads)
-    results.append(result)
-    sums_c.append(rest)
-    run.step("expand0", "reduce1", "reduce0")
-    project = gradient("project", mixed_at, branches, 0, inner, share, (0, share), (0, width), HEAVY)
-    mixed_part = qkv_part(0, width)
-    run.add("mixed", [jnp.concatenate(pair, axis=1) for pair in zip(project, mixed_part)])
-    run.step("expand1", "expand0", "reduce1", "reduce0")
+        run.ran(hidden)
+        state.update(mid=mid, branch=branch, hidden=net.shared(hidden), branches=net.shared(branch))
+        sums_a.append(some)
+        sums_b.append(more)
+
+    def attend_back(weight):
+        start = run.now(after(state["branch"], *state["branches"][1:], *state["hidden"][1:]))
+        grads, result, rest = backward(
+            (start, state["mid"]), inputs[last], inputs[last], kept[last], kept[last], None, wide, qkv,
+            params, infos[last], slots, length, mixed_at, weight,
+        )
+        run.ran(result)
+        state["grads"] = net.shared(grads)
+        results.append(result)
+        sums_c.append(rest)
+
+    def reduce_part(index, weight):
+        step = deep // 2
+        return gradient(
+            "reduce", 0, masked, 0, inner + width, deep, (index * step, step), (0, width), weight
+        )
+
+    def expand_part(begin, size, weight):
+        return gradient("expand", inner, state["hidden"], 0, 0, share, (0, share), (begin, size), weight)
+
+    def project_part(weight):
+        return gradient(
+            "project", mixed_at, state["branches"], 0, inner, share, (0, share), (0, width), weight
+        )
+
+    def qkv_part(begin, size, weight):
+        return gradient("qkv", at, state["grads"], 0, at, share, (0, share), (begin, size), weight)
 
     def over_batches(values):
         return sum(jnp.where(first, values[batch + 1], values[batch]) for batch in batches)
 
-    some, more, rest = over_batches(sums_a), over_batches(sums_b), over_batches(sums_c)
-    rows = jnp.concatenate([rest[0:1], some[0:1], rest[1:2], some[1:2], rest[2:4], some[2:4]])
-    rows = rows.reshape(8, parts, share).transpose(1, 0, 2)
-    rows = jnp.concatenate([rows, more.reshape(parts, -1, share)], axis=1)
-    rows = sum(net.shared(run.now(rows)))
-    rows = jnp.stack(
-        [lax.dynamic_index_in_dim(rows, net.order[block], 0, keepdims=False) for block in net.blocks]
-    )
-    count, step = rows.shape[1], 2 * width
-    rows = rows.reshape(len(net.blocks), -1)
-    rows = jnp.pad(rows, ((0, 0), (0, -rows.shape[1] % (16 * step)))).reshape(len(net.blocks), -1, step)
-    blocks = qkv_part(width, step)
-    run.add("qkv", [jnp.concatenate([one, two]) for one, two in zip(blocks, rows.astype(BF16))])
-    run.step("mixed", "expand1", "expand0", "reduce1", "qkv", "mixed", "expand1", "expand0", "qkv")
-    outputs = [
-        images_of(jnp.where(first, run.now(low), up))
-        for low, up in zip(early + results[1:], late + results[:-1])
-    ]
-    run.step("mixed", "expand1", "qkv", "mixed", "qkv")
-    weights = {name: run.finish(name) for name in run.sums}
-    vector = weights["qkv"][share:].reshape(-1)[: count * share].reshape(count, share).astype(F32)
+    def small_sums():
+        some, more, rest = over_batches(sums_a), over_batches(sums_b), over_batches(sums_c)
+        rows = jnp.concatenate([rest[0:1], some[0:1], rest[1:2], some[1:2], rest[2:4], some[2:4]])
+        rows = rows.reshape(8, parts, share).transpose(1, 0, 2)
+        rows = jnp.concatenate([rows, more.reshape(parts, -1, share)], axis=1)
+        rows = sum(net.shared(run.now(rows)))
+        rows = jnp.stack(
+            [lax.dynamic_index_in_dim(rows, net.order[block], 0, keepdims=False) for block in net.blocks]
+        )
+        state["count"] = rows.shape[1]
+        state["rows"] = rows.reshape(len(net.blocks), -1).astype(BF16)
+
+    def with_small(blocks):
+        step, rows = blocks[0].shape[1], state["rows"]
+        rows = jnp.pad(rows, ((0, 0), (0, -rows.shape[1] % (16 * step)))).reshape(len(blocks), -1, step)
+        return [jnp.concatenate([block, row]) for block, row in zip(blocks, rows)]
+
+    outputs = []
+
+    def assemble():
+        index = len(outputs)
+        low, up = (early + results[1:])[index], (late + results[:-1])[index]
+        outputs.append(images_of(jnp.where(first, run.now(low), up)))
 
     def joined(axis, *names):
-        return jnp.concatenate([weights[name] for name in names], axis=axis).astype(F32)[None]
-
+        found = [run.finish(name) for name in names]
+        found = [value[:share] if name == LAST.lower() else value for name, value in zip(names, found)]
+        return jnp.concatenate(found, axis=axis).astype(F32)[None]
+
+    shapes = {"q": (1, "q0", "q1"), "p": (1, "p0"), "e": (1, "e0", "e1"), "r": (0, "r0", "r1")}
+    gradients = {}
+
+    third = 3 * width // 2
+    kernels = {
+        "R0": lambda weight: reduce_part(0, weight),
+        "R1": lambda weight: reduce_part(1, weight),
+        "E0": lambda weight: expand_part(0, half, weight),
+        "E1": lambda weight: expand_part(half, half, weight),
+        "Q0": lambda weight: qkv_part(0, third, weight),
+        "Q1": lambda weight: qkv_part(third, third, weight),
+        "P0": lambda weight: project_part(weight),
+    }
+    for entry in " ".join(PLAN).split():
+        name, _, factor = entry.partition("*")
+        weight = float(factor or HEAVY) if "*" in entry else LIGHT
+        if name in kernels:
+            blocks = kernels[name](weight)
+            if name == LAST:
+                blocks = with_small(blocks)
+            run.add(name.lower(), blocks)
+        elif name == "BF":
+            feed_back(weight)
+        elif name == "BA":
+            attend_back(weight)
+        elif name == "V":
+            small_sums()
+        elif name == "O":
+            assemble()
+        elif name[0] == "C":
+            gradients[name[1]] = joined(*shapes[name[1]])
+        else:
+            run.step(name)
+    while len(outputs) < 2 * micro:
+        assemble()
+    for name in shapes:
+        if name not in gradients:
+            gradients[name] = joined(*shapes[name])
+    count = state["count"]
+    vector = run.finish(LAST.lower())[share:].reshape(-1)[: count * share].reshape(count, share).astype(F32)
     return (
         jnp.stack(outputs[:micro])[None],
         jnp.stack(outputs[micro:])[None],
-        jnp.concatenate([weights["mixed"][:, width:], weights["qkv"][:share]], axis=1).astype(F32)[None],
-        weights["mixed"][:, :width].astype(F32)[None],
-        joined(1, "expand0", "expand1"),
-        joined(0, "reduce0", "reduce1"),
+        gradients["q"],
+        gradients["p"],
+        gradients["e"],
+        gradients["r"],
         vector[None, 0:2],
         vector[None, 2:8],
         vector[8:].reshape(1, -1),

time: 677 us -> 634 us (0.936)
  waiting for transfers between devices: 139 us -> 111 us
  Pallas kernels: 358 us -> 346 us
    ppermute x6 -> x7, waiting for transfers between devices: 48.6 us -> 8.03 us  [total(): inward = lax.ppermute(mine, 'replica', [(0, 1), (3, 2)])]
    ppermute x10 -> x11, waiting for transfers between devices: 32.1 us -> 45.3 us  [across(): return lax.ppermute(block, 'group', [(i, i ^ 2) for i in range(4)])]
    pallas_call x22, Pallas kernels: 358 us -> 346 us  [call(): pl.pallas_call(body, out_shape=out_shape, in_specs=specs, out_specs=[VMEM...]
    ppermute x6 -> x7, starting transfers between devices: 31.8 us -> 27.7 us  [total(): inward = lax.ppermute(mine, 'replica', [(0, 1), (3, 2)])]
    convert_element_type x18 -> x21, other arithmetic: 26.3 us -> 28.2 us  [added(): return total.astype(values[0].dtype)]
    ppermute x6 -> x7, waiting for transfers between devices: 43.3 us -> 42.8 us  [total(): outward = lax.ppermute(summed, 'replica', [(1, 0), (2, 3)])]
  transfers between devices with their start and end apart: 56 -> 60, of which waited for: 15 -> 20; matrix products, arithmetic and copies ran while one was open for 12% -> 12% of each run, Pallas kernels for 51% -> 52%
where the time goes in v7:
time: 634 us; the launch traced here: 626 us
  Pallas kernels  346 us (55%)
  waiting for transfers between devices  111 us (18%)
  starting transfers between devices  79.6 us (13%)
  other arithmetic  60.5 us (10%)
  local copies, waits for them, and re-layouts  26.7 us (4%)
    pallas_call x22, Pallas kernels, call(): pl.pallas_call(body, out_shape=out_shape, in_specs=specs, out_specs=[VMEM...  346 us
    ppermute x11, waiting for transfers between devices, across(): return lax.ppermute(block, 'group', [(i, i ^ 2) for i in range(4)])  45.3 us
    ppermute x7, waiting for transfers between devices, total(): outward = lax.ppermute(summed, 'replica', [(1, 0), (2, 3)])  42.8 us
    convert_element_type x21, other arithmetic, added(): return total.astype(values[0].dtype)  28.2 us
    ppermute x7, starting transfers between devices, total(): inward = lax.ppermute(mine, 'replica', [(0, 1), (3, 2)])  27.7 us
    ppermute x20, waiting for transfers between devices, core(): return lax.ppermute(block, 'group', [(i, i ^ 1) for i in range(4)])  14.4 us
    ppermute x11, starting transfers between devices, across(): return lax.ppermute(block, 'group', [(i, i ^ 2) for i in range(4)])  13.4 us
  transfers between devices with their start and end apart: 60, of which 20 were waited for; matrix products, arithmetic and copies ran while one was open for 12% of the time, Pallas kernels for 52%

profile of v7, /device:TPU:0, one launch (start us, length us, event | category | flops | bytes accessed | tf_op | source)
XLA Modules:
  0.0 625.9 jit_solution(13929798538480510122)
XLA Ops:
  18.0 9.8 %collective-permute-done.refs_3_.refs_4_.refs_27_.refs_34_.refs_14_ = bf16[128,3072]{1,0:T(8,128)(2,1)S(1)} collective-permute-done((bf16[128,3072]{1,0:T(8,128)(2,1)}, bf16[128,3072]{1,0:T(8,128)(2,1)S(1)}, u32[]{:S(2)}, u32[]{:S(2)}) %collective-permute-start) | collective-permute-done | bytes 786464 | tf_op jit(solution)/shard_map/ppermute | solution.py:776
  38.4 16.8 %collective-permute-done.9.refs_4_.refs_10_.refs_16_.refs_15_.refs_21_.refs_22_.refs_28_.refs_11_.refs_8_ = bf16[128,5120]{1,0:T(8,128)(2,1)} collective-permute-done((bf16[128,5120]{1,0:T(8,128)(2,1)}, bf16[128,5120]{1,0:T(8,128)(2,1)}, u32[]{:S(2)}, u32[]{:S(2)}) %collective-permute-start.9) | collective-permute-done | bytes 1310752 | tf_op jit(solution)/shard_map/ppermute | solution.py:776
  61.6 16.2 %forward_attend.2.refs_1_ = bf16[416,1024]{1,0:T(8,128)(2,1)} custom-call(bf16[416,1024]{1,0:T(8,128)(2,1)} %bitcast.109, bf16[256,3072]{1,0:T(8,128)(2,1)} %bitcast.96, bf16[256,3072]{1,0:T(8,128)(2,1)} %collective-permute-done.1.refs_2_.refs_3_.refs_26_.refs_33_.refs_13_, bf16[128,3072]{1,0:T(8,128)(2,1)} %copy-done.8, bf16[128,3072]{1,0:T(8,128)(2,1)} %copy-done.9, ...), custom_call_target="tpu_custom_call" | custom-call | flops 46432256 | bytes 125696 | tf_op jit(solution)/shard_map/forward_attend/pallas_call | solution.py:67
  81.2 15.7 %forward_attend.3.refs_1_ = bf16[416,1024]{1,0:T(8,128)(2,1)} custom-call(bf16[416,1024]{1,0:T(8,128)(2,1)} %bitcast.103, bf16[256,3072]{1,0:T(8,128)(2,1)} %bitcast.97, bf16[256,3072]{1,0:T(8,128)(2,1)} %collective-permute-done.1.refs_2_.refs_3_.refs_26_.refs_33_.refs_13_, bf16[128,3072]{1,0:T(8,128)(2,1)} %copy-done.8, bf16[128,3072]{1,0:T(8,128)(2,1)} %copy-done.9, ...), custom_call_target="tpu_custom_call" | custom-call | flops 46432256 | bytes 125696 | tf_op jit(solution)/shard_map/forward_attend/pallas_call | solution.py:67
  104.2 13.7 %forward_feed.2 = (f32[416,1024]{1,0:T(8,128)}, bf16[416,4096]{1,0:T(8,128)(2,1)}) custom-call(bf16[416,1024]{1,0:T(8,128)(2,1)} %bitcast.110, bf16[416,1024]{1,0:T(8,128)(2,1)} %forward_attend.2.refs_1_, bf16[256,5120]{1,0:T(8,128)(2,1)} %copy-done, bf16[256,5120]{1,0:T(8,128)(2,1)} %copy-done.1, ...), custom_call_target="tpu_custom_call" | custom-call | flops 68157440 | bytes 434944 | tf_op jit(solution)/shard_map/forward_feed/pallas_call | solution.py:67
  117.9 13.7 %forward_feed.3 = (f32[416,1024]{1,0:T(8,128)}, bf16[416,4096]{1,0:T(8,128)(2,1)}) custom-call(bf16[416,1024]{1,0:T(8,128)(2,1)} %bitcast.104, bf16[416,1024]{1,0:T(8,128)(2,1)} %forward_attend.3.refs_1_, bf16[256,5120]{1,0:T(8,128)(2,1)} %copy-done, bf16[256,5120]{1,0:T(8,128)(2,1)} %copy-done.1, ...), custom_call_target="tpu_custom_call" | custom-call | flops 68157440 | bytes 434944 | tf_op jit(solution)/shard_map/forward_feed/pallas_call | solution.py:67
  138.3 9.2 %output_forward.5 = bf16[416,512]{1,0:T(8,128)(2,1)} custom-call(f32[416,1024]{1,0:T(8,128)} %get-tuple-element.125.refs_0_, bf16[416,4096]{1,0:T(8,128)(2,1)} %get-tuple-element.132.refs_1_, bf16[1024,1024]{1,0:T(8,128)(2,1)} %bitcast.87, bf16[1024,1024]{1,0:T(8,128)(2,1)} %copy-done.3, ...), custom_call_target="tpu_custom_call" | custom-call | flops 27262976 | bytes 218368 | tf_op jit(solution)/shard_map/output_forward/pallas_call | solution.py:67
  151.0 9.1 %output_forward.6 = bf16[416,512]{1,0:T(8,128)(2,1)} custom-call(f32[416,1024]{1,0:T(8,128)} %get-tuple-element.125.refs_0_, bf16[416,4096]{1,0:T(8,128)(2,1)} %get-tuple-element.132.refs_1_, bf16[1024,1024]{1,0:T(8,128)(2,1)} %bitcast.88, bf16[1024,1024]{1,0:T(8,128)(2,1)} %copy-done.3, ...), custom_call_target="tpu_custom_call" | custom-call | flops 27262976 | bytes 218368 | tf_op jit(solution)/shard_map/output_forward/pallas_call | solution.py:67
  163.2 10.7 %output_forward.7 = bf16[416,1024]{1,0:T(8,128)(2,1)} custom-call(f32[416,1024]{1,0:T(8,128)} %get-tuple-element.129.refs_0_, bf16[416,4096]{1,0:T(8,128)(2,1)} %get-tuple-element.134.refs_1_, bf16[1024,1024]{1,0:T(8,128)(2,1)} %bitcast.89, bf16[1024,1024]{1,0:T(8,128)(2,1)} %copy-done.3, ...), custom_call_target="tpu_custom_call" | custom-call | flops 54525952 | bytes 225024 | tf_op jit(solution)/shard_map/output_forward/pallas_call | solution.py:67
  177.2 30.6 %forward_attend_feed.2 = (bf16[416,7168]{1,0:T(8,128)(2,1)}, bf16[416,3072]{1,0:T(8,128)(2,1)}, f32[2,16,208]{2,1,0:T(8,128)}, f32[416,1024]{1,0:T(8,128)}, bf16[416,4096]{1,0:T(8,128)(2,1)}) custom-call(bf16[416,1024]{1,0:T(8,128)(2,1)} %bitcast.111, bf16[416,1024]{1,0:T(8,128)(2,1)} %copy-done.31, bf16[256,3072]{1,0:T(8,128)(2,1)} %bitcast.98, ...), custom_call_target="tpu_custom_call" | custom-call | flops 58669924352 | bytes 341393824 | tf_op jit(solution)/shard_map/forward_attend_feed/pallas_call | solution.py:67
  207.8 37.0 %backward_feed_attend.2 = (bf16[416,9216]{1,0:T(8,128)(2,1)}, f32[8,1024]{1,0:T(8,128)}, f32[1,4096]{1,0:T(1,128)}, bf16[416,1024]{1,0:T(8,128)(2,1)}, f32[8,1024]{1,0:T(8,128)}) custom-call(bf16[416,1024]{1,0:T(8,128)(2,1)} %bitcast.130, bf16[416,4096]{1,0:T(8,128)(2,1)} %get-tuple-element.137.refs_1_.refs_0_, ...), custom_call_target="tpu_custom_call" | custom-call | flops 90840236032 | bytes 477315488 | tf_op jit(solution)/shard_map/backward_feed_attend/pallas_call | solution.py:67
  246.6 30.5 %forward_attend_feed.3 = (bf16[416,7168]{1,0:T(8,128)(2,1)}, bf16[416,3072]{1,0:T(8,128)(2,1)}, f32[2,16,208]{2,1,0:T(8,128)}, f32[416,1024]{1,0:T(8,128)}, bf16[416,4096]{1,0:T(8,128)(2,1)}) custom-call(bf16[416,1024]{1,0:T(8,128)(2,1)} %bitcast.105, bf16[416,1024]{1,0:T(8,128)(2,1)} %collective-permute-done.21.refs_1_.refs_13_, ...), custom_call_target="tpu_custom_call" | custom-call | flops 58669924352 | bytes 341393824 | tf_op jit(solution)/shard_map/forward_attend_feed/pallas_call | solution.py:67
  278.2 37.0 %backward_feed_attend.3 = (bf16[416,9216]{1,0:T(8,128)(2,1)}, f32[8,1024]{1,0:T(8,128)}, f32[1,4096]{1,0:T(1,128)}, bf16[416,1024]{1,0:T(8,128)(2,1)}, f32[8,1024]{1,0:T(8,128)}) custom-call(bf16[416,4096]{1,0:T(8,128)(2,1)} %get-tuple-element.137.refs_1_.refs_0_, bf16[416,4096]{1,0:T(8,128)(2,1)} %get-tuple-element.144.refs_1_, ...), custom_call_target="tpu_custom_call" | custom-call | flops 90840236032 | bytes 600211840 | tf_op jit(solution)/shard_map/backward_feed_attend/pallas_call | solution.py:67
  318.2 10.7 %output_forward.8 = bf16[416,1024]{1,0:T(8,128)(2,1)} custom-call(f32[416,1024]{1,0:T(8,128)} %get-tuple-element.138.refs_2_.refs_0_, bf16[416,7168]{1,0:T(8,128)(2,1)} %get-tuple-element.151.refs_4_.refs_8_.refs_1_.refs_0_, bf16[1024,1024]{1,0:T(8,128)(2,1)} %bitcast.92, bf16[1024,1024]{1,0:T(8,128)(2,1)} %copy-done.3, ...), custom_call_target="tpu_custom_call" | custom-call | flops 27917287424 | bytes 135659936 | tf_op jit(solution)/shard_map/output_forward/pallas_call | solution.py:67
  328.9 10.7 %output_forward.9 = bf16[416,1024]{1,0:T(8,128)(2,1)} custom-call(f32[416,1024]{1,0:T(8,128)} %get-tuple-element.145.refs_3_.refs_0_.refs_2_, bf16[416,7168]{1,0:T(8,128)(2,1)} %get-tuple-element.152.refs_9_.refs_1_.refs_2_.refs_3_, bf16[1024,1024]{1,0:T(8,128)(2,1)} %bitcast.93, bf16[1024,1024]{1,0:T(8,128)(2,1)} %copy-done.3, ...), custom_call_target="tpu_custom_call" | custom-call | flops 27917287424 | bytes 135659936 | tf_op jit(solution)/shard_map/output_forward/pallas_call | solution.py:67
  343.2 8.9 %reduce.11 = (bf16[512,1024]{1,0:T(8,128)(2,1)}, bf16[512,1024]{1,0:T(8,128)(2,1)}) custom-call(bf16[416,7168]{1,0:T(8,128)(2,1)} %get-tuple-element.151.refs_4_.refs_8_.refs_1_.refs_0_, bf16[416,7168]{1,0:T(8,128)(2,1)} %collective-permute-done.20.refs_1_, bf16[416,7168]{1,0:T(8,128)(2,1)} %get-tuple-element.152.refs_9_.refs_1_.refs_2_.refs_3_, ...), custom_call_target="tpu_custom_call" | custom-call | flops 54525952 | bytes 911360 | tf_op jit(solution)/shard_map/reduce/pallas_call | solution.py:67
  352.7 18.3 %backward_feed.1 = (bf16[416,4096]{1,0:T(8,128)(2,1)}, bf16[416,1024]{1,0:T(8,128)(2,1)}, f32[8,1024]{1,0:T(8,128)}, f32[1,4096]{1,0:T(1,128)}, f32[416,1024]{1,0:T(8,128)}) custom-call(bf16[416,1024]{1,0:T(8,128)(2,1)} %copy-done.15, bf16[416,4096]{1,0:T(8,128)(2,1)} %get-tuple-element.144.refs_1_, f32[416,1024]{1,0:T(8,128)} %get-tuple-element.145.refs_3_.refs_0_.refs_2_, ...), custom_call_target="tpu_custom_call" | custom-call | flops 109051904 | bytes 482816 | tf_op jit(solution)/shard_map/backward_feed/pallas_call | solution.py:67
  371.7 6.0 collective-permute-done.30
  379.6 8.9 %reduce.12 = (bf16[512,1024]{1,0:T(8,128)(2,1)}, bf16[512,1024]{1,0:T(8,128)(2,1)}) custom-call(bf16[416,7168]{1,0:T(8,128)(2,1)} %get-tuple-element.151.refs_4_.refs_8_.refs_1_.refs_0_, bf16[416,7168]{1,0:T(8,128)(2,1)} %collective-permute-done.20.refs_1_, bf16[416,7168]{1,0:T(8,128)(2,1)} %get-tuple-element.152.refs_9_.refs_1_.refs_2_.refs_3_, ...), custom_call_target="tpu_custom_call" | custom-call | flops 55834574848 | bytes 933232960 | tf_op jit(solution)/shard_map/reduce/pallas_call | solution.py:67
  390.4 24.6 %backward_attend.1 = (bf16[416,3072]{1,0:T(8,128)(2,1)}, bf16[416,1024]{1,0:T(8,128)(2,1)}, f32[8,1024]{1,0:T(8,128)}) custom-call(bf16[416,1024]{1,0:T(8,128)(2,1)} %get-tuple-element.164.refs_0_.refs_8_, f32[416,1024]{1,0:T(8,128)} %get-tuple-element.165.refs_1_, bf16[416,3072]{1,0:T(8,128)(2,1)} %get-tuple-element.146.refs_7_.refs_2_, ...), custom_call_target="tpu_custom_call" | custom-call | flops 68370432 | bytes 503456 | tf_op jit(solution)/shard_map/backward_attend/pallas_call | solution.py:67
  423.4 9.3 %expand.2 = (bf16[256,2048]{1,0:T(8,128)(2,1)}, bf16[256,2048]{1,0:T(8,128)(2,1)}) custom-call(bf16[416,7168]{1,0:T(8,128)(2,1)} %get-tuple-element.151.refs_4_.refs_8_.refs_1_.refs_0_, bf16[416,7168]{1,0:T(8,128)(2,1)} %collective-permute-done.20.refs_1_, bf16[416,7168]{1,0:T(8,128)(2,1)} %get-tuple-element.152.refs_9_.refs_1_.refs_2_.refs_3_, ...), custom_call_target="tpu_custom_call" | custom-call | flops 55834574848 | bytes 1015021888 | tf_op jit(solution)/shard_map/expand/pallas_call | solution.py:67
  434.4 7.9 %qkv.2 = (bf16[256,1536]{1,0:T(8,128)(2,1)}, bf16[256,1536]{1,0:T(8,128)(2,1)}) custom-call(bf16[416,7168]{1,0:T(8,128)(2,1)} %get-tuple-element.151.refs_4_.refs_8_.refs_1_.refs_0_, bf16[416,7168]{1,0:T(8,128)(2,1)} %collective-permute-done.20.refs_1_, bf16[416,7168]{1,0:T(8,128)(2,1)} %get-tuple-element.152.refs_9_.refs_1_.refs_2_.refs_3_, ...), custom_call_target="tpu_custom_call" | custom-call | flops 40894464 | bytes 956416 | tf_op jit(solution)/shard_map/qkv/pallas_call | solution.py:67
  449.8 9.3 %collective-permute-done.36 = bf16[256,2048]{1,0:T(8,128)(2,1)} collective-permute-done((bf16[256,2048]{1,0:T(8,128)(2,1)}, bf16[256,2048]{1,0:T(8,128)(2,1)}, u32[]{:S(2)}, u32[]{:S(2)}) %collective-permute-start.36) | collective-permute-done | bytes 1048608 | tf_op jit(solution)/shard_map/ppermute | solution.py:776
  460.7 5.4 collective-permute-start.40
  466.2 9.4 %expand.3 = (bf16[256,2048]{1,0:T(8,128)(2,1)}, bf16[256,2048]{1,0:T(8,128)(2,1)}) custom-call(bf16[416,7168]{1,0:T(8,128)(2,1)} %get-tuple-element.151.refs_4_.refs_8_.refs_1_.refs_0_, bf16[416,7168]{1,0:T(8,128)(2,1)} %collective-permute-done.20.refs_1_, bf16[416,7168]{1,0:T(8,128)(2,1)} %get-tuple-element.152.refs_9_.refs_1_.refs_2_.refs_3_, ...), custom_call_target="tpu_custom_call" | custom-call | flops 54525952 | bytes 991232 | tf_op jit(solution)/shard_map/expand/pallas_call | solution.py:67
  493.9 7.8 %qkv.3 = (bf16[256,1536]{1,0:T(8,128)(2,1)}, bf16[256,1536]{1,0:T(8,128)(2,1)}) custom-call(bf16[416,7168]{1,0:T(8,128)(2,1)} %get-tuple-element.151.refs_4_.refs_8_.refs_1_.refs_0_, bf16[416,7168]{1,0:T(8,128)(2,1)} %collective-permute-done.20.refs_1_, bf16[416,7168]{1,0:T(8,128)(2,1)} %get-tuple-element.152.refs_9_.refs_1_.refs_2_.refs_3_, ...), custom_call_target="tpu_custom_call" | custom-call | flops 40894464 | bytes 956416 | tf_op jit(solution)/shard_map/qkv/pallas_call | solution.py:67
  503.3 7.5 %collective-permute-start.47 = (bf16[256,2048]{1,0:T(8,128)(2,1)S(1)}, bf16[256,2048]{1,0:T(8,128)(2,1)}, u32[]{:S(2)}, u32[]{:S(2)}) collective-permute-start(bf16[256,2048]{1,0:T(8,128)(2,1)S(1)} %add_convert_fusion.3), channel_id=1, source_target_pairs={{0,1},{3,2},{4,5},{7,6},{8,9},{11,10},{12,13},{15,14},{16,17},{19,... | collective-permute-start | bytes 3145736 | tf_op jit(solution)/shard_map/ppermute | solution.py:820
  521.4 6.4 %project.1 = (bf16[256,1024]{1,0:T(8,128)(2,1)}, bf16[256,1024]{1,0:T(8,128)(2,1)}) custom-call(bf16[416,7168]{1,0:T(8,128)(2,1)} %get-tuple-element.151.refs_4_.refs_8_.refs_1_.refs_0_, bf16[416,7168]{1,0:T(8,128)(2,1)} %collective-permute-done.20.refs_1_, bf16[416,7168]{1,0:T(8,128)(2,1)} %get-tuple-element.152.refs_9_.refs_1_.refs_2_.refs_3_, ...), custom_call_target="tpu_custom_call" | custom-call | flops 27262976 | bytes 894976 | tf_op jit(solution)/shard_map/project/pallas_call | solution.py:67
  546.0 10.7 %collective-permute-done.49 = bf16[256,2048]{1,0:T(8,128)(2,1)} collective-permute-done((bf16[256,2048]{1,0:T(8,128)(2,1)S(1)}, bf16[256,2048]{1,0:T(8,128)(2,1)}, u32[]{:S(2)}, u32[]{:S(2)}) %collective-permute-start.49) | collective-permute-done | bytes 1048608 | tf_op jit(solution)/shard_map/ppermute | solution.py:826
  582.9 12.3 %collective-permute-done.56 = bf16[256,2048]{1,0:T(8,128)(2,1)S(1)} collective-permute-done((bf16[256,2048]{1,0:T(8,128)(2,1)S(1)}, bf16[256,2048]{1,0:T(8,128)(2,1)S(1)}, u32[]{:S(2)}, u32[]{:S(2)}) %collective-permute-start.56) | collective-permute-done | bytes 1048608 | tf_op jit(solution)/shard_map/ppermute | solution.py:826
  605.1 7.0 %collective-permute-done.58 = bf16[256,1536]{1,0:T(8,128)(2,1)S(1)} collective-permute-done((bf16[256,1536]{1,0:T(8,128)(2,1)S(1)}, bf16[256,1536]{1,0:T(8,128)(2,1)S(1)}, u32[]{:S(2)}, u32[]{:S(2)}) %collective-permute-start.58) | collective-permute-done | bytes 786464 | tf_op jit(solution)/shard_map/ppermute | solution.py:826
  614.2 8.5 %collective-permute-done.59 = bf16[272,1024]{1,0:T(8,128)(2,1)S(1)} collective-permute-done((bf16[272,1024]{1,0:T(8,128)(2,1)S(1)}, bf16[272,1024]{1,0:T(8,128)(2,1)S(1)}, u32[]{:S(2)}, u32[]{:S(2)}) %collective-permute-start.59) | collective-permute-done | bytes 557088 | tf_op jit(solution)/shard_map/ppermute | solution.py:826
  (308 shorter events, 184.2 us)
Async XLA Ops:
  10.0 45.2 %collective-permute-start.9 = (bf16[128,5120]{1,0:T(8,128)(2,1)}, bf16[128,5120]{1,0:T(8,128)(2,1)}, u32[]{:S(2)}, u32[]{:S(2)}) collective-permute-start(bf16[128,5120]{1,0:T(8,128)(2,1)} %fusion), channel_id=1, source_target_pairs={{0,8},{4,12},{8,0},{12,4},{1,9},{5,13},{9,1},{13,5},{2,10},{6,14},... | collective-permute-start | bytes 3932168 | tf_op jit(solution)/shard_map/ppermute | solution.py:776
  17.6 80.4 %collective-permute-start.8 = (bf16[256,5120]{1,0:T(8,128)(2,1)S(1)}, bf16[256,5120]{1,0:T(8,128)(2,1)S(1)}, u32[]{:S(2)}, u32[]{:S(2)}) collective-permute-start(bf16[256,5120]{1,0:T(8,128)(2,1)S(1)} %pad_maximum_fusion.refs_2_.refs_8_.refs_14_.refs_13_.refs_19_.refs_20_.refs_26_.refs_9_.refs_6_), channel_id=1, source_target_pairs={{0,4},{4,0},{8,12},{12,8},{1,5},{5,1},{9,13},{13,9},{2,6},{6,2},{1... | collective-permute-start | bytes 7864328 | tf_op jit(solution)/shard_map/ppermute | solution.py:773
  27.8 27.4 %collective-permute-start.2 = (bf16[128,3072]{1,0:T(8,128)(2,1)S(1)}, bf16[128,3072]{1,0:T(8,128)(2,1)S(1)}, u32[]{:S(2)}, u32[]{:S(2)}) collective-permute-start(bf16[128,3072]{1,0:T(8,128)(2,1)S(1)} %collective-permute-done.refs_3_.refs_4_.refs_27_.refs_34_.refs_14_), channel_id=1, source_target_pairs={{0,1},{1,0},{2,3},{3,2},{4,5},{5,4},{6,7},{7,6},{8,9},{9,8},{10,11... | collective-permute-start | bytes 2359304 | tf_op jit(solution)/shard_map/ppermute | solution.py:779
  55.2 41.8 %collective-permute-start.10 = (bf16[128,5120]{1,0:T(8,128)(2,1)}, bf16[128,5120]{1,0:T(8,128)(2,1)}, u32[]{:S(2)}, u32[]{:S(2)}) collective-permute-start(bf16[128,5120]{1,0:T(8,128)(2,1)} %collective-permute-done.9.refs_4_.refs_10_.refs_16_.refs_15_.refs_21_.refs_22_.refs_28_.refs_11_.refs_8_), channel_id=1, source_target_pairs={{0,1},{1,0},{2,3},{3,2},{4,5},{5,4},{6,7},{7,6},{8,9},{9,8},{10,11... | collective-permute-start | bytes 3932168 | tf_op jit(solution)/shard_map/ppermute | solution.py:779
  97.6 34.0 %collective-permute-start.15 = (bf16[512,1024]{1,0:T(8,128)(2,1)}, bf16[512,1024]{1,0:T(8,128)(2,1)}, u32[]{:S(2)}, u32[]{:S(2)}) collective-permute-start(bf16[512,1024]{1,0:T(8,128)(2,1)} %collective-permute-done.11.refs_4_.refs_9_.refs_16_.refs_5_), channel_id=1, source_target_pairs={{0,1},{1,0},{2,3},{3,2},{4,5},{5,4},{6,7},{7,6},{8,9},{9,8},{10,11... | collective-permute-start | bytes 3145736 | tf_op jit(solution)/shard_map/ppermute | solution.py:779
  98.0 38.0 %collective-permute-start.14 = (bf16[1024,1024]{1,0:T(8,128)(2,1)}, bf16[1024,1024]{1,0:T(8,128)(2,1)S(1)}, u32[]{:S(2)}, u32[]{:S(2)}) collective-permute-start(bf16[1024,1024]{1,0:T(8,128)(2,1)} %bitcast.86), channel_id=1, source_target_pairs={{0,4},{4,0},{8,12},{12,8},{1,5},{5,1},{9,13},{13,9},{2,6},{6,2},{1... | collective-permute-start | bytes 6291464 | tf_op jit(solution)/shard_map/ppermute | solution.py:773
  147.5 28.6 %collective-permute-start.18 = (bf16[416,512]{1,0:T(8,128)(2,1)}, bf16[416,512]{1,0:T(8,128)(2,1)S(1)}, u32[]{:S(2)}, u32[]{:S(2)}) collective-permute-start(bf16[416,512]{1,0:T(8,128)(2,1)} %output_forward.5), channel_id=1, source_target_pairs={{0,16},{1,17},{2,18},{3,19},{4,20},{5,21},{6,22},{7,23},{8,24},{9,... | collective-permute-start | bytes 1277960 | tf_op jit(solution)/shard_map/ppermute | solution.py:861
  173.9 72.7 %collective-permute-start.21 = (bf16[416,1024]{1,0:T(8,128)(2,1)}, bf16[416,1024]{1,0:T(8,128)(2,1)}, u32[]{:S(2)}, u32[]{:S(2)}) collective-permute-start(bf16[416,1024]{1,0:T(8,128)(2,1)} %output_forward.7), channel_id=1, source_target_pairs={{0,16},{1,17},{2,18},{3,19},{4,20},{5,21},{6,22},{7,23},{8,24},{9,... | collective-permute-start | bytes 2555912 | tf_op jit(solution)/shard_map/ppermute | solution.py:861
  207.7 110.5 %collective-permute-start.20 = (bf16[416,7168]{1,0:T(8,128)(2,1)}, bf16[416,7168]{1,0:T(8,128)(2,1)}, u32[]{:S(2)}, u32[]{:S(2)}) collective-permute-start(bf16[416,7168]{1,0:T(8,128)(2,1)} %get-tuple-element.151.refs_4_.refs_8_.refs_1_.refs_0_), channel_id=1, source_target_pairs={{0,4},{4,0},{8,12},{12,8},{1,5},{5,1},{9,13},{13,9},{2,6},{6,2},{1... | collective-permute-start | bytes 17891336 | tf_op jit(solution)/shard_map/ppermute | solution.py:773
  244.8 32.4 %collective-permute-start.23 = (bf16[416,1024]{1,0:T(8,128)(2,1)}, bf16[416,1024]{1,0:T(8,128)(2,1)S(1)}, u32[]{:S(2)}, u32[]{:S(2)}) collective-permute-start(bf16[416,1024]{1,0:T(8,128)(2,1)} %get-tuple-element.141), channel_id=1, source_target_pairs={{16,0},{17,1},{18,2},{19,3},{20,4},{21,5},{22,6},{23,7},{24,8},{25... | collective-permute-start | bytes 2555912 | tf_op jit(solution)/shard_map/ppermute | solution.py:861
  246.1 72.1 %collective-permute-start.25 = (bf16[416,9216]{1,0:T(8,128)(2,1)}, bf16[416,9216]{1,0:T(8,128)(2,1)}, u32[]{:S(2)}, u32[]{:S(2)}) collective-permute-start(bf16[416,9216]{1,0:T(8,128)(2,1)} %get-tuple-element.149.refs_5_), channel_id=1, source_target_pairs={{0,4},{4,0},{8,12},{12,8},{1,5},{5,1},{9,13},{13,9},{2,6},{6,2},{1... | collective-permute-start | bytes 23003144 | tf_op jit(solution)/shard_map/ppermute | solution.py:773
  277.1 51.8 %collective-permute-start.22 = (bf16[416,7168]{1,0:T(8,128)(2,1)}, bf16[416,7168]{1,0:T(8,128)(2,1)}, u32[]{:S(2)}, u32[]{:S(2)}) collective-permute-start(bf16[416,7168]{1,0:T(8,128)(2,1)} %get-tuple-element.152.refs_9_.refs_1_.refs_2_.refs_3_), channel_id=1, source_target_pairs={{0,4},{4,0},{8,12},{12,8},{1,5},{5,1},{9,13},{13,9},{2,6},{6,2},{1... | collective-permute-start | bytes 17891336 | tf_op jit(solution)/shard_map/ppermute | solution.py:773
  315.1 27.2 %collective-permute-start.24 = (bf16[416,9216]{1,0:T(8,128)(2,1)}, bf16[416,9216]{1,0:T(8,128)(2,1)}, u32[]{:S(2)}, u32[]{:S(2)}) collective-permute-start(bf16[416,9216]{1,0:T(8,128)(2,1)} %get-tuple-element.148.refs_4_), channel_id=1, source_target_pairs={{0,4},{4,0},{8,12},{12,8},{1,5},{5,1},{9,13},{13,9},{2,6},{6,2},{1... | collective-permute-start | bytes 23003144 | tf_op jit(solution)/shard_map/ppermute | solution.py:773
  352.1 25.5 %collective-permute-start.30 = (bf16[512,1024]{1,0:T(8,128)(2,1)}, bf16[512,1024]{1,0:T(8,128)(2,1)S(1)}, u32[]{:S(2)}, u32[]{:S(2)}) collective-permute-start(bf16[512,1024]{1,0:T(8,128)(2,1)} %get-tuple-element.160), channel_id=1, source_target_pairs={{0,8},{4,12},{8,0},{12,4},{1,9},{5,13},{9,1},{13,5},{2,10},{6,14},... | collective-permute-start | bytes 3145736 | tf_op jit(solution)/shard_map/ppermute | solution.py:776
  378.1 36.9 %collective-permute-start.31 = (bf16[512,1024]{1,0:T(8,128)(2,1)S(1)}, bf16[512,1024]{1,0:T(8,128)(2,1)S(1)}, u32[]{:S(2)}, u32[]{:S(2)}) collective-permute-start(bf16[512,1024]{1,0:T(8,128)(2,1)S(1)} %add_convert_fusion.11), channel_id=1, source_target_pairs={{0,1},{3,2},{4,5},{7,6},{8,9},{11,10},{12,13},{15,14},{16,17},{19,... | collective-permute-start | bytes 3145736 | tf_op jit(solution)/shard_map/ppermute | solution.py:820
  388.5 27.9 %collective-permute-start.32 = (bf16[512,1024]{1,0:T(8,128)(2,1)}, bf16[512,1024]{1,0:T(8,128)(2,1)}, u32[]{:S(2)}, u32[]{:S(2)}) collective-permute-start(bf16[512,1024]{1,0:T(8,128)(2,1)} %get-tuple-element.169), channel_id=1, source_target_pairs={{0,8},{4,12},{8,0},{12,4},{1,9},{5,13},{9,1},{13,5},{2,10},{6,14},... | collective-permute-start | bytes 3145736 | tf_op jit(solution)/shard_map/ppermute | solution.py:776
  419.2 25.7 %collective-permute-start.35 = (bf16[512,1024]{1,0:T(8,128)(2,1)}, bf16[512,1024]{1,0:T(8,128)(2,1)}, u32[]{:S(2)}, u32[]{:S(2)}) collective-permute-start(bf16[512,1024]{1,0:T(8,128)(2,1)} %add_convert_fusion.9), channel_id=1, source_target_pairs={{0,1},{3,2},{4,5},{7,6},{8,9},{11,10},{12,13},{15,14},{16,17},{19,... | collective-permute-start | bytes 3145736 | tf_op jit(solution)/shard_map/ppermute | solution.py:820
  432.8 26.3 %collective-permute-start.36 = (bf16[256,2048]{1,0:T(8,128)(2,1)}, bf16[256,2048]{1,0:T(8,128)(2,1)}, u32[]{:S(2)}, u32[]{:S(2)}) collective-permute-start(bf16[256,2048]{1,0:T(8,128)(2,1)} %get-tuple-element.178), channel_id=1, source_target_pairs={{0,8},{4,12},{8,0},{12,4},{1,9},{5,13},{9,1},{13,5},{2,10},{6,14},... | collective-permute-start | bytes 3145736 | tf_op jit(solution)/shard_map/ppermute | solution.py:776
  444.3 32.8 %collective-permute-start.37 = (bf16[256,1536]{1,0:T(8,128)(2,1)}, bf16[256,1536]{1,0:T(8,128)(2,1)S(1)}, u32[]{:S(2)}, u32[]{:S(2)}) collective-permute-start(bf16[256,1536]{1,0:T(8,128)(2,1)} %get-tuple-element.182), channel_id=1, source_target_pairs={{0,8},{4,12},{8,0},{12,4},{1,9},{5,13},{9,1},{13,5},{2,10},{6,14},... | collective-permute-start | bytes 2359304 | tf_op jit(solution)/shard_map/ppermute | solution.py:776
  446.8 35.4 %collective-permute-start.39 = (bf16[512,1024]{1,0:T(8,128)(2,1)S(1)}, bf16[512,1024]{1,0:T(8,128)(2,1)}, u32[]{:S(2)}, u32[]{:S(2)}) collective-permute-start(bf16[512,1024]{1,0:T(8,128)(2,1)S(1)} %add_convert_fusion.7), channel_id=1, source_target_pairs={{1,2},{2,1},{5,6},{6,5},{9,10},{10,9},{13,14},{14,13},{17,18},{18,... | collective-permute-start | bytes 3145736 | tf_op jit(solution)/shard_map/ppermute | solution.py:823
  448.5 33.6 %collective-permute-start.38 = (bf16[512,1024]{1,0:T(8,128)(2,1)S(1)}, bf16[512,1024]{1,0:T(8,128)(2,1)S(1)}, u32[]{:S(2)}, u32[]{:S(2)}) collective-permute-start(bf16[512,1024]{1,0:T(8,128)(2,1)S(1)} %add_convert_fusion.8), channel_id=1, source_target_pairs={{1,0},{2,3},{5,4},{6,7},{9,8},{10,11},{13,12},{14,15},{17,16},{18,... | collective-permute-start | bytes 3145736 | tf_op jit(solution)/shard_map/ppermute | solution.py:826
  460.7 28.0 %collective-permute-start.40 = (bf16[256,2048]{1,0:T(8,128)(2,1)S(1)}, bf16[256,2048]{1,0:T(8,128)(2,1)}, u32[]{:S(2)}, u32[]{:S(2)}) collective-permute-start(bf16[256,2048]{1,0:T(8,128)(2,1)S(1)} %add_convert_fusion.6), channel_id=1, source_target_pairs={{0,1},{3,2},{4,5},{7,6},{8,9},{11,10},{12,13},{15,14},{16,17},{19,... | collective-permute-start | bytes 3145736 | tf_op jit(solution)/shard_map/ppermute | solution.py:820
  475.6 26.2 %collective-permute-start.41 = (bf16[256,2048]{1,0:T(8,128)(2,1)}, bf16[256,2048]{1,0:T(8,128)(2,1)}, u32[]{:S(2)}, u32[]{:S(2)}) collective-permute-start(bf16[256,2048]{1,0:T(8,128)(2,1)} %get-tuple-element.189), channel_id=1, source_target_pairs={{0,8},{4,12},{8,0},{12,4},{1,9},{5,13},{9,1},{13,5},{2,10},{6,14},... | collective-permute-start | bytes 3145736 | tf_op jit(solution)/shard_map/ppermute | solution.py:776
  478.2 34.1 %collective-permute-start.42 = (bf16[256,1536]{1,0:T(8,128)(2,1)}, bf16[256,1536]{1,0:T(8,128)(2,1)}, u32[]{:S(2)}, u32[]{:S(2)}) collective-permute-start(bf16[256,1536]{1,0:T(8,128)(2,1)} %add_convert_fusion.17), channel_id=1, source_target_pairs={{0,1},{3,2},{4,5},{7,6},{8,9},{11,10},{12,13},{15,14},{16,17},{19,... | collective-permute-start | bytes 2359304 | tf_op jit(solution)/shard_map/ppermute | solution.py:820
  490.4 29.4 %collective-permute-start.44 = (bf16[256,2048]{1,0:T(8,128)(2,1)S(1)}, bf16[256,2048]{1,0:T(8,128)(2,1)}, u32[]{:S(2)}, u32[]{:S(2)}) collective-permute-start(bf16[256,2048]{1,0:T(8,128)(2,1)S(1)} %add_convert_fusion.4), channel_id=1, source_target_pairs={{1,2},{2,1},{5,6},{6,5},{9,10},{10,9},{13,14},{14,13},{17,18},{18,... | collective-permute-start | bytes 3145736 | tf_op jit(solution)/shard_map/ppermute | solution.py:823
  503.3 29.3 %collective-permute-start.47 = (bf16[256,2048]{1,0:T(8,128)(2,1)S(1)}, bf16[256,2048]{1,0:T(8,128)(2,1)}, u32[]{:S(2)}, u32[]{:S(2)}) collective-permute-start(bf16[256,2048]{1,0:T(8,128)(2,1)S(1)} %add_convert_fusion.3), channel_id=1, source_target_pairs={{0,1},{3,2},{4,5},{7,6},{8,9},{11,10},{12,13},{15,14},{16,17},{19,... | collective-permute-start | bytes 3145736 | tf_op jit(solution)/shard_map/ppermute | solution.py:820
  514.7 28.3 %collective-permute-start.48 = (bf16[256,1536]{1,0:T(8,128)(2,1)}, bf16[256,1536]{1,0:T(8,128)(2,1)}, u32[]{:S(2)}, u32[]{:S(2)}) collective-permute-start(bf16[256,1536]{1,0:T(8,128)(2,1)} %add_convert_fusion.16), channel_id=1, source_target_pairs={{1,2},{2,1},{5,6},{6,5},{9,10},{10,9},{13,14},{14,13},{17,18},{18,... | collective-permute-start | bytes 2359304 | tf_op jit(solution)/shard_map/ppermute | solution.py:823
  528.9 34.1 %collective-permute-start.51 = (bf16[256,1536]{1,0:T(8,128)(2,1)}, bf16[256,1536]{1,0:T(8,128)(2,1)}, u32[]{:S(2)}, u32[]{:S(2)}) collective-permute-start(bf16[256,1536]{1,0:T(8,128)(2,1)} %add_convert_fusion.15), channel_id=1, source_target_pairs={{0,1},{3,2},{4,5},{7,6},{8,9},{11,10},{12,13},{15,14},{16,17},{19,... | collective-permute-start | bytes 2359304 | tf_op jit(solution)/shard_map/ppermute | solution.py:820
  534.3 31.0 %collective-permute-start.52 = (bf16[256,2048]{1,0:T(8,128)(2,1)S(1)}, bf16[256,2048]{1,0:T(8,128)(2,1)}, u32[]{:S(2)}, u32[]{:S(2)}) collective-permute-start(bf16[256,2048]{1,0:T(8,128)(2,1)S(1)} %add_convert_fusion.1), channel_id=1, source_target_pairs={{1,2},{2,1},{5,6},{6,5},{9,10},{10,9},{13,14},{14,13},{17,18},{18,... | collective-permute-start | bytes 3145736 | tf_op jit(solution)/shard_map/ppermute | solution.py:823
  544.7 26.9 %collective-permute-start.53 = (bf16[256,1536]{1,0:T(8,128)(2,1)S(1)}, bf16[256,1536]{1,0:T(8,128)(2,1)S(1)}, u32[]{:S(2)}, u32[]{:S(2)}) collective-permute-start(bf16[256,1536]{1,0:T(8,128)(2,1)S(1)} %add_convert_fusion.14), channel_id=1, source_target_pairs={{1,0},{2,3},{5,4},{6,7},{9,8},{10,11},{13,12},{14,15},{17,16},{18,... | collective-permute-start | bytes 2359304 | tf_op jit(solution)/shard_map/ppermute | solution.py:826
  567.0 28.2 %collective-permute-start.56 = (bf16[256,2048]{1,0:T(8,128)(2,1)S(1)}, bf16[256,2048]{1,0:T(8,128)(2,1)S(1)}, u32[]{:S(2)}, u32[]{:S(2)}) collective-permute-start(bf16[256,2048]{1,0:T(8,128)(2,1)S(1)} %add_convert_fusion), channel_id=1, source_target_pairs={{1,0},{2,3},{5,4},{6,7},{9,8},{10,11},{13,12},{14,15},{17,16},{18,... | collective-permute-start | bytes 3145736 | tf_op jit(solution)/shard_map/ppermute | solution.py:826
  581.6 30.4 %collective-permute-start.58 = (bf16[256,1536]{1,0:T(8,128)(2,1)S(1)}, bf16[256,1536]{1,0:T(8,128)(2,1)S(1)}, u32[]{:S(2)}, u32[]{:S(2)}) collective-permute-start(bf16[256,1536]{1,0:T(8,128)(2,1)S(1)} %add_convert_fusion.12), channel_id=1, source_target_pairs={{1,0},{2,3},{5,4},{6,7},{9,8},{10,11},{13,12},{14,15},{17,16},{18,... | collective-permute-start | bytes 2359304 | tf_op jit(solution)/shard_map/ppermute | solution.py:826
  (73 other events, 763.1 us)

commit v8 on v7

--- a/solution.py
+++ b/solution.py
@@ -17,13 +17,13 @@
     "R0 BF r0 R1*",
     "BA r0 r1 E0*",
     "Q0 r0 r1 e0",
-    "E1 q0 r0 r1",
-    "e0 Q1 e1 q0",
+    "E1 q0 r1 e0",
+    "r0 Q1 e1 q0",
     "r1 e0 V P0",
-    "q1 e1 q0 e0",
-    "p0 O q1 e1",
-    "q0 p0 O O",
-    "q1 e1 p0 O",
+    "e1 q1 q0 e0",
+    "p0 O q1 O",
+    "e1 q0 p0 O",
+    "O q1 e1 p0",
     "q1 p0",
 )
 LAST = "P0"
@@ -336,43 +336,47 @@
     )
 
 
-def output_forward(middle, active, pieces, params, meta, count, weight=LIGHT, columns=None):
+def output_forward(middle, active, pieces, params, meta, count, weight=LIGHT):
     rows, width = middle.shape
-    first, width = columns or (0, width)
     inner = sum(piece.shape[0] for piece in flat(pieces))
     space = rows // count
     parts, many = len(pieces), len(flat(pieces))
     spots = parts + 1 + count
-    blocks = 2
-    part_width = width // blocks
+    deep = inner // parts
 
     def body(*refs):
         refs = list(refs)
         mid_in, act_in = refs.pop(0), refs.pop(0)
         reduce = [refs.pop(0) for _ in range(many)]
-        vec, info, result, mid, act, full, x_sem, w_sem = refs
-        copies = [
-            pltpu.make_async_copy(act_in.at[:, pl.ds(0, inner)], act, x_sem.at[0]),
-            pltpu.make_async_copy(mid_in.at[:, pl.ds(first, width)], mid, x_sem.at[1]),
-        ]
-        copies[0].start()
-        loads = [
-            start_pieces(reduce, info, spots, full, w_sem, block, (block * part_width, part_width), first)
-            for block in range(blocks)
-        ]
-        copies[1].start()
-        copies[0].wait()
-        for block in range(blocks):
-            wait_all(loads[block])
-            if block == 0:
-                copies[1].wait()
-            part = slice(block * part_width, (block + 1) * part_width)
-            value = contract(act[...], full[:, part], 1, 0) + mid[:, part]
-            value = value + vec[FEED : FEED + 1, first + block * part_width : first + (block + 1) * part_width]
-            for image in range(count):
-                alive = jnp.where(info[parts + 1 + image] > 0, 1.0, 0.0)
-                here = slice(image * space, (image + 1) * space)
-                result[here, part] = (value[here] * alive).astype(BF16)
+        vec, info, result, mid, act, full, total, x_sem, w_sem = refs
+        every = start_pieces(reduce[:1], info, spots, full, w_sem, 0, (0, width))
+        columns = [pl.ds(pl.multiple_of(info[index] * deep, deep), deep) for index in range(parts)]
+        takes = []
+        for index in range(parts):
+            takes.append(
+                pltpu.make_async_copy(act_in.at[:, columns[index]], act.at[index], x_sem.at[index])
+            )
+            takes[-1].start()
+            if index == 0:
+                every += start_pieces(
+                    reduce[1:], info, spots + 1, full, w_sem.at[:, pl.ds(1, many - 1)], 0, (0, width)
+                )
+        last = pltpu.make_async_copy(mid_in, mid, x_sem.at[parts])
+        last.start()
+        for index, group in enumerate(pieces):
+            takes[index].wait()
+            wait_all([every.pop(0) for _ in group])
+            value = contract(act[index], full[columns[index]], 1, 0)
+            if index:
+                value = value + total[...]
+            if index < parts - 1:
+                total[...] = value
+        last.wait()
+        value = value + mid[...] + vec[FEED : FEED + 1]
+        for image in range(count):
+            alive = jnp.where(info[parts + 1 + image] > 0, 1.0, 0.0)
+            here = slice(image * space, (image + 1) * space)
+            result[here] = (value[here] * alive).astype(BF16)
 
     return call(
         body,
@@ -382,10 +386,11 @@
         [((rows, width), BF16)],
         [
             pltpu.VMEM((rows, width), F32),
-            pltpu.VMEM((rows, inner), BF16),
+            pltpu.VMEM((parts, rows, deep), BF16),
             pltpu.VMEM((inner, width), BF16),
-            pltpu.SemaphoreType.DMA((2,)),
-            pltpu.SemaphoreType.DMA((blocks, many)),
+            pltpu.VMEM((rows, width), F32),
+            pltpu.SemaphoreType.DMA((parts + 1,)),
+            pltpu.SemaphoreType.DMA((1, many)),
         ],
         2 * rows * width * inner,
         weight,
@@ -797,10 +802,10 @@
         for index, half in enumerate(halves):
             earlier = others[-1:] if index == 1 else []
             others.append(self.beside(after(half, *earlier, *(tokens if index == 1 else []))))
-        self.arrived = halves[-1]
-
-        def pieces(index, *tokens):
-            one, two = (after(half, *tokens) for half in (halves[index], others[index]))
+        self.arrived, self.swapped = halves[-1], others[-1]
+
+        def pieces(index, before_one=(), before_two=()):
+            one, two = after(halves[index], *before_one), after(others[index], *before_two)
             return [
                 [blocks[index]],
                 [sibling[index]],
@@ -841,7 +846,7 @@
 
     def gather(self, blocks, prepare):
         prepare(blocks[0])
-        self.arrived = blocks[0]
+        self.arrived = self.swapped = blocks[0]
         found = [[[piece] for piece in self.gather_small(block)] for block in blocks]
         return [lambda *tokens, groups=groups: groups for groups in found]
 
@@ -974,37 +979,27 @@
         attended.append(
             forward(start, start, None, qkv, None, params, infos[batch], slots, length)
         )
-    wide = wide(attended[-1][0])
+    wide = wide(attended[0], attended[-1])
     fed = []
     for batch in batches:
-        start = inputs[batch] if batch == 0 else after(inputs[batch], fed[-1][0])
+        start = inputs[batch] if batch == 0 else after(inputs[batch], fed[-1][0], net.swapped)
         fed.append(
             forward(start, start, attended[batch][0], None, wide, params, infos[batch], slots, length)
         )
-    reduce = reduce(fed[-1][0])
+    reduce = reduce(attended[-1], fed[0][:1])
     early, incoming = [], []
     for batch in batches:
         middle, active = fed[batch]
         if batch:
-            active = after(active, made[-1])
-        cuts = 2 if batch == 0 else 1
-        made, sent = [], []
-        for cut in range(cuts):
-            part = width // cuts
-            made.append(
-                output_forward(
-                    middle, after(active, *made), reduce, params, infos[batch], slots, LIGHT, (cut * part, part)
-                )
-            )
-            sent.append(shifted(made[-1], 1))
-        early.append(jnp.concatenate(made, axis=1))
-        incoming.append(jnp.concatenate(sent, axis=1))
+            active = after(active, early[-1])
+        early.append(output_forward(middle, active, reduce, params, infos[batch], slots))
+        incoming.append(shifted(early[batch], 1))
 
     inner = wide[0][0].shape[1] - width
     mixed_at = inner + width
     kept, lefts, rights, results = [], [], [], []
     sums_a, sums_b, sums_c, returning = [], [], [], []
-    token = made[-1]
+    token = early[-1]
     for batch in batches:
         start = after(incoming[batch], token)
         left, packed, logs, middle, slope = forward(

time: 634 us -> 621 us (0.979)
  Pallas kernels: 346 us -> 328 us
    pallas_call x22 -> x21, Pallas kernels: 346 us -> 328 us  [call(): pl.pallas_call(body, out_shape=out_shape, in_specs=specs, out_specs=[VMEM...]
    ppermute x3, waiting for transfers between devices: 0.01 us -> 8.75 us  [beside(): return lax.ppermute(block, 'replica', [(i, i ^ 1) for i in range(4)])]
    ppermute x11, waiting for transfers between devices: 45.3 us -> 53.6 us  [across(): return lax.ppermute(block, 'group', [(i, i ^ 2) for i in range(4)])]
    ppermute x7, waiting for transfers between devices: 42.8 us -> 35.2 us  [total(): outward = lax.ppermute(summed, 'replica', [(1, 0), (2, 3)])]
  transfers between devices with their start and end apart: 60 -> 59, of which waited for: 20 -> 18; matrix products, arithmetic and copies ran while one was open for 12% -> 12% of each run, Pallas kernels for 52% -> 51%
where the time goes in v8:
time: 621 us; the launch traced here: 613 us
  Pallas kernels  328 us (53%)
  waiting for transfers between devices  115 us (19%)
  starting transfers between devices  78.2 us (13%)
  other arithmetic  61.4 us (10%)
  local copies, waits for them, and re-layouts  27.6 us (4%)
    pallas_call x21, Pallas kernels, call(): pl.pallas_call(body, out_shape=out_shape, in_specs=specs, out_specs=[VMEM...  328 us
    ppermute x11, waiting for transfers between devices, across(): return lax.ppermute(block, 'group', [(i, i ^ 2) for i in range(4)])  53.6 us
    ppermute x7, waiting for transfers between devices, total(): outward = lax.ppermute(summed, 'replica', [(1, 0), (2, 3)])  35.2 us
    convert_element_type x21, other arithmetic, added(): return total.astype(values[0].dtype)  31.7 us
    ppermute x7, starting transfers between devices, total(): inward = lax.ppermute(mine, 'replica', [(0, 1), (3, 2)])  29.1 us
  transfers between devices with their start and end apart: 59, of which 18 were waited for; matrix products, arithmetic and copies ran while one was open for 12% of the time, Pallas kernels for 51%

profile of v8, /device:TPU:0, one launch (start us, length us, event | category | flops | bytes accessed | tf_op | source)
XLA Modules:
  0.0 613.2 jit_solution(8875374250640971817)
XLA Ops:
  17.9 9.9 %collective-permute-done.refs_3_.refs_4_.refs_27_.refs_34_.refs_14_ = bf16[128,3072]{1,0:T(8,128)(2,1)S(1)} collective-permute-done((bf16[128,3072]{1,0:T(8,128)(2,1)}, bf16[128,3072]{1,0:T(8,128)(2,1)S(1)}, u32[]{:S(2)}, u32[]{:S(2)}) %collective-permute-start) | collective-permute-done | bytes 786464 | tf_op jit(solution)/shard_map/ppermute | solution.py:781
  38.6 16.7 %collective-permute-done.9.refs_4_.refs_10_.refs_16_.refs_15_.refs_21_.refs_22_.refs_28_.refs_11_.refs_8_ = bf16[128,5120]{1,0:T(8,128)(2,1)} collective-permute-done((bf16[128,5120]{1,0:T(8,128)(2,1)}, bf16[128,5120]{1,0:T(8,128)(2,1)}, u32[]{:S(2)}, u32[]{:S(2)}) %collective-permute-start.9) | collective-permute-done | bytes 1310752 | tf_op jit(solution)/shard_map/ppermute | solution.py:781
  61.6 16.2 %forward_attend.2.refs_1_ = bf16[416,1024]{1,0:T(8,128)(2,1)} custom-call(bf16[416,1024]{1,0:T(8,128)(2,1)} %bitcast.108, bf16[256,3072]{1,0:T(8,128)(2,1)} %bitcast.95, bf16[256,3072]{1,0:T(8,128)(2,1)} %collective-permute-done.1.refs_2_.refs_3_.refs_26_.refs_33_.refs_13_, bf16[128,3072]{1,0:T(8,128)(2,1)} %copy-done.9, bf16[128,3072]{1,0:T(8,128)(2,1)} %copy-done.10, ...), custom_call_target="tpu_custom_call" | custom-call | flops 46432256 | bytes 125696 | tf_op jit(solution)/shard_map/forward_attend/pallas_call | solution.py:67
  81.2 15.7 %forward_attend.3.refs_1_ = bf16[416,1024]{1,0:T(8,128)(2,1)} custom-call(bf16[416,1024]{1,0:T(8,128)(2,1)} %bitcast.102, bf16[256,3072]{1,0:T(8,128)(2,1)} %bitcast.96, bf16[256,3072]{1,0:T(8,128)(2,1)} %collective-permute-done.1.refs_2_.refs_3_.refs_26_.refs_33_.refs_13_, bf16[128,3072]{1,0:T(8,128)(2,1)} %copy-done.9, bf16[128,3072]{1,0:T(8,128)(2,1)} %copy-done.10, ...), custom_call_target="tpu_custom_call" | custom-call | flops 46432256 | bytes 125696 | tf_op jit(solution)/shard_map/forward_attend/pallas_call | solution.py:67
  100.6 13.7 %forward_feed.2 = (f32[416,1024]{1,0:T(8,128)}, bf16[416,4096]{1,0:T(8,128)(2,1)}) custom-call(bf16[416,1024]{1,0:T(8,128)(2,1)} %bitcast.109, bf16[416,1024]{1,0:T(8,128)(2,1)} %forward_attend.2.refs_1_, bf16[256,5120]{1,0:T(8,128)(2,1)} %copy-done, bf16[256,5120]{1,0:T(8,128)(2,1)} %copy-done.1, ...), custom_call_target="tpu_custom_call" | custom-call | flops 68157440 | bytes 434944 | tf_op jit(solution)/shard_map/forward_feed/pallas_call | solution.py:67
  114.3 8.7 %collective-permute-done.15.refs_5_.refs_10_.refs_17_.refs_6_ = bf16[512,1024]{1,0:T(8,128)(2,1)} collective-permute-done((bf16[512,1024]{1,0:T(8,128)(2,1)}, bf16[512,1024]{1,0:T(8,128)(2,1)}, u32[]{:S(2)}, u32[]{:S(2)}) %collective-permute-start.15) | collective-permute-done | bytes 1048608 | tf_op jit(solution)/shard_map/ppermute | solution.py:784
  127.6 8.0 %output_forward.4 = bf16[416,1024]{1,0:T(8,128)(2,1)} custom-call(f32[416,1024]{1,0:T(8,128)} %get-tuple-element.124.refs_0_, bf16[416,4096]{1,0:T(8,128)(2,1)} %get-tuple-element.125.refs_1_, bf16[1024,1024]{1,0:T(8,128)(2,1)} %bitcast.87, bf16[1024,1024]{1,0:T(8,128)(2,1)} %copy-done.3, ...), custom_call_target="tpu_custom_call" | custom-call | flops 54525952 | bytes 225024 | tf_op jit(solution)/shard_map/output_forward/pallas_call | solution.py:67
  141.0 13.7 %forward_feed.3 = (f32[416,1024]{1,0:T(8,128)}, bf16[416,4096]{1,0:T(8,128)(2,1)}) custom-call(bf16[416,1024]{1,0:T(8,128)(2,1)} %bitcast.103, bf16[416,1024]{1,0:T(8,128)(2,1)} %forward_attend.3.refs_1_, bf16[256,5120]{1,0:T(8,128)(2,1)} %copy-done, bf16[256,5120]{1,0:T(8,128)(2,1)} %copy-done.1, ...), custom_call_target="tpu_custom_call" | custom-call | flops 68157440 | bytes 434944 | tf_op jit(solution)/shard_map/forward_feed/pallas_call | solution.py:67
  154.7 8.0 %output_forward.5 = bf16[416,1024]{1,0:T(8,128)(2,1)} custom-call(f32[416,1024]{1,0:T(8,128)} %get-tuple-element.130.refs_0_, bf16[416,4096]{1,0:T(8,128)(2,1)} %get-tuple-element.132.refs_1_, bf16[1024,1024]{1,0:T(8,128)(2,1)} %bitcast.88, bf16[1024,1024]{1,0:T(8,128)(2,1)} %copy-done.3, ...), custom_call_target="tpu_custom_call" | custom-call | flops 54525952 | bytes 225024 | tf_op jit(solution)/shard_map/output_forward/pallas_call | solution.py:67
  165.8 30.6 %forward_attend_feed.2 = (bf16[416,7168]{1,0:T(8,128)(2,1)}, bf16[416,3072]{1,0:T(8,128)(2,1)}, f32[2,16,208]{2,1,0:T(8,128)}, f32[416,1024]{1,0:T(8,128)}, bf16[416,4096]{1,0:T(8,128)(2,1)}) custom-call(bf16[416,1024]{1,0:T(8,128)(2,1)} %bitcast.110, bf16[416,1024]{1,0:T(8,128)(2,1)} %copy-done.43, bf16[256,3072]{1,0:T(8,128)(2,1)} %bitcast.97, ...), custom_call_target="tpu_custom_call" | custom-call | flops 58669924352 | bytes 341393824 | tf_op jit(solution)/shard_map/forward_attend_feed/pallas_call | solution.py:67
  196.5 37.2 %backward_feed_attend.2 = (bf16[416,9216]{1,0:T(8,128)(2,1)}, f32[8,1024]{1,0:T(8,128)}, f32[1,4096]{1,0:T(1,128)}, bf16[416,1024]{1,0:T(8,128)(2,1)}, f32[8,1024]{1,0:T(8,128)}) custom-call(bf16[416,1024]{1,0:T(8,128)(2,1)} %bitcast.129, bf16[416,4096]{1,0:T(8,128)(2,1)} %get-tuple-element.135.refs_1_.refs_0_, ...), custom_call_target="tpu_custom_call" | custom-call | flops 90840236032 | bytes 477315488 | tf_op jit(solution)/shard_map/backward_feed_attend/pallas_call | solution.py:67
  235.5 30.5 %forward_attend_feed.3 = (bf16[416,7168]{1,0:T(8,128)(2,1)}, bf16[416,3072]{1,0:T(8,128)(2,1)}, f32[2,16,208]{2,1,0:T(8,128)}, f32[416,1024]{1,0:T(8,128)}, bf16[416,4096]{1,0:T(8,128)(2,1)}) custom-call(bf16[416,1024]{1,0:T(8,128)(2,1)} %bitcast.104, bf16[416,1024]{1,0:T(8,128)(2,1)} %collective-permute-done.20.refs_1_.refs_13_, ...), custom_call_target="tpu_custom_call" | custom-call | flops 58669924352 | bytes 341393824 | tf_op jit(solution)/shard_map/forward_attend_feed/pallas_call | solution.py:67
  267.1 37.2 %backward_feed_attend.3 = (bf16[416,9216]{1,0:T(8,128)(2,1)}, f32[8,1024]{1,0:T(8,128)}, f32[1,4096]{1,0:T(1,128)}, bf16[416,1024]{1,0:T(8,128)(2,1)}, f32[8,1024]{1,0:T(8,128)}) custom-call(bf16[416,4096]{1,0:T(8,128)(2,1)} %get-tuple-element.135.refs_1_.refs_0_, bf16[416,4096]{1,0:T(8,128)(2,1)} %get-tuple-element.142.refs_1_, ...), custom_call_target="tpu_custom_call" | custom-call | flops 90840236032 | bytes 600211840 | tf_op jit(solution)/shard_map/backward_feed_attend/pallas_call | solution.py:67
  307.2 8.0 %output_forward.6 = bf16[416,1024]{1,0:T(8,128)(2,1)} custom-call(f32[416,1024]{1,0:T(8,128)} %get-tuple-element.136.refs_2_.refs_0_, bf16[416,7168]{1,0:T(8,128)(2,1)} %get-tuple-element.149.refs_4_.refs_8_.refs_1_.refs_0_, bf16[1024,1024]{1,0:T(8,128)(2,1)} %bitcast.91, bf16[1024,1024]{1,0:T(8,128)(2,1)} %copy-done.3, ...), custom_call_target="tpu_custom_call" | custom-call | flops 27917287424 | bytes 135659936 | tf_op jit(solution)/shard_map/output_forward/pallas_call | solution.py:67
  315.3 7.9 %output_forward.7 = bf16[416,1024]{1,0:T(8,128)(2,1)} custom-call(f32[416,1024]{1,0:T(8,128)} %get-tuple-element.143.refs_3_.refs_0_.refs_2_, bf16[416,7168]{1,0:T(8,128)(2,1)} %get-tuple-element.150.refs_9_.refs_1_.refs_2_.refs_3_, bf16[1024,1024]{1,0:T(8,128)(2,1)} %bitcast.92, bf16[1024,1024]{1,0:T(8,128)(2,1)} %copy-done.3, ...), custom_call_target="tpu_custom_call" | custom-call | flops 27917287424 | bytes 135659936 | tf_op jit(solution)/shard_map/output_forward/pallas_call | solution.py:67
  332.4 8.9 %reduce.11 = (bf16[512,1024]{1,0:T(8,128)(2,1)}, bf16[512,1024]{1,0:T(8,128)(2,1)}) custom-call(bf16[416,7168]{1,0:T(8,128)(2,1)} %get-tuple-element.149.refs_4_.refs_8_.refs_1_.refs_0_, bf16[416,7168]{1,0:T(8,128)(2,1)} %collective-permute-done.19.refs_1_, bf16[416,7168]{1,0:T(8,128)(2,1)} %get-tuple-element.150.refs_9_.refs_1_.refs_2_.refs_3_, ...), custom_call_target="tpu_custom_call" | custom-call | flops 54525952 | bytes 911360 | tf_op jit(solution)/shard_map/reduce/pallas_call | solution.py:67
  341.9 18.4 %backward_feed.1 = (bf16[416,4096]{1,0:T(8,128)(2,1)}, bf16[416,1024]{1,0:T(8,128)(2,1)}, f32[8,1024]{1,0:T(8,128)}, f32[1,4096]{1,0:T(1,128)}, f32[416,1024]{1,0:T(8,128)}) custom-call(bf16[416,1024]{1,0:T(8,128)(2,1)} %copy-done.16, bf16[416,4096]{1,0:T(8,128)(2,1)} %get-tuple-element.142.refs_1_, f32[416,1024]{1,0:T(8,128)} %get-tuple-element.143.refs_3_.refs_0_.refs_2_, ...), custom_call_target="tpu_custom_call" | custom-call | flops 109051904 | bytes 482816 | tf_op jit(solution)/shard_map/backward_feed/pallas_call | solution.py:67
  360.8 6.0 collective-permute-done.29
  369.8 8.9 %reduce.12 = (bf16[512,1024]{1,0:T(8,128)(2,1)}, bf16[512,1024]{1,0:T(8,128)(2,1)}) custom-call(bf16[416,7168]{1,0:T(8,128)(2,1)} %get-tuple-element.149.refs_4_.refs_8_.refs_1_.refs_0_, bf16[416,7168]{1,0:T(8,128)(2,1)} %collective-permute-done.19.refs_1_, bf16[416,7168]{1,0:T(8,128)(2,1)} %get-tuple-element.150.refs_9_.refs_1_.refs_2_.refs_3_, ...), custom_call_target="tpu_custom_call" | custom-call | flops 55834574848 | bytes 933232960 | tf_op jit(solution)/shard_map/reduce/pallas_call | solution.py:67
  379.5 24.7 %backward_attend.1 = (bf16[416,3072]{1,0:T(8,128)(2,1)}, bf16[416,1024]{1,0:T(8,128)(2,1)}, f32[8,1024]{1,0:T(8,128)}) custom-call(bf16[416,1024]{1,0:T(8,128)(2,1)} %get-tuple-element.162.refs_0_.refs_8_, f32[416,1024]{1,0:T(8,128)} %get-tuple-element.163.refs_1_, bf16[416,3072]{1,0:T(8,128)(2,1)} %get-tuple-element.144.refs_7_.refs_2_, ...), custom_call_target="tpu_custom_call" | custom-call | flops 68370432 | bytes 503456 | tf_op jit(solution)/shard_map/backward_attend/pallas_call | solution.py:67
  412.7 9.4 %expand.2 = (bf16[256,2048]{1,0:T(8,128)(2,1)}, bf16[256,2048]{1,0:T(8,128)(2,1)}) custom-call(bf16[416,7168]{1,0:T(8,128)(2,1)} %get-tuple-element.149.refs_4_.refs_8_.refs_1_.refs_0_, bf16[416,7168]{1,0:T(8,128)(2,1)} %collective-permute-done.19.refs_1_, bf16[416,7168]{1,0:T(8,128)(2,1)} %get-tuple-element.150.refs_9_.refs_1_.refs_2_.refs_3_, ...), custom_call_target="tpu_custom_call" | custom-call | flops 55834574848 | bytes 1015021888 | tf_op jit(solution)/shard_map/expand/pallas_call | solution.py:67
  425.2 7.8 %qkv.2 = (bf16[256,1536]{1,0:T(8,128)(2,1)}, bf16[256,1536]{1,0:T(8,128)(2,1)}) custom-call(bf16[416,7168]{1,0:T(8,128)(2,1)} %get-tuple-element.149.refs_4_.refs_8_.refs_1_.refs_0_, bf16[416,7168]{1,0:T(8,128)(2,1)} %collective-permute-done.19.refs_1_, bf16[416,7168]{1,0:T(8,128)(2,1)} %get-tuple-element.150.refs_9_.refs_1_.refs_2_.refs_3_, ...), custom_call_target="tpu_custom_call" | custom-call | flops 40894464 | bytes 956416 | tf_op jit(solution)/shard_map/qkv/pallas_call | solution.py:67
  439.3 9.2 %collective-permute-done.35 = bf16[256,2048]{1,0:T(8,128)(2,1)} collective-permute-done((bf16[256,2048]{1,0:T(8,128)(2,1)}, bf16[256,2048]{1,0:T(8,128)(2,1)}, u32[]{:S(2)}, u32[]{:S(2)}) %collective-permute-start.35) | collective-permute-done | bytes 1048608 | tf_op jit(solution)/shard_map/ppermute | solution.py:781
  455.8 9.4 %expand.3 = (bf16[256,2048]{1,0:T(8,128)(2,1)}, bf16[256,2048]{1,0:T(8,128)(2,1)}) custom-call(bf16[416,7168]{1,0:T(8,128)(2,1)} %get-tuple-element.149.refs_4_.refs_8_.refs_1_.refs_0_, bf16[416,7168]{1,0:T(8,128)(2,1)} %collective-permute-done.19.refs_1_, bf16[416,7168]{1,0:T(8,128)(2,1)} %get-tuple-element.150.refs_9_.refs_1_.refs_2_.refs_3_, ...), custom_call_target="tpu_custom_call" | custom-call | flops 54525952 | bytes 991232 | tf_op jit(solution)/shard_map/expand/pallas_call | solution.py:67
  483.2 8.0 %qkv.3 = (bf16[256,1536]{1,0:T(8,128)(2,1)}, bf16[256,1536]{1,0:T(8,128)(2,1)}) custom-call(bf16[416,7168]{1,0:T(8,128)(2,1)} %get-tuple-element.149.refs_4_.refs_8_.refs_1_.refs_0_, bf16[416,7168]{1,0:T(8,128)(2,1)} %collective-permute-done.19.refs_1_, bf16[416,7168]{1,0:T(8,128)(2,1)} %get-tuple-element.150.refs_9_.refs_1_.refs_2_.refs_3_, ...), custom_call_target="tpu_custom_call" | custom-call | flops 40894464 | bytes 956416 | tf_op jit(solution)/shard_map/qkv/pallas_call | solution.py:67
  492.8 6.3 %collective-permute-start.45 = (bf16[256,2048]{1,0:T(8,128)(2,1)S(1)}, bf16[256,2048]{1,0:T(8,128)(2,1)}, u32[]{:S(2)}, u32[]{:S(2)}) collective-permute-start(bf16[256,2048]{1,0:T(8,128)(2,1)S(1)} %add_convert_fusion.3), channel_id=1, source_target_pairs={{0,1},{3,2},{4,5},{7,6},{8,9},{11,10},{12,13},{15,14},{16,17},{19,... | collective-permute-start | bytes 3145736 | tf_op jit(solution)/shard_map/ppermute | solution.py:825
  508.7 6.3 %project.1 = (bf16[256,1024]{1,0:T(8,128)(2,1)}, bf16[256,1024]{1,0:T(8,128)(2,1)}) custom-call(bf16[416,7168]{1,0:T(8,128)(2,1)} %get-tuple-element.149.refs_4_.refs_8_.refs_1_.refs_0_, bf16[416,7168]{1,0:T(8,128)(2,1)} %collective-permute-done.19.refs_1_, bf16[416,7168]{1,0:T(8,128)(2,1)} %get-tuple-element.150.refs_9_.refs_1_.refs_2_.refs_3_, ...), custom_call_target="tpu_custom_call" | custom-call | flops 27262976 | bytes 894976 | tf_op jit(solution)/shard_map/project/pallas_call | solution.py:67
  523.2 6.8 %collective-permute-start.50 = (bf16[256,1536]{1,0:T(8,128)(2,1)}, bf16[256,1536]{1,0:T(8,128)(2,1)}, u32[]{:S(2)}, u32[]{:S(2)}) collective-permute-start(bf16[256,1536]{1,0:T(8,128)(2,1)} %add_convert_fusion.15), channel_id=1, source_target_pairs={{0,1},{3,2},{4,5},{7,6},{8,9},{11,10},{12,13},{15,14},{16,17},{19,... | collective-permute-start | bytes 2359304 | tf_op jit(solution)/shard_map/ppermute | solution.py:825
  540.2 8.4 %collective-permute-done.49 = bf16[272,1024]{1,0:T(8,128)(2,1)S(1)} collective-permute-done((bf16[272,1024]{1,0:T(8,128)(2,1)S(1)}, bf16[272,1024]{1,0:T(8,128)(2,1)S(1)}, u32[]{:S(2)}, u32[]{:S(2)}) %collective-permute-start.49) | collective-permute-done | bytes 557088 | tf_op jit(solution)/shard_map/ppermute | solution.py:781
  570.9 11.5 %collective-permute-done.55 = bf16[256,2048]{1,0:T(8,128)(2,1)S(1)} collective-permute-done((bf16[256,2048]{1,0:T(8,128)(2,1)S(1)}, bf16[256,2048]{1,0:T(8,128)(2,1)S(1)}, u32[]{:S(2)}, u32[]{:S(2)}) %collective-permute-start.55) | collective-permute-done | bytes 1048608 | tf_op jit(solution)/shard_map/ppermute | solution.py:831
  586.5 12.7 %collective-permute-done.57 = bf16[256,1536]{1,0:T(8,128)(2,1)S(1)} collective-permute-done((bf16[256,1536]{1,0:T(8,128)(2,1)S(1)}, bf16[256,1536]{1,0:T(8,128)(2,1)S(1)}, u32[]{:S(2)}, u32[]{:S(2)}) %collective-permute-start.57) | collective-permute-done | bytes 786464 | tf_op jit(solution)/shard_map/ppermute | solution.py:831
  601.4 8.7 %collective-permute-done.58 = bf16[272,1024]{1,0:T(8,128)(2,1)S(1)} collective-permute-done((bf16[272,1024]{1,0:T(8,128)(2,1)S(1)}, bf16[272,1024]{1,0:T(8,128)(2,1)S(1)}, u32[]{:S(2)}, u32[]{:S(2)}) %collective-permute-start.58) | collective-permute-done | bytes 557088 | tf_op jit(solution)/shard_map/ppermute | solution.py:831
  (302 shorter events, 177.7 us)
Async XLA Ops:
  10.0 45.2 %collective-permute-start.9 = (bf16[128,5120]{1,0:T(8,128)(2,1)}, bf16[128,5120]{1,0:T(8,128)(2,1)}, u32[]{:S(2)}, u32[]{:S(2)}) collective-permute-start(bf16[128,5120]{1,0:T(8,128)(2,1)} %fusion), channel_id=1, source_target_pairs={{0,8},{4,12},{8,0},{12,4},{1,9},{5,13},{9,1},{13,5},{2,10},{6,14},... | collective-permute-start | bytes 3932168 | tf_op jit(solution)/shard_map/ppermute | solution.py:781
  17.5 80.5 %collective-permute-start.8 = (bf16[256,5120]{1,0:T(8,128)(2,1)S(1)}, bf16[256,5120]{1,0:T(8,128)(2,1)S(1)}, u32[]{:S(2)}, u32[]{:S(2)}) collective-permute-start(bf16[256,5120]{1,0:T(8,128)(2,1)S(1)} %pad_maximum_fusion.refs_2_.refs_8_.refs_14_.refs_13_.refs_19_.refs_20_.refs_26_.refs_9_.refs_6_), channel_id=1, source_target_pairs={{0,4},{4,0},{8,12},{12,8},{1,5},{5,1},{9,13},{13,9},{2,6},{6,2},{1... | collective-permute-start | bytes 7864328 | tf_op jit(solution)/shard_map/ppermute | solution.py:778
  27.8 27.4 %collective-permute-start.2 = (bf16[128,3072]{1,0:T(8,128)(2,1)S(1)}, bf16[128,3072]{1,0:T(8,128)(2,1)S(1)}, u32[]{:S(2)}, u32[]{:S(2)}) collective-permute-start(bf16[128,3072]{1,0:T(8,128)(2,1)S(1)} %collective-permute-done.refs_3_.refs_4_.refs_27_.refs_34_.refs_14_), channel_id=1, source_target_pairs={{0,1},{1,0},{2,3},{3,2},{4,5},{5,4},{6,7},{7,6},{8,9},{9,8},{10,11... | collective-permute-start | bytes 2359304 | tf_op jit(solution)/shard_map/ppermute | solution.py:784
  55.2 41.8 %collective-permute-start.10 = (bf16[128,5120]{1,0:T(8,128)(2,1)}, bf16[128,5120]{1,0:T(8,128)(2,1)}, u32[]{:S(2)}, u32[]{:S(2)}) collective-permute-start(bf16[128,5120]{1,0:T(8,128)(2,1)} %collective-permute-done.9.refs_4_.refs_10_.refs_16_.refs_15_.refs_21_.refs_22_.refs_28_.refs_11_.refs_8_), channel_id=1, source_target_pairs={{0,1},{1,0},{2,3},{3,2},{4,5},{5,4},{6,7},{7,6},{8,9},{9,8},{10,11... | collective-permute-start | bytes 3932168 | tf_op jit(solution)/shard_map/ppermute | solution.py:784
  97.6 25.5 %collective-permute-start.15 = (bf16[512,1024]{1,0:T(8,128)(2,1)}, bf16[512,1024]{1,0:T(8,128)(2,1)}, u32[]{:S(2)}, u32[]{:S(2)}) collective-permute-start(bf16[512,1024]{1,0:T(8,128)(2,1)} %collective-permute-done.12.refs_4_.refs_9_.refs_16_.refs_5_), channel_id=1, source_target_pairs={{0,1},{1,0},{2,3},{3,2},{4,5},{5,4},{6,7},{7,6},{8,9},{9,8},{10,11... | collective-permute-start | bytes 3145736 | tf_op jit(solution)/shard_map/ppermute | solution.py:784
  98.0 27.9 %collective-permute-start.14 = (bf16[1024,1024]{1,0:T(8,128)(2,1)}, bf16[1024,1024]{1,0:T(8,128)(2,1)S(1)}, u32[]{:S(2)}, u32[]{:S(2)}) collective-permute-start(bf16[1024,1024]{1,0:T(8,128)(2,1)} %bitcast.86), channel_id=1, source_target_pairs={{0,4},{4,0},{8,12},{12,8},{1,5},{5,1},{9,13},{13,9},{2,6},{6,2},{1... | collective-permute-start | bytes 6291464 | tf_op jit(solution)/shard_map/ppermute | solution.py:778
  135.5 29.4 %collective-permute-start.18 = (bf16[416,1024]{1,0:T(8,128)(2,1)}, bf16[416,1024]{1,0:T(8,128)(2,1)S(1)}, u32[]{:S(2)}, u32[]{:S(2)}) collective-permute-start(bf16[416,1024]{1,0:T(8,128)(2,1)} %output_forward.4), channel_id=1, source_target_pairs={{0,16},{1,17},{2,18},{3,19},{4,20},{5,21},{6,22},{7,23},{8,24},{9,... | collective-permute-start | bytes 2555912 | tf_op jit(solution)/shard_map/ppermute | solution.py:866
  162.7 72.3 %collective-permute-start.20 = (bf16[416,1024]{1,0:T(8,128)(2,1)}, bf16[416,1024]{1,0:T(8,128)(2,1)}, u32[]{:S(2)}, u32[]{:S(2)}) collective-permute-start(bf16[416,1024]{1,0:T(8,128)(2,1)} %output_forward.5), channel_id=1, source_target_pairs={{0,16},{1,17},{2,18},{3,19},{4,20},{5,21},{6,22},{7,23},{8,24},{9,... | collective-permute-start | bytes 2555912 | tf_op jit(solution)/shard_map/ppermute | solution.py:866
  196.4 110.8 %collective-permute-start.19 = (bf16[416,7168]{1,0:T(8,128)(2,1)}, bf16[416,7168]{1,0:T(8,128)(2,1)}, u32[]{:S(2)}, u32[]{:S(2)}) collective-permute-start(bf16[416,7168]{1,0:T(8,128)(2,1)} %get-tuple-element.149.refs_4_.refs_8_.refs_1_.refs_0_), channel_id=1, source_target_pairs={{0,4},{4,0},{8,12},{12,8},{1,5},{5,1},{9,13},{13,9},{2,6},{6,2},{1... | collective-permute-start | bytes 17891336 | tf_op jit(solution)/shard_map/ppermute | solution.py:778
  233.7 32.4 %collective-permute-start.22 = (bf16[416,1024]{1,0:T(8,128)(2,1)}, bf16[416,1024]{1,0:T(8,128)(2,1)S(1)}, u32[]{:S(2)}, u32[]{:S(2)}) collective-permute-start(bf16[416,1024]{1,0:T(8,128)(2,1)} %get-tuple-element.139), channel_id=1, source_target_pairs={{16,0},{17,1},{18,2},{19,3},{20,4},{21,5},{22,6},{23,7},{24,8},{25... | collective-permute-start | bytes 2555912 | tf_op jit(solution)/shard_map/ppermute | solution.py:866
  235.0 72.2 %collective-permute-start.24 = (bf16[416,9216]{1,0:T(8,128)(2,1)}, bf16[416,9216]{1,0:T(8,128)(2,1)}, u32[]{:S(2)}, u32[]{:S(2)}) collective-permute-start(bf16[416,9216]{1,0:T(8,128)(2,1)} %get-tuple-element.147.refs_5_), channel_id=1, source_target_pairs={{0,4},{4,0},{8,12},{12,8},{1,5},{5,1},{9,13},{13,9},{2,6},{6,2},{1... | collective-permute-start | bytes 23003144 | tf_op jit(solution)/shard_map/ppermute | solution.py:778
  266.0 49.3 %collective-permute-start.21 = (bf16[416,7168]{1,0:T(8,128)(2,1)}, bf16[416,7168]{1,0:T(8,128)(2,1)}, u32[]{:S(2)}, u32[]{:S(2)}) collective-permute-start(bf16[416,7168]{1,0:T(8,128)(2,1)} %get-tuple-element.150.refs_9_.refs_1_.refs_2_.refs_3_), channel_id=1, source_target_pairs={{0,4},{4,0},{8,12},{12,8},{1,5},{5,1},{9,13},{13,9},{2,6},{6,2},{1... | collective-permute-start | bytes 17891336 | tf_op jit(solution)/shard_map/ppermute | solution.py:778
  304.2 27.2 %collective-permute-start.23 = (bf16[416,9216]{1,0:T(8,128)(2,1)}, bf16[416,9216]{1,0:T(8,128)(2,1)}, u32[]{:S(2)}, u32[]{:S(2)}) collective-permute-start(bf16[416,9216]{1,0:T(8,128)(2,1)} %get-tuple-element.146.refs_4_), channel_id=1, source_target_pairs={{0,4},{4,0},{8,12},{12,8},{1,5},{5,1},{9,13},{13,9},{2,6},{6,2},{1... | collective-permute-start | bytes 23003144 | tf_op jit(solution)/shard_map/ppermute | solution.py:778
  341.3 25.5 %collective-permute-start.29 = (bf16[512,1024]{1,0:T(8,128)(2,1)}, bf16[512,1024]{1,0:T(8,128)(2,1)S(1)}, u32[]{:S(2)}, u32[]{:S(2)}) collective-permute-start(bf16[512,1024]{1,0:T(8,128)(2,1)} %get-tuple-element.158), channel_id=1, source_target_pairs={{0,8},{4,12},{8,0},{12,4},{1,9},{5,13},{9,1},{13,5},{2,10},{6,14},... | collective-permute-start | bytes 3145736 | tf_op jit(solution)/shard_map/ppermute | solution.py:781
  367.3 37.0 %collective-permute-start.30 = (bf16[512,1024]{1,0:T(8,128)(2,1)S(1)}, bf16[512,1024]{1,0:T(8,128)(2,1)S(1)}, u32[]{:S(2)}, u32[]{:S(2)}) collective-permute-start(bf16[512,1024]{1,0:T(8,128)(2,1)S(1)} %add_convert_fusion.11), channel_id=1, source_target_pairs={{0,1},{3,2},{4,5},{7,6},{8,9},{11,10},{12,13},{15,14},{16,17},{19,... | collective-permute-start | bytes 3145736 | tf_op jit(solution)/shard_map/ppermute | solution.py:825
  378.7 27.0 %collective-permute-start.31 = (bf16[512,1024]{1,0:T(8,128)(2,1)}, bf16[512,1024]{1,0:T(8,128)(2,1)}, u32[]{:S(2)}, u32[]{:S(2)}) collective-permute-start(bf16[512,1024]{1,0:T(8,128)(2,1)} %get-tuple-element.167), channel_id=1, source_target_pairs={{0,8},{4,12},{8,0},{12,4},{1,9},{5,13},{9,1},{13,5},{2,10},{6,14},... | collective-permute-start | bytes 3145736 | tf_op jit(solution)/shard_map/ppermute | solution.py:781
  408.4 26.5 %collective-permute-start.34 = (bf16[512,1024]{1,0:T(8,128)(2,1)}, bf16[512,1024]{1,0:T(8,128)(2,1)}, u32[]{:S(2)}, u32[]{:S(2)}) collective-permute-start(bf16[512,1024]{1,0:T(8,128)(2,1)} %add_convert_fusion.9), channel_id=1, source_target_pairs={{0,1},{3,2},{4,5},{7,6},{8,9},{11,10},{12,13},{15,14},{16,17},{19,... | collective-permute-start | bytes 3145736 | tf_op jit(solution)/shard_map/ppermute | solution.py:825
  422.1 26.3 %collective-permute-start.35 = (bf16[256,2048]{1,0:T(8,128)(2,1)}, bf16[256,2048]{1,0:T(8,128)(2,1)}, u32[]{:S(2)}, u32[]{:S(2)}) collective-permute-start(bf16[256,2048]{1,0:T(8,128)(2,1)} %get-tuple-element.176), channel_id=1, source_target_pairs={{0,8},{4,12},{8,0},{12,4},{1,9},{5,13},{9,1},{13,5},{2,10},{6,14},... | collective-permute-start | bytes 3145736 | tf_op jit(solution)/shard_map/ppermute | solution.py:781
  437.0 37.5 %collective-permute-start.37 = (bf16[512,1024]{1,0:T(8,128)(2,1)S(1)}, bf16[512,1024]{1,0:T(8,128)(2,1)}, u32[]{:S(2)}, u32[]{:S(2)}) collective-permute-start(bf16[512,1024]{1,0:T(8,128)(2,1)S(1)} %add_convert_fusion.7), channel_id=1, source_target_pairs={{1,2},{2,1},{5,6},{6,5},{9,10},{10,9},{13,14},{14,13},{17,18},{18,... | collective-permute-start | bytes 3145736 | tf_op jit(solution)/shard_map/ppermute | solution.py:828
  438.7 28.1 %collective-permute-start.36 = (bf16[256,1536]{1,0:T(8,128)(2,1)}, bf16[256,1536]{1,0:T(8,128)(2,1)}, u32[]{:S(2)}, u32[]{:S(2)}) collective-permute-start(bf16[256,1536]{1,0:T(8,128)(2,1)} %get-tuple-element.180), channel_id=1, source_target_pairs={{0,8},{4,12},{8,0},{12,4},{1,9},{5,13},{9,1},{13,5},{2,10},{6,14},... | collective-permute-start | bytes 2359304 | tf_op jit(solution)/shard_map/ppermute | solution.py:781
  450.1 27.1 %collective-permute-start.38 = (bf16[256,2048]{1,0:T(8,128)(2,1)S(1)}, bf16[256,2048]{1,0:T(8,128)(2,1)}, u32[]{:S(2)}, u32[]{:S(2)}) collective-permute-start(bf16[256,2048]{1,0:T(8,128)(2,1)S(1)} %add_convert_fusion.6), channel_id=1, source_target_pairs={{0,1},{3,2},{4,5},{7,6},{8,9},{11,10},{12,13},{15,14},{16,17},{19,... | collective-permute-start | bytes 3145736 | tf_op jit(solution)/shard_map/ppermute | solution.py:825
  454.4 27.7 %collective-permute-start.39 = (bf16[512,1024]{1,0:T(8,128)(2,1)S(1)}, bf16[512,1024]{1,0:T(8,128)(2,1)S(1)}, u32[]{:S(2)}, u32[]{:S(2)}) collective-permute-start(bf16[512,1024]{1,0:T(8,128)(2,1)S(1)} %add_convert_fusion.8), channel_id=1, source_target_pairs={{1,0},{2,3},{5,4},{6,7},{9,8},{10,11},{13,12},{14,15},{17,16},{18,... | collective-permute-start | bytes 3145736 | tf_op jit(solution)/shard_map/ppermute | solution.py:831
  465.2 25.9 %collective-permute-start.40 = (bf16[256,2048]{1,0:T(8,128)(2,1)}, bf16[256,2048]{1,0:T(8,128)(2,1)}, u32[]{:S(2)}, u32[]{:S(2)}) collective-permute-start(bf16[256,2048]{1,0:T(8,128)(2,1)} %get-tuple-element.187), channel_id=1, source_target_pairs={{0,8},{4,12},{8,0},{12,4},{1,9},{5,13},{9,1},{13,5},{2,10},{6,14},... | collective-permute-start | bytes 3145736 | tf_op jit(solution)/shard_map/ppermute | solution.py:781
  469.0 31.6 %collective-permute-start.41 = (bf16[256,1536]{1,0:T(8,128)(2,1)}, bf16[256,1536]{1,0:T(8,128)(2,1)}, u32[]{:S(2)}, u32[]{:S(2)}) collective-permute-start(bf16[256,1536]{1,0:T(8,128)(2,1)} %add_convert_fusion.17), channel_id=1, source_target_pairs={{0,1},{3,2},{4,5},{7,6},{8,9},{11,10},{12,13},{15,14},{16,17},{19,... | collective-permute-start | bytes 2359304 | tf_op jit(solution)/shard_map/ppermute | solution.py:825
  478.7 27.0 %collective-permute-start.43 = (bf16[256,2048]{1,0:T(8,128)(2,1)S(1)}, bf16[256,2048]{1,0:T(8,128)(2,1)}, u32[]{:S(2)}, u32[]{:S(2)}) collective-permute-start(bf16[256,2048]{1,0:T(8,128)(2,1)S(1)} %add_convert_fusion.4), channel_id=1, source_target_pairs={{1,2},{2,1},{5,6},{6,5},{9,10},{10,9},{13,14},{14,13},{17,18},{18,... | collective-permute-start | bytes 3145736 | tf_op jit(solution)/shard_map/ppermute | solution.py:828
  480.4 25.2 %collective-permute-start.42 = (bf16[512,1024]{1,0:T(8,128)(2,1)}, bf16[512,1024]{1,0:T(8,128)(2,1)S(1)}, u32[]{:S(2)}, u32[]{:S(2)}) collective-permute-start(bf16[512,1024]{1,0:T(8,128)(2,1)} %add_convert_fusion.5), channel_id=1, source_target_pairs={{1,0},{2,3},{5,4},{6,7},{9,8},{10,11},{13,12},{14,15},{17,16},{18,... | collective-permute-start | bytes 3145736 | tf_op jit(solution)/shard_map/ppermute | solution.py:831
  503.1 32.9 %collective-permute-start.47 = (bf16[256,1536]{1,0:T(8,128)(2,1)}, bf16[256,1536]{1,0:T(8,128)(2,1)}, u32[]{:S(2)}, u32[]{:S(2)}) collective-permute-start(bf16[256,1536]{1,0:T(8,128)(2,1)} %add_convert_fusion.16), channel_id=1, source_target_pairs={{1,2},{2,1},{5,6},{6,5},{9,10},{10,9},{13,14},{14,13},{17,18},{18,... | collective-permute-start | bytes 2359304 | tf_op jit(solution)/shard_map/ppermute | solution.py:828
  507.4 31.5 %collective-permute-start.48 = (bf16[256,2048]{1,0:T(8,128)(2,1)S(1)}, bf16[256,2048]{1,0:T(8,128)(2,1)}, u32[]{:S(2)}, u32[]{:S(2)}) collective-permute-start(bf16[256,2048]{1,0:T(8,128)(2,1)S(1)} %add_convert_fusion.2), channel_id=1, source_target_pairs={{1,0},{2,3},{5,4},{6,7},{9,8},{10,11},{13,12},{14,15},{17,16},{18,... | collective-permute-start | bytes 3145736 | tf_op jit(solution)/shard_map/ppermute | solution.py:831
  519.4 33.4 %collective-permute-start.51 = (bf16[256,2048]{1,0:T(8,128)(2,1)S(1)}, bf16[256,2048]{1,0:T(8,128)(2,1)}, u32[]{:S(2)}, u32[]{:S(2)}) collective-permute-start(bf16[256,2048]{1,0:T(8,128)(2,1)S(1)} %add_convert_fusion.1), channel_id=1, source_target_pairs={{1,2},{2,1},{5,6},{6,5},{9,10},{10,9},{13,14},{14,13},{17,18},{18,... | collective-permute-start | bytes 3145736 | tf_op jit(solution)/shard_map/ppermute | solution.py:828
  523.2 27.0 %collective-permute-start.50 = (bf16[256,1536]{1,0:T(8,128)(2,1)}, bf16[256,1536]{1,0:T(8,128)(2,1)}, u32[]{:S(2)}, u32[]{:S(2)}) collective-permute-start(bf16[256,1536]{1,0:T(8,128)(2,1)} %add_convert_fusion.15), channel_id=1, source_target_pairs={{0,1},{3,2},{4,5},{7,6},{8,9},{11,10},{12,13},{15,14},{16,17},{19,... | collective-permute-start | bytes 2359304 | tf_op jit(solution)/shard_map/ppermute | solution.py:825
  554.4 28.0 %collective-permute-start.55 = (bf16[256,2048]{1,0:T(8,128)(2,1)S(1)}, bf16[256,2048]{1,0:T(8,128)(2,1)S(1)}, u32[]{:S(2)}, u32[]{:S(2)}) collective-permute-start(bf16[256,2048]{1,0:T(8,128)(2,1)S(1)} %add_convert_fusion), channel_id=1, source_target_pairs={{1,0},{2,3},{5,4},{6,7},{9,8},{10,11},{13,12},{14,15},{17,16},{18,... | collective-permute-start | bytes 3145736 | tf_op jit(solution)/shard_map/ppermute | solution.py:831
  569.6 29.6 %collective-permute-start.57 = (bf16[256,1536]{1,0:T(8,128)(2,1)S(1)}, bf16[256,1536]{1,0:T(8,128)(2,1)S(1)}, u32[]{:S(2)}, u32[]{:S(2)}) collective-permute-start(bf16[256,1536]{1,0:T(8,128)(2,1)S(1)} %add_convert_fusion.12), channel_id=1, source_target_pairs={{1,0},{2,3},{5,4},{6,7},{9,8},{10,11},{13,12},{14,15},{17,16},{18,... | collective-permute-start | bytes 2359304 | tf_op jit(solution)/shard_map/ppermute | solution.py:831
  (72 other events, 765.5 us)

commit v9 on v8

--- a/solution.py
+++ b/solution.py
@@ -16,12 +16,12 @@
 PLAN = (
     "R0 BF r0 R1*",
     "BA r0 r1 E0*",
-    "Q0 r0 r1 e0",
+    "r1 Q0 r0 e0",
     "E1 q0 r1 e0",
     "r0 Q1 e1 q0",
     "r1 e0 V P0",
-    "e1 q1 q0 e0",
-    "p0 O q1 O",
+    "e1 q1 O q0",
+    "e0 p0 q1 O",
     "e1 q0 p0 O",
     "O q1 e1 p0",
     "q1 p0",
@@ -80,13 +80,13 @@
     return [piece for group in groups for piece in group]
 
 
-def start_pieces(pieces, info, first, target, sems, slot, columns, shift=0):
+def start_pieces(pieces, info, first, target, sems, slot, columns, block, shift=0):
     begin, size = columns
     columns = pl.ds(begin, size)
     copies = []
     for index, piece in enumerate(pieces):
         rows = piece.shape[0]
-        where = pl.multiple_of(info[first + index] * rows, rows)
+        where = pl.multiple_of(info[first + index] * (block // 4), block // 4)
         copy = pltpu.make_async_copy(
             piece.at[:, pl.ds(begin + shift, size)],
             target.at[pl.ds(where, rows), columns],
@@ -226,6 +226,7 @@
     many = len(flat(qkv if attend else wide))
     spots = parts + 1 + count
     inner = wide[0][0].shape[1] - width if feed else 0
+    share = width // parts
     blocks = inner // width
     same = lower is upper
 
@@ -256,7 +257,7 @@
                 norm, packed, logs = refs.pop(0), refs.pop(0), None
             weight = lists.pop(0)
             loads = [
-                start_pieces(weight, info, spots, full, a_sem, block, (block * width, width))
+                start_pieces(weight, info, spots, full, a_sem, block, (block * width, width), share)
                 for block in range(3)
             ]
         if feed:
@@ -265,9 +266,9 @@
                 mixed, second, slope = refs.pop(0), refs.pop(0), None
                 extra = pltpu.make_async_copy(arrived, mixed, x_sem.at[1])
                 extra.start()
-            first_load = start_pieces(lists[0], info, spots, full_out, o_sem, 0, (0, width))
+            first_load = start_pieces(lists[0], info, spots, full_out, o_sem, 0, (0, width), share)
             inner_loads = [
-                start_pieces(lists[1], info, spots, full_in, w_sem, block, (block * width, width), width)
+                start_pieces(lists[1], info, spots, full_in, w_sem, block, (block * width, width), share, width)
                 for block in range(blocks)
             ]
         take.wait()
@@ -349,7 +350,7 @@
         mid_in, act_in = refs.pop(0), refs.pop(0)
         reduce = [refs.pop(0) for _ in range(many)]
         vec, info, result, mid, act, full, total, x_sem, w_sem = refs
-        every = start_pieces(reduce[:1], info, spots, full, w_sem, 0, (0, width))
+        every = start_pieces(reduce[:1], info, spots + many, full, w_sem, 0, (0, width), deep)
         columns = [pl.ds(pl.multiple_of(info[index] * deep, deep), deep) for index in range(parts)]
         takes = []
         for index in range(parts):
@@ -359,7 +360,8 @@
             takes[-1].start()
             if index == 0:
                 every += start_pieces(
-                    reduce[1:], info, spots + 1, full, w_sem.at[:, pl.ds(1, many - 1)], 0, (0, width)
+                    reduce[1:], info, spots + many + 1, full, w_sem.at[:, pl.ds(1, many - 1)], 0,
+                    (0, width), deep,
                 )
         last = pltpu.make_async_copy(mid_in, mid, x_sem.at[parts])
         last.start()
@@ -541,7 +543,7 @@
     many = len(flat(reduce if feed else qkv))
     spots = parts + 1 + count
     inner = wide[0][0].shape[1] - width if feed else 0
-    deep = inner // parts
+    deep, share = inner // parts, width // parts
     both = feed and attend
     choices = []
     if feed:
@@ -591,10 +593,10 @@
             begin = pairs.pop(2) if start[0] is not start[1] else (firsts[0], firsts[0])
             take = start_chosen(section, *begin, grad, x_sem.at[0])
             for_slope = start_chosen(section, *pairs.pop(0), slope, x_sem.at[1])
-            every = start_pieces(lists.pop(0), info, spots, full_out, o_sem, 0, (0, width))
+            every = start_pieces(lists.pop(0), info, spots + many, full_out, o_sem, 0, (0, width), deep)
             first_load = [[every.pop(0) for _ in group] for group in reduce]
             for_middle = start_chosen(section, *pairs.pop(0), middle, x_sem.at[2])
-            load = start_pieces(lists.pop(0), info, spots, full, w_sem, 0, (0, inner), width)
+            load = start_pieces(lists.pop(0), info, spots, full, w_sem, 0, (0, inner), share, width)
         if attend:
             x, packed, mixed, logs, down, normal, stage, full_o, full_q, p_sem, q_sem = (
                 refs.pop(0) for _ in range(11)
@@ -607,14 +609,14 @@
                 ]
                 for given in givens:
                     given.start()
-            project_load = start_pieces(lists.pop(0), info, spots, full_o, p_sem, 0, (0, width))
+            project_load = start_pieces(lists.pop(0), info, spots, full_o, p_sem, 0, (0, width), share)
             sames = [one is two for one, two in pairs]
             pairs[1] = tuple(one.at[:, pl.ds(mixed_at, width)] for one in pairs[1])
             takes = [
                 start_chosen(section, *pairs[index], target, x_sem.at[3 + index], sames[index])
                 for index, target in ((1, mixed), (0, packed), (2, logs), (3, x))
             ]
-            last_load = start_pieces(lists.pop(0), info, spots, full_q, q_sem, 0, (0, 3 * width))
+            last_load = start_pieces(lists.pop(0), info, spots, full_q, q_sem, 0, (0, 3 * width), share)
             if not feed:
                 wait_all(givens)
         if feed:
@@ -693,6 +695,7 @@
     terms = len(lefts)
     first_row, height = rows_of
     first_column, breadth = columns_of
+    step = breadth // 2
     rows = lefts[0].shape[0]
     operands = list(lefts)
     places = []
@@ -709,30 +712,40 @@
         results = refs[len(operands) + 1 : len(operands) + 1 + len(blocks)]
         left_full, right_full, l_sem, r_sem = refs[len(operands) + 1 + len(blocks) :]
         section = info[parts]
-        waits = []
-        for term in range(terms):
-            sides = [
-                sources[place].at[:, pl.ds(column + first_column, breadth)]
-                for place, (_, column) in zip(places[term], rights[term])
-            ]
-            same = rights[term][0] is rights[term][1]
-            target = right_full.at[pl.ds(term * rows, rows)]
-            waits.append(start_chosen(section, *sides, target, r_sem.at[term], same))
-        loads = []
-        for index, block in enumerate(blocks):
-            start = pl.multiple_of(info[block] * quarter + first_row, 128)
+
+        def start_lefts():
+            loads = [[] for _ in blocks]
+            for index, block in reversed(list(enumerate(blocks))):
+                start = pl.multiple_of(info[block] * quarter + first_row, 128)
+                for term in range(terms):
+                    copy = pltpu.make_async_copy(
+                        sources[term].at[:, pl.ds(start, height)],
+                        left_full.at[index, pl.ds(term * rows, rows)],
+                        l_sem.at[index, term],
+                    )
+                    copy.start()
+                    loads[index].append(copy)
+            return loads
+
+        waits = [[], []]
+        for cut in range(2):
             for term in range(terms):
-                copy = pltpu.make_async_copy(
-                    sources[term].at[:, pl.ds(start, height)],
-                    left_full.at[index, pl.ds(term * rows, rows)],
-                    l_sem.at[index, term],
-                )
-                copy.start()
-                loads.append(copy)
-        wait_all(waits)
-        for index in reversed(range(len(blocks))):
-            wait_all(loads[index * terms : (index + 1) * terms])
-            results[index][...] = contract(left_full[index], right_full[...], 0, 0).astype(BF16)
+                sides = [
+                    sources[place].at[:, pl.ds(column + first_column + cut * step, step)]
+                    for place, (_, column) in zip(places[term], rights[term])
+                ]
+                same = rights[term][0] is rights[term][1]
+                target = right_full.at[cut, pl.ds(term * rows, rows)]
+                waits[cut].append(start_chosen(section, *sides, target, r_sem.at[cut, term], same))
+            if cut == 0:
+                loads = start_lefts()
+        for cut in range(2):
+            wait_all(waits[cut])
+            for index in reversed(range(len(blocks))):
+                if cut == 0:
+                    wait_all(loads[index])
+                done = contract(left_full[index], right_full[cut], 0, 0)
+                results[index][:, cut * step : (cut + 1) * step] = done.astype(BF16)
 
     return call(
         body,
@@ -742,9 +755,9 @@
         [((height, breadth), BF16)] * len(blocks),
         [
             pltpu.VMEM((len(blocks), terms * rows, height), BF16),
-            pltpu.VMEM((terms * rows, breadth), BF16),
+            pltpu.VMEM((2, terms * rows, step), BF16),
             pltpu.SemaphoreType.DMA((len(blocks), terms)),
-            pltpu.SemaphoreType.DMA((terms,)),
+            pltpu.SemaphoreType.DMA((2, terms)),
         ],
         2 * len(blocks) * terms * rows * height * breadth,
         weight,
@@ -771,8 +784,10 @@
         self.place = lax.axis_index("replica")
         self.order = [self.group ^ part for part in range(4)]
         odd = self.place % 2
-        halves = [2 * self.order[part] + half for part in (2, 3) for half in (odd, 1 - odd)]
-        self.spots = self.order[:2] + halves
+        near = [4 * self.order[part] for part in (0, 1)]
+        far = [4 * self.order[part] for part in (2, 3)]
+        self.spots = near + [block + place for block in far for place in (2 * odd, 2 - 2 * odd)]
+        self.last_spots = near + [block + place for block in far for place in (odd, 3 - 3 * odd)]
 
     def core(self, block):
         return lax.ppermute(block, "group", [(i, i ^ 1) for i in range(4)])
@@ -789,20 +804,25 @@
 
     def gather(self, blocks, prepare):
         odd = self.place % 2
+        quarters = [block.shape[0] // 4 for block in blocks]
         asked = [
-            lax.dynamic_slice_in_dim(block, odd * (block.shape[0] // 2), block.shape[0] // 2)
-            for block in blocks
+            lax.dynamic_slice_in_dim(block, 2 * odd * rows, 2 * rows)
+            for block, rows in zip(blocks[:-1], quarters)
         ]
+        asked.append(lax.dynamic_slice_in_dim(blocks[-1], odd * quarters[-1], 3 * quarters[-1]))
         halves, sibling = [], []
         for index, block in enumerate(blocks):
             halves.append(self.across(after(asked[index], *halves[: max(index - 1, 0)])))
             sibling.append(self.core(after(block, sibling[-1]) if index else block))
         others = []
         tokens = prepare(halves[0]) + asked[2:]
-        for index, half in enumerate(halves):
+        swaps = halves[:-1] + [
+            lax.dynamic_slice_in_dim(halves[-1], 2 * odd * quarters[-1], quarters[-1])
+        ]
+        for index, half in enumerate(swaps):
             earlier = others[-1:] if index == 1 else []
             others.append(self.beside(after(half, *earlier, *(tokens if index == 1 else []))))
-        self.arrived, self.swapped = halves[-1], others[-1]
+        self.swapped = others[-1]
 
         def pieces(index, before_one=(), before_two=()):
             one, two = after(halves[index], *before_one), after(others[index], *before_two)
@@ -838,7 +858,8 @@
     def __init__(self):
         self.parts = lax.axis_size("group")
         self.blocks = tuple(range(self.parts))
-        self.order = self.spots = [jnp.int32(part) for part in range(self.parts)]
+        self.order = [jnp.int32(part) for part in range(self.parts)]
+        self.spots = self.last_spots = [4 * part for part in self.order]
 
     def gather_small(self, block):
         whole = lax.all_gather(block, "group", axis=0)
@@ -846,7 +867,7 @@
 
     def gather(self, blocks, prepare):
         prepare(blocks[0])
-        self.arrived = self.swapped = blocks[0]
+        self.swapped = blocks[0]
         found = [[[piece] for piece in self.gather_small(block)] for block in blocks]
         return [lambda *tokens, groups=groups: groups for groups in found]
 
@@ -940,7 +961,7 @@
     alive = [(slot < counts[batch, 0]).astype(jnp.int32) for batch in batches]
     head = jnp.stack(net.order + [section]).astype(jnp.int32)
 
-    spots = jnp.stack(net.spots).astype(jnp.int32)
+    spots = jnp.stack(net.spots + net.last_spots).astype(jnp.int32)
 
     def meta(living):
         return jnp.concatenate([head, living, spots])
@@ -954,7 +975,7 @@
     slot = jnp.arange(slots, dtype=jnp.int32)
     alive = [(slot < counts[batch, 0]).astype(jnp.int32) for batch in batches]
     head = jnp.stack(net.order + [section]).astype(jnp.int32)
-    spots = jnp.stack(net.spots).astype(jnp.int32)
+    spots = jnp.stack(net.spots + net.last_spots).astype(jnp.int32)
 
     def meta(living):
         return jnp.concatenate([head, living, spots])
@@ -975,7 +996,7 @@
     qkv = qkv()
     attended = []
     for batch in batches:
-        start = inputs[batch] if batch == 0 else after(inputs[batch], attended[-1][0], net.arrived)
+        start = inputs[batch] if batch == 0 else after(inputs[batch], attended[-1][0])
         attended.append(
             forward(start, start, None, qkv, None, params, infos[batch], slots, length)
         )

time: 621 us -> 614 us (0.989)
  waiting for transfers between devices: 115 us -> 98.5 us
    ppermute x11, waiting for transfers between devices: 53.6 us -> 38.2 us  [across(): return lax.ppermute(block, 'group', [(i, i ^ 2) for i in range(4)])]
    ppermute x3, waiting for transfers between devices: 8.75 us -> 0.01 us  [beside(): return lax.ppermute(block, 'replica', [(i, i ^ 1) for i in range(4)])]
    ppermute x7, waiting for transfers between devices: 2.8 us -> 9.26 us  [total(): inward = lax.ppermute(mine, 'replica', [(0, 1), (3, 2)])]
  transfers between devices with their start and end apart: 59 -> 59, of which waited for: 18 -> 18; matrix products, arithmetic and copies ran while one was open for 12% -> 13% of each run, Pallas kernels for 51% -> 51%
where the time goes in v9:
time: 614 us; the launch traced here: 605 us
  Pallas kernels  326 us (53%)
  waiting for transfers between devices  98.5 us (16%)
  starting transfers between devices  84.1 us (14%)
  other arithmetic  60.3 us (10%)
  local copies, waits for them, and re-layouts  33.5 us (5%)
    pallas_call x21, Pallas kernels, call(): pl.pallas_call(body, out_shape=out_shape, in_specs=specs, out_specs=[VMEM...  326 us
    ppermute x11, waiting for transfers between devices, across(): return lax.ppermute(block, 'group', [(i, i ^ 2) for i in range(4)])  38.2 us
    ppermute x7, waiting for transfers between devices, total(): outward = lax.ppermute(summed, 'replica', [(1, 0), (2, 3)])  35.6 us
    ppermute x7, starting transfers between devices, total(): inward = lax.ppermute(mine, 'replica', [(0, 1), (3, 2)])  34.6 us
    convert_element_type x21, other arithmetic, added(): return total.astype(values[0].dtype)  29.6 us
  transfers between devices with their start and end apart: 59, of which 18 were waited for; matrix products, arithmetic and copies ran while one was open for 13% of the time, Pallas kernels for 51%

profile of v9, /device:TPU:0, one launch (start us, length us, event | category | flops | bytes accessed | tf_op | source)
XLA Modules:
  0.0 604.9 jit_solution(13681916904282292890)
XLA Ops:
  22.2 5.8 collective-permute-done.refs_3_.refs_4_.refs_27_.refs_34_.refs_14_
  38.7 16.9 %collective-permute-done.9.refs_4_.refs_10_.refs_16_.refs_15_.refs_21_.refs_22_.refs_28_.refs_11_.refs_8_ = bf16[128,5120]{1,0:T(8,128)(2,1)} collective-permute-done((bf16[128,5120]{1,0:T(8,128)(2,1)}, bf16[128,5120]{1,0:T(8,128)(2,1)}, u32[]{:S(2)}, u32[]{:S(2)}) %collective-permute-start.9) | collective-permute-done | bytes 1310752 | tf_op jit(solution)/shard_map/ppermute | solution.py:796
  63.1 16.0 %forward_attend.2.refs_1_ = bf16[416,1024]{1,0:T(8,128)(2,1)} custom-call(bf16[416,1024]{1,0:T(8,128)(2,1)} %bitcast.106, bf16[256,3072]{1,0:T(8,128)(2,1)} %bitcast.93, bf16[256,3072]{1,0:T(8,128)(2,1)} %collective-permute-done.1.refs_2_.refs_3_.refs_26_.refs_33_.refs_13_, bf16[128,3072]{1,0:T(8,128)(2,1)} %copy-done.5, bf16[128,3072]{1,0:T(8,128)(2,1)} %copy-done.6, ...), custom_call_target="tpu_custom_call" | custom-call | flops 46432256 | bytes 125697 | tf_op jit(solution)/shard_map/forward_attend/pallas_call | solution.py:67
  79.3 15.7 %forward_attend.3.refs_1_ = bf16[416,1024]{1,0:T(8,128)(2,1)} custom-call(bf16[416,1024]{1,0:T(8,128)(2,1)} %bitcast.100, bf16[256,3072]{1,0:T(8,128)(2,1)} %bitcast.94, bf16[256,3072]{1,0:T(8,128)(2,1)} %collective-permute-done.1.refs_2_.refs_3_.refs_26_.refs_33_.refs_13_, bf16[128,3072]{1,0:T(8,128)(2,1)} %copy-done.5, bf16[128,3072]{1,0:T(8,128)(2,1)} %copy-done.6, ...), custom_call_target="tpu_custom_call" | custom-call | flops 46432256 | bytes 125697 | tf_op jit(solution)/shard_map/forward_attend/pallas_call | solution.py:67
  99.9 13.7 %forward_feed.2 = (f32[416,1024]{1,0:T(8,128)}, bf16[416,4096]{1,0:T(8,128)(2,1)}) custom-call(bf16[416,1024]{1,0:T(8,128)(2,1)} %bitcast.107, bf16[416,1024]{1,0:T(8,128)(2,1)} %forward_attend.2.refs_1_, bf16[256,5120]{1,0:T(8,128)(2,1)} %copy-done, ...), custom_call_target="tpu_custom_call" | custom-call | flops 68157440 | bytes 434945 | tf_op jit(solution)/shard_map/forward_feed/pallas_call | solution.py:67
  116.4 8.1 %output_forward.4 = bf16[416,1024]{1,0:T(8,128)(2,1)} custom-call(f32[416,1024]{1,0:T(8,128)} %get-tuple-element.123.refs_0_, bf16[416,4096]{1,0:T(8,128)(2,1)} %get-tuple-element.124.refs_1_, bf16[1024,1024]{1,0:T(8,128)(2,1)} %bitcast.38.refs_2_.refs_7_.refs_14_.refs_3_, bf16[1024,1024]{1,0:T(8,128)(2,1)} %collective-permute-done.13.refs_3_.refs_8_.refs_15_.refs_4_, ...), custom_call_target="tpu_custom_call" | custom-call | flops 54525952 | bytes 225025 | tf_op jit(solution)/shard_map/output_forward/pallas_call | solution.py:67
  130.5 13.7 %forward_feed.3 = (f32[416,1024]{1,0:T(8,128)}, bf16[416,4096]{1,0:T(8,128)(2,1)}) custom-call(bf16[416,1024]{1,0:T(8,128)(2,1)} %bitcast.101, bf16[416,1024]{1,0:T(8,128)(2,1)} %forward_attend.3.refs_1_, bf16[256,5120]{1,0:T(8,128)(2,1)} %copy-done, ...), custom_call_target="tpu_custom_call" | custom-call | flops 68157440 | bytes 434945 | tf_op jit(solution)/shard_map/forward_feed/pallas_call | solution.py:67
  144.2 8.1 %output_forward.5 = bf16[416,1024]{1,0:T(8,128)(2,1)} custom-call(f32[416,1024]{1,0:T(8,128)} %get-tuple-element.130.refs_0_, bf16[416,4096]{1,0:T(8,128)(2,1)} %get-tuple-element.132.refs_1_, bf16[1024,1024]{1,0:T(8,128)(2,1)} %bitcast.38.refs_2_.refs_7_.refs_14_.refs_3_, bf16[1024,1024]{1,0:T(8,128)(2,1)} %collective-permute-done.13.refs_3_.refs_8_.refs_15_.refs_4_, ...), custom_call_target="tpu_custom_call" | custom-call | flops 54525952 | bytes 225025 | tf_op jit(solution)/shard_map/output_forward/pallas_call | solution.py:67
  155.4 30.5 %forward_attend_feed.2 = (bf16[416,7168]{1,0:T(8,128)(2,1)}, bf16[416,3072]{1,0:T(8,128)(2,1)}, f32[2,16,208]{2,1,0:T(8,128)}, f32[416,1024]{1,0:T(8,128)}, bf16[416,4096]{1,0:T(8,128)(2,1)}) custom-call(bf16[416,1024]{1,0:T(8,128)(2,1)} %bitcast.108, bf16[416,1024]{1,0:T(8,128)(2,1)} %copy-done.45, bf16[256,3072]{1,0:T(8,128)(2,1)} %bitcast.95, ...), custom_call_target="tpu_custom_call" | custom-call | flops 58669924352 | bytes 341394016 | tf_op jit(solution)/shard_map/forward_attend_feed/pallas_call | solution.py:67
  186.1 37.2 %backward_feed_attend.2 = (bf16[416,9216]{1,0:T(8,128)(2,1)}, f32[8,1024]{1,0:T(8,128)}, f32[1,4096]{1,0:T(1,128)}, bf16[416,1024]{1,0:T(8,128)(2,1)}, f32[8,1024]{1,0:T(8,128)}) custom-call(bf16[416,1024]{1,0:T(8,128)(2,1)} %bitcast.127, bf16[416,4096]{1,0:T(8,128)(2,1)} %get-tuple-element.135.refs_1_.refs_0_, ...), custom_call_target="tpu_custom_call" | custom-call | flops 90840236032 | bytes 477315680 | tf_op jit(solution)/shard_map/backward_feed_attend/pallas_call | solution.py:67
  225.1 30.5 %forward_attend_feed.3 = (bf16[416,7168]{1,0:T(8,128)(2,1)}, bf16[416,3072]{1,0:T(8,128)(2,1)}, f32[2,16,208]{2,1,0:T(8,128)}, f32[416,1024]{1,0:T(8,128)}, bf16[416,4096]{1,0:T(8,128)(2,1)}) custom-call(bf16[416,1024]{1,0:T(8,128)(2,1)} %bitcast.102, bf16[416,1024]{1,0:T(8,128)(2,1)} %collective-permute-done.20.refs_1_.refs_13_, ...), custom_call_target="tpu_custom_call" | custom-call | flops 58669924352 | bytes 341394016 | tf_op jit(solution)/shard_map/forward_attend_feed/pallas_call | solution.py:67
  256.6 37.2 %backward_feed_attend.3 = (bf16[416,9216]{1,0:T(8,128)(2,1)}, f32[8,1024]{1,0:T(8,128)}, f32[1,4096]{1,0:T(1,128)}, bf16[416,1024]{1,0:T(8,128)(2,1)}, f32[8,1024]{1,0:T(8,128)}) custom-call(bf16[416,4096]{1,0:T(8,128)(2,1)} %get-tuple-element.135.refs_1_.refs_0_, bf16[416,4096]{1,0:T(8,128)(2,1)} %get-tuple-element.142.refs_1_, ...), custom_call_target="tpu_custom_call" | custom-call | flops 90840236032 | bytes 600212096 | tf_op jit(solution)/shard_map/backward_feed_attend/pallas_call | solution.py:67
  297.0 8.1 %output_forward.6 = bf16[416,1024]{1,0:T(8,128)(2,1)} custom-call(f32[416,1024]{1,0:T(8,128)} %get-tuple-element.136.refs_2_.refs_0_, bf16[416,7168]{1,0:T(8,128)(2,1)} %get-tuple-element.149.refs_4_.refs_8_.refs_1_.refs_0_, bf16[1024,1024]{1,0:T(8,128)(2,1)} %bitcast.38.refs_2_.refs_7_.refs_14_.refs_3_, ...), custom_call_target="tpu_custom_call" | custom-call | flops 27917287424 | bytes 135660128 | tf_op jit(solution)/shard_map/output_forward/pallas_call | solution.py:67
  305.1 8.1 %output_forward.7 = bf16[416,1024]{1,0:T(8,128)(2,1)} custom-call(f32[416,1024]{1,0:T(8,128)} %get-tuple-element.143.refs_3_.refs_0_.refs_2_, bf16[416,7168]{1,0:T(8,128)(2,1)} %get-tuple-element.150.refs_9_.refs_1_.refs_2_.refs_3_, bf16[1024,1024]{1,0:T(8,128)(2,1)} %bitcast.38.refs_2_.refs_7_.refs_14_.refs_3_, ...), custom_call_target="tpu_custom_call" | custom-call | flops 27917287424 | bytes 135660128 | tf_op jit(solution)/shard_map/output_forward/pallas_call | solution.py:67
  321.7 8.3 %reduce.11 = (bf16[512,1024]{1,0:T(8,128)(2,1)}, bf16[512,1024]{1,0:T(8,128)(2,1)}) custom-call(bf16[416,7168]{1,0:T(8,128)(2,1)} %get-tuple-element.149.refs_4_.refs_8_.refs_1_.refs_0_, bf16[416,7168]{1,0:T(8,128)(2,1)} %collective-permute-done.19.refs_1_, bf16[416,7168]{1,0:T(8,128)(2,1)} %get-tuple-element.150.refs_9_.refs_1_.refs_2_.refs_3_, ...), custom_call_target="tpu_custom_call" | custom-call | flops 54525952 | bytes 911360 | tf_op jit(solution)/shard_map/reduce/pallas_call | solution.py:67
  331.6 18.4 %backward_feed.1 = (bf16[416,4096]{1,0:T(8,128)(2,1)}, bf16[416,1024]{1,0:T(8,128)(2,1)}, f32[8,1024]{1,0:T(8,128)}, f32[1,4096]{1,0:T(1,128)}, f32[416,1024]{1,0:T(8,128)}) custom-call(bf16[416,1024]{1,0:T(8,128)(2,1)} %copy-done.15, bf16[416,4096]{1,0:T(8,128)(2,1)} %get-tuple-element.142.refs_1_, f32[416,1024]{1,0:T(8,128)} %get-tuple-element.143.refs_3_.refs_0_.refs_2_, ...), custom_call_target="tpu_custom_call" | custom-call | flops 109051904 | bytes 482817 | tf_op jit(solution)/shard_map/backward_feed/pallas_call | solution.py:67
  359.1 8.3 %reduce.12 = (bf16[512,1024]{1,0:T(8,128)(2,1)}, bf16[512,1024]{1,0:T(8,128)(2,1)}) custom-call(bf16[416,7168]{1,0:T(8,128)(2,1)} %get-tuple-element.149.refs_4_.refs_8_.refs_1_.refs_0_, bf16[416,7168]{1,0:T(8,128)(2,1)} %collective-permute-done.19.refs_1_, bf16[416,7168]{1,0:T(8,128)(2,1)} %get-tuple-element.150.refs_9_.refs_1_.refs_2_.refs_3_, ...), custom_call_target="tpu_custom_call" | custom-call | flops 55834574848 | bytes 933232960 | tf_op jit(solution)/shard_map/reduce/pallas_call | solution.py:67
  371.2 24.6 %backward_attend.1 = (bf16[416,3072]{1,0:T(8,128)(2,1)}, bf16[416,1024]{1,0:T(8,128)(2,1)}, f32[8,1024]{1,0:T(8,128)}) custom-call(bf16[416,1024]{1,0:T(8,128)(2,1)} %get-tuple-element.162.refs_0_.refs_8_, f32[416,1024]{1,0:T(8,128)} %get-tuple-element.163.refs_1_, bf16[416,3072]{1,0:T(8,128)(2,1)} %get-tuple-element.144.refs_7_.refs_2_, ...), custom_call_target="tpu_custom_call" | custom-call | flops 68370432 | bytes 503457 | tf_op jit(solution)/shard_map/backward_attend/pallas_call | solution.py:67
  403.4 8.9 %expand.2 = (bf16[256,2048]{1,0:T(8,128)(2,1)}, bf16[256,2048]{1,0:T(8,128)(2,1)}) custom-call(bf16[416,7168]{1,0:T(8,128)(2,1)} %get-tuple-element.149.refs_4_.refs_8_.refs_1_.refs_0_, bf16[416,7168]{1,0:T(8,128)(2,1)} %collective-permute-done.19.refs_1_, bf16[416,7168]{1,0:T(8,128)(2,1)} %get-tuple-element.150.refs_9_.refs_1_.refs_2_.refs_3_, ...), custom_call_target="tpu_custom_call" | custom-call | flops 55834574848 | bytes 1015021888 | tf_op jit(solution)/shard_map/expand/pallas_call | solution.py:67
  414.2 7.8 %collective-permute-done.33 = bf16[512,1024]{1,0:T(8,128)(2,1)} collective-permute-done((bf16[512,1024]{1,0:T(8,128)(2,1)S(1)}, bf16[512,1024]{1,0:T(8,128)(2,1)}, u32[]{:S(2)}, u32[]{:S(2)}) %collective-permute-start.33) | collective-permute-done | bytes 1048608 | tf_op jit(solution)/shard_map/ppermute | solution.py:845
  427.1 7.9 %qkv.2 = (bf16[256,1536]{1,0:T(8,128)(2,1)}, bf16[256,1536]{1,0:T(8,128)(2,1)}) custom-call(bf16[416,7168]{1,0:T(8,128)(2,1)} %get-tuple-element.149.refs_4_.refs_8_.refs_1_.refs_0_, bf16[416,7168]{1,0:T(8,128)(2,1)} %collective-permute-done.19.refs_1_, bf16[416,7168]{1,0:T(8,128)(2,1)} %get-tuple-element.150.refs_9_.refs_1_.refs_2_.refs_3_, ...), custom_call_target="tpu_custom_call" | custom-call | flops 40894464 | bytes 956416 | tf_op jit(solution)/shard_map/qkv/pallas_call | solution.py:67
  439.8 7.5 %collective-permute-start.38 = (bf16[256,2048]{1,0:T(8,128)(2,1)S(1)}, bf16[256,2048]{1,0:T(8,128)(2,1)}, u32[]{:S(2)}, u32[]{:S(2)}) collective-permute-start(bf16[256,2048]{1,0:T(8,128)(2,1)S(1)} %add_convert_fusion.6), channel_id=1, source_target_pairs={{0,1},{3,2},{4,5},{7,6},{8,9},{11,10},{12,13},{15,14},{16,17},{19,... | collective-permute-start | bytes 3145736 | tf_op jit(solution)/shard_map/ppermute | solution.py:845
  448.9 8.8 %expand.3 = (bf16[256,2048]{1,0:T(8,128)(2,1)}, bf16[256,2048]{1,0:T(8,128)(2,1)}) custom-call(bf16[416,7168]{1,0:T(8,128)(2,1)} %get-tuple-element.149.refs_4_.refs_8_.refs_1_.refs_0_, bf16[416,7168]{1,0:T(8,128)(2,1)} %collective-permute-done.19.refs_1_, bf16[416,7168]{1,0:T(8,128)(2,1)} %get-tuple-element.150.refs_9_.refs_1_.refs_2_.refs_3_, ...), custom_call_target="tpu_custom_call" | custom-call | flops 54525952 | bytes 991232 | tf_op jit(solution)/shard_map/expand/pallas_call | solution.py:67
  461.6 5.5 collective-permute-start.41
  474.8 8.0 %qkv.3 = (bf16[256,1536]{1,0:T(8,128)(2,1)}, bf16[256,1536]{1,0:T(8,128)(2,1)}) custom-call(bf16[416,7168]{1,0:T(8,128)(2,1)} %get-tuple-element.149.refs_4_.refs_8_.refs_1_.refs_0_, bf16[416,7168]{1,0:T(8,128)(2,1)} %collective-permute-done.19.refs_1_, bf16[416,7168]{1,0:T(8,128)(2,1)} %get-tuple-element.150.refs_9_.refs_1_.refs_2_.refs_3_, ...), custom_call_target="tpu_custom_call" | custom-call | flops 40894464 | bytes 956416 | tf_op jit(solution)/shard_map/qkv/pallas_call | solution.py:67
  484.5 6.8 %collective-permute-start.44 = (bf16[256,2048]{1,0:T(8,128)(2,1)S(1)}, bf16[256,2048]{1,0:T(8,128)(2,1)}, u32[]{:S(2)}, u32[]{:S(2)}) collective-permute-start(bf16[256,2048]{1,0:T(8,128)(2,1)S(1)} %add_convert_fusion.3), channel_id=1, source_target_pairs={{0,1},{3,2},{4,5},{7,6},{8,9},{11,10},{12,13},{15,14},{16,17},{19,... | collective-permute-start | bytes 3145736 | tf_op jit(solution)/shard_map/ppermute | solution.py:845
  501.6 6.0 project.1
  512.9 8.2 %collective-permute-start.50 = (bf16[256,1536]{1,0:T(8,128)(2,1)}, bf16[256,1536]{1,0:T(8,128)(2,1)}, u32[]{:S(2)}, u32[]{:S(2)}) collective-permute-start(bf16[256,1536]{1,0:T(8,128)(2,1)} %add_convert_fusion.15), channel_id=1, source_target_pairs={{0,1},{3,2},{4,5},{7,6},{8,9},{11,10},{12,13},{15,14},{16,17},{19,... | collective-permute-start | bytes 2359304 | tf_op jit(solution)/shard_map/ppermute | solution.py:845
  528.7 10.2 %collective-permute-done.49 = bf16[272,1024]{1,0:T(8,128)(2,1)S(1)} collective-permute-done((bf16[272,1024]{1,0:T(8,128)(2,1)S(1)}, bf16[272,1024]{1,0:T(8,128)(2,1)S(1)}, u32[]{:S(2)}, u32[]{:S(2)}) %collective-permute-start.49) | collective-permute-done | bytes 557088 | tf_op jit(solution)/shard_map/ppermute | solution.py:796
  559.9 14.6 %collective-permute-done.55 = bf16[256,2048]{1,0:T(8,128)(2,1)S(1)} collective-permute-done((bf16[256,2048]{1,0:T(8,128)(2,1)S(1)}, bf16[256,2048]{1,0:T(8,128)(2,1)S(1)}, u32[]{:S(2)}, u32[]{:S(2)}) %collective-permute-start.55) | collective-permute-done | bytes 1048608 | tf_op jit(solution)/shard_map/ppermute | solution.py:851
  578.7 12.7 %collective-permute-done.57 = bf16[256,1536]{1,0:T(8,128)(2,1)S(1)} collective-permute-done((bf16[256,1536]{1,0:T(8,128)(2,1)S(1)}, bf16[256,1536]{1,0:T(8,128)(2,1)S(1)}, u32[]{:S(2)}, u32[]{:S(2)}) %collective-permute-start.57) | collective-permute-done | bytes 786464 | tf_op jit(solution)/shard_map/ppermute | solution.py:851
  593.5 8.3 %collective-permute-done.58 = bf16[272,1024]{1,0:T(8,128)(2,1)S(1)} collective-permute-done((bf16[272,1024]{1,0:T(8,128)(2,1)S(1)}, bf16[272,1024]{1,0:T(8,128)(2,1)S(1)}, u32[]{:S(2)}, u32[]{:S(2)}) %collective-permute-start.58) | collective-permute-done | bytes 557088 | tf_op jit(solution)/shard_map/ppermute | solution.py:851
  (307 shorter events, 172.2 us)
Async XLA Ops:
  10.0 45.5 %collective-permute-start.9 = (bf16[128,5120]{1,0:T(8,128)(2,1)}, bf16[128,5120]{1,0:T(8,128)(2,1)}, u32[]{:S(2)}, u32[]{:S(2)}) collective-permute-start(bf16[128,5120]{1,0:T(8,128)(2,1)} %fusion), channel_id=1, source_target_pairs={{0,8},{4,12},{8,0},{12,4},{1,9},{5,13},{9,1},{13,5},{2,10},{6,14},... | collective-permute-start | bytes 3932168 | tf_op jit(solution)/shard_map/ppermute | solution.py:796
  17.1 41.1 %collective-permute-start.8 = (bf16[256,5120]{1,0:T(8,128)(2,1)S(1)}, bf16[256,5120]{1,0:T(8,128)(2,1)}, u32[]{:S(2)}, u32[]{:S(2)}) collective-permute-start(bf16[256,5120]{1,0:T(8,128)(2,1)S(1)} %pad_maximum_fusion.refs_2_.refs_8_.refs_14_.refs_13_.refs_19_.refs_20_.refs_26_.refs_9_.refs_6_), channel_id=1, source_target_pairs={{0,4},{4,0},{8,12},{12,8},{1,5},{5,1},{9,13},{13,9},{2,6},{6,2},{1... | collective-permute-start | bytes 7864328 | tf_op jit(solution)/shard_map/ppermute | solution.py:793
  27.9 27.6 %collective-permute-start.2 = (bf16[128,3072]{1,0:T(8,128)(2,1)S(1)}, bf16[128,3072]{1,0:T(8,128)(2,1)S(1)}, u32[]{:S(2)}, u32[]{:S(2)}) collective-permute-start(bf16[128,3072]{1,0:T(8,128)(2,1)S(1)} %collective-permute-done.refs_3_.refs_4_.refs_27_.refs_34_.refs_14_), channel_id=1, source_target_pairs={{0,1},{1,0},{2,3},{3,2},{4,5},{5,4},{6,7},{7,6},{8,9},{9,8},{10,11... | collective-permute-start | bytes 2359304 | tf_op jit(solution)/shard_map/ppermute | solution.py:799
  55.6 39.5 %collective-permute-start.10 = (bf16[128,5120]{1,0:T(8,128)(2,1)}, bf16[128,5120]{1,0:T(8,128)(2,1)}, u32[]{:S(2)}, u32[]{:S(2)}) collective-permute-start(bf16[128,5120]{1,0:T(8,128)(2,1)} %collective-permute-done.9.refs_4_.refs_10_.refs_16_.refs_15_.refs_21_.refs_22_.refs_28_.refs_11_.refs_8_), channel_id=1, source_target_pairs={{0,1},{1,0},{2,3},{3,2},{4,5},{5,4},{6,7},{7,6},{8,9},{9,8},{10,11... | collective-permute-start | bytes 3932168 | tf_op jit(solution)/shard_map/ppermute | solution.py:799
  57.2 38.3 %collective-permute-start.14 = (bf16[768,1024]{1,0:T(8,128)(2,1)}, bf16[768,1024]{1,0:T(8,128)(2,1)}, u32[]{:S(2)}, u32[]{:S(2)}) collective-permute-start(bf16[768,1024]{1,0:T(8,128)(2,1)} %dynamic-slice_bitcast_fusion), channel_id=1, source_target_pairs={{0,8},{4,12},{8,0},{12,4},{1,9},{5,13},{9,1},{13,5},{2,10},{6,14},... | collective-permute-start | bytes 4718600 | tf_op jit(solution)/shard_map/ppermute | solution.py:796
  58.2 57.4 %collective-permute-start.13 = (bf16[1024,1024]{1,0:T(8,128)(2,1)}, bf16[1024,1024]{1,0:T(8,128)(2,1)}, u32[]{:S(2)}, u32[]{:S(2)}) collective-permute-start(bf16[1024,1024]{1,0:T(8,128)(2,1)} %bitcast.38.refs_2_.refs_7_.refs_14_.refs_3_), channel_id=1, source_target_pairs={{0,4},{4,0},{8,12},{12,8},{1,5},{5,1},{9,13},{13,9},{2,6},{6,2},{1... | collective-permute-start | bytes 6291464 | tf_op jit(solution)/shard_map/ppermute | solution.py:793
  124.5 30.0 %collective-permute-start.18 = (bf16[416,1024]{1,0:T(8,128)(2,1)}, bf16[416,1024]{1,0:T(8,128)(2,1)S(1)}, u32[]{:S(2)}, u32[]{:S(2)}) collective-permute-start(bf16[416,1024]{1,0:T(8,128)(2,1)} %output_forward.4), channel_id=1, source_target_pairs={{0,16},{1,17},{2,18},{3,19},{4,20},{5,21},{6,22},{7,23},{8,24},{9,... | collective-permute-start | bytes 2555912 | tf_op jit(solution)/shard_map/ppermute | solution.py:887
  152.3 72.3 %collective-permute-start.20 = (bf16[416,1024]{1,0:T(8,128)(2,1)}, bf16[416,1024]{1,0:T(8,128)(2,1)}, u32[]{:S(2)}, u32[]{:S(2)}) collective-permute-start(bf16[416,1024]{1,0:T(8,128)(2,1)} %output_forward.5), channel_id=1, source_target_pairs={{0,16},{1,17},{2,18},{3,19},{4,20},{5,21},{6,22},{7,23},{8,24},{9,... | collective-permute-start | bytes 2555912 | tf_op jit(solution)/shard_map/ppermute | solution.py:887
  186.0 111.0 %collective-permute-start.19 = (bf16[416,7168]{1,0:T(8,128)(2,1)}, bf16[416,7168]{1,0:T(8,128)(2,1)}, u32[]{:S(2)}, u32[]{:S(2)}) collective-permute-start(bf16[416,7168]{1,0:T(8,128)(2,1)} %get-tuple-element.149.refs_4_.refs_8_.refs_1_.refs_0_), channel_id=1, source_target_pairs={{0,4},{4,0},{8,12},{12,8},{1,5},{5,1},{9,13},{13,9},{2,6},{6,2},{1... | collective-permute-start | bytes 17891336 | tf_op jit(solution)/shard_map/ppermute | solution.py:793
  223.3 32.4 %collective-permute-start.22 = (bf16[416,1024]{1,0:T(8,128)(2,1)}, bf16[416,1024]{1,0:T(8,128)(2,1)S(1)}, u32[]{:S(2)}, u32[]{:S(2)}) collective-permute-start(bf16[416,1024]{1,0:T(8,128)(2,1)} %get-tuple-element.139), channel_id=1, source_target_pairs={{16,0},{17,1},{18,2},{19,3},{20,4},{21,5},{22,6},{23,7},{24,8},{25... | collective-permute-start | bytes 2555912 | tf_op jit(solution)/shard_map/ppermute | solution.py:887
  224.6 72.3 %collective-permute-start.24 = (bf16[416,9216]{1,0:T(8,128)(2,1)}, bf16[416,9216]{1,0:T(8,128)(2,1)}, u32[]{:S(2)}, u32[]{:S(2)}) collective-permute-start(bf16[416,9216]{1,0:T(8,128)(2,1)} %get-tuple-element.147.refs_5_), channel_id=1, source_target_pairs={{0,4},{4,0},{8,12},{12,8},{1,5},{5,1},{9,13},{13,9},{2,6},{6,2},{1... | collective-permute-start | bytes 23003144 | tf_op jit(solution)/shard_map/ppermute | solution.py:793
  255.6 49.5 %collective-permute-start.21 = (bf16[416,7168]{1,0:T(8,128)(2,1)}, bf16[416,7168]{1,0:T(8,128)(2,1)}, u32[]{:S(2)}, u32[]{:S(2)}) collective-permute-start(bf16[416,7168]{1,0:T(8,128)(2,1)} %get-tuple-element.150.refs_9_.refs_1_.refs_2_.refs_3_), channel_id=1, source_target_pairs={{0,4},{4,0},{8,12},{12,8},{1,5},{5,1},{9,13},{13,9},{2,6},{6,2},{1... | collective-permute-start | bytes 17891336 | tf_op jit(solution)/shard_map/ppermute | solution.py:793
  293.8 27.0 %collective-permute-start.23 = (bf16[416,9216]{1,0:T(8,128)(2,1)}, bf16[416,9216]{1,0:T(8,128)(2,1)}, u32[]{:S(2)}, u32[]{:S(2)}) collective-permute-start(bf16[416,9216]{1,0:T(8,128)(2,1)} %get-tuple-element.146.refs_4_), channel_id=1, source_target_pairs={{0,4},{4,0},{8,12},{12,8},{1,5},{5,1},{9,13},{13,9},{2,6},{6,2},{1... | collective-permute-start | bytes 23003144 | tf_op jit(solution)/shard_map/ppermute | solution.py:793
  330.1 25.5 %collective-permute-start.29 = (bf16[512,1024]{1,0:T(8,128)(2,1)}, bf16[512,1024]{1,0:T(8,128)(2,1)S(1)}, u32[]{:S(2)}, u32[]{:S(2)}) collective-permute-start(bf16[512,1024]{1,0:T(8,128)(2,1)} %get-tuple-element.159), channel_id=1, source_target_pairs={{0,8},{4,12},{8,0},{12,4},{1,9},{5,13},{9,1},{13,5},{2,10},{6,14},... | collective-permute-start | bytes 3145736 | tf_op jit(solution)/shard_map/ppermute | solution.py:796
  356.0 39.9 %collective-permute-start.31 = (bf16[512,1024]{1,0:T(8,128)(2,1)S(1)}, bf16[512,1024]{1,0:T(8,128)(2,1)S(1)}, u32[]{:S(2)}, u32[]{:S(2)}) collective-permute-start(bf16[512,1024]{1,0:T(8,128)(2,1)S(1)} %add_convert_fusion.11), channel_id=1, source_target_pairs={{0,1},{3,2},{4,5},{7,6},{8,9},{11,10},{12,13},{15,14},{16,17},{19,... | collective-permute-start | bytes 3145736 | tf_op jit(solution)/shard_map/ppermute | solution.py:845
  367.5 29.9 %collective-permute-start.32 = (bf16[512,1024]{1,0:T(8,128)(2,1)}, bf16[512,1024]{1,0:T(8,128)(2,1)}, u32[]{:S(2)}, u32[]{:S(2)}) collective-permute-start(bf16[512,1024]{1,0:T(8,128)(2,1)} %get-tuple-element.168), channel_id=1, source_target_pairs={{0,8},{4,12},{8,0},{12,4},{1,9},{5,13},{9,1},{13,5},{2,10},{6,14},... | collective-permute-start | bytes 3145736 | tf_op jit(solution)/shard_map/ppermute | solution.py:796
  401.4 33.6 %collective-permute-start.34 = (bf16[512,1024]{1,0:T(8,128)(2,1)}, bf16[512,1024]{1,0:T(8,128)(2,1)}, u32[]{:S(2)}, u32[]{:S(2)}) collective-permute-start(bf16[512,1024]{1,0:T(8,128)(2,1)} %add_convert_fusion.10), channel_id=1, source_target_pairs={{1,2},{2,1},{5,6},{6,5},{9,10},{10,9},{13,14},{14,13},{17,18},{18,... | collective-permute-start | bytes 3145736 | tf_op jit(solution)/shard_map/ppermute | solution.py:848
  412.2 25.9 %collective-permute-start.35 = (bf16[256,2048]{1,0:T(8,128)(2,1)}, bf16[256,2048]{1,0:T(8,128)(2,1)}, u32[]{:S(2)}, u32[]{:S(2)}) collective-permute-start(bf16[256,2048]{1,0:T(8,128)(2,1)} %get-tuple-element.176), channel_id=1, source_target_pairs={{0,8},{4,12},{8,0},{12,4},{1,9},{5,13},{9,1},{13,5},{2,10},{6,14},... | collective-permute-start | bytes 3145736 | tf_op jit(solution)/shard_map/ppermute | solution.py:796
  424.0 43.1 %collective-permute-start.37 = (bf16[512,1024]{1,0:T(8,128)(2,1)S(1)}, bf16[512,1024]{1,0:T(8,128)(2,1)}, u32[]{:S(2)}, u32[]{:S(2)}) collective-permute-start(bf16[512,1024]{1,0:T(8,128)(2,1)S(1)} %add_convert_fusion.8), channel_id=1, source_target_pairs={{1,2},{2,1},{5,6},{6,5},{9,10},{10,9},{13,14},{14,13},{17,18},{18,... | collective-permute-start | bytes 3145736 | tf_op jit(solution)/shard_map/ppermute | solution.py:848
  439.8 31.1 %collective-permute-start.38 = (bf16[256,2048]{1,0:T(8,128)(2,1)S(1)}, bf16[256,2048]{1,0:T(8,128)(2,1)}, u32[]{:S(2)}, u32[]{:S(2)}) collective-permute-start(bf16[256,2048]{1,0:T(8,128)(2,1)S(1)} %add_convert_fusion.6), channel_id=1, source_target_pairs={{0,1},{3,2},{4,5},{7,6},{8,9},{11,10},{12,13},{15,14},{16,17},{19,... | collective-permute-start | bytes 3145736 | tf_op jit(solution)/shard_map/ppermute | solution.py:845
  447.4 27.2 %collective-permute-start.39 = (bf16[512,1024]{1,0:T(8,128)(2,1)S(1)}, bf16[512,1024]{1,0:T(8,128)(2,1)S(1)}, u32[]{:S(2)}, u32[]{:S(2)}) collective-permute-start(bf16[512,1024]{1,0:T(8,128)(2,1)S(1)} %add_convert_fusion.7), channel_id=1, source_target_pairs={{1,0},{2,3},{5,4},{6,7},{9,8},{10,11},{13,12},{14,15},{17,16},{18,... | collective-permute-start | bytes 3145736 | tf_op jit(solution)/shard_map/ppermute | solution.py:851
  457.7 25.1 %collective-permute-start.40 = (bf16[256,2048]{1,0:T(8,128)(2,1)}, bf16[256,2048]{1,0:T(8,128)(2,1)}, u32[]{:S(2)}, u32[]{:S(2)}) collective-permute-start(bf16[256,2048]{1,0:T(8,128)(2,1)} %get-tuple-element.187), channel_id=1, source_target_pairs={{0,8},{4,12},{8,0},{12,4},{1,9},{5,13},{9,1},{13,5},{2,10},{6,14},... | collective-permute-start | bytes 3145736 | tf_op jit(solution)/shard_map/ppermute | solution.py:796
  461.6 30.2 %collective-permute-start.41 = (bf16[256,1536]{1,0:T(8,128)(2,1)}, bf16[256,1536]{1,0:T(8,128)(2,1)}, u32[]{:S(2)}, u32[]{:S(2)}) collective-permute-start(bf16[256,1536]{1,0:T(8,128)(2,1)} %add_convert_fusion.17), channel_id=1, source_target_pairs={{0,1},{3,2},{4,5},{7,6},{8,9},{11,10},{12,13},{15,14},{16,17},{19,... | collective-permute-start | bytes 2359304 | tf_op jit(solution)/shard_map/ppermute | solution.py:845
  469.7 25.2 %collective-permute-start.42 = (bf16[512,1024]{1,0:T(8,128)(2,1)}, bf16[512,1024]{1,0:T(8,128)(2,1)}, u32[]{:S(2)}, u32[]{:S(2)}) collective-permute-start(bf16[512,1024]{1,0:T(8,128)(2,1)} %add_convert_fusion.5), channel_id=1, source_target_pairs={{1,0},{2,3},{5,4},{6,7},{9,8},{10,11},{13,12},{14,15},{17,16},{18,... | collective-permute-start | bytes 3145736 | tf_op jit(solution)/shard_map/ppermute | solution.py:851
  472.6 26.1 %collective-permute-start.43 = (bf16[256,2048]{1,0:T(8,128)(2,1)S(1)}, bf16[256,2048]{1,0:T(8,128)(2,1)}, u32[]{:S(2)}, u32[]{:S(2)}) collective-permute-start(bf16[256,2048]{1,0:T(8,128)(2,1)S(1)} %add_convert_fusion.4), channel_id=1, source_target_pairs={{1,2},{2,1},{5,6},{6,5},{9,10},{10,9},{13,14},{14,13},{17,18},{18,... | collective-permute-start | bytes 3145736 | tf_op jit(solution)/shard_map/ppermute | solution.py:848
  484.5 24.5 %collective-permute-start.44 = (bf16[256,2048]{1,0:T(8,128)(2,1)S(1)}, bf16[256,2048]{1,0:T(8,128)(2,1)}, u32[]{:S(2)}, u32[]{:S(2)}) collective-permute-start(bf16[256,2048]{1,0:T(8,128)(2,1)S(1)} %add_convert_fusion.3), channel_id=1, source_target_pairs={{0,1},{3,2},{4,5},{7,6},{8,9},{11,10},{12,13},{15,14},{16,17},{19,... | collective-permute-start | bytes 3145736 | tf_op jit(solution)/shard_map/ppermute | solution.py:845
  493.3 31.4 %collective-permute-start.47 = (bf16[256,1536]{1,0:T(8,128)(2,1)S(1)}, bf16[256,1536]{1,0:T(8,128)(2,1)}, u32[]{:S(2)}, u32[]{:S(2)}) collective-permute-start(bf16[256,1536]{1,0:T(8,128)(2,1)S(1)} %add_convert_fusion.16), channel_id=1, source_target_pairs={{1,2},{2,1},{5,6},{6,5},{9,10},{10,9},{13,14},{14,13},{17,18},{18,... | collective-permute-start | bytes 2359304 | tf_op jit(solution)/shard_map/ppermute | solution.py:848
  500.3 27.0 %collective-permute-start.48 = (bf16[256,2048]{1,0:T(8,128)(2,1)S(1)}, bf16[256,2048]{1,0:T(8,128)(2,1)}, u32[]{:S(2)}, u32[]{:S(2)}) collective-permute-start(bf16[256,2048]{1,0:T(8,128)(2,1)S(1)} %add_convert_fusion.2), channel_id=1, source_target_pairs={{1,0},{2,3},{5,4},{6,7},{9,8},{10,11},{13,12},{14,15},{17,16},{18,... | collective-permute-start | bytes 3145736 | tf_op jit(solution)/shard_map/ppermute | solution.py:851
  512.9 27.5 %collective-permute-start.50 = (bf16[256,1536]{1,0:T(8,128)(2,1)}, bf16[256,1536]{1,0:T(8,128)(2,1)}, u32[]{:S(2)}, u32[]{:S(2)}) collective-permute-start(bf16[256,1536]{1,0:T(8,128)(2,1)} %add_convert_fusion.15), channel_id=1, source_target_pairs={{0,1},{3,2},{4,5},{7,6},{8,9},{11,10},{12,13},{15,14},{16,17},{19,... | collective-permute-start | bytes 2359304 | tf_op jit(solution)/shard_map/ppermute | solution.py:845
  544.6 29.9 %collective-permute-start.55 = (bf16[256,2048]{1,0:T(8,128)(2,1)S(1)}, bf16[256,2048]{1,0:T(8,128)(2,1)S(1)}, u32[]{:S(2)}, u32[]{:S(2)}) collective-permute-start(bf16[256,2048]{1,0:T(8,128)(2,1)S(1)} %add_convert_fusion), channel_id=1, source_target_pairs={{1,0},{2,3},{5,4},{6,7},{9,8},{10,11},{13,12},{14,15},{17,16},{18,... | collective-permute-start | bytes 3145736 | tf_op jit(solution)/shard_map/ppermute | solution.py:851
  552.2 24.9 %collective-permute-start.56 = (bf16[272,1024]{1,0:T(8,128)(2,1)S(1)}, bf16[272,1024]{1,0:T(8,128)(2,1)S(1)}, u32[]{:S(2)}, u32[]{:S(2)}) collective-permute-start(bf16[272,1024]{1,0:T(8,128)(2,1)S(1)} %add_convert_fusion.19), channel_id=1, source_target_pairs={{1,2},{2,1},{5,6},{6,5},{9,10},{10,9},{13,14},{14,13},{17,18},{18,... | collective-permute-start | bytes 1671176 | tf_op jit(solution)/shard_map/ppermute | solution.py:848
  558.6 32.8 %collective-permute-start.57 = (bf16[256,1536]{1,0:T(8,128)(2,1)S(1)}, bf16[256,1536]{1,0:T(8,128)(2,1)S(1)}, u32[]{:S(2)}, u32[]{:S(2)}) collective-permute-start(bf16[256,1536]{1,0:T(8,128)(2,1)S(1)} %add_convert_fusion.12), channel_id=1, source_target_pairs={{1,0},{2,3},{5,4},{6,7},{9,8},{10,11},{13,12},{14,15},{17,16},{18,... | collective-permute-start | bytes 2359304 | tf_op jit(solution)/shard_map/ppermute | solution.py:851
  (74 other events, 765.4 us)

commit v10 on v9

--- a/solution.py
+++ b/solution.py
@@ -176,18 +176,16 @@
             mixed[span, pl.ds(offset, pair)] = (inside / turned).astype(BF16)
             if logs is None:
                 continue
-            logged = jnp.log(turned)
-            first = tops[0] + logged[:, 0:1]
-            second = tops[1] + logged[:, head : head + 1]
-            known = columns[image]
-            known = jnp.where(lane == 2 * index, first, known)
-            columns[image] = jnp.where(lane == 2 * index + 1, second, known)
+            logged = jnp.where(left, tops[0], tops[1]) + jnp.log(turned)
+            columns[image] = jnp.where((lane & (head - 1)) == index, logged, columns[image])
         return carry
 
-    lax.fori_loop(0, HEADS // 2, heads, 0)
+    lax.fori_loop(0, HEADS // 2, heads, 0, unroll=2)
     if logs is not None:
         for image in range(count):
-            logs[image] = columns[image].T[0:HEADS]
+            rows_of = columns[image].T
+            logs[image, 0 : HEADS // 2] = rows_of[0 : HEADS // 2]
+            logs[image, HEADS // 2 : HEADS] = rows_of[head : head + HEADS // 2]
 
 
 def hidden_stage(x, vec, mixed, middle, active, second, slope, full_out, full, first_load, loads):
@@ -489,7 +487,7 @@
             found = []
             for side in range(2):
                 mine = left if side == 0 else ~left
-                log = logs[image, pl.ds(2 * index + side, 1), :]
+                log = logs[image, pl.ds(side * (HEADS // 2) + index, 1), :]
                 dot = stage[image, pl.ds(2 * index + side, 1), 0:space]
                 scores = contract(jnp.where(mine, wide, 0.0).astype(BF16), query, 1, 1)
                 chance = jnp.exp(jnp.where(key_live, scores - log, NEGATIVE))
@@ -508,7 +506,7 @@
                 grads[span, pl.ds(offset, pair)] = jnp.where(live, total, 0.0).astype(BF16)
         return carry
 
-    lax.fori_loop(0, HEADS // 2, heads, 0)
+    lax.fori_loop(0, HEADS // 2, heads, 0, unroll=4)
     wait_all(load)
     for block in range(2):
         normal[:, block * half : (block + 1) * half] = contract(

time: 614 us -> 600 us (0.977)
  Pallas kernels: 326 us -> 312 us
    pallas_call x21, Pallas kernels: 326 us -> 312 us  [call(): pl.pallas_call(body, out_shape=out_shape, in_specs=specs, out_specs=[VMEM...]
  transfers between devices with their start and end apart: 59 -> 59, of which waited for: 18 -> 17; matrix products, arithmetic and copies ran while one was open for 13% -> 13% of each run, Pallas kernels for 51% -> 50%
where the time goes in v10:
time: 600 us; the launch traced here: 592 us
  Pallas kernels  312 us (52%)
  waiting for transfers between devices  97.2 us (16%)
  starting transfers between devices  85.1 us (14%)
  other arithmetic  60.3 us (10%)
  local copies, waits for them, and re-layouts  34.5 us (6%)
    pallas_call x21, Pallas kernels, call(): pl.pallas_call(body, out_shape=out_shape, in_specs=specs, out_specs=[VMEM...  312 us
    ppermute x11, waiting for transfers between devices, across(): return lax.ppermute(block, 'group', [(i, i ^ 2) for i in range(4)])  40.2 us
    ppermute x7, waiting for transfers between devices, total(): outward = lax.ppermute(summed, 'replica', [(1, 0), (2, 3)])  35.9 us
    ppermute x7, starting transfers between devices, total(): inward = lax.ppermute(mine, 'replica', [(0, 1), (3, 2)])  35.1 us
    convert_element_type x21, other arithmetic, added(): return total.astype(values[0].dtype)  29.7 us
    unnamed x104, local copies, waits for them, and re-layouts  13.2 us
    ppermute x11, starting transfers between devices, across(): return lax.ppermute(block, 'group', [(i, i ^ 2) for i in range(4)])  13.2 us
  transfers between devices with their start and end apart: 59, of which 17 were waited for; matrix products, arithmetic and copies ran while one was open for 13% of the time, Pallas kernels for 50%

profile of v10, /device:TPU:0, one launch (start us, length us, event | category | flops | bytes accessed | tf_op | source)
XLA Modules:
  0.0 591.7 jit_solution(6741695971235631602)
XLA Ops:
  22.2 5.8 collective-permute-done.refs_3_.refs_4_.refs_27_.refs_34_.refs_14_
  38.7 16.9 %collective-permute-done.9.refs_4_.refs_10_.refs_16_.refs_15_.refs_21_.refs_22_.refs_28_.refs_11_.refs_8_ = bf16[128,5120]{1,0:T(8,128)(2,1)} collective-permute-done((bf16[128,5120]{1,0:T(8,128)(2,1)}, bf16[128,5120]{1,0:T(8,128)(2,1)}, u32[]{:S(2)}, u32[]{:S(2)}) %collective-permute-start.9) | collective-permute-done | bytes 1310752 | tf_op jit(solution)/shard_map/ppermute | solution.py:794
  63.1 13.4 %forward_attend.2.refs_1_ = bf16[416,1024]{1,0:T(8,128)(2,1)} custom-call(bf16[416,1024]{1,0:T(8,128)(2,1)} %bitcast.106, bf16[256,3072]{1,0:T(8,128)(2,1)} %bitcast.93, bf16[256,3072]{1,0:T(8,128)(2,1)} %collective-permute-done.1.refs_2_.refs_3_.refs_26_.refs_33_.refs_13_, bf16[128,3072]{1,0:T(8,128)(2,1)} %copy-done.5, bf16[128,3072]{1,0:T(8,128)(2,1)} %copy-done.6, ...), custom_call_target="tpu_custom_call" | custom-call | flops 46432256 | bytes 125697 | tf_op jit(solution)/shard_map/forward_attend/pallas_call | solution.py:67
  76.7 13.3 %forward_attend.3.refs_1_ = bf16[416,1024]{1,0:T(8,128)(2,1)} custom-call(bf16[416,1024]{1,0:T(8,128)(2,1)} %bitcast.100, bf16[256,3072]{1,0:T(8,128)(2,1)} %bitcast.94, bf16[256,3072]{1,0:T(8,128)(2,1)} %collective-permute-done.1.refs_2_.refs_3_.refs_26_.refs_33_.refs_13_, bf16[128,3072]{1,0:T(8,128)(2,1)} %copy-done.5, bf16[128,3072]{1,0:T(8,128)(2,1)} %copy-done.6, ...), custom_call_target="tpu_custom_call" | custom-call | flops 46432256 | bytes 125697 | tf_op jit(solution)/shard_map/forward_attend/pallas_call | solution.py:67
  96.7 13.7 %forward_feed.2 = (f32[416,1024]{1,0:T(8,128)}, bf16[416,4096]{1,0:T(8,128)(2,1)}) custom-call(bf16[416,1024]{1,0:T(8,128)(2,1)} %bitcast.107, bf16[416,1024]{1,0:T(8,128)(2,1)} %forward_attend.2.refs_1_, bf16[256,5120]{1,0:T(8,128)(2,1)} %copy-done, ...), custom_call_target="tpu_custom_call" | custom-call | flops 68157440 | bytes 434945 | tf_op jit(solution)/shard_map/forward_feed/pallas_call | solution.py:67
  113.2 8.1 %output_forward.4 = bf16[416,1024]{1,0:T(8,128)(2,1)} custom-call(f32[416,1024]{1,0:T(8,128)} %get-tuple-element.123.refs_0_, bf16[416,4096]{1,0:T(8,128)(2,1)} %get-tuple-element.124.refs_1_, bf16[1024,1024]{1,0:T(8,128)(2,1)} %bitcast.38.refs_2_.refs_7_.refs_14_.refs_3_, bf16[1024,1024]{1,0:T(8,128)(2,1)} %collective-permute-done.13.refs_3_.refs_8_.refs_15_.refs_4_, ...), custom_call_target="tpu_custom_call" | custom-call | flops 54525952 | bytes 225025 | tf_op jit(solution)/shard_map/output_forward/pallas_call | solution.py:67
  127.4 13.7 %forward_feed.3 = (f32[416,1024]{1,0:T(8,128)}, bf16[416,4096]{1,0:T(8,128)(2,1)}) custom-call(bf16[416,1024]{1,0:T(8,128)(2,1)} %bitcast.101, bf16[416,1024]{1,0:T(8,128)(2,1)} %forward_attend.3.refs_1_, bf16[256,5120]{1,0:T(8,128)(2,1)} %copy-done, ...), custom_call_target="tpu_custom_call" | custom-call | flops 68157440 | bytes 434945 | tf_op jit(solution)/shard_map/forward_feed/pallas_call | solution.py:67
  141.1 8.1 %output_forward.5 = bf16[416,1024]{1,0:T(8,128)(2,1)} custom-call(f32[416,1024]{1,0:T(8,128)} %get-tuple-element.130.refs_0_, bf16[416,4096]{1,0:T(8,128)(2,1)} %get-tuple-element.132.refs_1_, bf16[1024,1024]{1,0:T(8,128)(2,1)} %bitcast.38.refs_2_.refs_7_.refs_14_.refs_3_, bf16[1024,1024]{1,0:T(8,128)(2,1)} %collective-permute-done.13.refs_3_.refs_8_.refs_15_.refs_4_, ...), custom_call_target="tpu_custom_call" | custom-call | flops 54525952 | bytes 225025 | tf_op jit(solution)/shard_map/output_forward/pallas_call | solution.py:67
  152.3 27.1 %forward_attend_feed.2 = (bf16[416,7168]{1,0:T(8,128)(2,1)}, bf16[416,3072]{1,0:T(8,128)(2,1)}, f32[2,16,208]{2,1,0:T(8,128)}, f32[416,1024]{1,0:T(8,128)}, bf16[416,4096]{1,0:T(8,128)(2,1)}) custom-call(bf16[416,1024]{1,0:T(8,128)(2,1)} %bitcast.108, bf16[416,1024]{1,0:T(8,128)(2,1)} %copy-done.45, bf16[256,3072]{1,0:T(8,128)(2,1)} %bitcast.95, ...), custom_call_target="tpu_custom_call" | custom-call | flops 58669924352 | bytes 341394016 | tf_op jit(solution)/shard_map/forward_attend_feed/pallas_call | solution.py:67
  179.5 36.2 %backward_feed_attend.2 = (bf16[416,9216]{1,0:T(8,128)(2,1)}, f32[8,1024]{1,0:T(8,128)}, f32[1,4096]{1,0:T(1,128)}, bf16[416,1024]{1,0:T(8,128)(2,1)}, f32[8,1024]{1,0:T(8,128)}) custom-call(bf16[416,1024]{1,0:T(8,128)(2,1)} %bitcast.127, bf16[416,4096]{1,0:T(8,128)(2,1)} %get-tuple-element.135.refs_1_.refs_0_, ...), custom_call_target="tpu_custom_call" | custom-call | flops 90840236032 | bytes 477315680 | tf_op jit(solution)/shard_map/backward_feed_attend/pallas_call | solution.py:67
  217.5 27.0 %forward_attend_feed.3 = (bf16[416,7168]{1,0:T(8,128)(2,1)}, bf16[416,3072]{1,0:T(8,128)(2,1)}, f32[2,16,208]{2,1,0:T(8,128)}, f32[416,1024]{1,0:T(8,128)}, bf16[416,4096]{1,0:T(8,128)(2,1)}) custom-call(bf16[416,1024]{1,0:T(8,128)(2,1)} %bitcast.102, bf16[416,1024]{1,0:T(8,128)(2,1)} %collective-permute-done.20.refs_1_.refs_13_, ...), custom_call_target="tpu_custom_call" | custom-call | flops 58669924352 | bytes 341394016 | tf_op jit(solution)/shard_map/forward_attend_feed/pallas_call | solution.py:67
  245.6 36.4 %backward_feed_attend.3 = (bf16[416,9216]{1,0:T(8,128)(2,1)}, f32[8,1024]{1,0:T(8,128)}, f32[1,4096]{1,0:T(1,128)}, bf16[416,1024]{1,0:T(8,128)(2,1)}, f32[8,1024]{1,0:T(8,128)}) custom-call(bf16[416,4096]{1,0:T(8,128)(2,1)} %get-tuple-element.135.refs_1_.refs_0_, bf16[416,4096]{1,0:T(8,128)(2,1)} %get-tuple-element.142.refs_1_, ...), custom_call_target="tpu_custom_call" | custom-call | flops 90840236032 | bytes 600212096 | tf_op jit(solution)/shard_map/backward_feed_attend/pallas_call | solution.py:67
  284.8 8.1 %output_forward.6 = bf16[416,1024]{1,0:T(8,128)(2,1)} custom-call(f32[416,1024]{1,0:T(8,128)} %get-tuple-element.136.refs_2_.refs_0_, bf16[416,7168]{1,0:T(8,128)(2,1)} %get-tuple-element.149.refs_4_.refs_8_.refs_1_.refs_0_, bf16[1024,1024]{1,0:T(8,128)(2,1)} %bitcast.38.refs_2_.refs_7_.refs_14_.refs_3_, ...), custom_call_target="tpu_custom_call" | custom-call | flops 27917287424 | bytes 135660128 | tf_op jit(solution)/shard_map/output_forward/pallas_call | solution.py:67
  292.9 8.1 %output_forward.7 = bf16[416,1024]{1,0:T(8,128)(2,1)} custom-call(f32[416,1024]{1,0:T(8,128)} %get-tuple-element.143.refs_3_.refs_0_.refs_2_, bf16[416,7168]{1,0:T(8,128)(2,1)} %get-tuple-element.150.refs_9_.refs_1_.refs_2_.refs_3_, bf16[1024,1024]{1,0:T(8,128)(2,1)} %bitcast.38.refs_2_.refs_7_.refs_14_.refs_3_, ...), custom_call_target="tpu_custom_call" | custom-call | flops 27917287424 | bytes 135660128 | tf_op jit(solution)/shard_map/output_forward/pallas_call | solution.py:67
  309.9 8.3 %reduce.11 = (bf16[512,1024]{1,0:T(8,128)(2,1)}, bf16[512,1024]{1,0:T(8,128)(2,1)}) custom-call(bf16[416,7168]{1,0:T(8,128)(2,1)} %get-tuple-element.149.refs_4_.refs_8_.refs_1_.refs_0_, bf16[416,7168]{1,0:T(8,128)(2,1)} %collective-permute-done.19.refs_1_, bf16[416,7168]{1,0:T(8,128)(2,1)} %get-tuple-element.150.refs_9_.refs_1_.refs_2_.refs_3_, ...), custom_call_target="tpu_custom_call" | custom-call | flops 54525952 | bytes 911360 | tf_op jit(solution)/shard_map/reduce/pallas_call | solution.py:67
  318.9 18.4 %backward_feed.1 = (bf16[416,4096]{1,0:T(8,128)(2,1)}, bf16[416,1024]{1,0:T(8,128)(2,1)}, f32[8,1024]{1,0:T(8,128)}, f32[1,4096]{1,0:T(1,128)}, f32[416,1024]{1,0:T(8,128)}) custom-call(bf16[416,1024]{1,0:T(8,128)(2,1)} %copy-done.15, bf16[416,4096]{1,0:T(8,128)(2,1)} %get-tuple-element.142.refs_1_, f32[416,1024]{1,0:T(8,128)} %get-tuple-element.143.refs_3_.refs_0_.refs_2_, ...), custom_call_target="tpu_custom_call" | custom-call | flops 109051904 | bytes 482817 | tf_op jit(solution)/shard_map/backward_feed/pallas_call | solution.py:67
  337.9 5.9 collective-permute-done.29
  347.9 8.3 %reduce.12 = (bf16[512,1024]{1,0:T(8,128)(2,1)}, bf16[512,1024]{1,0:T(8,128)(2,1)}) custom-call(bf16[416,7168]{1,0:T(8,128)(2,1)} %get-tuple-element.149.refs_4_.refs_8_.refs_1_.refs_0_, bf16[416,7168]{1,0:T(8,128)(2,1)} %collective-permute-done.19.refs_1_, bf16[416,7168]{1,0:T(8,128)(2,1)} %get-tuple-element.150.refs_9_.refs_1_.refs_2_.refs_3_, ...), custom_call_target="tpu_custom_call" | custom-call | flops 55834574848 | bytes 933232960 | tf_op jit(solution)/shard_map/reduce/pallas_call | solution.py:67
  359.0 24.0 %backward_attend.1 = (bf16[416,3072]{1,0:T(8,128)(2,1)}, bf16[416,1024]{1,0:T(8,128)(2,1)}, f32[8,1024]{1,0:T(8,128)}) custom-call(bf16[416,1024]{1,0:T(8,128)(2,1)} %get-tuple-element.162.refs_0_.refs_8_, f32[416,1024]{1,0:T(8,128)} %get-tuple-element.163.refs_1_, bf16[416,3072]{1,0:T(8,128)(2,1)} %get-tuple-element.144.refs_7_.refs_2_, ...), custom_call_target="tpu_custom_call" | custom-call | flops 68370432 | bytes 503457 | tf_op jit(solution)/shard_map/backward_attend/pallas_call | solution.py:67
  390.5 8.9 %expand.2 = (bf16[256,2048]{1,0:T(8,128)(2,1)}, bf16[256,2048]{1,0:T(8,128)(2,1)}) custom-call(bf16[416,7168]{1,0:T(8,128)(2,1)} %get-tuple-element.149.refs_4_.refs_8_.refs_1_.refs_0_, bf16[416,7168]{1,0:T(8,128)(2,1)} %collective-permute-done.19.refs_1_, bf16[416,7168]{1,0:T(8,128)(2,1)} %get-tuple-element.150.refs_9_.refs_1_.refs_2_.refs_3_, ...), custom_call_target="tpu_custom_call" | custom-call | flops 55834574848 | bytes 1015021888 | tf_op jit(solution)/shard_map/expand/pallas_call | solution.py:67
  402.3 6.9 %collective-permute-done.33 = bf16[512,1024]{1,0:T(8,128)(2,1)} collective-permute-done((bf16[512,1024]{1,0:T(8,128)(2,1)S(1)}, bf16[512,1024]{1,0:T(8,128)(2,1)}, u32[]{:S(2)}, u32[]{:S(2)}) %collective-permute-start.33) | collective-permute-done | bytes 1048608 | tf_op jit(solution)/shard_map/ppermute | solution.py:843
  414.3 7.9 %qkv.2 = (bf16[256,1536]{1,0:T(8,128)(2,1)}, bf16[256,1536]{1,0:T(8,128)(2,1)}) custom-call(bf16[416,7168]{1,0:T(8,128)(2,1)} %get-tuple-element.149.refs_4_.refs_8_.refs_1_.refs_0_, bf16[416,7168]{1,0:T(8,128)(2,1)} %collective-permute-done.19.refs_1_, bf16[416,7168]{1,0:T(8,128)(2,1)} %get-tuple-element.150.refs_9_.refs_1_.refs_2_.refs_3_, ...), custom_call_target="tpu_custom_call" | custom-call | flops 40894464 | bytes 956416 | tf_op jit(solution)/shard_map/qkv/pallas_call | solution.py:67
  427.5 7.4 %collective-permute-start.38 = (bf16[256,2048]{1,0:T(8,128)(2,1)S(1)}, bf16[256,2048]{1,0:T(8,128)(2,1)}, u32[]{:S(2)}, u32[]{:S(2)}) collective-permute-start(bf16[256,2048]{1,0:T(8,128)(2,1)S(1)} %add_convert_fusion.6), channel_id=1, source_target_pairs={{0,1},{3,2},{4,5},{7,6},{8,9},{11,10},{12,13},{15,14},{16,17},{19,... | collective-permute-start | bytes 3145736 | tf_op jit(solution)/shard_map/ppermute | solution.py:843
  436.5 8.9 %expand.3 = (bf16[256,2048]{1,0:T(8,128)(2,1)}, bf16[256,2048]{1,0:T(8,128)(2,1)}) custom-call(bf16[416,7168]{1,0:T(8,128)(2,1)} %get-tuple-element.149.refs_4_.refs_8_.refs_1_.refs_0_, bf16[416,7168]{1,0:T(8,128)(2,1)} %collective-permute-done.19.refs_1_, bf16[416,7168]{1,0:T(8,128)(2,1)} %get-tuple-element.150.refs_9_.refs_1_.refs_2_.refs_3_, ...), custom_call_target="tpu_custom_call" | custom-call | flops 54525952 | bytes 991232 | tf_op jit(solution)/shard_map/expand/pallas_call | solution.py:67
  461.5 8.1 %qkv.3 = (bf16[256,1536]{1,0:T(8,128)(2,1)}, bf16[256,1536]{1,0:T(8,128)(2,1)}) custom-call(bf16[416,7168]{1,0:T(8,128)(2,1)} %get-tuple-element.149.refs_4_.refs_8_.refs_1_.refs_0_, bf16[416,7168]{1,0:T(8,128)(2,1)} %collective-permute-done.19.refs_1_, bf16[416,7168]{1,0:T(8,128)(2,1)} %get-tuple-element.150.refs_9_.refs_1_.refs_2_.refs_3_, ...), custom_call_target="tpu_custom_call" | custom-call | flops 40894464 | bytes 956416 | tf_op jit(solution)/shard_map/qkv/pallas_call | solution.py:67
  471.2 6.9 %collective-permute-start.44 = (bf16[256,2048]{1,0:T(8,128)(2,1)S(1)}, bf16[256,2048]{1,0:T(8,128)(2,1)}, u32[]{:S(2)}, u32[]{:S(2)}) collective-permute-start(bf16[256,2048]{1,0:T(8,128)(2,1)S(1)} %add_convert_fusion.3), channel_id=1, source_target_pairs={{0,1},{3,2},{4,5},{7,6},{8,9},{11,10},{12,13},{15,14},{16,17},{19,... | collective-permute-start | bytes 3145736 | tf_op jit(solution)/shard_map/ppermute | solution.py:843
  489.5 6.0 %project.1 = (bf16[256,1024]{1,0:T(8,128)(2,1)}, bf16[256,1024]{1,0:T(8,128)(2,1)}) custom-call(bf16[416,7168]{1,0:T(8,128)(2,1)} %get-tuple-element.149.refs_4_.refs_8_.refs_1_.refs_0_, bf16[416,7168]{1,0:T(8,128)(2,1)} %collective-permute-done.19.refs_1_, bf16[416,7168]{1,0:T(8,128)(2,1)} %get-tuple-element.150.refs_9_.refs_1_.refs_2_.refs_3_, ...), custom_call_target="tpu_custom_call" | custom-call | flops 27262976 | bytes 894976 | tf_op jit(solution)/shard_map/project/pallas_call | solution.py:67
  499.6 8.1 %collective-permute-start.50 = (bf16[256,1536]{1,0:T(8,128)(2,1)}, bf16[256,1536]{1,0:T(8,128)(2,1)}, u32[]{:S(2)}, u32[]{:S(2)}) collective-permute-start(bf16[256,1536]{1,0:T(8,128)(2,1)} %add_convert_fusion.15), channel_id=1, source_target_pairs={{0,1},{3,2},{4,5},{7,6},{8,9},{11,10},{12,13},{15,14},{16,17},{19,... | collective-permute-start | bytes 2359304 | tf_op jit(solution)/shard_map/ppermute | solution.py:843
  516.3 9.2 %collective-permute-done.49 = bf16[272,1024]{1,0:T(8,128)(2,1)S(1)} collective-permute-done((bf16[272,1024]{1,0:T(8,128)(2,1)S(1)}, bf16[272,1024]{1,0:T(8,128)(2,1)S(1)}, u32[]{:S(2)}, u32[]{:S(2)}) %collective-permute-start.49) | collective-permute-done | bytes 557088 | tf_op jit(solution)/shard_map/ppermute | solution.py:794
  546.5 14.6 %collective-permute-done.55 = bf16[256,2048]{1,0:T(8,128)(2,1)S(1)} collective-permute-done((bf16[256,2048]{1,0:T(8,128)(2,1)S(1)}, bf16[256,2048]{1,0:T(8,128)(2,1)S(1)}, u32[]{:S(2)}, u32[]{:S(2)}) %collective-permute-start.55) | collective-permute-done | bytes 1048608 | tf_op jit(solution)/shard_map/ppermute | solution.py:849
  565.2 12.7 %collective-permute-done.57 = bf16[256,1536]{1,0:T(8,128)(2,1)S(1)} collective-permute-done((bf16[256,1536]{1,0:T(8,128)(2,1)S(1)}, bf16[256,1536]{1,0:T(8,128)(2,1)S(1)}, u32[]{:S(2)}, u32[]{:S(2)}) %collective-permute-start.57) | collective-permute-done | bytes 786464 | tf_op jit(solution)/shard_map/ppermute | solution.py:849
  580.1 8.3 %collective-permute-done.58 = bf16[272,1024]{1,0:T(8,128)(2,1)S(1)} collective-permute-done((bf16[272,1024]{1,0:T(8,128)(2,1)S(1)}, bf16[272,1024]{1,0:T(8,128)(2,1)S(1)}, u32[]{:S(2)}, u32[]{:S(2)}) %collective-permute-start.58) | collective-permute-done | bytes 557088 | tf_op jit(solution)/shard_map/ppermute | solution.py:849
  (307 shorter events, 174.7 us)
Async XLA Ops:
  10.0 45.5 %collective-permute-start.9 = (bf16[128,5120]{1,0:T(8,128)(2,1)}, bf16[128,5120]{1,0:T(8,128)(2,1)}, u32[]{:S(2)}, u32[]{:S(2)}) collective-permute-start(bf16[128,5120]{1,0:T(8,128)(2,1)} %fusion), channel_id=1, source_target_pairs={{0,8},{4,12},{8,0},{12,4},{1,9},{5,13},{9,1},{13,5},{2,10},{6,14},... | collective-permute-start | bytes 3932168 | tf_op jit(solution)/shard_map/ppermute | solution.py:794
  17.1 41.1 %collective-permute-start.8 = (bf16[256,5120]{1,0:T(8,128)(2,1)S(1)}, bf16[256,5120]{1,0:T(8,128)(2,1)}, u32[]{:S(2)}, u32[]{:S(2)}) collective-permute-start(bf16[256,5120]{1,0:T(8,128)(2,1)S(1)} %pad_maximum_fusion.refs_2_.refs_8_.refs_14_.refs_13_.refs_19_.refs_20_.refs_26_.refs_9_.refs_6_), channel_id=1, source_target_pairs={{0,4},{4,0},{8,12},{12,8},{1,5},{5,1},{9,13},{13,9},{2,6},{6,2},{1... | collective-permute-start | bytes 7864328 | tf_op jit(solution)/shard_map/ppermute | solution.py:791
  27.9 27.6 %collective-permute-start.2 = (bf16[128,3072]{1,0:T(8,128)(2,1)S(1)}, bf16[128,3072]{1,0:T(8,128)(2,1)S(1)}, u32[]{:S(2)}, u32[]{:S(2)}) collective-permute-start(bf16[128,3072]{1,0:T(8,128)(2,1)S(1)} %collective-permute-done.refs_3_.refs_4_.refs_27_.refs_34_.refs_14_), channel_id=1, source_target_pairs={{0,1},{1,0},{2,3},{3,2},{4,5},{5,4},{6,7},{7,6},{8,9},{9,8},{10,11... | collective-permute-start | bytes 2359304 | tf_op jit(solution)/shard_map/ppermute | solution.py:797
  55.6 34.5 %collective-permute-start.10 = (bf16[128,5120]{1,0:T(8,128)(2,1)}, bf16[128,5120]{1,0:T(8,128)(2,1)}, u32[]{:S(2)}, u32[]{:S(2)}) collective-permute-start(bf16[128,5120]{1,0:T(8,128)(2,1)} %collective-permute-done.9.refs_4_.refs_10_.refs_16_.refs_15_.refs_21_.refs_22_.refs_28_.refs_11_.refs_8_), channel_id=1, source_target_pairs={{0,1},{1,0},{2,3},{3,2},{4,5},{5,4},{6,7},{7,6},{8,9},{9,8},{10,11... | collective-permute-start | bytes 3932168 | tf_op jit(solution)/shard_map/ppermute | solution.py:797
  57.2 35.9 %collective-permute-start.14 = (bf16[768,1024]{1,0:T(8,128)(2,1)}, bf16[768,1024]{1,0:T(8,128)(2,1)}, u32[]{:S(2)}, u32[]{:S(2)}) collective-permute-start(bf16[768,1024]{1,0:T(8,128)(2,1)} %dynamic-slice_bitcast_fusion), channel_id=1, source_target_pairs={{0,8},{4,12},{8,0},{12,4},{1,9},{5,13},{9,1},{13,5},{2,10},{6,14},... | collective-permute-start | bytes 4718600 | tf_op jit(solution)/shard_map/ppermute | solution.py:794
  58.2 54.3 %collective-permute-start.13 = (bf16[1024,1024]{1,0:T(8,128)(2,1)}, bf16[1024,1024]{1,0:T(8,128)(2,1)}, u32[]{:S(2)}, u32[]{:S(2)}) collective-permute-start(bf16[1024,1024]{1,0:T(8,128)(2,1)} %bitcast.38.refs_2_.refs_7_.refs_14_.refs_3_), channel_id=1, source_target_pairs={{0,4},{4,0},{8,12},{12,8},{1,5},{5,1},{9,13},{13,9},{2,6},{6,2},{1... | collective-permute-start | bytes 6291464 | tf_op jit(solution)/shard_map/ppermute | solution.py:791
  121.4 30.0 %collective-permute-start.18 = (bf16[416,1024]{1,0:T(8,128)(2,1)}, bf16[416,1024]{1,0:T(8,128)(2,1)S(1)}, u32[]{:S(2)}, u32[]{:S(2)}) collective-permute-start(bf16[416,1024]{1,0:T(8,128)(2,1)} %output_forward.4), channel_id=1, source_target_pairs={{0,16},{1,17},{2,18},{3,19},{4,20},{5,21},{6,22},{7,23},{8,24},{9,... | collective-permute-start | bytes 2555912 | tf_op jit(solution)/shard_map/ppermute | solution.py:885
  149.2 67.8 %collective-permute-start.20 = (bf16[416,1024]{1,0:T(8,128)(2,1)}, bf16[416,1024]{1,0:T(8,128)(2,1)}, u32[]{:S(2)}, u32[]{:S(2)}) collective-permute-start(bf16[416,1024]{1,0:T(8,128)(2,1)} %output_forward.5), channel_id=1, source_target_pairs={{0,16},{1,17},{2,18},{3,19},{4,20},{5,21},{6,22},{7,23},{8,24},{9,... | collective-permute-start | bytes 2555912 | tf_op jit(solution)/shard_map/ppermute | solution.py:885
  179.4 105.4 %collective-permute-start.19 = (bf16[416,7168]{1,0:T(8,128)(2,1)}, bf16[416,7168]{1,0:T(8,128)(2,1)}, u32[]{:S(2)}, u32[]{:S(2)}) collective-permute-start(bf16[416,7168]{1,0:T(8,128)(2,1)} %get-tuple-element.149.refs_4_.refs_8_.refs_1_.refs_0_), channel_id=1, source_target_pairs={{0,4},{4,0},{8,12},{12,8},{1,5},{5,1},{9,13},{13,9},{2,6},{6,2},{1... | collective-permute-start | bytes 17891336 | tf_op jit(solution)/shard_map/ppermute | solution.py:791
  215.7 29.0 %collective-permute-start.22 = (bf16[416,1024]{1,0:T(8,128)(2,1)}, bf16[416,1024]{1,0:T(8,128)(2,1)S(1)}, u32[]{:S(2)}, u32[]{:S(2)}) collective-permute-start(bf16[416,1024]{1,0:T(8,128)(2,1)} %get-tuple-element.139), channel_id=1, source_target_pairs={{16,0},{17,1},{18,2},{19,3},{20,4},{21,5},{22,6},{23,7},{24,8},{25... | collective-permute-start | bytes 2555912 | tf_op jit(solution)/shard_map/ppermute | solution.py:885
  217.0 67.8 %collective-permute-start.24 = (bf16[416,9216]{1,0:T(8,128)(2,1)}, bf16[416,9216]{1,0:T(8,128)(2,1)}, u32[]{:S(2)}, u32[]{:S(2)}) collective-permute-start(bf16[416,9216]{1,0:T(8,128)(2,1)} %get-tuple-element.147.refs_5_), channel_id=1, source_target_pairs={{0,4},{4,0},{8,12},{12,8},{1,5},{5,1},{9,13},{13,9},{2,6},{6,2},{1... | collective-permute-start | bytes 23003144 | tf_op jit(solution)/shard_map/ppermute | solution.py:791
  244.5 48.4 %collective-permute-start.21 = (bf16[416,7168]{1,0:T(8,128)(2,1)}, bf16[416,7168]{1,0:T(8,128)(2,1)}, u32[]{:S(2)}, u32[]{:S(2)}) collective-permute-start(bf16[416,7168]{1,0:T(8,128)(2,1)} %get-tuple-element.150.refs_9_.refs_1_.refs_2_.refs_3_), channel_id=1, source_target_pairs={{0,4},{4,0},{8,12},{12,8},{1,5},{5,1},{9,13},{13,9},{2,6},{6,2},{1... | collective-permute-start | bytes 17891336 | tf_op jit(solution)/shard_map/ppermute | solution.py:791
  282.0 27.0 %collective-permute-start.23 = (bf16[416,9216]{1,0:T(8,128)(2,1)}, bf16[416,9216]{1,0:T(8,128)(2,1)}, u32[]{:S(2)}, u32[]{:S(2)}) collective-permute-start(bf16[416,9216]{1,0:T(8,128)(2,1)} %get-tuple-element.146.refs_4_), channel_id=1, source_target_pairs={{0,4},{4,0},{8,12},{12,8},{1,5},{5,1},{9,13},{13,9},{2,6},{6,2},{1... | collective-permute-start | bytes 23003144 | tf_op jit(solution)/shard_map/ppermute | solution.py:791
  318.3 25.5 %collective-permute-start.29 = (bf16[512,1024]{1,0:T(8,128)(2,1)}, bf16[512,1024]{1,0:T(8,128)(2,1)S(1)}, u32[]{:S(2)}, u32[]{:S(2)}) collective-permute-start(bf16[512,1024]{1,0:T(8,128)(2,1)} %get-tuple-element.159), channel_id=1, source_target_pairs={{0,8},{4,12},{8,0},{12,4},{1,9},{5,13},{9,1},{13,5},{2,10},{6,14},... | collective-permute-start | bytes 3145736 | tf_op jit(solution)/shard_map/ppermute | solution.py:794
  344.2 38.9 %collective-permute-start.31 = (bf16[512,1024]{1,0:T(8,128)(2,1)S(1)}, bf16[512,1024]{1,0:T(8,128)(2,1)S(1)}, u32[]{:S(2)}, u32[]{:S(2)}) collective-permute-start(bf16[512,1024]{1,0:T(8,128)(2,1)S(1)} %add_convert_fusion.11), channel_id=1, source_target_pairs={{0,1},{3,2},{4,5},{7,6},{8,9},{11,10},{12,13},{15,14},{16,17},{19,... | collective-permute-start | bytes 3145736 | tf_op jit(solution)/shard_map/ppermute | solution.py:843
  356.2 28.3 %collective-permute-start.32 = (bf16[512,1024]{1,0:T(8,128)(2,1)}, bf16[512,1024]{1,0:T(8,128)(2,1)}, u32[]{:S(2)}, u32[]{:S(2)}) collective-permute-start(bf16[512,1024]{1,0:T(8,128)(2,1)} %get-tuple-element.168), channel_id=1, source_target_pairs={{0,8},{4,12},{8,0},{12,4},{1,9},{5,13},{9,1},{13,5},{2,10},{6,14},... | collective-permute-start | bytes 3145736 | tf_op jit(solution)/shard_map/ppermute | solution.py:794
  388.6 33.6 %collective-permute-start.34 = (bf16[512,1024]{1,0:T(8,128)(2,1)}, bf16[512,1024]{1,0:T(8,128)(2,1)}, u32[]{:S(2)}, u32[]{:S(2)}) collective-permute-start(bf16[512,1024]{1,0:T(8,128)(2,1)} %add_convert_fusion.10), channel_id=1, source_target_pairs={{1,2},{2,1},{5,6},{6,5},{9,10},{10,9},{13,14},{14,13},{17,18},{18,... | collective-permute-start | bytes 3145736 | tf_op jit(solution)/shard_map/ppermute | solution.py:846
  399.4 26.5 %collective-permute-start.35 = (bf16[256,2048]{1,0:T(8,128)(2,1)}, bf16[256,2048]{1,0:T(8,128)(2,1)}, u32[]{:S(2)}, u32[]{:S(2)}) collective-permute-start(bf16[256,2048]{1,0:T(8,128)(2,1)} %get-tuple-element.176), channel_id=1, source_target_pairs={{0,8},{4,12},{8,0},{12,4},{1,9},{5,13},{9,1},{13,5},{2,10},{6,14},... | collective-permute-start | bytes 3145736 | tf_op jit(solution)/shard_map/ppermute | solution.py:794
  411.1 42.5 %collective-permute-start.37 = (bf16[512,1024]{1,0:T(8,128)(2,1)S(1)}, bf16[512,1024]{1,0:T(8,128)(2,1)}, u32[]{:S(2)}, u32[]{:S(2)}) collective-permute-start(bf16[512,1024]{1,0:T(8,128)(2,1)S(1)} %add_convert_fusion.8), channel_id=1, source_target_pairs={{1,2},{2,1},{5,6},{6,5},{9,10},{10,9},{13,14},{14,13},{17,18},{18,... | collective-permute-start | bytes 3145736 | tf_op jit(solution)/shard_map/ppermute | solution.py:846
  427.5 30.0 %collective-permute-start.38 = (bf16[256,2048]{1,0:T(8,128)(2,1)S(1)}, bf16[256,2048]{1,0:T(8,128)(2,1)}, u32[]{:S(2)}, u32[]{:S(2)}) collective-permute-start(bf16[256,2048]{1,0:T(8,128)(2,1)S(1)} %add_convert_fusion.6), channel_id=1, source_target_pairs={{0,1},{3,2},{4,5},{7,6},{8,9},{11,10},{12,13},{15,14},{16,17},{19,... | collective-permute-start | bytes 3145736 | tf_op jit(solution)/shard_map/ppermute | solution.py:843
  435.0 26.3 %collective-permute-start.39 = (bf16[512,1024]{1,0:T(8,128)(2,1)S(1)}, bf16[512,1024]{1,0:T(8,128)(2,1)S(1)}, u32[]{:S(2)}, u32[]{:S(2)}) collective-permute-start(bf16[512,1024]{1,0:T(8,128)(2,1)S(1)} %add_convert_fusion.7), channel_id=1, source_target_pairs={{1,0},{2,3},{5,4},{6,7},{9,8},{10,11},{13,12},{14,15},{17,16},{18,... | collective-permute-start | bytes 3145736 | tf_op jit(solution)/shard_map/ppermute | solution.py:849
  448.1 31.5 %collective-permute-start.41 = (bf16[256,1536]{1,0:T(8,128)(2,1)}, bf16[256,1536]{1,0:T(8,128)(2,1)}, u32[]{:S(2)}, u32[]{:S(2)}) collective-permute-start(bf16[256,1536]{1,0:T(8,128)(2,1)} %add_convert_fusion.17), channel_id=1, source_target_pairs={{0,1},{3,2},{4,5},{7,6},{8,9},{11,10},{12,13},{15,14},{16,17},{19,... | collective-permute-start | bytes 2359304 | tf_op jit(solution)/shard_map/ppermute | solution.py:843
  456.2 26.5 %collective-permute-start.42 = (bf16[512,1024]{1,0:T(8,128)(2,1)}, bf16[512,1024]{1,0:T(8,128)(2,1)}, u32[]{:S(2)}, u32[]{:S(2)}) collective-permute-start(bf16[512,1024]{1,0:T(8,128)(2,1)} %add_convert_fusion.5), channel_id=1, source_target_pairs={{1,0},{2,3},{5,4},{6,7},{9,8},{10,11},{13,12},{14,15},{17,16},{18,... | collective-permute-start | bytes 3145736 | tf_op jit(solution)/shard_map/ppermute | solution.py:849
  459.1 27.4 %collective-permute-start.43 = (bf16[256,2048]{1,0:T(8,128)(2,1)S(1)}, bf16[256,2048]{1,0:T(8,128)(2,1)}, u32[]{:S(2)}, u32[]{:S(2)}) collective-permute-start(bf16[256,2048]{1,0:T(8,128)(2,1)S(1)} %add_convert_fusion.4), channel_id=1, source_target_pairs={{1,2},{2,1},{5,6},{6,5},{9,10},{10,9},{13,14},{14,13},{17,18},{18,... | collective-permute-start | bytes 3145736 | tf_op jit(solution)/shard_map/ppermute | solution.py:846
  471.2 24.4 %collective-permute-start.44 = (bf16[256,2048]{1,0:T(8,128)(2,1)S(1)}, bf16[256,2048]{1,0:T(8,128)(2,1)}, u32[]{:S(2)}, u32[]{:S(2)}) collective-permute-start(bf16[256,2048]{1,0:T(8,128)(2,1)S(1)} %add_convert_fusion.3), channel_id=1, source_target_pairs={{0,1},{3,2},{4,5},{7,6},{8,9},{11,10},{12,13},{15,14},{16,17},{19,... | collective-permute-start | bytes 3145736 | tf_op jit(solution)/shard_map/ppermute | solution.py:843
  481.2 31.1 %collective-permute-start.47 = (bf16[256,1536]{1,0:T(8,128)(2,1)S(1)}, bf16[256,1536]{1,0:T(8,128)(2,1)}, u32[]{:S(2)}, u32[]{:S(2)}) collective-permute-start(bf16[256,1536]{1,0:T(8,128)(2,1)S(1)} %add_convert_fusion.16), channel_id=1, source_target_pairs={{1,2},{2,1},{5,6},{6,5},{9,10},{10,9},{13,14},{14,13},{17,18},{18,... | collective-permute-start | bytes 2359304 | tf_op jit(solution)/shard_map/ppermute | solution.py:846
  488.2 26.7 %collective-permute-start.48 = (bf16[256,2048]{1,0:T(8,128)(2,1)S(1)}, bf16[256,2048]{1,0:T(8,128)(2,1)}, u32[]{:S(2)}, u32[]{:S(2)}) collective-permute-start(bf16[256,2048]{1,0:T(8,128)(2,1)S(1)} %add_convert_fusion.2), channel_id=1, source_target_pairs={{1,0},{2,3},{5,4},{6,7},{9,8},{10,11},{13,12},{14,15},{17,16},{18,... | collective-permute-start | bytes 3145736 | tf_op jit(solution)/shard_map/ppermute | solution.py:849
  499.6 27.4 %collective-permute-start.50 = (bf16[256,1536]{1,0:T(8,128)(2,1)}, bf16[256,1536]{1,0:T(8,128)(2,1)}, u32[]{:S(2)}, u32[]{:S(2)}) collective-permute-start(bf16[256,1536]{1,0:T(8,128)(2,1)} %add_convert_fusion.15), channel_id=1, source_target_pairs={{0,1},{3,2},{4,5},{7,6},{8,9},{11,10},{12,13},{15,14},{16,17},{19,... | collective-permute-start | bytes 2359304 | tf_op jit(solution)/shard_map/ppermute | solution.py:843
  531.1 29.9 %collective-permute-start.55 = (bf16[256,2048]{1,0:T(8,128)(2,1)S(1)}, bf16[256,2048]{1,0:T(8,128)(2,1)S(1)}, u32[]{:S(2)}, u32[]{:S(2)}) collective-permute-start(bf16[256,2048]{1,0:T(8,128)(2,1)S(1)} %add_convert_fusion), channel_id=1, source_target_pairs={{1,0},{2,3},{5,4},{6,7},{9,8},{10,11},{13,12},{14,15},{17,16},{18,... | collective-permute-start | bytes 3145736 | tf_op jit(solution)/shard_map/ppermute | solution.py:849
  538.8 24.9 %collective-permute-start.56 = (bf16[272,1024]{1,0:T(8,128)(2,1)S(1)}, bf16[272,1024]{1,0:T(8,128)(2,1)S(1)}, u32[]{:S(2)}, u32[]{:S(2)}) collective-permute-start(bf16[272,1024]{1,0:T(8,128)(2,1)S(1)} %add_convert_fusion.19), channel_id=1, source_target_pairs={{1,2},{2,1},{5,6},{6,5},{9,10},{10,9},{13,14},{14,13},{17,18},{18,... | collective-permute-start | bytes 1671176 | tf_op jit(solution)/shard_map/ppermute | solution.py:846
  545.2 32.8 %collective-permute-start.57 = (bf16[256,1536]{1,0:T(8,128)(2,1)S(1)}, bf16[256,1536]{1,0:T(8,128)(2,1)S(1)}, u32[]{:S(2)}, u32[]{:S(2)}) collective-permute-start(bf16[256,1536]{1,0:T(8,128)(2,1)S(1)} %add_convert_fusion.12), channel_id=1, source_target_pairs={{1,0},{2,3},{5,4},{6,7},{9,8},{10,11},{13,12},{14,15},{17,16},{18,... | collective-permute-start | bytes 2359304 | tf_op jit(solution)/shard_map/ppermute | solution.py:849
  563.9 24.4 %collective-permute-start.58 = (bf16[272,1024]{1,0:T(8,128)(2,1)S(1)}, bf16[272,1024]{1,0:T(8,128)(2,1)S(1)}, u32[]{:S(2)}, u32[]{:S(2)}) collective-permute-start(bf16[272,1024]{1,0:T(8,128)(2,1)S(1)} %add_convert_fusion.18), channel_id=1, source_target_pairs={{1,0},{2,3},{5,4},{6,7},{9,8},{10,11},{13,12},{14,15},{17,16},{18,... | collective-permute-start | bytes 1671176 | tf_op jit(solution)/shard_map/ppermute | solution.py:849
  (74 other events, 762.9 us)

commit v11 on v10

--- a/solution.py
+++ b/solution.py
@@ -180,7 +180,7 @@
             columns[image] = jnp.where((lane & (head - 1)) == index, logged, columns[image])
         return carry
 
-    lax.fori_loop(0, HEADS // 2, heads, 0, unroll=2)
+    lax.fori_loop(0, HEADS // 2, heads, 0, unroll=4)
     if logs is not None:
         for image in range(count):
             rows_of = columns[image].T
@@ -506,7 +506,7 @@
                 grads[span, pl.ds(offset, pair)] = jnp.where(live, total, 0.0).astype(BF16)
         return carry
 
-    lax.fori_loop(0, HEADS // 2, heads, 0, unroll=4)
+    lax.fori_loop(0, HEADS // 2, heads, 0, unroll=8)
     wait_all(load)
     for block in range(2):
         normal[:, block * half : (block + 1) * half] = contract(

time: 600 us -> 599 us (level)
  transfers between devices with their start and end apart: 59 -> 59, of which waited for: 17 -> 18; matrix products, arithmetic and copies ran while one was open for 13% -> 14% of each run, Pallas kernels for 50% -> 50%
where the time goes in v11:
time: 599 us; the launch traced here: 590 us
  Pallas kernels  311 us (52%)
  waiting for transfers between devices  97.8 us (16%)
  starting transfers between devices  84.7 us (14%)
  other arithmetic  60.3 us (10%)
  local copies, waits for them, and re-layouts  34.5 us (6%)
    pallas_call x21, Pallas kernels, call(): pl.pallas_call(body, out_shape=out_shape, in_specs=specs, out_specs=[VMEM...  311 us
    ppermute x11, waiting for transfers between devices, across(): return lax.ppermute(block, 'group', [(i, i ^ 2) for i in range(4)])  40.1 us
    ppermute x7, waiting for transfers between devices, total(): outward = lax.ppermute(summed, 'replica', [(1, 0), (2, 3)])  36.1 us
    ppermute x7, starting transfers between devices, total(): inward = lax.ppermute(mine, 'replica', [(0, 1), (3, 2)])  34.8 us
    convert_element_type x21, other arithmetic, added(): return total.astype(values[0].dtype)  29.7 us
    unnamed x104, local copies, waits for them, and re-layouts  13.2 us
    ppermute x11, starting transfers between devices, across(): return lax.ppermute(block, 'group', [(i, i ^ 2) for i in range(4)])  13.1 us
  transfers between devices with their start and end apart: 59, of which 18 were waited for; matrix products, arithmetic and copies ran while one was open for 14% of the time, Pallas kernels for 50%

profile of v11, /device:TPU:0, one launch (start us, length us, event | category | flops | bytes accessed | tf_op | source)
XLA Modules:
  0.0 590.1 jit_solution(11806909992815966100)
XLA Ops:
  22.2 5.8 collective-permute-done.refs_3_.refs_4_.refs_27_.refs_34_.refs_14_
  38.7 16.9 %collective-permute-done.9.refs_4_.refs_10_.refs_16_.refs_15_.refs_21_.refs_22_.refs_28_.refs_11_.refs_8_ = bf16[128,5120]{1,0:T(8,128)(2,1)} collective-permute-done((bf16[128,5120]{1,0:T(8,128)(2,1)}, bf16[128,5120]{1,0:T(8,128)(2,1)}, u32[]{:S(2)}, u32[]{:S(2)}) %collective-permute-start.9) | collective-permute-done | bytes 1310752 | tf_op jit(solution)/shard_map/ppermute | solution.py:794
  63.1 13.3 %forward_attend.2.refs_1_ = bf16[416,1024]{1,0:T(8,128)(2,1)} custom-call(bf16[416,1024]{1,0:T(8,128)(2,1)} %bitcast.106, bf16[256,3072]{1,0:T(8,128)(2,1)} %bitcast.93, bf16[256,3072]{1,0:T(8,128)(2,1)} %collective-permute-done.1.refs_2_.refs_3_.refs_26_.refs_33_.refs_13_, bf16[128,3072]{1,0:T(8,128)(2,1)} %copy-done.5, bf16[128,3072]{1,0:T(8,128)(2,1)} %copy-done.6, ...), custom_call_target="tpu_custom_call" | custom-call | flops 46432256 | bytes 125697 | tf_op jit(solution)/shard_map/forward_attend/pallas_call | solution.py:67
  76.7 13.3 %forward_attend.3.refs_1_ = bf16[416,1024]{1,0:T(8,128)(2,1)} custom-call(bf16[416,1024]{1,0:T(8,128)(2,1)} %bitcast.100, bf16[256,3072]{1,0:T(8,128)(2,1)} %bitcast.94, bf16[256,3072]{1,0:T(8,128)(2,1)} %collective-permute-done.1.refs_2_.refs_3_.refs_26_.refs_33_.refs_13_, bf16[128,3072]{1,0:T(8,128)(2,1)} %copy-done.5, bf16[128,3072]{1,0:T(8,128)(2,1)} %copy-done.6, ...), custom_call_target="tpu_custom_call" | custom-call | flops 46432256 | bytes 125697 | tf_op jit(solution)/shard_map/forward_attend/pallas_call | solution.py:67
  96.7 13.7 %forward_feed.2 = (f32[416,1024]{1,0:T(8,128)}, bf16[416,4096]{1,0:T(8,128)(2,1)}) custom-call(bf16[416,1024]{1,0:T(8,128)(2,1)} %bitcast.107, bf16[416,1024]{1,0:T(8,128)(2,1)} %forward_attend.2.refs_1_, bf16[256,5120]{1,0:T(8,128)(2,1)} %copy-done, ...), custom_call_target="tpu_custom_call" | custom-call | flops 68157440 | bytes 434945 | tf_op jit(solution)/shard_map/forward_feed/pallas_call | solution.py:67
  113.2 8.1 %output_forward.4 = bf16[416,1024]{1,0:T(8,128)(2,1)} custom-call(f32[416,1024]{1,0:T(8,128)} %get-tuple-element.123.refs_0_, bf16[416,4096]{1,0:T(8,128)(2,1)} %get-tuple-element.124.refs_1_, bf16[1024,1024]{1,0:T(8,128)(2,1)} %bitcast.38.refs_2_.refs_7_.refs_14_.refs_3_, bf16[1024,1024]{1,0:T(8,128)(2,1)} %collective-permute-done.13.refs_3_.refs_8_.refs_15_.refs_4_, ...), custom_call_target="tpu_custom_call" | custom-call | flops 54525952 | bytes 225025 | tf_op jit(solution)/shard_map/output_forward/pallas_call | solution.py:67
  127.4 13.7 %forward_feed.3 = (f32[416,1024]{1,0:T(8,128)}, bf16[416,4096]{1,0:T(8,128)(2,1)}) custom-call(bf16[416,1024]{1,0:T(8,128)(2,1)} %bitcast.101, bf16[416,1024]{1,0:T(8,128)(2,1)} %forward_attend.3.refs_1_, bf16[256,5120]{1,0:T(8,128)(2,1)} %copy-done, ...), custom_call_target="tpu_custom_call" | custom-call | flops 68157440 | bytes 434945 | tf_op jit(solution)/shard_map/forward_feed/pallas_call | solution.py:67
  141.1 8.1 %output_forward.5 = bf16[416,1024]{1,0:T(8,128)(2,1)} custom-call(f32[416,1024]{1,0:T(8,128)} %get-tuple-element.130.refs_0_, bf16[416,4096]{1,0:T(8,128)(2,1)} %get-tuple-element.132.refs_1_, bf16[1024,1024]{1,0:T(8,128)(2,1)} %bitcast.38.refs_2_.refs_7_.refs_14_.refs_3_, bf16[1024,1024]{1,0:T(8,128)(2,1)} %collective-permute-done.13.refs_3_.refs_8_.refs_15_.refs_4_, ...), custom_call_target="tpu_custom_call" | custom-call | flops 54525952 | bytes 225025 | tf_op jit(solution)/shard_map/output_forward/pallas_call | solution.py:67
  152.3 27.0 %forward_attend_feed.2 = (bf16[416,7168]{1,0:T(8,128)(2,1)}, bf16[416,3072]{1,0:T(8,128)(2,1)}, f32[2,16,208]{2,1,0:T(8,128)}, f32[416,1024]{1,0:T(8,128)}, bf16[416,4096]{1,0:T(8,128)(2,1)}) custom-call(bf16[416,1024]{1,0:T(8,128)(2,1)} %bitcast.108, bf16[416,1024]{1,0:T(8,128)(2,1)} %copy-done.45, bf16[256,3072]{1,0:T(8,128)(2,1)} %bitcast.95, ...), custom_call_target="tpu_custom_call" | custom-call | flops 58669924352 | bytes 341394016 | tf_op jit(solution)/shard_map/forward_attend_feed/pallas_call | solution.py:67
  179.4 35.7 %backward_feed_attend.2 = (bf16[416,9216]{1,0:T(8,128)(2,1)}, f32[8,1024]{1,0:T(8,128)}, f32[1,4096]{1,0:T(1,128)}, bf16[416,1024]{1,0:T(8,128)(2,1)}, f32[8,1024]{1,0:T(8,128)}) custom-call(bf16[416,1024]{1,0:T(8,128)(2,1)} %bitcast.127, bf16[416,4096]{1,0:T(8,128)(2,1)} %get-tuple-element.135.refs_1_.refs_0_, ...), custom_call_target="tpu_custom_call" | custom-call | flops 90840236032 | bytes 477315680 | tf_op jit(solution)/shard_map/backward_feed_attend/pallas_call | solution.py:67
  216.9 27.0 %forward_attend_feed.3 = (bf16[416,7168]{1,0:T(8,128)(2,1)}, bf16[416,3072]{1,0:T(8,128)(2,1)}, f32[2,16,208]{2,1,0:T(8,128)}, f32[416,1024]{1,0:T(8,128)}, bf16[416,4096]{1,0:T(8,128)(2,1)}) custom-call(bf16[416,1024]{1,0:T(8,128)(2,1)} %bitcast.102, bf16[416,1024]{1,0:T(8,128)(2,1)} %collective-permute-done.20.refs_1_.refs_13_, ...), custom_call_target="tpu_custom_call" | custom-call | flops 58669924352 | bytes 341394016 | tf_op jit(solution)/shard_map/forward_attend_feed/pallas_call | solution.py:67
  244.9 35.9 %backward_feed_attend.3 = (bf16[416,9216]{1,0:T(8,128)(2,1)}, f32[8,1024]{1,0:T(8,128)}, f32[1,4096]{1,0:T(1,128)}, bf16[416,1024]{1,0:T(8,128)(2,1)}, f32[8,1024]{1,0:T(8,128)}) custom-call(bf16[416,4096]{1,0:T(8,128)(2,1)} %get-tuple-element.135.refs_1_.refs_0_, bf16[416,4096]{1,0:T(8,128)(2,1)} %get-tuple-element.142.refs_1_, ...), custom_call_target="tpu_custom_call" | custom-call | flops 90840236032 | bytes 600212096 | tf_op jit(solution)/shard_map/backward_feed_attend/pallas_call | solution.py:67
  283.5 8.1 %output_forward.6 = bf16[416,1024]{1,0:T(8,128)(2,1)} custom-call(f32[416,1024]{1,0:T(8,128)} %get-tuple-element.136.refs_2_.refs_0_, bf16[416,7168]{1,0:T(8,128)(2,1)} %get-tuple-element.149.refs_4_.refs_8_.refs_1_.refs_0_, bf16[1024,1024]{1,0:T(8,128)(2,1)} %bitcast.38.refs_2_.refs_7_.refs_14_.refs_3_, ...), custom_call_target="tpu_custom_call" | custom-call | flops 27917287424 | bytes 135660128 | tf_op jit(solution)/shard_map/output_forward/pallas_call | solution.py:67
  291.6 8.1 %output_forward.7 = bf16[416,1024]{1,0:T(8,128)(2,1)} custom-call(f32[416,1024]{1,0:T(8,128)} %get-tuple-element.143.refs_3_.refs_0_.refs_2_, bf16[416,7168]{1,0:T(8,128)(2,1)} %get-tuple-element.150.refs_9_.refs_1_.refs_2_.refs_3_, bf16[1024,1024]{1,0:T(8,128)(2,1)} %bitcast.38.refs_2_.refs_7_.refs_14_.refs_3_, ...), custom_call_target="tpu_custom_call" | custom-call | flops 27917287424 | bytes 135660128 | tf_op jit(solution)/shard_map/output_forward/pallas_call | solution.py:67
  308.9 8.3 %reduce.11 = (bf16[512,1024]{1,0:T(8,128)(2,1)}, bf16[512,1024]{1,0:T(8,128)(2,1)}) custom-call(bf16[416,7168]{1,0:T(8,128)(2,1)} %get-tuple-element.149.refs_4_.refs_8_.refs_1_.refs_0_, bf16[416,7168]{1,0:T(8,128)(2,1)} %collective-permute-done.19.refs_1_, bf16[416,7168]{1,0:T(8,128)(2,1)} %get-tuple-element.150.refs_9_.refs_1_.refs_2_.refs_3_, ...), custom_call_target="tpu_custom_call" | custom-call | flops 54525952 | bytes 911360 | tf_op jit(solution)/shard_map/reduce/pallas_call | solution.py:67
  317.9 18.6 %backward_feed.1 = (bf16[416,4096]{1,0:T(8,128)(2,1)}, bf16[416,1024]{1,0:T(8,128)(2,1)}, f32[8,1024]{1,0:T(8,128)}, f32[1,4096]{1,0:T(1,128)}, f32[416,1024]{1,0:T(8,128)}) custom-call(bf16[416,1024]{1,0:T(8,128)(2,1)} %copy-done.15, bf16[416,4096]{1,0:T(8,128)(2,1)} %get-tuple-element.142.refs_1_, f32[416,1024]{1,0:T(8,128)} %get-tuple-element.143.refs_3_.refs_0_.refs_2_, ...), custom_call_target="tpu_custom_call" | custom-call | flops 109051904 | bytes 482817 | tf_op jit(solution)/shard_map/backward_feed/pallas_call | solution.py:67
  337.1 5.7 collective-permute-done.29
  346.9 8.4 %reduce.12 = (bf16[512,1024]{1,0:T(8,128)(2,1)}, bf16[512,1024]{1,0:T(8,128)(2,1)}) custom-call(bf16[416,7168]{1,0:T(8,128)(2,1)} %get-tuple-element.149.refs_4_.refs_8_.refs_1_.refs_0_, bf16[416,7168]{1,0:T(8,128)(2,1)} %collective-permute-done.19.refs_1_, bf16[416,7168]{1,0:T(8,128)(2,1)} %get-tuple-element.150.refs_9_.refs_1_.refs_2_.refs_3_, ...), custom_call_target="tpu_custom_call" | custom-call | flops 55834574848 | bytes 933232960 | tf_op jit(solution)/shard_map/reduce/pallas_call | solution.py:67
  358.1 23.4 %backward_attend.1 = (bf16[416,3072]{1,0:T(8,128)(2,1)}, bf16[416,1024]{1,0:T(8,128)(2,1)}, f32[8,1024]{1,0:T(8,128)}) custom-call(bf16[416,1024]{1,0:T(8,128)(2,1)} %get-tuple-element.162.refs_0_.refs_8_, f32[416,1024]{1,0:T(8,128)} %get-tuple-element.163.refs_1_, bf16[416,3072]{1,0:T(8,128)(2,1)} %get-tuple-element.144.refs_7_.refs_2_, ...), custom_call_target="tpu_custom_call" | custom-call | flops 68370432 | bytes 503457 | tf_op jit(solution)/shard_map/backward_attend/pallas_call | solution.py:67
  388.7 9.0 %expand.2 = (bf16[256,2048]{1,0:T(8,128)(2,1)}, bf16[256,2048]{1,0:T(8,128)(2,1)}) custom-call(bf16[416,7168]{1,0:T(8,128)(2,1)} %get-tuple-element.149.refs_4_.refs_8_.refs_1_.refs_0_, bf16[416,7168]{1,0:T(8,128)(2,1)} %collective-permute-done.19.refs_1_, bf16[416,7168]{1,0:T(8,128)(2,1)} %get-tuple-element.150.refs_9_.refs_1_.refs_2_.refs_3_, ...), custom_call_target="tpu_custom_call" | custom-call | flops 55834574848 | bytes 1015021888 | tf_op jit(solution)/shard_map/expand/pallas_call | solution.py:67
  400.6 7.0 %collective-permute-done.33 = bf16[512,1024]{1,0:T(8,128)(2,1)} collective-permute-done((bf16[512,1024]{1,0:T(8,128)(2,1)S(1)}, bf16[512,1024]{1,0:T(8,128)(2,1)}, u32[]{:S(2)}, u32[]{:S(2)}) %collective-permute-start.33) | collective-permute-done | bytes 1048608 | tf_op jit(solution)/shard_map/ppermute | solution.py:843
  412.9 7.9 %qkv.2 = (bf16[256,1536]{1,0:T(8,128)(2,1)}, bf16[256,1536]{1,0:T(8,128)(2,1)}) custom-call(bf16[416,7168]{1,0:T(8,128)(2,1)} %get-tuple-element.149.refs_4_.refs_8_.refs_1_.refs_0_, bf16[416,7168]{1,0:T(8,128)(2,1)} %collective-permute-done.19.refs_1_, bf16[416,7168]{1,0:T(8,128)(2,1)} %get-tuple-element.150.refs_9_.refs_1_.refs_2_.refs_3_, ...), custom_call_target="tpu_custom_call" | custom-call | flops 40894464 | bytes 956416 | tf_op jit(solution)/shard_map/qkv/pallas_call | solution.py:67
  426.1 7.4 %collective-permute-start.38 = (bf16[256,2048]{1,0:T(8,128)(2,1)S(1)}, bf16[256,2048]{1,0:T(8,128)(2,1)}, u32[]{:S(2)}, u32[]{:S(2)}) collective-permute-start(bf16[256,2048]{1,0:T(8,128)(2,1)S(1)} %add_convert_fusion.6), channel_id=1, source_target_pairs={{0,1},{3,2},{4,5},{7,6},{8,9},{11,10},{12,13},{15,14},{16,17},{19,... | collective-permute-start | bytes 3145736 | tf_op jit(solution)/shard_map/ppermute | solution.py:843
  435.0 8.8 %expand.3 = (bf16[256,2048]{1,0:T(8,128)(2,1)}, bf16[256,2048]{1,0:T(8,128)(2,1)}) custom-call(bf16[416,7168]{1,0:T(8,128)(2,1)} %get-tuple-element.149.refs_4_.refs_8_.refs_1_.refs_0_, bf16[416,7168]{1,0:T(8,128)(2,1)} %collective-permute-done.19.refs_1_, bf16[416,7168]{1,0:T(8,128)(2,1)} %get-tuple-element.150.refs_9_.refs_1_.refs_2_.refs_3_, ...), custom_call_target="tpu_custom_call" | custom-call | flops 54525952 | bytes 991232 | tf_op jit(solution)/shard_map/expand/pallas_call | solution.py:67
  460.0 8.1 %qkv.3 = (bf16[256,1536]{1,0:T(8,128)(2,1)}, bf16[256,1536]{1,0:T(8,128)(2,1)}) custom-call(bf16[416,7168]{1,0:T(8,128)(2,1)} %get-tuple-element.149.refs_4_.refs_8_.refs_1_.refs_0_, bf16[416,7168]{1,0:T(8,128)(2,1)} %collective-permute-done.19.refs_1_, bf16[416,7168]{1,0:T(8,128)(2,1)} %get-tuple-element.150.refs_9_.refs_1_.refs_2_.refs_3_, ...), custom_call_target="tpu_custom_call" | custom-call | flops 40894464 | bytes 956416 | tf_op jit(solution)/shard_map/qkv/pallas_call | solution.py:67
  469.7 6.7 %collective-permute-start.44 = (bf16[256,2048]{1,0:T(8,128)(2,1)S(1)}, bf16[256,2048]{1,0:T(8,128)(2,1)}, u32[]{:S(2)}, u32[]{:S(2)}) collective-permute-start(bf16[256,2048]{1,0:T(8,128)(2,1)S(1)} %add_convert_fusion.3), channel_id=1, source_target_pairs={{0,1},{3,2},{4,5},{7,6},{8,9},{11,10},{12,13},{15,14},{16,17},{19,... | collective-permute-start | bytes 3145736 | tf_op jit(solution)/shard_map/ppermute | solution.py:843
  488.2 6.0 %project.1 = (bf16[256,1024]{1,0:T(8,128)(2,1)}, bf16[256,1024]{1,0:T(8,128)(2,1)}) custom-call(bf16[416,7168]{1,0:T(8,128)(2,1)} %get-tuple-element.149.refs_4_.refs_8_.refs_1_.refs_0_, bf16[416,7168]{1,0:T(8,128)(2,1)} %collective-permute-done.19.refs_1_, bf16[416,7168]{1,0:T(8,128)(2,1)} %get-tuple-element.150.refs_9_.refs_1_.refs_2_.refs_3_, ...), custom_call_target="tpu_custom_call" | custom-call | flops 27262976 | bytes 894976 | tf_op jit(solution)/shard_map/project/pallas_call | solution.py:67
  498.3 8.0 %collective-permute-start.50 = (bf16[256,1536]{1,0:T(8,128)(2,1)}, bf16[256,1536]{1,0:T(8,128)(2,1)}, u32[]{:S(2)}, u32[]{:S(2)}) collective-permute-start(bf16[256,1536]{1,0:T(8,128)(2,1)} %add_convert_fusion.15), channel_id=1, source_target_pairs={{0,1},{3,2},{4,5},{7,6},{8,9},{11,10},{12,13},{15,14},{16,17},{19,... | collective-permute-start | bytes 2359304 | tf_op jit(solution)/shard_map/ppermute | solution.py:843
  514.9 9.2 %collective-permute-done.49 = bf16[272,1024]{1,0:T(8,128)(2,1)S(1)} collective-permute-done((bf16[272,1024]{1,0:T(8,128)(2,1)S(1)}, bf16[272,1024]{1,0:T(8,128)(2,1)S(1)}, u32[]{:S(2)}, u32[]{:S(2)}) %collective-permute-start.49) | collective-permute-done | bytes 557088 | tf_op jit(solution)/shard_map/ppermute | solution.py:794
  545.3 14.4 %collective-permute-done.55 = bf16[256,2048]{1,0:T(8,128)(2,1)S(1)} collective-permute-done((bf16[256,2048]{1,0:T(8,128)(2,1)S(1)}, bf16[256,2048]{1,0:T(8,128)(2,1)S(1)}, u32[]{:S(2)}, u32[]{:S(2)}) %collective-permute-start.55) | collective-permute-done | bytes 1048608 | tf_op jit(solution)/shard_map/ppermute | solution.py:849
  563.9 12.7 %collective-permute-done.57 = bf16[256,1536]{1,0:T(8,128)(2,1)S(1)} collective-permute-done((bf16[256,1536]{1,0:T(8,128)(2,1)S(1)}, bf16[256,1536]{1,0:T(8,128)(2,1)S(1)}, u32[]{:S(2)}, u32[]{:S(2)}) %collective-permute-start.57) | collective-permute-done | bytes 786464 | tf_op jit(solution)/shard_map/ppermute | solution.py:849
  578.7 8.3 %collective-permute-done.58 = bf16[272,1024]{1,0:T(8,128)(2,1)S(1)} collective-permute-done((bf16[272,1024]{1,0:T(8,128)(2,1)S(1)}, bf16[272,1024]{1,0:T(8,128)(2,1)S(1)}, u32[]{:S(2)}, u32[]{:S(2)}) %collective-permute-start.58) | collective-permute-done | bytes 557088 | tf_op jit(solution)/shard_map/ppermute | solution.py:849
  (307 shorter events, 175.4 us)
Async XLA Ops:
  10.0 45.5 %collective-permute-start.9 = (bf16[128,5120]{1,0:T(8,128)(2,1)}, bf16[128,5120]{1,0:T(8,128)(2,1)}, u32[]{:S(2)}, u32[]{:S(2)}) collective-permute-start(bf16[128,5120]{1,0:T(8,128)(2,1)} %fusion), channel_id=1, source_target_pairs={{0,8},{4,12},{8,0},{12,4},{1,9},{5,13},{9,1},{13,5},{2,10},{6,14},... | collective-permute-start | bytes 3932168 | tf_op jit(solution)/shard_map/ppermute | solution.py:794
  17.1 41.1 %collective-permute-start.8 = (bf16[256,5120]{1,0:T(8,128)(2,1)S(1)}, bf16[256,5120]{1,0:T(8,128)(2,1)}, u32[]{:S(2)}, u32[]{:S(2)}) collective-permute-start(bf16[256,5120]{1,0:T(8,128)(2,1)S(1)} %pad_maximum_fusion.refs_2_.refs_8_.refs_14_.refs_13_.refs_19_.refs_20_.refs_26_.refs_9_.refs_6_), channel_id=1, source_target_pairs={{0,4},{4,0},{8,12},{12,8},{1,5},{5,1},{9,13},{13,9},{2,6},{6,2},{1... | collective-permute-start | bytes 7864328 | tf_op jit(solution)/shard_map/ppermute | solution.py:791
  27.9 27.6 %collective-permute-start.2 = (bf16[128,3072]{1,0:T(8,128)(2,1)S(1)}, bf16[128,3072]{1,0:T(8,128)(2,1)S(1)}, u32[]{:S(2)}, u32[]{:S(2)}) collective-permute-start(bf16[128,3072]{1,0:T(8,128)(2,1)S(1)} %collective-permute-done.refs_3_.refs_4_.refs_27_.refs_34_.refs_14_), channel_id=1, source_target_pairs={{0,1},{1,0},{2,3},{3,2},{4,5},{5,4},{6,7},{7,6},{8,9},{9,8},{10,11... | collective-permute-start | bytes 2359304 | tf_op jit(solution)/shard_map/ppermute | solution.py:797
  55.6 34.4 %collective-permute-start.10 = (bf16[128,5120]{1,0:T(8,128)(2,1)}, bf16[128,5120]{1,0:T(8,128)(2,1)}, u32[]{:S(2)}, u32[]{:S(2)}) collective-permute-start(bf16[128,5120]{1,0:T(8,128)(2,1)} %collective-permute-done.9.refs_4_.refs_10_.refs_16_.refs_15_.refs_21_.refs_22_.refs_28_.refs_11_.refs_8_), channel_id=1, source_target_pairs={{0,1},{1,0},{2,3},{3,2},{4,5},{5,4},{6,7},{7,6},{8,9},{9,8},{10,11... | collective-permute-start | bytes 3932168 | tf_op jit(solution)/shard_map/ppermute | solution.py:797
  57.2 35.9 %collective-permute-start.14 = (bf16[768,1024]{1,0:T(8,128)(2,1)}, bf16[768,1024]{1,0:T(8,128)(2,1)}, u32[]{:S(2)}, u32[]{:S(2)}) collective-permute-start(bf16[768,1024]{1,0:T(8,128)(2,1)} %dynamic-slice_bitcast_fusion), channel_id=1, source_target_pairs={{0,8},{4,12},{8,0},{12,4},{1,9},{5,13},{9,1},{13,5},{2,10},{6,14},... | collective-permute-start | bytes 4718600 | tf_op jit(solution)/shard_map/ppermute | solution.py:794
  58.2 54.3 %collective-permute-start.13 = (bf16[1024,1024]{1,0:T(8,128)(2,1)}, bf16[1024,1024]{1,0:T(8,128)(2,1)}, u32[]{:S(2)}, u32[]{:S(2)}) collective-permute-start(bf16[1024,1024]{1,0:T(8,128)(2,1)} %bitcast.38.refs_2_.refs_7_.refs_14_.refs_3_), channel_id=1, source_target_pairs={{0,4},{4,0},{8,12},{12,8},{1,5},{5,1},{9,13},{13,9},{2,6},{6,2},{1... | collective-permute-start | bytes 6291464 | tf_op jit(solution)/shard_map/ppermute | solution.py:791
  121.4 30.0 %collective-permute-start.18 = (bf16[416,1024]{1,0:T(8,128)(2,1)}, bf16[416,1024]{1,0:T(8,128)(2,1)S(1)}, u32[]{:S(2)}, u32[]{:S(2)}) collective-permute-start(bf16[416,1024]{1,0:T(8,128)(2,1)} %output_forward.4), channel_id=1, source_target_pairs={{0,16},{1,17},{2,18},{3,19},{4,20},{5,21},{6,22},{7,23},{8,24},{9,... | collective-permute-start | bytes 2555912 | tf_op jit(solution)/shard_map/ppermute | solution.py:885
  149.2 67.2 %collective-permute-start.20 = (bf16[416,1024]{1,0:T(8,128)(2,1)}, bf16[416,1024]{1,0:T(8,128)(2,1)}, u32[]{:S(2)}, u32[]{:S(2)}) collective-permute-start(bf16[416,1024]{1,0:T(8,128)(2,1)} %output_forward.5), channel_id=1, source_target_pairs={{0,16},{1,17},{2,18},{3,19},{4,20},{5,21},{6,22},{7,23},{8,24},{9,... | collective-permute-start | bytes 2555912 | tf_op jit(solution)/shard_map/ppermute | solution.py:885
  179.3 104.2 %collective-permute-start.19 = (bf16[416,7168]{1,0:T(8,128)(2,1)}, bf16[416,7168]{1,0:T(8,128)(2,1)}, u32[]{:S(2)}, u32[]{:S(2)}) collective-permute-start(bf16[416,7168]{1,0:T(8,128)(2,1)} %get-tuple-element.149.refs_4_.refs_8_.refs_1_.refs_0_), channel_id=1, source_target_pairs={{0,4},{4,0},{8,12},{12,8},{1,5},{5,1},{9,13},{13,9},{2,6},{6,2},{1... | collective-permute-start | bytes 17891336 | tf_op jit(solution)/shard_map/ppermute | solution.py:791
  215.1 28.9 %collective-permute-start.22 = (bf16[416,1024]{1,0:T(8,128)(2,1)}, bf16[416,1024]{1,0:T(8,128)(2,1)S(1)}, u32[]{:S(2)}, u32[]{:S(2)}) collective-permute-start(bf16[416,1024]{1,0:T(8,128)(2,1)} %get-tuple-element.139), channel_id=1, source_target_pairs={{16,0},{17,1},{18,2},{19,3},{20,4},{21,5},{22,6},{23,7},{24,8},{25... | collective-permute-start | bytes 2555912 | tf_op jit(solution)/shard_map/ppermute | solution.py:885
  216.4 67.1 %collective-permute-start.24 = (bf16[416,9216]{1,0:T(8,128)(2,1)}, bf16[416,9216]{1,0:T(8,128)(2,1)}, u32[]{:S(2)}, u32[]{:S(2)}) collective-permute-start(bf16[416,9216]{1,0:T(8,128)(2,1)} %get-tuple-element.147.refs_5_), channel_id=1, source_target_pairs={{0,4},{4,0},{8,12},{12,8},{1,5},{5,1},{9,13},{13,9},{2,6},{6,2},{1... | collective-permute-start | bytes 23003144 | tf_op jit(solution)/shard_map/ppermute | solution.py:791
  243.9 47.7 %collective-permute-start.21 = (bf16[416,7168]{1,0:T(8,128)(2,1)}, bf16[416,7168]{1,0:T(8,128)(2,1)}, u32[]{:S(2)}, u32[]{:S(2)}) collective-permute-start(bf16[416,7168]{1,0:T(8,128)(2,1)} %get-tuple-element.150.refs_9_.refs_1_.refs_2_.refs_3_), channel_id=1, source_target_pairs={{0,4},{4,0},{8,12},{12,8},{1,5},{5,1},{9,13},{13,9},{2,6},{6,2},{1... | collective-permute-start | bytes 17891336 | tf_op jit(solution)/shard_map/ppermute | solution.py:791
  280.8 27.2 %collective-permute-start.23 = (bf16[416,9216]{1,0:T(8,128)(2,1)}, bf16[416,9216]{1,0:T(8,128)(2,1)}, u32[]{:S(2)}, u32[]{:S(2)}) collective-permute-start(bf16[416,9216]{1,0:T(8,128)(2,1)} %get-tuple-element.146.refs_4_), channel_id=1, source_target_pairs={{0,4},{4,0},{8,12},{12,8},{1,5},{5,1},{9,13},{13,9},{2,6},{6,2},{1... | collective-permute-start | bytes 23003144 | tf_op jit(solution)/shard_map/ppermute | solution.py:791
  317.3 25.5 %collective-permute-start.29 = (bf16[512,1024]{1,0:T(8,128)(2,1)}, bf16[512,1024]{1,0:T(8,128)(2,1)S(1)}, u32[]{:S(2)}, u32[]{:S(2)}) collective-permute-start(bf16[512,1024]{1,0:T(8,128)(2,1)} %get-tuple-element.159), channel_id=1, source_target_pairs={{0,8},{4,12},{8,0},{12,4},{1,9},{5,13},{9,1},{13,5},{2,10},{6,14},... | collective-permute-start | bytes 3145736 | tf_op jit(solution)/shard_map/ppermute | solution.py:794
  343.2 38.2 %collective-permute-start.31 = (bf16[512,1024]{1,0:T(8,128)(2,1)S(1)}, bf16[512,1024]{1,0:T(8,128)(2,1)S(1)}, u32[]{:S(2)}, u32[]{:S(2)}) collective-permute-start(bf16[512,1024]{1,0:T(8,128)(2,1)S(1)} %add_convert_fusion.11), channel_id=1, source_target_pairs={{0,1},{3,2},{4,5},{7,6},{8,9},{11,10},{12,13},{15,14},{16,17},{19,... | collective-permute-start | bytes 3145736 | tf_op jit(solution)/shard_map/ppermute | solution.py:843
  355.3 27.6 %collective-permute-start.32 = (bf16[512,1024]{1,0:T(8,128)(2,1)}, bf16[512,1024]{1,0:T(8,128)(2,1)}, u32[]{:S(2)}, u32[]{:S(2)}) collective-permute-start(bf16[512,1024]{1,0:T(8,128)(2,1)} %get-tuple-element.168), channel_id=1, source_target_pairs={{0,8},{4,12},{8,0},{12,4},{1,9},{5,13},{9,1},{13,5},{2,10},{6,14},... | collective-permute-start | bytes 3145736 | tf_op jit(solution)/shard_map/ppermute | solution.py:794
  387.0 33.8 %collective-permute-start.34 = (bf16[512,1024]{1,0:T(8,128)(2,1)}, bf16[512,1024]{1,0:T(8,128)(2,1)}, u32[]{:S(2)}, u32[]{:S(2)}) collective-permute-start(bf16[512,1024]{1,0:T(8,128)(2,1)} %add_convert_fusion.10), channel_id=1, source_target_pairs={{1,2},{2,1},{5,6},{6,5},{9,10},{10,9},{13,14},{14,13},{17,18},{18,... | collective-permute-start | bytes 3145736 | tf_op jit(solution)/shard_map/ppermute | solution.py:846
  397.7 26.8 %collective-permute-start.35 = (bf16[256,2048]{1,0:T(8,128)(2,1)}, bf16[256,2048]{1,0:T(8,128)(2,1)}, u32[]{:S(2)}, u32[]{:S(2)}) collective-permute-start(bf16[256,2048]{1,0:T(8,128)(2,1)} %get-tuple-element.176), channel_id=1, source_target_pairs={{0,8},{4,12},{8,0},{12,4},{1,9},{5,13},{9,1},{13,5},{2,10},{6,14},... | collective-permute-start | bytes 3145736 | tf_op jit(solution)/shard_map/ppermute | solution.py:794
  409.6 42.7 %collective-permute-start.37 = (bf16[512,1024]{1,0:T(8,128)(2,1)S(1)}, bf16[512,1024]{1,0:T(8,128)(2,1)}, u32[]{:S(2)}, u32[]{:S(2)}) collective-permute-start(bf16[512,1024]{1,0:T(8,128)(2,1)S(1)} %add_convert_fusion.8), channel_id=1, source_target_pairs={{1,2},{2,1},{5,6},{6,5},{9,10},{10,9},{13,14},{14,13},{17,18},{18,... | collective-permute-start | bytes 3145736 | tf_op jit(solution)/shard_map/ppermute | solution.py:846
  426.1 30.0 %collective-permute-start.38 = (bf16[256,2048]{1,0:T(8,128)(2,1)S(1)}, bf16[256,2048]{1,0:T(8,128)(2,1)}, u32[]{:S(2)}, u32[]{:S(2)}) collective-permute-start(bf16[256,2048]{1,0:T(8,128)(2,1)S(1)} %add_convert_fusion.6), channel_id=1, source_target_pairs={{0,1},{3,2},{4,5},{7,6},{8,9},{11,10},{12,13},{15,14},{16,17},{19,... | collective-permute-start | bytes 3145736 | tf_op jit(solution)/shard_map/ppermute | solution.py:843
  433.6 26.3 %collective-permute-start.39 = (bf16[512,1024]{1,0:T(8,128)(2,1)S(1)}, bf16[512,1024]{1,0:T(8,128)(2,1)S(1)}, u32[]{:S(2)}, u32[]{:S(2)}) collective-permute-start(bf16[512,1024]{1,0:T(8,128)(2,1)S(1)} %add_convert_fusion.7), channel_id=1, source_target_pairs={{1,0},{2,3},{5,4},{6,7},{9,8},{10,11},{13,12},{14,15},{17,16},{18,... | collective-permute-start | bytes 3145736 | tf_op jit(solution)/shard_map/ppermute | solution.py:849
  446.8 31.2 %collective-permute-start.41 = (bf16[256,1536]{1,0:T(8,128)(2,1)}, bf16[256,1536]{1,0:T(8,128)(2,1)}, u32[]{:S(2)}, u32[]{:S(2)}) collective-permute-start(bf16[256,1536]{1,0:T(8,128)(2,1)} %add_convert_fusion.17), channel_id=1, source_target_pairs={{0,1},{3,2},{4,5},{7,6},{8,9},{11,10},{12,13},{15,14},{16,17},{19,... | collective-permute-start | bytes 2359304 | tf_op jit(solution)/shard_map/ppermute | solution.py:843
  454.8 26.6 %collective-permute-start.42 = (bf16[512,1024]{1,0:T(8,128)(2,1)}, bf16[512,1024]{1,0:T(8,128)(2,1)}, u32[]{:S(2)}, u32[]{:S(2)}) collective-permute-start(bf16[512,1024]{1,0:T(8,128)(2,1)} %add_convert_fusion.5), channel_id=1, source_target_pairs={{1,0},{2,3},{5,4},{6,7},{9,8},{10,11},{13,12},{14,15},{17,16},{18,... | collective-permute-start | bytes 3145736 | tf_op jit(solution)/shard_map/ppermute | solution.py:849
  457.8 27.5 %collective-permute-start.43 = (bf16[256,2048]{1,0:T(8,128)(2,1)S(1)}, bf16[256,2048]{1,0:T(8,128)(2,1)}, u32[]{:S(2)}, u32[]{:S(2)}) collective-permute-start(bf16[256,2048]{1,0:T(8,128)(2,1)S(1)} %add_convert_fusion.4), channel_id=1, source_target_pairs={{1,2},{2,1},{5,6},{6,5},{9,10},{10,9},{13,14},{14,13},{17,18},{18,... | collective-permute-start | bytes 3145736 | tf_op jit(solution)/shard_map/ppermute | solution.py:846
  469.7 24.6 %collective-permute-start.44 = (bf16[256,2048]{1,0:T(8,128)(2,1)S(1)}, bf16[256,2048]{1,0:T(8,128)(2,1)}, u32[]{:S(2)}, u32[]{:S(2)}) collective-permute-start(bf16[256,2048]{1,0:T(8,128)(2,1)S(1)} %add_convert_fusion.3), channel_id=1, source_target_pairs={{0,1},{3,2},{4,5},{7,6},{8,9},{11,10},{12,13},{15,14},{16,17},{19,... | collective-permute-start | bytes 3145736 | tf_op jit(solution)/shard_map/ppermute | solution.py:843
  479.5 31.4 %collective-permute-start.47 = (bf16[256,1536]{1,0:T(8,128)(2,1)S(1)}, bf16[256,1536]{1,0:T(8,128)(2,1)}, u32[]{:S(2)}, u32[]{:S(2)}) collective-permute-start(bf16[256,1536]{1,0:T(8,128)(2,1)S(1)} %add_convert_fusion.16), channel_id=1, source_target_pairs={{1,2},{2,1},{5,6},{6,5},{9,10},{10,9},{13,14},{14,13},{17,18},{18,... | collective-permute-start | bytes 2359304 | tf_op jit(solution)/shard_map/ppermute | solution.py:846
  486.9 26.6 %collective-permute-start.48 = (bf16[256,2048]{1,0:T(8,128)(2,1)S(1)}, bf16[256,2048]{1,0:T(8,128)(2,1)}, u32[]{:S(2)}, u32[]{:S(2)}) collective-permute-start(bf16[256,2048]{1,0:T(8,128)(2,1)S(1)} %add_convert_fusion.2), channel_id=1, source_target_pairs={{1,0},{2,3},{5,4},{6,7},{9,8},{10,11},{13,12},{14,15},{17,16},{18,... | collective-permute-start | bytes 3145736 | tf_op jit(solution)/shard_map/ppermute | solution.py:849
  498.3 27.3 %collective-permute-start.50 = (bf16[256,1536]{1,0:T(8,128)(2,1)}, bf16[256,1536]{1,0:T(8,128)(2,1)}, u32[]{:S(2)}, u32[]{:S(2)}) collective-permute-start(bf16[256,1536]{1,0:T(8,128)(2,1)} %add_convert_fusion.15), channel_id=1, source_target_pairs={{0,1},{3,2},{4,5},{7,6},{8,9},{11,10},{12,13},{15,14},{16,17},{19,... | collective-permute-start | bytes 2359304 | tf_op jit(solution)/shard_map/ppermute | solution.py:843
  529.8 29.9 %collective-permute-start.55 = (bf16[256,2048]{1,0:T(8,128)(2,1)S(1)}, bf16[256,2048]{1,0:T(8,128)(2,1)S(1)}, u32[]{:S(2)}, u32[]{:S(2)}) collective-permute-start(bf16[256,2048]{1,0:T(8,128)(2,1)S(1)} %add_convert_fusion), channel_id=1, source_target_pairs={{1,0},{2,3},{5,4},{6,7},{9,8},{10,11},{13,12},{14,15},{17,16},{18,... | collective-permute-start | bytes 3145736 | tf_op jit(solution)/shard_map/ppermute | solution.py:849
  537.4 24.9 %collective-permute-start.56 = (bf16[272,1024]{1,0:T(8,128)(2,1)S(1)}, bf16[272,1024]{1,0:T(8,128)(2,1)S(1)}, u32[]{:S(2)}, u32[]{:S(2)}) collective-permute-start(bf16[272,1024]{1,0:T(8,128)(2,1)S(1)} %add_convert_fusion.19), channel_id=1, source_target_pairs={{1,2},{2,1},{5,6},{6,5},{9,10},{10,9},{13,14},{14,13},{17,18},{18,... | collective-permute-start | bytes 1671176 | tf_op jit(solution)/shard_map/ppermute | solution.py:846
  544.0 32.6 %collective-permute-start.57 = (bf16[256,1536]{1,0:T(8,128)(2,1)S(1)}, bf16[256,1536]{1,0:T(8,128)(2,1)S(1)}, u32[]{:S(2)}, u32[]{:S(2)}) collective-permute-start(bf16[256,1536]{1,0:T(8,128)(2,1)S(1)} %add_convert_fusion.12), channel_id=1, source_target_pairs={{1,0},{2,3},{5,4},{6,7},{9,8},{10,11},{13,12},{14,15},{17,16},{18,... | collective-permute-start | bytes 2359304 | tf_op jit(solution)/shard_map/ppermute | solution.py:849
  562.6 24.4 %collective-permute-start.58 = (bf16[272,1024]{1,0:T(8,128)(2,1)S(1)}, bf16[272,1024]{1,0:T(8,128)(2,1)S(1)}, u32[]{:S(2)}, u32[]{:S(2)}) collective-permute-start(bf16[272,1024]{1,0:T(8,128)(2,1)S(1)} %add_convert_fusion.18), channel_id=1, source_target_pairs={{1,0},{2,3},{5,4},{6,7},{9,8},{10,11},{13,12},{14,15},{17,16},{18,... | collective-permute-start | bytes 1671176 | tf_op jit(solution)/shard_map/ppermute | solution.py:849
  (74 other events, 762.8 us)
